TPU v7x, 32 devices: a whole 2x2x4 slice. The times are simulated.
32 devices in a mesh: frame: 8 (over z, x), row: 4 (over y, core).
Axes of the slice: x: 2, y: 2, z: 4, core: 2. Of those that a mesh axis runs over, the one named last changes fastest.
Arguments:
- block_input: bfloat16 [4096, 1024], P(('frame', 'row')), may hold values from -6 to 6
- cotangent: bfloat16 [4096, 1024], P(('frame', 'row')), may hold values from -6 to 6
- frame_lengths: int32 [8], replicated, may hold values from 170 to 512, as said below
- frame_scenes: int32 [8], replicated, may hold values from 0 to 1, as said below
- qkv_weight: bfloat16 [2, 1024, 3, 1024], P(None, 'frame', None, 'row'), may hold values from -0.1875 to 0.1875
- out_weight: bfloat16 [2, 1024, 1024], P(None, 'row', 'frame')
- up_weight: bfloat16 [2, 1024, 4096], P(None, 'frame', 'row'), may hold values from -0.1875 to 0.1875
- down_weight: bfloat16 [2, 4096, 1024], P(None, 'row', 'frame'), may hold values from -0.09375 to 0.09375
- block_gains: bfloat16 [2, 6, 1024], P(None, None, 'frame'), may hold values from 0.25 to 1.75
Outputs:
- block_output: bfloat16 [4096, 1024], P(('frame', 'row'))
- input_grad: bfloat16 [4096, 1024], P(('frame', 'row'))
- qkv_grad: float32 [2, 1024, 3, 1024], P(None, 'frame', None, 'row')
- out_grad: float32 [2, 1024, 1024], P(None, 'row', 'frame')
- up_grad: float32 [2, 1024, 4096], P(None, 'frame', 'row')
- down_grad: float32 [2, 4096, 1024], P(None, 'row', 'frame')
- gains_grad: float32 [2, 6, 1024], P(None, None, 'frame')
Inputs may be any that keep to these rules, and one draw needn't show every extreme that they name: `frame_lengths`: every draw has a frame of 512 tokens. `frame_scenes`: 4 frames in each scene; frames 0, 4 and 7 are in scene 0.
All inputs are finite; a program needn't handle non-finite values.
Results may differ from a plain program's by a relative error of at most 0.02.
Values may be sent and summed in bfloat16 or wider, within the bound.
No kernel may reach another device: no remote copies, remote signals or barrier semaphores. Data moves between devices by JAX's collectives and lax.ppermute only.
A program may use at most 448 MiB of HBM per device.

v0:
```python
import math

import jax
import jax.numpy as jnp
from jax import lax
from jax.sharding import PartitionSpec as P

HEAD_DIM = 64
FLEN = 512


MASKED = -1e30
EPSILON = 1e-06


def layer_norm(values, gain_vec):
    center = values - jnp.mean(values, axis=-1, keepdims=True)
    spread = jnp.mean(center * center, axis=-1, keepdims=True)
    return center * lax.rsqrt(spread + EPSILON) * gain_vec


def head_norm(values, gain_vec):
    shaped = values.reshape(values.shape[0], -1, HEAD_DIM)
    return layer_norm(shaped, gain_vec.reshape(-1, HEAD_DIM)).reshape(values.shape)


def exact_gelu(values):
    return jax.nn.gelu(values, approximate=False)


def lookup(small_table, indices):
    matches = indices[:, None] == jnp.arange(small_table.shape[0], dtype=jnp.int32)[None, :]
    return jnp.sum(jnp.where(matches, small_table[None, :], 0), axis=1)


def row_facts(offset, row_span, lengths, scenes):
    indices = offset + jnp.arange(row_span, dtype=jnp.int32)
    frame_ids = indices // FLEN
    inside = indices - frame_ids * FLEN
    return (inside < lookup(lengths, frame_ids), lookup(scenes, frame_ids))


def by_heads(values):
    return values.reshape(values.shape[0], -1, HEAD_DIM)


def split_rows(values, pieces):
    return values.reshape(values.shape[0], pieces, -1)


def merge_heads(values):
    return jnp.swapaxes(values, 0, 1).reshape(values.shape[1], -1)


def initial_state(row_count, head_count):
    return (
        jnp.full((head_count, row_count), MASKED, jnp.float32),
        jnp.zeros((head_count, row_count), jnp.float32),
        jnp.zeros((head_count, row_count, HEAD_DIM), jnp.float32),
    )


def zero_grads(row_count, head_count):
    blank = jnp.zeros((head_count, row_count, HEAD_DIM), jnp.float32)
    return (blank, blank, blank)


def forward_fold(queries, my_scene, lengths, scenes):
    scaling = HEAD_DIM ** (-0.5)

    def absorb(running, portion, offset):
        key_rows, value_rows = portion
        row_total = key_rows.shape[0]
        block_rows = math.gcd(row_total, 512)
        live_keys, key_scene = row_facts(offset, row_total, lengths, scenes)
        usable = (live_keys & (key_scene == my_scene)).reshape(-1, block_rows)
        key_blocks = key_rows.reshape(row_total // block_rows, block_rows, -1, HEAD_DIM)
        value_blocks = value_rows.reshape(row_total // block_rows, block_rows, -1, HEAD_DIM)

        def compute(carried, key_block, value_block, usable_block):
            running_max, summed, accumulated = carried
            scores = (
                jnp.einsum("qhd,khd->hqk", queries, key_block, preferred_element_type=jnp.float32)
                * scaling
            )
            scores = jnp.where(usable_block[None, None, :], scores, MASKED)
            new_max = jnp.maximum(running_max, jnp.max(scores, axis=-1))
            factor = jnp.exp(running_max - new_max)
            exponentials = jnp.exp(scores - new_max[:, :, None])
            summed = summed * factor + jnp.sum(exponentials, axis=-1)
            accumulated = accumulated * factor[:, :, None] + jnp.einsum(
                "hqk,khd->hqd",
                exponentials.astype(jnp.bfloat16),
                value_block,
                preferred_element_type=jnp.float32,
            )
            return (new_max, summed, accumulated)

        def step(carried, operands):
            key_block, value_block, usable_block = operands
            carried = lax.cond(
                jnp.any(usable_block),
                lambda carried_in: compute(carried_in, key_block, value_block, usable_block),
                lambda carried_in: carried_in,
                carried,
            )
            return (carried, None)

        running, unused = lax.scan(step, running, (key_blocks, value_blocks, usable))
        return running

    return absorb


def finish_forward(running):
    running_max, summed, accumulated = running
    attended = merge_heads(accumulated / summed[:, :, None]).astype(jnp.bfloat16)
    return (attended, running_max + jnp.log(summed))


def backward_fold(mine, tables, my_live, my_scene, lengths, scenes):
    queries, grads_out, key_rows, value_rows, log_total, deltas = mine
    log_table, delta_table = tables
    scaling = HEAD_DIM ** (-0.5)

    def absorb(running, portion, offset):
        piece_rows = portion[0].shape[0]
        block_rows = math.gcd(piece_rows, 512)
        count_blocks = piece_rows // block_rows
        live_keys, key_scene = row_facts(offset, piece_rows, lengths, scenes)
        same_scene = key_scene == my_scene
        blocks = tuple(
            (member.reshape(count_blocks, block_rows, -1, HEAD_DIM) for member in portion)
        )

        def compute(carried, operands):
            other_q, other_grad, other_keys, other_values, other_live, other_same, block_index = (
                operands
            )
            grad_q, grad_k, grad_v = carried
            first_row = block_index * block_rows
            other_log = lax.dynamic_slice_in_dim(log_table, first_row, block_rows, 0).T
            other_delta = lax.dynamic_slice_in_dim(delta_table, first_row, block_rows, 0).T
            scores = (
                jnp.einsum("qhd,khd->hqk", queries, other_keys, preferred_element_type=jnp.float32)
                * scaling
            )
            scores = jnp.where((other_live & other_same)[None, None, :], scores, MASKED)
            probs_mine = jnp.exp(scores - log_total[:, :, None])
            grad_probs = jnp.einsum(
                "qhd,khd->hqk", grads_out, other_values, preferred_element_type=jnp.float32
            )
            grad_scores = (probs_mine * (grad_probs - deltas[:, :, None])).astype(jnp.bfloat16)
            grad_q = (
                grad_q
                + jnp.einsum(
                    "hqk,khd->hqd", grad_scores, other_keys, preferred_element_type=jnp.float32
                )
                * scaling
            )
            back_scores = (
                jnp.einsum("phd,khd->hpk", other_q, key_rows, preferred_element_type=jnp.float32)
                * scaling
            )
            back_scores = jnp.where(
                other_same[None, :, None] & my_live[None, None, :], back_scores, MASKED
            )
            back_probs = jnp.exp(back_scores - other_log[:, :, None])
            grad_v = grad_v + jnp.einsum(
                "hpk,phd->hkd",
                back_probs.astype(jnp.bfloat16),
                other_grad,
                preferred_element_type=jnp.float32,
            )
            back_grad = jnp.einsum(
                "phd,khd->hpk", other_grad, value_rows, preferred_element_type=jnp.float32
            )
            back_steep = (back_probs * (back_grad - other_delta[:, :, None])).astype(jnp.bfloat16)
            grad_k = (
                grad_k
                + jnp.einsum(
                    "hpk,phd->hkd", back_steep, other_q, preferred_element_type=jnp.float32
                )
                * scaling
            )
            return (grad_q, grad_k, grad_v)

        def step(carried, operands):
            carried = lax.cond(
                jnp.any(operands[5]),
                lambda carried_in: compute(carried_in, operands),
                lambda carried_in: carried_in,
                carried,
            )
            return (carried, None)

        xs_list = blocks + (
            live_keys.reshape(count_blocks, block_rows),
            same_scene.reshape(count_blocks, block_rows),
            jnp.arange(count_blocks, dtype=jnp.int32),
        )
        running, unused = lax.scan(step, running, xs_list)
        return running

    return absorb


def frame_forward(queries, keys_all, values_all, key_live):
    scaling = HEAD_DIM ** (-0.5)
    scores = (
        jnp.einsum("qhd,khd->hqk", queries, keys_all, preferred_element_type=jnp.float32) * scaling
    )
    scores = jnp.where(key_live[None, None, :], scores, MASKED)
    row_max = jnp.max(scores, axis=-1, keepdims=True)
    exponentials = jnp.exp(scores - row_max)
    summed = jnp.sum(exponentials, axis=-1, keepdims=True)
    weights_low = (exponentials / summed).astype(jnp.bfloat16)
    attended = jnp.einsum(
        "hqk,khd->qhd", weights_low, values_all, preferred_element_type=jnp.float32
    )
    attended = attended.reshape(attended.shape[0], -1).astype(jnp.bfloat16)
    return (attended, (row_max + jnp.log(summed))[:, :, 0])


def frame_backward(queries, grads_out, attended, log_total, keys_all, values_all, key_live):
    scaling = HEAD_DIM ** (-0.5)
    row_total = queries.shape[0]
    scores = (
        jnp.einsum("qhd,khd->hqk", queries, keys_all, preferred_element_type=jnp.float32) * scaling
    )
    scores = jnp.where(key_live[None, None, :], scores, MASKED)
    probs = jnp.exp(scores - log_total[:, :, None])
    deltas = jnp.einsum("qhd,qhd->hq", grads_out, attended, preferred_element_type=jnp.float32)
    grad_probs = jnp.einsum(
        "qhd,khd->hqk", grads_out, values_all, preferred_element_type=jnp.float32
    )
    grad_scores = (probs * (grad_probs - deltas[:, :, None])).astype(jnp.bfloat16)
    grad_q = (
        jnp.einsum("hqk,khd->qhd", grad_scores, keys_all, preferred_element_type=jnp.float32)
        * scaling
    )
    grad_k = (
        jnp.einsum("hqk,qhd->khd", grad_scores, queries, preferred_element_type=jnp.float32)
        * scaling
    )
    grad_v = jnp.einsum(
        "hqk,qhd->khd", probs.astype(jnp.bfloat16), grads_out, preferred_element_type=jnp.float32
    )
    return (
        grad_q.reshape(row_total, -1),
        grad_k.reshape(row_total, -1),
        grad_v.reshape(row_total, -1),
    )


def attention_forward(block_id, head_q, head_k, head_v, frame_live, my_scene, lengths, scenes):
    if block_id == 0:
        return frame_forward(by_heads(head_q), by_heads(head_k), by_heads(head_v), frame_live)
    head_count = head_q.shape[1] // HEAD_DIM
    absorb = forward_fold(by_heads(head_q), my_scene, lengths, scenes)
    running = absorb(
        initial_state(head_q.shape[0], head_count),
        (
            lax.all_gather(head_k, "frame", axis=0, tiled=True),
            lax.all_gather(head_v, "frame", axis=0, tiled=True),
        ),
        jnp.int32(0),
    )
    return finish_forward(running)


def attention_backward(
    block_id,
    head_q,
    head_k,
    head_v,
    head_attended,
    head_grad,
    log_total,
    frame_live,
    my_scene,
    lengths,
    scenes,
):
    if block_id == 0:
        return frame_backward(
            by_heads(head_q),
            by_heads(head_grad),
            by_heads(head_attended),
            log_total,
            by_heads(head_k),
            by_heads(head_v),
            frame_live,
        )
    head_count = head_q.shape[1] // HEAD_DIM
    deltas = jnp.einsum(
        "qhd,qhd->qh",
        by_heads(head_grad),
        by_heads(head_attended),
        preferred_element_type=jnp.float32,
    )
    tables = (
        lax.all_gather(log_total.T, "frame", axis=0, tiled=True),
        lax.all_gather(deltas, "frame", axis=0, tiled=True),
    )
    mine = (
        by_heads(head_q),
        by_heads(head_grad),
        by_heads(head_k),
        by_heads(head_v),
        log_total,
        deltas.T,
    )
    absorb = backward_fold(mine, tables, frame_live, my_scene, lengths, scenes)
    summed = absorb(
        zero_grads(head_q.shape[0], head_count),
        (
            lax.all_gather(head_q, "frame", axis=0, tiled=True),
            lax.all_gather(head_grad, "frame", axis=0, tiled=True),
            lax.all_gather(head_k, "frame", axis=0, tiled=True),
            lax.all_gather(head_v, "frame", axis=0, tiled=True),
        ),
        jnp.int32(0),
    )
    return (merge_heads(summed[0]), merge_heads(summed[1]), merge_heads(summed[2]))


def project_in(hidden, qkv_full, gain_rows):
    model_width = hidden.shape[1]
    normed = layer_norm(hidden, gain_rows[0]).astype(jnp.bfloat16)
    projected = jnp.dot(normed, qkv_full, preferred_element_type=jnp.float32)
    queries = head_norm(projected[:, :model_width], gain_rows[4]).astype(jnp.bfloat16)
    key_rows = head_norm(projected[:, model_width : 2 * model_width], gain_rows[5]).astype(
        jnp.bfloat16
    )
    value_rows = projected[:, 2 * model_width :].astype(jnp.bfloat16)
    return (normed, projected, queries, key_rows, value_rows)


def project_out(hidden, attended, out_full, up_full, down_full, gain_rows):
    branch = jnp.dot(attended, out_full, preferred_element_type=jnp.float32)
    middle = hidden + gain_rows[2] * branch
    second = layer_norm(middle, gain_rows[1]).astype(jnp.bfloat16)
    up_values = jnp.dot(second, up_full, preferred_element_type=jnp.float32)
    active = exact_gelu(up_values).astype(jnp.bfloat16)
    down_values = jnp.dot(active, down_full, preferred_element_type=jnp.float32)
    return (
        (branch, middle, second, up_values, active, down_values),
        middle + gain_rows[3] * down_values,
    )


def backward_out(grad_result, kept_out, attended, out_full, up_full, down_full, gain_rows):
    branch, middle, second, up_values, active, down_values = kept_out
    scale_two_grad = jnp.sum(grad_result * down_values, axis=0)
    grad_down = (gain_rows[3] * grad_result).astype(jnp.bfloat16)
    down_grad = jnp.einsum("rf,rd->fd", active, grad_down, preferred_element_type=jnp.float32)
    grad_active = jnp.einsum("rd,fd->rf", grad_down, down_full, preferred_element_type=jnp.float32)
    unused, gelu_back = jax.vjp(exact_gelu, up_values)
    grad_up = gelu_back(grad_active)[0].astype(jnp.bfloat16)
    up_grad = jnp.einsum("rd,rf->df", second, grad_up, preferred_element_type=jnp.float32)
    grad_second = jnp.einsum("rf,df->rd", grad_up, up_full, preferred_element_type=jnp.float32)
    unused, norm_back = jax.vjp(layer_norm, middle, gain_rows[1])
    grad_norm_in, norm_two_grad = norm_back(grad_second)
    grad_middle = grad_result + grad_norm_in
    scale_one_grad = jnp.sum(grad_middle * branch, axis=0)
    grad_branch = (gain_rows[2] * grad_middle).astype(jnp.bfloat16)
    out_grad = jnp.einsum("rd,re->de", attended, grad_branch, preferred_element_type=jnp.float32)
    grad_attended = jnp.einsum(
        "re,de->rd", grad_branch, out_full, preferred_element_type=jnp.float32
    ).astype(jnp.bfloat16)
    return (
        grad_middle,
        grad_attended,
        out_grad,
        up_grad,
        down_grad,
        (norm_two_grad, scale_one_grad, scale_two_grad),
    )


def backward_in(
    grad_middle, grad_q, grad_k, grad_v, hidden, normed, projected, qkv_full, gain_rows
):
    model_width = hidden.shape[1]
    unused, query_back = jax.vjp(head_norm, projected[:, :model_width], gain_rows[4])
    grad_q_in, query_gain_grad = query_back(grad_q)
    unused, key_back = jax.vjp(head_norm, projected[:, model_width : 2 * model_width], gain_rows[5])
    grad_k_in, key_gain_grad = key_back(grad_k)
    grad_mixed = jnp.concatenate([grad_q_in, grad_k_in, grad_v], axis=1).astype(jnp.bfloat16)
    qkv_grad = jnp.einsum("rd,re->de", normed, grad_mixed, preferred_element_type=jnp.float32)
    grad_normed = jnp.einsum("re,de->rd", grad_mixed, qkv_full, preferred_element_type=jnp.float32)
    unused, norm_back = jax.vjp(layer_norm, hidden, gain_rows[0])
    grad_hidden_in, norm_one_grad = norm_back(grad_normed)
    return (grad_middle + grad_hidden_in, qkv_grad, norm_one_grad, query_gain_grad, key_gain_grad)


def per_device(
    block_input,
    cotangent,
    frame_lengths,
    frame_scenes,
    qkv_weight,
    out_weight,
    up_weight,
    down_weight,
    block_gains,
):
    row_count = block_input.shape[0]
    model_width = block_input.shape[1]
    row_devices = lax.axis_size("row")
    frame_rows = row_count * row_devices
    my_frame = lax.axis_index("frame")
    my_row = lax.axis_index("row")
    frame_first = my_frame * frame_rows
    token_first = frame_first + my_row * row_count
    row_live, row_scene = row_facts(token_first, row_count, frame_lengths, frame_scenes)
    frame_live = row_facts(frame_first, frame_rows, frame_lengths, frame_scenes)[0]
    my_scene = row_scene[0]
    local = (
        lax.all_gather(qkv_weight, "frame", axis=1, tiled=True),
        lax.all_gather(out_weight, "frame", axis=2, tiled=True),
        lax.all_gather(up_weight, "frame", axis=1, tiled=True),
        lax.all_gather(down_weight, "frame", axis=2, tiled=True),
        lax.all_gather(block_gains, "frame", axis=2, tiled=True),
    )
    whole = (
        lax.all_gather(local[0], "row", axis=3, tiled=True),
        lax.all_gather(local[1], "row", axis=1, tiled=True),
        lax.all_gather(local[2], "row", axis=2, tiled=True),
        lax.all_gather(local[3], "row", axis=1, tiled=True),
    )
    hidden = block_input.astype(jnp.float32)
    stored = []
    for block_id in range(2):
        gain_rows = local[4][block_id].astype(jnp.float32)
        qkv_full = whole[0][block_id].reshape(model_width, -1)
        normed, projected, queries, key_rows, value_rows = project_in(hidden, qkv_full, gain_rows)
        head_q, head_k, head_v = (
            lax.all_to_all(
                split_rows(queries, row_devices), "row", split_axis=1, concat_axis=0, tiled=True
            ),
            lax.all_to_all(
                split_rows(key_rows, row_devices), "row", split_axis=1, concat_axis=0, tiled=True
            ),
            lax.all_to_all(
                split_rows(value_rows, row_devices), "row", split_axis=1, concat_axis=0, tiled=True
            ),
        )
        head_q = head_q.reshape(frame_rows, -1)
        head_k = head_k.reshape(frame_rows, -1)
        head_v = head_v.reshape(frame_rows, -1)
        head_attended, log_total = attention_forward(
            block_id, head_q, head_k, head_v, frame_live, my_scene, frame_lengths, frame_scenes
        )
        attended = lax.all_to_all(
            head_attended.reshape(frame_rows, 1, -1), "row", split_axis=0, concat_axis=1, tiled=True
        ).reshape(row_count, model_width)
        kept_out, result = project_out(
            hidden, attended, whole[1][block_id], whole[2][block_id], whole[3][block_id], gain_rows
        )
        stored.append(
            (
                hidden,
                normed,
                projected,
                head_q,
                head_k,
                head_v,
                head_attended,
                log_total,
                attended,
                kept_out,
            )
        )
        hidden = result
    grad_hidden = cotangent.astype(jnp.float32) * row_live[:, None].astype(jnp.float32)
    shares = [None, None]
    for block_id in (1, 0):
        (
            hidden_in,
            normed,
            projected,
            head_q,
            head_k,
            head_v,
            head_attended,
            log_total,
            attended,
            kept_out,
        ) = stored[block_id]
        gain_rows = local[4][block_id].astype(jnp.float32)
        qkv_full = whole[0][block_id].reshape(model_width, -1)
        grad_middle, grad_attended, out_grad, up_grad, down_grad, late_gains = backward_out(
            grad_hidden,
            kept_out,
            attended,
            whole[1][block_id],
            whole[2][block_id],
            whole[3][block_id],
            gain_rows,
        )
        head_grad = lax.all_to_all(
            split_rows(grad_attended, row_devices), "row", split_axis=1, concat_axis=0, tiled=True
        ).reshape(frame_rows, -1)
        query_part, key_part, value_part = attention_backward(
            block_id,
            head_q,
            head_k,
            head_v,
            head_attended,
            head_grad,
            log_total,
            frame_live,
            my_scene,
            frame_lengths,
            frame_scenes,
        )
        grad_q, grad_k, grad_v = (
            lax.all_to_all(
                query_part.reshape(frame_rows, 1, -1).astype(jnp.bfloat16),
                "row",
                split_axis=0,
                concat_axis=1,
                tiled=True,
            ).astype(jnp.float32),
            lax.all_to_all(
                key_part.reshape(frame_rows, 1, -1).astype(jnp.bfloat16),
                "row",
                split_axis=0,
                concat_axis=1,
                tiled=True,
            ).astype(jnp.float32),
            lax.all_to_all(
                value_part.reshape(frame_rows, 1, -1).astype(jnp.bfloat16),
                "row",
                split_axis=0,
                concat_axis=1,
                tiled=True,
            ).astype(jnp.float32),
        )
        grad_q = grad_q.reshape(row_count, model_width)
        grad_k = grad_k.reshape(row_count, model_width)
        grad_v = grad_v.reshape(row_count, model_width)
        grad_hidden, qkv_grad, norm_one_grad, query_gain_grad, key_gain_grad = backward_in(
            grad_middle, grad_q, grad_k, grad_v, hidden_in, normed, projected, qkv_full, gain_rows
        )
        gains_grad = jnp.stack(
            [
                norm_one_grad,
                late_gains[0],
                late_gains[1],
                late_gains[2],
                query_gain_grad,
                key_gain_grad,
            ]
        )
        row_shares = (
            lax.psum_scatter(
                qkv_grad.reshape(model_width, 3, model_width).astype(jnp.bfloat16),
                "row",
                scatter_dimension=2,
                tiled=True,
            ).astype(jnp.float32),
            lax.psum_scatter(
                out_grad.astype(jnp.bfloat16), "row", scatter_dimension=0, tiled=True
            ).astype(jnp.float32),
            lax.psum_scatter(
                up_grad.astype(jnp.bfloat16), "row", scatter_dimension=1, tiled=True
            ).astype(jnp.float32),
            lax.psum_scatter(
                down_grad.astype(jnp.bfloat16), "row", scatter_dimension=0, tiled=True
            ).astype(jnp.float32),
        )
        gains_total = lax.psum(gains_grad, "row")
        shares[block_id] = (
            lax.psum_scatter(row_shares[0], "frame", scatter_dimension=0, tiled=True),
            lax.psum_scatter(row_shares[1], "frame", scatter_dimension=1, tiled=True),
            lax.psum_scatter(row_shares[2], "frame", scatter_dimension=0, tiled=True),
            lax.psum_scatter(row_shares[3], "frame", scatter_dimension=1, tiled=True),
            lax.psum_scatter(gains_total, "frame", scatter_dimension=1, tiled=True),
        )
    return (
        hidden.astype(jnp.bfloat16),
        grad_hidden.astype(jnp.bfloat16),
        jnp.stack([shares[0][0], shares[1][0]]),
        jnp.stack([shares[0][1], shares[1][1]]),
        jnp.stack([shares[0][2], shares[1][2]]),
        jnp.stack([shares[0][3], shares[1][3]]),
        jnp.stack([shares[0][4], shares[1][4]]),
    )


def solution(mesh):
    return jax.shard_map(
        per_device,
        mesh=mesh,
        in_specs=(
            P(("frame", "row"), None),
            P(("frame", "row"), None),
            P(),
            P(),
            P(None, "frame", None, "row"),
            P(None, "row", "frame"),
            P(None, "frame", "row"),
            P(None, "row", "frame"),
            P(None, None, "frame"),
        ),
        out_specs=(
            P(("frame", "row"), None),
            P(("frame", "row"), None),
            P(None, "frame", None, "row"),
            P(None, "row", "frame"),
            P(None, "frame", "row"),
            P(None, "row", "frame"),
            P(None, None, "frame"),
        ),
        check_vma=False,
    )
```

profile of v0, /device:TPU:0, one launch (start us, length us, event | category | flops | bytes accessed | tf_op | source)
XLA Modules:
  0.0 2414.0 jit_solution(17596910178848751934)
XLA Ops:
  11.3 65.1 %all-gather.13.cloned.1.call-done = bf16[2,1024,3,256]{1,3,2,0:T(8,128)(2,1)} async-done(((bf16[2,128,3,256]{1,3,2,0:T(8,128)(2,1)}), bf16[2,1024,3,256]{1,3,2,0:T(8,128)(2,1)}) %all-gather.13.cloned.1.call-update) | async-done | bytes 3145744 | tf_op jit(solution)/shard_map/all_gather | solution.py:421
  76.5 39.7 %all-gather.17.cloned.1.call-done = bf16[2,256,1024]{2,1,0:T(8,128)(2,1)} async-done(((bf16[2,256,128]{2,1,0:T(8,128)(2,1)}), bf16[2,256,1024]{2,1,0:T(8,128)(2,1)}) %all-gather.17.cloned.1.call-update) | async-done | bytes 1048592 | tf_op jit(solution)/shard_map/all_gather | solution.py:422
  116.3 74.4 %all-gather.21.cloned.1.call-done = bf16[2,1024,1024]{2,1,0:T(8,128)(2,1)} async-done(((bf16[2,128,1024]{2,1,0:T(8,128)(2,1)}), bf16[2,1024,1024]{2,1,0:T(8,128)(2,1)}) %all-gather.21.cloned.1.call-update) | async-done | bytes 4194320 | tf_op jit(solution)/shard_map/all_gather | solution.py:423
  190.8 75.2 %all-gather.25.cloned.1.call-done = bf16[2,1024,1024]{2,1,0:T(8,128)(2,1)} async-done(((bf16[2,1024,128]{2,1,0:T(8,128)(2,1)}), bf16[2,1024,1024]{2,1,0:T(8,128)(2,1)}) %all-gather.25.cloned.1.call-update) | async-done | bytes 4194320 | tf_op jit(solution)/shard_map/all_gather | solution.py:424
  286.0 61.7 %all-gather.15.cloned.1.call-done = bf16[2,1024,3,1024]{1,3,2,0:T(8,128)(2,1)} async-done(((bf16[2,1024,3,256]{1,3,2,0:T(8,128)(2,1)}), bf16[2,1024,3,1024]{1,3,2,0:T(8,128)(2,1)}) %all-gather.15.cloned.1.call-update) | async-done | bytes 12582928 | tf_op jit(solution)/shard_map/all_gather | solution.py:428
  419.0 78.4 %all-gather.23.cloned.1.call-done = bf16[2,1024,4096]{2,1,0:T(8,128)(2,1)} async-done(((bf16[2,1024,1024]{2,1,0:T(8,128)(2,1)}), bf16[2,1024,4096]{2,1,0:T(8,128)(2,1)}) %all-gather.23.cloned.1.call-update) | async-done | bytes 16777232 | tf_op jit(solution)/shard_map/all_gather | solution.py:430
  506.4 98.5 %all-gather.27.cloned.1.call-done = bf16[2,4096,1024]{2,1,0:T(8,128)(2,1)} async-done(((bf16[2,1024,1024]{2,1,0:T(8,128)(2,1)}), bf16[2,4096,1024]{2,1,0:T(8,128)(2,1)}) %all-gather.27.cloned.1.call-update) | async-done | bytes 16777232 | tf_op jit(solution)/shard_map/all_gather | solution.py:431
  701.7 35.8 %all-gather.31.cloned.1.call-done = bf16[4096,256]{1,0:T(8,128)(2,1)} async-done(((bf16[512,256]{1,0:T(8,128)(2,1)}), bf16[4096,256]{1,0:T(8,128)(2,1)}) %all-gather.31.cloned.1.call-update) | async-done | bytes 2097168 | tf_op jit(solution)/shard_map/all_gather | solution.py:265
  752.3 34.4 %while.29 = (s32[]{:T(128)}, f32[4,512]{1,0:T(4,128)S(1)}, f32[4,512]{1,0:T(4,128)S(1)}, f32[4,512,64]{1,2,0:T(8,128)}, pred[8,512]{1,0:T(8,128)(4,1)S(1)}, /*in...) while((s32[]{:T(128)}, f32[4,512]{1,0:T(4,128)S(1)}, ...), condition=%wide.region_26.27_spmd, body=%wide.region_20.26_spmd.sunk | while | flops 280236544 | bytes 18748192 | solution.py:109
  953.2 118.7 %while.30 = (s32[]{:T(128)}, f32[4,512,64]{1,2,0:T(8,128)}, f32[4,512,64]{1,2,0:T(8,128)}, f32[4,512,64]{1,2,0:T(8,128)}, pred[8,512]{1,0:T(8,128)(4,1)S(1)}, /*...) while((s32[]{:T(128)}, f32[4,512,64]{1,2,0:T(8,128)}, ...), condition=%wide.region_36.37_spmd.clone, body=%wide.region_32.36_spmd.clone.sunk | while | flops 957219840 | bytes 27906108 | solution.py:202
  1341.6 70.7 %reduce-scatter.39.cloned.1.call-done = bf16[1024,1024]{1,0:T(8,128)(2,1)} async-done(((bf16[1024,4096]{1,0:T(8,128)(2,1)}), bf16[1024,1024]{1,0:T(8,128)(2,1)}) %reduce-scatter.39.cloned.1.call-update) | async-done | bytes 2097168 | tf_op jit(solution)/shard_map/reduce_scatter | solution.py:568
  1416.5 70.2 %reduce-scatter.35.cloned.1.call-done = bf16[1024,1024]{1,0:T(8,128)(2,1)} async-done(((bf16[1024,4096]{1,0:T(8,128)(2,1)}), bf16[1024,1024]{1,0:T(8,128)(2,1)}) %reduce-scatter.35.cloned.1.call-update) | async-done | bytes 2097168 | tf_op jit(solution)/shard_map/reduce_scatter | solution.py:568
  1490.7 70.2 %reduce-scatter.47.cloned.1.call-done = bf16[1024,1024]{1,0:T(8,128)(2,1)} async-done(((bf16[4096,1024]{1,0:T(8,128)(2,1)}), bf16[1024,1024]{1,0:T(8,128)(2,1)}) %reduce-scatter.47.cloned.1.call-update) | async-done | bytes 2097168 | tf_op jit(solution)/shard_map/reduce_scatter | solution.py:571
  1565.1 70.2 %reduce-scatter.43.cloned.1.call-done = bf16[1024,1024]{1,0:T(8,128)(2,1)} async-done(((bf16[4096,1024]{1,0:T(8,128)(2,1)}), bf16[1024,1024]{1,0:T(8,128)(2,1)}) %reduce-scatter.43.cloned.1.call-update) | async-done | bytes 2097168 | tf_op jit(solution)/shard_map/reduce_scatter | solution.py:571
  1641.4 50.6 %reduce-scatter.53.cloned.1.call-done = f32[6,128]{1,0:T(8,128)} async-done(((f32[6,1024]{1,0:T(8,128)}), f32[6,128]{1,0:T(8,128)}) %reduce-scatter.53.cloned.1.call-update) | async-done | bytes 3088 | tf_op jit(solution)/shard_map/reduce_scatter | solution.py:581
  1692.0 56.3 %reduce-scatter.51.cloned.1.call-done = f32[6,128]{1,0:T(8,128)} async-done(((f32[6,1024]{1,0:T(8,128)}), f32[6,128]{1,0:T(8,128)}) %reduce-scatter.51.cloned.1.call-update) | async-done | bytes 3088 | tf_op jit(solution)/shard_map/reduce_scatter | solution.py:581
  1754.8 60.5 %reduce-scatter.33.cloned.1.call-done = f32[256,128]{1,0:T(8,128)} async-done(((f32[256,1024]{1,0:T(8,128)}), f32[256,128]{1,0:T(8,128)}) %reduce-scatter.33.cloned.1.call-update) | async-done | bytes 131088 | tf_op jit(solution)/shard_map/reduce_scatter | solution.py:578
  1815.3 67.2 %reduce-scatter.29.cloned.1.call-done = f32[256,128]{1,0:T(8,128)} async-done(((f32[256,1024]{1,0:T(8,128)}), f32[256,128]{1,0:T(8,128)}) %reduce-scatter.29.cloned.1.call-update) | async-done | bytes 131088 | tf_op jit(solution)/shard_map/reduce_scatter | solution.py:578
  1884.2 76.0 %reduce-scatter.25.cloned.1.call-done = f32[128,3,256]{0,2,1:T(8,128)} async-done(((f32[1024,3,256]{0,2,1:T(8,128)}), f32[128,3,256]{0,2,1:T(8,128)}) %reduce-scatter.25.cloned.1.call-update) | async-done | bytes 393232 | tf_op jit(solution)/shard_map/reduce_scatter | solution.py:577
  1960.2 77.8 %reduce-scatter.21.cloned.1.call-done = f32[128,3,256]{0,2,1:T(8,128)} async-done(((f32[1024,3,256]{0,2,1:T(8,128)}), f32[128,3,256]{0,2,1:T(8,128)}) %reduce-scatter.21.cloned.1.call-update) | async-done | bytes 393232 | tf_op jit(solution)/shard_map/reduce_scatter | solution.py:577
  2040.3 88.3 %reduce-scatter.41.cloned.1.call-done = f32[128,1024]{1,0:T(8,128)} async-done(((f32[1024,1024]{1,0:T(8,128)}), f32[128,1024]{1,0:T(8,128)}) %reduce-scatter.41.cloned.1.call-update) | async-done | bytes 524304 | tf_op jit(solution)/shard_map/reduce_scatter | solution.py:579
  2128.7 91.9 %reduce-scatter.37.cloned.1.call-done = f32[128,1024]{1,0:T(8,128)} async-done(((f32[1024,1024]{1,0:T(8,128)}), f32[128,1024]{1,0:T(8,128)}) %reduce-scatter.37.cloned.1.call-update) | async-done | bytes 524304 | tf_op jit(solution)/shard_map/reduce_scatter | solution.py:579
  2222.9 89.6 %reduce-scatter.49.cloned.1.call-done = f32[1024,128]{1,0:T(8,128)} async-done(((f32[1024,1024]{1,0:T(8,128)}), f32[1024,128]{1,0:T(8,128)}) %reduce-scatter.49.cloned.1.call-update) | async-done | bytes 524304 | tf_op jit(solution)/shard_map/reduce_scatter | solution.py:580
  2312.5 92.0 %reduce-scatter.45.cloned.1.call-done = f32[1024,128]{1,0:T(8,128)} async-done(((f32[1024,1024]{1,0:T(8,128)}), f32[1024,128]{1,0:T(8,128)}) %reduce-scatter.45.cloned.1.call-update) | async-done | bytes 524304 | tf_op jit(solution)/shard_map/reduce_scatter | solution.py:580
  (849 shorter events, 954.3 us)
Async XLA Ops:
  9.9 180.8 %all-gather.21.cloned.1.call-start = ((), (), s32[]{:S(2)}) async-start(), calls=%async_computation.38 | async-start | bytes 4718592 | tf_op jit(solution)/shard_map/all_gather | solution.py:423
  10.6 255.3 %all-gather.25.cloned.1.call-start = ((), (), s32[]{:S(2)}) async-start(), calls=%async_computation.40 | async-start | bytes 4718592 | tf_op jit(solution)/shard_map/all_gather | solution.py:424
  11.2 336.4 %all-gather.15.cloned.1.call-start = ((), (), s32[]{:S(2)}) async-start(), calls=%async_computation.35 | async-start | bytes 15728640 | tf_op jit(solution)/shard_map/all_gather | solution.py:428
  76.4 339.4 %all-gather.19.cloned.1.call-start = ((), (), s32[]{:S(2)}) async-start(), calls=%async_computation.37 | async-start | bytes 5242880 | tf_op jit(solution)/shard_map/all_gather | solution.py:429
  116.2 381.2 %all-gather.23.cloned.1.call-start = ((), (), s32[]{:S(2)}) async-start(), calls=%async_computation.39 | async-start | bytes 20971520 | tf_op jit(solution)/shard_map/all_gather | solution.py:430
  190.7 414.2 %all-gather.27.cloned.1.call-start = ((), (), s32[]{:S(2)}) async-start(), calls=%async_computation.41 | async-start | bytes 20971520 | tf_op jit(solution)/shard_map/all_gather | solution.py:431
  391.0 296.7 %all-gather.29.cloned.1.call-start = ((), (), s32[]{:S(2)}) async-start(), calls=%async_computation.42 | async-start | bytes 2359296 | tf_op jit(solution)/shard_map/all_gather | solution.py:264
  799.1 137.6 %all-gather.35.cloned.1.call-start = ((), (), s32[]{:S(2)}) async-start(), calls=%async_computation.45 | async-start | bytes 2359296 | tf_op jit(solution)/shard_map/all_gather | solution.py:319
  1083.7 233.5 %reduce-scatter.31.cloned.1.call-start = ((), (), s32[]{:S(2)}) async-start(), calls=%async_computation.52 | async-start | bytes 2621440 | tf_op jit(solution)/shard_map/reduce_scatter | solution.py:565
  1111.7 207.7 %reduce-scatter.27.cloned.1.call-start = ((), (), s32[]{:S(2)}) async-start(), calls=%async_computation.50 | async-start | bytes 2621440 | tf_op jit(solution)/shard_map/reduce_scatter | solution.py:565
  1168.2 153.4 %reduce-scatter.23.cloned.1.call-start = ((), (), s32[]{:S(2)}) async-start(), calls=%async_computation.48 | async-start | bytes 7864320 | tf_op jit(solution)/shard_map/reduce_scatter | solution.py:559
  1288.9 197.7 %reduce-scatter.35.cloned.1.call-start = ((), (), s32[]{:S(2)}) async-start(), calls=%async_computation.54 | async-start | bytes 10485760 | tf_op jit(solution)/shard_map/reduce_scatter | solution.py:568
  1296.2 264.7 %reduce-scatter.47.cloned.1.call-start = ((), (), s32[]{:S(2)}) async-start(), calls=%async_computation.60 | async-start | bytes 10485760 | tf_op jit(solution)/shard_map/reduce_scatter | solution.py:571
  1303.6 331.7 %reduce-scatter.43.cloned.1.call-start = ((), (), s32[]{:S(2)}) async-start(), calls=%async_computation.58 | async-start | bytes 10485760 | tf_op jit(solution)/shard_map/reduce_scatter | solution.py:571
  1310.6 381.4 %reduce-scatter.53.cloned.1.call-start = ((), (), s32[]{:S(2)}) async-start(), calls=%async_computation.63 | async-start | bytes 36864 | tf_op jit(solution)/shard_map/reduce_scatter | solution.py:581
  1312.0 436.3 %reduce-scatter.51.cloned.1.call-start = ((), (), s32[]{:S(2)}) async-start(), calls=%async_computation.62 | async-start | bytes 36864 | tf_op jit(solution)/shard_map/reduce_scatter | solution.py:581
  1317.1 498.2 %reduce-scatter.33.cloned.1.call-start = ((), (), s32[]{:S(2)}) async-start(), calls=%async_computation.53 | async-start | bytes 1179648 | tf_op jit(solution)/shard_map/reduce_scatter | solution.py:578
  1319.3 563.2 %reduce-scatter.29.cloned.1.call-start = ((), (), s32[]{:S(2)}) async-start(), calls=%async_computation.51 | async-start | bytes 1179648 | tf_op jit(solution)/shard_map/reduce_scatter | solution.py:578
  1321.6 638.7 %reduce-scatter.25.cloned.1.call-start = ((), (), s32[]{:S(2)}) async-start(), calls=%async_computation.49 | async-start | bytes 3538944 | tf_op jit(solution)/shard_map/reduce_scatter | solution.py:577
  1325.2 712.8 %reduce-scatter.21.cloned.1.call-start = ((), (), s32[]{:S(2)}) async-start(), calls=%async_computation.47 | async-start | bytes 3538944 | tf_op jit(solution)/shard_map/reduce_scatter | solution.py:577
  1341.5 787.1 %reduce-scatter.41.cloned.1.call-start = ((), (), s32[]{:S(2)}) async-start(), calls=%async_computation.57 | async-start | bytes 4718592 | tf_op jit(solution)/shard_map/reduce_scatter | solution.py:579
  1416.4 804.2 %reduce-scatter.37.cloned.1.call-start = ((), (), s32[]{:S(2)}) async-start(), calls=%async_computation.55 | async-start | bytes 4718592 | tf_op jit(solution)/shard_map/reduce_scatter | solution.py:579
  1490.7 821.8 %reduce-scatter.49.cloned.1.call-start = ((), (), s32[]{:S(2)}) async-start(), calls=%async_computation.61 | async-start | bytes 4718592 | tf_op jit(solution)/shard_map/reduce_scatter | solution.py:580
  1565.0 839.5 %reduce-scatter.45.cloned.1.call-start = ((), (), s32[]{:S(2)}) async-start(), calls=%async_computation.59 | async-start | bytes 4718592 | tf_op jit(solution)/shard_map/reduce_scatter | solution.py:580
  (194 other events, 5016.7 us)
Sparse Core Ops, SparseCore 0:
  10.6 65.7 all-gather.12
  118.4 72.2 all-gather.20
  192.6 73.2 all-gather.24
  267.3 80.2 all-gather.14
  388.4 108.9 all-gather.22
  499.0 105.9 all-gather.26
  638.3 49.2 all-gather.28
  852.2 48.4 all-gather.34
  1203.7 63.9 reduce-scatter.22
  1281.2 56.7 reduce-scatter.18
  1340.5 71.7 reduce-scatter.38
  1414.9 71.6 reduce-scatter.34
  1489.2 71.7 reduce-scatter.46
  1563.6 71.6 reduce-scatter.42
  1638.4 53.5 reduce-scatter.52
  1695.7 52.5 reduce-scatter.50
  1752.3 62.9 reduce-scatter.32
  1819.5 62.9 reduce-scatter.28
  1886.1 74.0 reduce-scatter.24
  1963.7 74.2 reduce-scatter.20
  2041.5 87.1 reduce-scatter.40
  2132.7 87.8 reduce-scatter.36
  2224.2 88.2 reduce-scatter.48
  2316.4 88.0 reduce-scatter.44
  (6 shorter events, 236.7 us)
where the time goes:
time: 2430 us; the launch traced here: 2410 us
  waiting for transfers between devices  1650 us (68%)
  matrix products  233 us (10%)
  local copies, waits for them, and re-layouts  230 us (9%)
  blocking collectives  126 us (5%)
  other arithmetic  98.3 us (4%)
  starting transfers between devices  46.6 us (2%)
    reduce_scatter x2, waiting for transfers between devices, per_device(): lax.psum_scatter(row_shares[3], 'frame', scatter_dimension=1, tiled=True)  182 us
    reduce_scatter x2, waiting for transfers between devices, per_device(): lax.psum_scatter(row_shares[2], 'frame', scatter_dimension=0, tiled=True)  180 us
    reduce_scatter x2, waiting for transfers between devices, per_device(): lax.psum_scatter(row_shares[0], 'frame', scatter_dimension=0, tiled=True)  154 us
    reduce_scatter x2, waiting for transfers between devices, per_device(): lax.psum_scatter(up_grad.astype(jnp.bfloat16), 'row', scatter_dimension=1...  141 us
    reduce_scatter x2, waiting for transfers between devices, per_device(): lax.psum_scatter(down_grad.astype(jnp.bfloat16), 'row', scatter_dimension...  140 us
    reduce_scatter x2, waiting for transfers between devices, per_device(): lax.psum_scatter(row_shares[1], 'frame', scatter_dimension=1, tiled=True)  128 us
    reduce_scatter x2, waiting for transfers between devices, per_device(): lax.psum_scatter(gains_total, 'frame', scatter_dimension=1, tiled=True)  107 us
    all_gather x1, waiting for transfers between devices, per_device(): lax.all_gather(local[3], 'row', axis=1, tiled=True)  98.5 us
  transfers between devices with their start and end apart: 42, of which 33 were waited for; matrix products, arithmetic and copies ran while one was open for 14% of the time, Pallas kernels for 0%

commit v1 on v0

v1 whole, which is shorter than its diff:
```python
import functools

import jax
import jax.numpy as jnp
from jax import lax
from jax.experimental import pallas as pl
from jax.experimental.pallas import tpu as pltpu
from jax.sharding import PartitionSpec as P

HEAD_DIM = 64
FLEN = 512
EPSILON = 1e-06
F32 = jnp.float32
BF16 = jnp.bfloat16


def ring_split(frames):
    return (4, 2) if frames == 8 else None


def frame_permute(value, frames, down, across):
    rows, cols = ring_split(frames)
    pairs = []
    for z in range(rows):
        for x in range(cols):
            pairs.append((((z + down) % rows) * cols + (x ^ across), z * cols + x))
    return lax.ppermute(value, "frame", pairs)


def row_permute(value, bit):
    return lax.ppermute(value, "row", [(i ^ bit, i) for i in range(4)])


def gather_frame(shard):
    frames = lax.axis_size("frame")
    if ring_split(frames) is None:
        whole = lax.all_gather(shard, "frame", axis=0, tiled=False)
        return [whole[i] for i in range(frames)]
    rows, cols = ring_split(frames)
    blocks = []
    for down in range(rows):
        own = frame_permute(shard, frames, down, 0) if down else shard
        blocks.append(own)
        blocks.append(frame_permute(own, frames, 0, 1))
    return blocks


def scatter_frame(blocks):
    frames = lax.axis_size("frame")
    if ring_split(frames) is None:
        return lax.psum_scatter(jnp.stack(blocks), "frame", scatter_dimension=0, tiled=False).astype(F32)
    rows, cols = ring_split(frames)
    total = None
    for down in list(range(1, rows)) + [0]:
        keep, give = blocks[down * cols], blocks[down * cols + 1]
        both = keep.astype(F32) + frame_permute(give, frames, 0, 1).astype(F32)
        if down:
            both = frame_permute(both.astype(BF16), frames, rows - down, 0).astype(F32)
        total = both if total is None else total + both
    return total


def to_relative(values):
    frames = lax.axis_size("frame")
    if ring_split(frames) is None:
        return values
    rows, cols = ring_split(frames)
    me = lax.axis_index("frame")
    width = values.shape[-1] // frames
    lead = values.shape[:-1]
    twice = jnp.concatenate([values, values], axis=-1)
    turned = lax.dynamic_slice_in_dim(twice, (me // cols) * cols * width, frames * width, -1)
    shaped = turned.reshape(lead + (rows, cols, width))
    swapped = jnp.concatenate([shaped[..., 1:2, :], shaped[..., 0:1, :]], axis=-2)
    return jnp.where(me % cols == 1, swapped, shaped).reshape(values.shape)


def to_absolute(values):
    frames = lax.axis_size("frame")
    if ring_split(frames) is None:
        return values
    rows, cols = ring_split(frames)
    me = lax.axis_index("frame")
    width = values.shape[-1] // frames
    lead = values.shape[:-1]
    shaped = values.reshape(lead + (rows, cols, width))
    swapped = jnp.concatenate([shaped[..., 1:2, :], shaped[..., 0:1, :]], axis=-2)
    values = jnp.where(me % cols == 1, swapped, shaped).reshape(values.shape)
    twice = jnp.concatenate([values, values], axis=-1)
    start = ((rows - me // cols) % rows) * cols * width
    return lax.dynamic_slice_in_dim(twice, start, frames * width, -1)


def relative_frames():
    frames = lax.axis_size("frame")
    if ring_split(frames) is None:
        return jnp.arange(frames, dtype=jnp.int32)
    rows, cols = ring_split(frames)
    me = lax.axis_index("frame")
    places = jnp.arange(frames, dtype=jnp.int32)
    return ((me // cols + places // cols) % rows) * cols + ((me % cols) ^ (places % cols))


def gather_rows(own):
    across = row_permute(own, 2)
    near = jnp.concatenate([own, row_permute(own, 1)], axis=0)
    far = jnp.concatenate([across, row_permute(across, 1)], axis=0)
    return near, far


def scatter_rows(near, far):
    count = near.shape[0] // 2
    far_sum = far[:count] + row_permute(far[count:].astype(BF16), 1).astype(F32)
    far_in = row_permute(far_sum.astype(BF16), 2).astype(F32)
    near_sum = near[:count] + row_permute(near[count:].astype(BF16), 1).astype(F32)
    return near_sum + far_in


def head_mask(shape, head):
    lanes = lax.broadcasted_iota(jnp.int32, shape, len(shape) - 1)
    return (lanes // HEAD_DIM) == head


def dot_nt(a, b):
    return lax.dot_general(a, b, (((1,), (1,)), ((), ())), preferred_element_type=F32)


def dot_nn(a, b):
    return lax.dot_general(a, b, (((1,), (0,)), ((), ())), preferred_element_type=F32)


def live_rows(place_ref, lens_ref, block, count):
    slots = lax.broadcasted_iota(jnp.int32, (count, 1), 0) ^ (place_ref[0] * (count // 4))
    return slots < lens_ref[block]


def forward_kernel(table_ref, lens_ref, place_ref, q_ref, k_ref, v_ref, out_ref, lse_ref, acc, sums):
    step = pl.program_id(0)
    count, width = q_ref.shape
    heads = width // HEAD_DIM

    @pl.when(step == 0)
    def _():
        acc[...] = jnp.zeros_like(acc)
        sums[...] = jnp.zeros_like(sums)

    live = live_rows(place_ref, lens_ref, table_ref[step], k_ref.shape[1])
    keys = k_ref[0]
    values_t = v_ref[0].T
    queries = q_ref[...]
    for head in range(heads):
        mine = jnp.where(head_mask(queries.shape, head), queries, 0) * BF16(HEAD_DIM**-0.5)
        scores = dot_nt(keys, mine)
        powers = jnp.where(live, jnp.exp(scores), 0.0)
        sums[head : head + 1, :] += jnp.sum(powers, axis=0, keepdims=True)
        lanes = slice(head * HEAD_DIM, (head + 1) * HEAD_DIM)
        acc[lanes, :] += dot_nn(values_t[lanes, :], powers.astype(BF16))

    @pl.when(step == pl.num_programs(0) - 1)
    def _():
        lse_ref[...] = jnp.log(sums[...])
        for head in range(heads):
            lanes = slice(head * HEAD_DIM, (head + 1) * HEAD_DIM)
            acc[lanes, :] = acc[lanes, :] / sums[head : head + 1, :]
        out_ref[...] = acc[...].T.astype(BF16)


def backward_kernel(
    table_ref, lens_ref, place_ref, q_ref, g_ref, o_ref, lse_ref, k_ref, v_ref, unused_ref, dq_ref, dkv_ref, acc, delta
):
    step = pl.program_id(0)
    count, width = q_ref.shape
    heads = width // HEAD_DIM

    @pl.when(step == 0)
    def _():
        acc[...] = jnp.zeros_like(acc)
        product = g_ref[...].astype(F32) * o_ref[...].astype(F32)
        turned = product.T
        for head in range(heads):
            lanes = slice(head * HEAD_DIM, (head + 1) * HEAD_DIM)
            delta[head : head + 1, :] = jnp.sum(turned[lanes, :], axis=0, keepdims=True)

    live = live_rows(place_ref, lens_ref, table_ref[step], k_ref.shape[1])
    keys = k_ref[0]
    keys_t = keys.T
    values = v_ref[0]
    queries = q_ref[...]
    grads = g_ref[...]
    grad_k = jnp.zeros(keys.shape, F32)
    grad_v = jnp.zeros(keys.shape, F32)
    for head in range(heads):
        inside = head_mask(queries.shape, head)
        mine = jnp.where(inside, queries, 0) * BF16(HEAD_DIM**-0.5)
        mine_g = jnp.where(inside, grads, 0)
        scores = dot_nt(keys, mine)
        full = jnp.where(live, jnp.exp(scores - lse_ref[head : head + 1, :]), 0.0)
        grad_probs = dot_nt(values, mine_g)
        steep = (full * (grad_probs - delta[head : head + 1, :])).astype(BF16)
        grad_v += dot_nn(full.astype(BF16), mine_g)
        grad_k += dot_nn(steep, mine)
        lanes = slice(head * HEAD_DIM, (head + 1) * HEAD_DIM)
        acc[lanes, :] += dot_nn(keys_t[lanes, :], steep)
    dkv_ref[0, :, :width] = grad_k.astype(dkv_ref.dtype)
    dkv_ref[0, :, width:] = grad_v.astype(dkv_ref.dtype)

    @pl.when(step == pl.num_programs(0) - 1)
    def _():
        dq_ref[...] = acc[...].T * (HEAD_DIM**-0.5)


def attend(queries, kv_blocks, table, lens, place):
    count, width = queries.shape
    flen = kv_blocks.shape[1]
    whole = lambda j, t, l, p: (0, 0)
    return pl.pallas_call(
        forward_kernel,
        grid_spec=pltpu.PrefetchScalarGridSpec(
            num_scalar_prefetch=3,
            grid=(table.shape[0],),
            in_specs=[
                pl.BlockSpec((count, width), whole),
                pl.BlockSpec((1, flen, width), lambda j, t, l, p: (t[j], 0, 0)),
                pl.BlockSpec((1, flen, width), lambda j, t, l, p: (t[j], 0, 1)),
            ],
            out_specs=[
                pl.BlockSpec((count, width), whole),
                pl.BlockSpec((8, count), whole),
            ],
            scratch_shapes=[pltpu.VMEM((width, count), F32), pltpu.VMEM((8, count), F32)],
        ),
        out_shape=[
            jax.ShapeDtypeStruct((count, width), BF16),
            jax.ShapeDtypeStruct((8, count), F32),
        ],
        compiler_params=pltpu.CompilerParams(vmem_limit_bytes=48 * 1024 * 1024),
        cost_estimate=pl.CostEstimate(
            flops=4 * count * flen * width * table.shape[0] * 4,
            bytes_accessed=4 * flen * width * table.shape[0],
            transcendentals=count * flen * table.shape[0] * 4,
        ),
    )(table, lens, place, queries, kv_blocks, kv_blocks)


def attend_back(queries, grads, attended, lse, kv_blocks, table, lens, place, dtype):
    count, width = queries.shape
    flen = kv_blocks.shape[1]
    whole = lambda j, t, l, p: (0, 0)
    blank = jnp.zeros(kv_blocks.shape, dtype)
    return pl.pallas_call(
        backward_kernel,
        grid_spec=pltpu.PrefetchScalarGridSpec(
            num_scalar_prefetch=3,
            grid=(table.shape[0],),
            in_specs=[
                pl.BlockSpec((count, width), whole),
                pl.BlockSpec((count, width), whole),
                pl.BlockSpec((count, width), whole),
                pl.BlockSpec((8, count), whole),
                pl.BlockSpec((1, flen, width), lambda j, t, l, p: (t[j], 0, 0)),
                pl.BlockSpec((1, flen, width), lambda j, t, l, p: (t[j], 0, 1)),
                pl.BlockSpec(memory_space=pl.ANY),
            ],
            out_specs=[
                pl.BlockSpec((count, width), whole),
                pl.BlockSpec((1, flen, 2 * width), lambda j, t, l, p: (t[j], 0, 0)),
            ],
            scratch_shapes=[pltpu.VMEM((width, count), F32), pltpu.VMEM((8, count), F32)],
        ),
        out_shape=[
            jax.ShapeDtypeStruct((count, width), F32),
            jax.ShapeDtypeStruct(kv_blocks.shape, dtype),
        ],
        input_output_aliases={9: 1},
        compiler_params=pltpu.CompilerParams(vmem_limit_bytes=48 * 1024 * 1024),
        cost_estimate=pl.CostEstimate(
            flops=10 * count * flen * width * table.shape[0] * 4,
            bytes_accessed=8 * flen * width * table.shape[0],
            transcendentals=count * flen * table.shape[0] * 4,
        ),
    )(table, lens, place, queries, grads, attended, lse, kv_blocks, kv_blocks, blank)


def norm_parts(values):
    center = values - jnp.mean(values, axis=-1, keepdims=True)
    scale = lax.rsqrt(jnp.mean(center * center, axis=-1, keepdims=True) + EPSILON)
    return center * scale, scale


def norm_back(unit, scale, gain, grad):
    inner = grad * gain
    return scale * (
        inner
        - jnp.mean(inner, axis=-1, keepdims=True)
        - unit * jnp.mean(inner * unit, axis=-1, keepdims=True)
    )


def head_means(values):
    width = values.shape[-1]
    ids = jnp.arange(width, dtype=jnp.int32) // HEAD_DIM
    spread = jnp.where(ids[:, None] == ids[None, :], F32(1.0 / HEAD_DIM), F32(0))
    return jnp.dot(values, spread, precision=lax.Precision.HIGHEST, preferred_element_type=F32)


def head_parts(values):
    center = values - head_means(values)
    scale = lax.rsqrt(head_means(center * center) + EPSILON)
    return center * scale, scale


def head_back(unit, scale, gain, grad):
    inner = grad * gain
    return scale * (inner - head_means(inner) - unit * head_means(inner * unit))


def gelu(values):
    return 0.5 * values * (1.0 + lax.erf(values * F32(0.7071067811865476)))


def gelu_slope(values):
    bell = jnp.exp(-0.5 * values * values) * F32(0.3989422804014327)
    return 0.5 * (1.0 + lax.erf(values * F32(0.7071067811865476))) + values * bell


def dot(a, b):
    return jnp.dot(a, b, preferred_element_type=F32)


def dot_t(a, b):
    return lax.dot_general(a, b, (((1,), (1,)), ((), ())), preferred_element_type=F32)


def t_dot(a, b):
    return lax.dot_general(a, b, (((0,), (0,)), ((), ())), preferred_element_type=F32)


def per_device(
    block_input,
    cotangent,
    frame_lengths,
    frame_scenes,
    qkv_weight,
    out_weight,
    up_weight,
    down_weight,
    block_gains,
):
    row_count, model_width = block_input.shape
    frames = lax.axis_size("frame")
    my_frame = lax.axis_index("frame")
    my_row = lax.axis_index("row")
    local_width = qkv_weight.shape[3]
    shard = model_width // frames
    place = my_row.astype(jnp.int32).reshape(1)
    slots = my_row * row_count + jnp.arange(row_count, dtype=jnp.int32)
    row_live = (slots < frame_lengths[my_frame]).astype(F32)

    order = relative_frames()
    rel_lens = frame_lengths[order]
    other = (frame_scenes[order] != frame_scenes[my_frame]).astype(jnp.int32)
    picked = jnp.argsort(other * frames + jnp.arange(frames, dtype=jnp.int32))
    scene_table = picked[: frames // 2].astype(jnp.int32)
    frame_table = jnp.zeros((1,), jnp.int32)
    frame_lens = frame_lengths[my_frame].reshape(1)

    qkv_shard = jnp.transpose(qkv_weight, (0, 2, 1, 3))
    gain_abs = lax.all_gather(block_gains, "frame", axis=2, tiled=True).astype(F32)
    gain_rel = to_relative(gain_abs)
    gain_heads = lax.dynamic_slice_in_dim(gain_abs, my_row * local_width, local_width, 2)

    hidden = to_relative(block_input).astype(F32)
    stored = []
    for block in range(2):
        gain = gain_rel[block]
        gain_q, gain_k = gain_heads[block, 4], gain_heads[block, 5]
        w_qkv = jnp.concatenate(gather_frame(qkv_shard[block]), axis=1)
        w_out = jnp.concatenate(gather_frame(out_weight[block]), axis=1)
        w_up = jnp.concatenate(gather_frame(up_weight[block]), axis=0)
        w_down = jnp.concatenate(gather_frame(down_weight[block]), axis=1)

        unit_one, scale_one = norm_parts(hidden)
        normed = gather_rows((unit_one * gain[0]).astype(BF16))
        mixed = [[dot(part, w_qkv[i]) for part in normed] for i in range(3)]
        q_parts = [head_parts(part) for part in mixed[0]]
        k_parts = [head_parts(part) for part in mixed[1]]
        queries = jnp.concatenate([(u * gain_q).astype(BF16) for u, _ in q_parts])
        kv = jnp.concatenate(
            [
                jnp.concatenate([(u * gain_k).astype(BF16), v.astype(BF16)], axis=1)
                for (u, _), v in zip(k_parts, mixed[2], strict=True)
            ]
        )
        if block == 0:
            kv_blocks, table, lens = kv[None], frame_table, frame_lens
        else:
            kv_blocks, table, lens = jnp.stack(gather_frame(kv)), scene_table, rel_lens
        attended, lse = attend(queries, kv_blocks, table, lens, place)
        half = attended.shape[0] // 2
        branch_far = dot(attended[half:], w_out)
        branch = scatter_rows(dot(attended[:half], w_out), branch_far)
        middle = hidden + gain[2] * branch
        unit_two, scale_two = norm_parts(middle)
        second = gather_rows((unit_two * gain[1]).astype(BF16))
        up_values = [dot(part, w_up) for part in second]
        active = [gelu(part).astype(BF16) for part in up_values]
        down_far = dot(active[1], w_down)
        down_values = scatter_rows(dot(active[0], w_down), down_far)
        result = middle + gain[3] * down_values
        stored.append(
            (
                (w_qkv, w_out, w_up, w_down),
                (unit_one, scale_one, jnp.concatenate(normed), q_parts, k_parts),
                (queries, kv_blocks, table, lens, attended, lse),
                (branch, unit_two, scale_two, jnp.concatenate(second), up_values),
                (jnp.concatenate(active), down_values),
            )
        )
        hidden = result
    output = to_absolute(hidden.astype(BF16))

    grad = to_relative(cotangent).astype(F32) * row_live[:, None]
    shares = [None, None]
    for block in (1, 0):
        gain = gain_rel[block]
        gain_q, gain_k = gain_heads[block, 4], gain_heads[block, 5]
        (
            (w_qkv, w_out, w_up, w_down),
            (unit_one, scale_one, normed, q_parts, k_parts),
            (queries, kv_blocks, table, lens, attended, lse),
            (branch, unit_two, scale_two, second, up_values),
            (active, down_values),
        ) = stored[block]
        gain_three = jnp.sum(grad * down_values, axis=0)
        grad_down = gather_rows((gain[3] * grad).astype(BF16))
        grad_up = [
            (dot_t(part, w_down) * gelu_slope(up)).astype(BF16)
            for part, up in zip(grad_down, up_values, strict=True)
        ]
        grad_second_far = dot_t(grad_up[1], w_up)
        grad_second = scatter_rows(dot_t(grad_up[0], w_up), grad_second_far)
        down_grad = t_dot(active, jnp.concatenate(grad_down)).astype(BF16)
        up_grad = t_dot(second, jnp.concatenate(grad_up)).astype(BF16)
        gain_one = jnp.sum(grad_second * unit_two, axis=0)
        grad_middle = grad + norm_back(unit_two, scale_two, gain[1], grad_second)
        gain_two = jnp.sum(grad_middle * branch, axis=0)
        grad_branch = gather_rows((gain[2] * grad_middle).astype(BF16))
        grad_attended = jnp.concatenate([dot_t(part, w_out).astype(BF16) for part in grad_branch])
        out_grad = t_dot(attended, jnp.concatenate(grad_branch)).astype(BF16)
        if block == 0:
            grad_q, grad_kv = attend_back(
                queries, grad_attended, attended, lse, kv_blocks, table, lens, place, F32
            )
            grad_kv = grad_kv[0]
        else:
            grad_q, partial_kv = attend_back(
                queries, grad_attended, attended, lse, kv_blocks, table, lens, place, BF16
            )
            grad_kv = scatter_frame([partial_kv[i] for i in range(frames)])
        grad_k, grad_v = grad_kv[:, :local_width], grad_kv[:, local_width:]
        unit_q = jnp.concatenate([u for u, _ in q_parts])
        unit_k = jnp.concatenate([u for u, _ in k_parts])
        scale_q = jnp.concatenate([s for _, s in q_parts])
        scale_k = jnp.concatenate([s for _, s in k_parts])
        gain_four = jnp.sum(grad_q * unit_q, axis=0)
        gain_five = jnp.sum(grad_k * unit_k, axis=0)
        mixed_grads = [
            head_back(unit_q, scale_q, gain_q, grad_q).astype(BF16),
            head_back(unit_k, scale_k, gain_k, grad_k).astype(BF16),
            grad_v.astype(BF16),
        ]
        half = unit_q.shape[0] // 2
        halves = [
            sum(dot_t(part[rows], w_qkv[i]) for i, part in enumerate(mixed_grads))
            for rows in (slice(0, half), slice(half, None))
        ]
        grad_normed = scatter_rows(*halves)
        qkv_grad = jnp.stack([t_dot(normed, part) for part in mixed_grads]).astype(BF16)
        gain_zero = jnp.sum(grad_normed * unit_one, axis=0)
        grad = grad_middle + norm_back(unit_one, scale_one, gain[0], grad_normed)

        def cut(array, axis):
            return [
                lax.slice_in_dim(array, i * shard, (i + 1) * shard, axis=axis) for i in range(frames)
            ]

        per_row = to_absolute(jnp.stack([gain_zero, gain_one, gain_two, gain_three]))
        per_head = lax.dynamic_update_slice_in_dim(
            jnp.zeros((2, model_width), F32),
            jnp.stack([gain_four, gain_five]),
            my_row * local_width,
            1,
        )
        shares[block] = (
            scatter_frame(cut(qkv_grad, 1)),
            scatter_frame(cut(out_grad, 1)),
            scatter_frame(cut(up_grad, 0)),
            scatter_frame(cut(down_grad, 1)),
            jnp.concatenate([per_row, per_head]),
        )
    gains = lax.psum(jnp.stack([shares[0][4], shares[1][4]]), ("frame", "row"))
    return (
        output,
        to_absolute(grad.astype(BF16)),
        jnp.transpose(jnp.stack([shares[0][0], shares[1][0]]), (0, 2, 1, 3)),
        jnp.stack([shares[0][1], shares[1][1]]),
        jnp.stack([shares[0][2], shares[1][2]]),
        jnp.stack([shares[0][3], shares[1][3]]),
        lax.dynamic_slice_in_dim(gains, my_frame * shard, shard, 2),
    )


def solution(mesh):
    return jax.shard_map(
        per_device,
        mesh=mesh,
        in_specs=(
            P(("frame", "row"), None),
            P(("frame", "row"), None),
            P(),
            P(),
            P(None, "frame", None, "row"),
            P(None, "row", "frame"),
            P(None, "frame", "row"),
            P(None, "row", "frame"),
            P(None, None, "frame"),
        ),
        out_specs=(
            P(("frame", "row"), None),
            P(("frame", "row"), None),
            P(None, "frame", None, "row"),
            P(None, "row", "frame"),
            P(None, "frame", "row"),
            P(None, "row", "frame"),
            P(None, None, "frame"),
        ),
        check_vma=False,
    )
```

time: 2430 us -> 879 us (0.36)
  waiting for transfers between devices: 1650 us -> 408 us
  local copies, waits for them, and re-layouts: 230 us -> 51.7 us
  starting transfers between devices: 46.6 us -> 220 us
  matrix products: 233 us -> 60.4 us
  blocking collectives: 126 us -> 63.5 us
  other arithmetic: 98.3 us -> 35.9 us
  Pallas kernels: 0 us -> 29 us
    reduce_scatter x18 -> x0, waiting for transfers between devices: 1040 us -> none  [the longest x2 182 us: per_device(): lax.psum_scatter(row_shares[3], 'frame', scatter_dimension=1, tiled=True)]
    all_gather x12 -> x0, waiting for transfers between devices: 556 us -> none  [the longest x1 98.5 us: per_device(): lax.all_gather(local[3], 'row', axis=1, tiled=True)]
    ppermute x0 -> x174, waiting for transfers between devices: none -> 408 us  [the longest x126 368 us: frame_permute(): return lax.ppermute(value, 'frame', pairs)]
    ppermute x0 -> x174, starting transfers between devices: none -> 220 us  [the longest x126 195 us: frame_permute(): return lax.ppermute(value, 'frame', pairs)]
    dot_general x58 -> x84, matrix products: 233 us -> 60.4 us  [the longest x24 17.5 us: dot_t(): lax.dot_general(a, b, (((1,), (1,)), ((), ())), preferred_element_type=F32)]
    all_gather x3 -> x1, blocking collectives: 81.2 us -> 21.2 us  [per_device(): lax.all_gather(block_gains, 'frame', axis=2, tiled=True).astype(F32)]
    convert_element_type x29 -> x28, other arithmetic: 52.9 us -> 6.87 us  [the longest x9 1.94 us: scatter_frame(): both = frame_permute(both.astype(BF16), frames, rows - down, 0).astype(F32)]
    all_to_all x12 -> x0, waiting for transfers between devices: 45.3 us -> none  [the longest x2 10 us: per_device(): lax.all_to_all(split_rows(queries, row_devices), 'row', split_axis=1, con...]
  transfers between devices with their start and end apart: 42 -> 174, of which waited for: 33 -> 80; matrix products, arithmetic and copies ran while one was open for 14% -> 14% of each run, Pallas kernels for 0% -> 1%
where the time goes in v1:
time: 879 us; the launch traced here: 873 us
  waiting for transfers between devices  408 us (46%)
  starting transfers between devices  220 us (25%)
  blocking collectives  63.5 us (7%)
  matrix products  60.4 us (7%)
  local copies, waits for them, and re-layouts  51.7 us (6%)
  other arithmetic  35.9 us (4%)
  Pallas kernels  29 us (3%)
    ppermute x126, waiting for transfers between devices, frame_permute(): return lax.ppermute(value, 'frame', pairs)  368 us
    ppermute x126, starting transfers between devices, frame_permute(): return lax.ppermute(value, 'frame', pairs)  195 us
    psum x1, blocking collectives, per_device(): gains = lax.psum(jnp.stack([shares[0][4], shares[1][4]]), ('frame', 'row'))  42.3 us
    ppermute x48, waiting for transfers between devices, row_permute(): return lax.ppermute(value, 'row', [(i ^ bit, i) for i in range(4)])  39.9 us
    unnamed x339, local copies, waits for them, and re-layouts  25.4 us
    ppermute x48, starting transfers between devices, row_permute(): return lax.ppermute(value, 'row', [(i ^ bit, i) for i in range(4)])  24.9 us
    all_gather x1, blocking collectives, per_device(): lax.all_gather(block_gains, 'frame', axis=2, tiled=True).astype(F32)  21.2 us
    pallas_call x2, Pallas kernels, attend_back(): pl.pallas_call(backward_kernel, grid_spec=pltpu.PrefetchScalarGridSpec(nu...  18.5 us
  transfers between devices with their start and end apart: 174, of which 80 were waited for; matrix products, arithmetic and copies ran while one was open for 14% of the time, Pallas kernels for 1%

profile of v1, /device:TPU:0, one launch (start us, length us, event | category | flops | bytes accessed | tf_op | source)
XLA Modules:
  0.0 872.7 jit_solution(8684672477935687517)
XLA Ops:
  23.9 21.2 %all_gather.3 = bf16[2,6,1024]{2,0,1:T(2,128)(2,1)S(1)} all-gather(bf16[2,6,128]{2,0,1:T(2,128)(2,1)S(1)} %copy-done.116), channel_id=1, replica_groups=mesh['frame'=8,'row'=4] {'frame'}, dimensions={2}, use_global_device_ids=true | all-gather | bytes 27648 | tf_op jit(solution)/shard_map/all_gather | solution.py:368
  97.0 6.1 collective-permute-done.62
  162.1 13.1 %collective-permute-done.44 = bf16[3,128,256]{2,1,0:T(8,128)(2,1)S(1)} collective-permute-done((bf16[3,128,256]{2,1,0:T(8,128)(2,1)S(1)}, bf16[3,128,256]{2,1,0:T(8,128)(2,1)S(1)}, u32[]{:S(2)}, u32[]{:S(2)}) %collective-permute-start.44) | collective-permute-done | bytes 196640 | tf_op jit(solution)/shard_map/ppermute | solution.py:27
  199.2 6.7 collective-permute-done.25
  277.3 36.4 %collective-permute-done.53 = bf16[512,512]{1,0:T(8,128)(2,1)S(1)} collective-permute-done((bf16[512,512]{1,0:T(8,128)(2,1)S(1)}, bf16[512,512]{1,0:T(8,128)(2,1)S(1)}, u32[]{:S(2)}, u32[]{:S(2)}) %collective-permute-start.53) | collective-permute-done | bytes 524320 | tf_op jit(solution)/shard_map/ppermute | solution.py:27
  318.8 9.8 %collective-permute-done.54 = bf16[512,512]{1,0:T(8,128)(2,1)S(1)} collective-permute-done((bf16[512,512]{1,0:T(8,128)(2,1)S(1)}, bf16[512,512]{1,0:T(8,128)(2,1)S(1)}, u32[]{:S(2)}, u32[]{:S(2)}) %collective-permute-start.54) | collective-permute-done | bytes 524320 | tf_op jit(solution)/shard_map/ppermute | solution.py:27
  329.3 16.1 %collective-permute-done.56 = bf16[512,512]{1,0:T(8,128)(2,1)S(1)} collective-permute-done((bf16[512,512]{1,0:T(8,128)(2,1)S(1)}, bf16[512,512]{1,0:T(8,128)(2,1)S(1)}, u32[]{:S(2)}, u32[]{:S(2)}) %collective-permute-start.56) | collective-permute-done | bytes 524320 | tf_op jit(solution)/shard_map/ppermute | solution.py:27
  345.5 8.1 shard_map.145
  357.7 6.7 collective-permute-done.66
  367.0 6.8 collective-permute-done.83
  439.0 10.0 %collective-permute-done.153 = bf16[128,1024]{1,0:T(8,128)(2,1)S(1)} collective-permute-done((bf16[128,1024]{1,0:T(8,128)(2,1)S(1)}, bf16[128,1024]{1,0:T(8,128)(2,1)S(1)}, u32[]{:S(2)}, u32[]{:S(2)}) %collective-permute-start.153) | collective-permute-done | bytes 262176 | tf_op jit(solution)/shard_map/ppermute | solution.py:27
  471.5 18.2 %collective-permute-done.170 = bf16[1024,128]{1,0:T(8,128)(2,1)S(1)} collective-permute-done((bf16[1024,128]{1,0:T(8,128)(2,1)S(1)}, bf16[1024,128]{1,0:T(8,128)(2,1)S(1)}, u32[]{:S(2)}, u32[]{:S(2)}) %collective-permute-start.170) | collective-permute-done | bytes 262176 | tf_op jit(solution)/shard_map/ppermute | solution.py:27
  496.1 7.0 collective-permute-done.156
  505.2 14.6 %shard_map.146 = (f32[512,256]{1,0:T(8,128)S(1)}, bf16[8,512,512]{2,1,0:T(8,128)(2,1)S(1)}) custom-call(s32[4]{0:T(128)S(1)} %bitcast.240, s32[8]{0:T(128)S(1)} %gather_fusion.1, s32[1]{0:T(128)} %bitcast.1.place_ref, bf16[512,256]{1,0:T(8,128)(2,1)S(1)} %pad_maximum_fusion.18.q_ref, ...), custom_call_target="tpu_custom_call", output_to_operand_aliasing={{1}: (9, {})} | custom-call | flops 10737418240 | bytes 4194304 | tf_op jit(solution)/shard_map/pallas_call | solution.py:250
  526.4 31.1 %collective-permute-done.139 = bf16[256,128]{1,0:T(8,128)(2,1)S(1)} collective-permute-done((bf16[256,128]{1,0:T(8,128)(2,1)S(1)}, bf16[256,128]{1,0:T(8,128)(2,1)S(1)}, u32[]{:S(2)}, u32[]{:S(2)}) %collective-permute-start.139) | collective-permute-done | bytes 65568 | tf_op jit(solution)/shard_map/ppermute | solution.py:27
  563.5 6.2 collective-permute-start.140
  584.3 20.8 %collective-permute-done.144 = bf16[256,128]{1,0:T(8,128)(2,1)S(1)} collective-permute-done((bf16[256,128]{1,0:T(8,128)(2,1)S(1)}, bf16[256,128]{1,0:T(8,128)(2,1)S(1)}, u32[]{:S(2)}, u32[]{:S(2)}) %collective-permute-start.144) | collective-permute-done | bytes 65568 | tf_op jit(solution)/shard_map/ppermute | solution.py:27
  605.8 12.0 %collective-permute-done.99 = bf16[512,512]{1,0:T(8,128)(2,1)S(1)} collective-permute-done((bf16[512,512]{1,0:T(8,128)(2,1)S(1)}, bf16[512,512]{1,0:T(8,128)(2,1)S(1)}, u32[]{:S(2)}, u32[]{:S(2)}) %collective-permute-start.99) | collective-permute-done | bytes 524320 | tf_op jit(solution)/shard_map/ppermute | solution.py:27
  649.1 6.7 collective-permute-done.128
  658.6 7.7 collective-permute-done.108
  696.8 9.9 %collective-permute-done.146 = bf16[128,1024]{1,0:T(8,128)(2,1)S(1)} collective-permute-done((bf16[128,1024]{1,0:T(8,128)(2,1)S(1)}, bf16[128,1024]{1,0:T(8,128)(2,1)S(1)}, u32[]{:S(2)}, u32[]{:S(2)}) %collective-permute-start.146) | collective-permute-done | bytes 262176 | tf_op jit(solution)/shard_map/ppermute | solution.py:27
  730.6 10.5 %collective-permute-start.149 = (bf16[128,1024]{1,0:T(8,128)(2,1)S(1)}, bf16[128,1024]{1,0:T(8,128)(2,1)S(1)}, u32[]{:S(2)}, u32[]{:S(2)}) collective-permute-start(bf16[128,1024]{1,0:T(8,128)(2,1)S(1)} %get-tuple-element.105), channel_id=1, source_target_pairs={{16,0},{20,4},{24,8},{28,12},{0,16},{4,20},{8,24},{12,28},{17,1},{... | collective-permute-start | bytes 786440 | tf_op jit(solution)/shard_map/ppermute | solution.py:27
  741.9 16.0 %collective-permute-start.151 = (bf16[128,1024]{1,0:T(8,128)(2,1)S(1)}, bf16[128,1024]{1,0:T(8,128)(2,1)S(1)}, u32[]{:S(2)}, u32[]{:S(2)}) collective-permute-start(bf16[128,1024]{1,0:T(8,128)(2,1)S(1)} %get-tuple-element.104), channel_id=1, source_target_pairs={{8,0},{12,4},{16,8},{20,12},{24,16},{28,20},{0,24},{4,28},{9,1},{1... | collective-permute-start | bytes 786440 | tf_op jit(solution)/shard_map/ppermute | solution.py:27
  826.8 42.3 %psum.7 = f32[2,6,1024]{2,1,0:T(8,128)S(1)} all-reduce(f32[2,6,1024]{2,1,0:T(8,128)S(1)} %pad_maximum_fusion.31), channel_id=1, replica_groups=mesh['frame'=8,'row'=4] {'frame','row'}, use_global_device_ids=true, to_apply=%region_29.30 | all-reduce | flops 12288 | bytes 98304 | tf_op jit(solution)/shard_map/psum | solution.py:501
  (939 shorter events, 523.8 us)
Async XLA Ops:
  2.5 113.2 %collective-permute-start.1 = (bf16[3,128,256]{2,1,0:T(8,128)(2,1)}, bf16[3,128,256]{2,1,0:T(8,128)(2,1)}, u32[]{:S(2)}, u32[]{:S(2)}) collective-permute-start(bf16[3,128,256]{2,1,0:T(8,128)(2,1)} %get-tuple-element.155), channel_id=1, source_target_pairs={{4,0},{0,4},{12,8},{8,12},{20,16},{16,20},{28,24},{24,28},{5,1},{1... | collective-permute-start | bytes 589832 | tf_op jit(solution)/shard_map/ppermute | solution.py:27
  5.5 111.4 %collective-permute-start.2 = (bf16[3,128,256]{2,1,0:T(8,128)(2,1)}, bf16[3,128,256]{2,1,0:T(8,128)(2,1)}, u32[]{:S(2)}, u32[]{:S(2)}) collective-permute-start(bf16[3,128,256]{2,1,0:T(8,128)(2,1)} %get-tuple-element.155), channel_id=1, source_target_pairs={{8,0},{12,4},{16,8},{20,12},{24,16},{28,20},{0,24},{4,28},{9,1},{1... | collective-permute-start | bytes 589832 | tf_op jit(solution)/shard_map/ppermute | solution.py:27
  9.1 135.7 %collective-permute-start.4 = (bf16[3,128,256]{2,1,0:T(8,128)(2,1)}, bf16[3,128,256]{2,1,0:T(8,128)(2,1)}, u32[]{:S(2)}, u32[]{:S(2)}) collective-permute-start(bf16[3,128,256]{2,1,0:T(8,128)(2,1)} %get-tuple-element.155), channel_id=1, source_target_pairs={{16,0},{20,4},{24,8},{28,12},{0,16},{4,20},{8,24},{12,28},{17,1},{... | collective-permute-start | bytes 589832 | tf_op jit(solution)/shard_map/ppermute | solution.py:27
  10.6 44.3 %collective-permute-start.10 = (bf16[256,128]{1,0:T(8,128)(2,1)}, bf16[256,128]{1,0:T(8,128)(2,1)}, u32[]{:S(2)}, u32[]{:S(2)}) collective-permute-start(bf16[256,128]{1,0:T(8,128)(2,1)} %get-tuple-element.167), channel_id=1, source_target_pairs={{4,0},{0,4},{12,8},{8,12},{20,16},{16,20},{28,24},{24,28},{5,1},{1... | collective-permute-start | bytes 196616 | tf_op jit(solution)/shard_map/ppermute | solution.py:27
  11.1 45.3 %collective-permute-start.11 = (bf16[256,128]{1,0:T(8,128)(2,1)}, bf16[256,128]{1,0:T(8,128)(2,1)}, u32[]{:S(2)}, u32[]{:S(2)}) collective-permute-start(bf16[256,128]{1,0:T(8,128)(2,1)} %get-tuple-element.167), channel_id=1, source_target_pairs={{8,0},{12,4},{16,8},{20,12},{24,16},{28,20},{0,24},{4,28},{9,1},{1... | collective-permute-start | bytes 196616 | tf_op jit(solution)/shard_map/ppermute | solution.py:27
  68.2 83.1 %collective-permute-start.6 = (bf16[3,128,256]{2,1,0:T(8,128)(2,1)}, bf16[3,128,256]{2,1,0:T(8,128)(2,1)S(1)}, u32[]{:S(2)}, u32[]{:S(2)}) collective-permute-start(bf16[3,128,256]{2,1,0:T(8,128)(2,1)} %get-tuple-element.155), channel_id=1, source_target_pairs={{24,0},{28,4},{0,8},{4,12},{8,16},{12,20},{16,24},{20,28},{25,1},{... | collective-permute-start | bytes 589832 | tf_op jit(solution)/shard_map/ppermute | solution.py:27
  144.7 51.9 %collective-permute-start.24 = (bf16[128,1024]{1,0:T(8,128)(2,1)S(1)}, bf16[128,1024]{1,0:T(8,128)(2,1)S(1)}, u32[]{:S(2)}, u32[]{:S(2)}) collective-permute-start(bf16[128,1024]{1,0:T(8,128)(2,1)S(1)} %copy-done.104), channel_id=1, source_target_pairs={{16,0},{20,4},{24,8},{28,12},{0,16},{4,20},{8,24},{12,28},{17,1},{... | collective-permute-start | bytes 786440 | tf_op jit(solution)/shard_map/ppermute | solution.py:27
  144.8 62.7 %collective-permute-start.26 = (bf16[128,1024]{1,0:T(8,128)(2,1)S(1)}, bf16[128,1024]{1,0:T(8,128)(2,1)S(1)}, u32[]{:S(2)}, u32[]{:S(2)}) collective-permute-start(bf16[128,1024]{1,0:T(8,128)(2,1)S(1)} %copy-done.104), channel_id=1, source_target_pairs={{24,0},{28,4},{0,8},{4,12},{8,16},{12,20},{16,24},{20,28},{25,1},{... | collective-permute-start | bytes 786440 | tf_op jit(solution)/shard_map/ppermute | solution.py:27
  232.8 83.9 %collective-permute-start.78 = (bf16[1024,128]{1,0:T(8,128)(2,1)}, bf16[1024,128]{1,0:T(8,128)(2,1)S(1)}, u32[]{:S(2)}, u32[]{:S(2)}) collective-permute-start(bf16[1024,128]{1,0:T(8,128)(2,1)} %get-tuple-element.146), channel_id=1, source_target_pairs={{16,0},{20,4},{24,8},{28,12},{0,16},{4,20},{8,24},{12,28},{17,1},{... | collective-permute-start | bytes 786440 | tf_op jit(solution)/shard_map/ppermute | solution.py:27
  258.9 54.8 %collective-permute-start.53 = (bf16[512,512]{1,0:T(8,128)(2,1)S(1)}, bf16[512,512]{1,0:T(8,128)(2,1)S(1)}, u32[]{:S(2)}, u32[]{:S(2)}) collective-permute-start(bf16[512,512]{1,0:T(8,128)(2,1)S(1)} %maximum_maximum_fusion), channel_id=1, source_target_pairs={{16,0},{20,4},{24,8},{28,12},{0,16},{4,20},{8,24},{12,28},{17,1},{... | collective-permute-start | bytes 1572872 | tf_op jit(solution)/shard_map/ppermute | solution.py:27
  262.4 52.0 %collective-permute-start.55 = (bf16[512,512]{1,0:T(8,128)(2,1)S(1)}, bf16[512,512]{1,0:T(8,128)(2,1)S(1)}, u32[]{:S(2)}, u32[]{:S(2)}) collective-permute-start(bf16[512,512]{1,0:T(8,128)(2,1)S(1)} %maximum_maximum_fusion), channel_id=1, source_target_pairs={{24,0},{28,4},{0,8},{4,12},{8,16},{12,20},{16,24},{20,28},{25,1},{... | collective-permute-start | bytes 1572872 | tf_op jit(solution)/shard_map/ppermute | solution.py:27
  272.5 43.4 %collective-permute-start.52 = (bf16[512,512]{1,0:T(8,128)(2,1)S(1)}, bf16[512,512]{1,0:T(8,128)(2,1)S(1)}, u32[]{:S(2)}, u32[]{:S(2)}) collective-permute-start(bf16[512,512]{1,0:T(8,128)(2,1)S(1)} %collective-permute-done.51), channel_id=1, source_target_pairs={{4,0},{0,4},{12,8},{8,12},{20,16},{16,20},{28,24},{24,28},{5,1},{1... | collective-permute-start | bytes 1572872 | tf_op jit(solution)/shard_map/ppermute | solution.py:27
  273.2 44.9 %collective-permute-start.80 = (bf16[1024,128]{1,0:T(8,128)(2,1)}, bf16[1024,128]{1,0:T(8,128)(2,1)S(1)}, u32[]{:S(2)}, u32[]{:S(2)}) collective-permute-start(bf16[1024,128]{1,0:T(8,128)(2,1)} %get-tuple-element.146), channel_id=1, source_target_pairs={{24,0},{28,4},{0,8},{4,12},{8,16},{12,20},{16,24},{20,28},{25,1},{... | collective-permute-start | bytes 786440 | tf_op jit(solution)/shard_map/ppermute | solution.py:27
  314.5 52.4 %collective-permute-start.74 = (bf16[128,1024]{1,0:T(8,128)(2,1)S(1)}, bf16[128,1024]{1,0:T(8,128)(2,1)S(1)}, u32[]{:S(2)}, u32[]{:S(2)}) collective-permute-start(bf16[128,1024]{1,0:T(8,128)(2,1)S(1)} %collective-permute-done.73), channel_id=1, source_target_pairs={{4,0},{0,4},{12,8},{8,12},{20,16},{16,20},{28,24},{24,28},{5,1},{1... | collective-permute-start | bytes 786440 | tf_op jit(solution)/shard_map/ppermute | solution.py:27
  410.1 50.5 %collective-permute-start.88 = (bf16[128,1024]{1,0:T(8,128)(2,1)S(1)}, bf16[128,1024]{1,0:T(8,128)(2,1)S(1)}, u32[]{:S(2)}, u32[]{:S(2)}) collective-permute-start(bf16[128,1024]{1,0:T(8,128)(2,1)S(1)} %slice.1109), channel_id=1, source_target_pairs={{1,0},{0,1},{3,2},{2,3},{5,4},{4,5},{7,6},{6,7},{9,8},{8,9},{11,10... | collective-permute-start | bytes 786440 | tf_op jit(solution)/shard_map/ppermute | solution.py:31
  421.8 43.6 %collective-permute-start.173 = (bf16[1024,128]{1,0:T(8,128)(2,1)S(1)}, bf16[1024,128]{1,0:T(8,128)(2,1)S(1)}, u32[]{:S(2)}, u32[]{:S(2)}) collective-permute-start(bf16[1024,128]{1,0:T(8,128)(2,1)S(1)} %get-tuple-element.100), channel_id=1, source_target_pairs={{4,0},{0,4},{12,8},{8,12},{20,16},{16,20},{28,24},{24,28},{5,1},{1... | collective-permute-start | bytes 786440 | tf_op jit(solution)/shard_map/ppermute | solution.py:27
  520.0 43.5 %collective-permute-start.100 = (bf16[512,512]{1,0:T(8,128)(2,1)S(1)}, bf16[512,512]{1,0:T(8,128)(2,1)S(1)}, u32[]{:S(2)}, u32[]{:S(2)}) collective-permute-start(bf16[512,512]{1,0:T(8,128)(2,1)S(1)} %get-tuple-element.87), channel_id=1, source_target_pairs={{4,0},{0,4},{12,8},{8,12},{20,16},{16,20},{28,24},{24,28},{5,1},{1... | collective-permute-start | bytes 1572872 | tf_op jit(solution)/shard_map/ppermute | solution.py:27
  521.0 48.7 %collective-permute-start.96 = (bf16[512,512]{1,0:T(8,128)(2,1)S(1)}, bf16[512,512]{1,0:T(8,128)(2,1)S(1)}, u32[]{:S(2)}, u32[]{:S(2)}) collective-permute-start(bf16[512,512]{1,0:T(8,128)(2,1)S(1)} %get-tuple-element.85), channel_id=1, source_target_pairs={{4,0},{0,4},{12,8},{8,12},{20,16},{16,20},{28,24},{24,28},{5,1},{1... | collective-permute-start | bytes 1572872 | tf_op jit(solution)/shard_map/ppermute | solution.py:27
  522.1 47.7 %collective-permute-start.98 = (bf16[512,512]{1,0:T(8,128)(2,1)S(1)}, bf16[512,512]{1,0:T(8,128)(2,1)S(1)}, u32[]{:S(2)}, u32[]{:S(2)}) collective-permute-start(bf16[512,512]{1,0:T(8,128)(2,1)S(1)} %get-tuple-element.88), channel_id=1, source_target_pairs={{4,0},{0,4},{12,8},{8,12},{20,16},{16,20},{28,24},{24,28},{5,1},{1... | collective-permute-start | bytes 1572872 | tf_op jit(solution)/shard_map/ppermute | solution.py:27
  559.1 46.7 %collective-permute-start.102 = (bf16[512,512]{1,0:T(8,128)(2,1)S(1)}, bf16[512,512]{1,0:T(8,128)(2,1)S(1)}, u32[]{:S(2)}, u32[]{:S(2)}) collective-permute-start(bf16[512,512]{1,0:T(8,128)(2,1)S(1)} %get-tuple-element.86), channel_id=1, source_target_pairs={{4,0},{0,4},{12,8},{8,12},{20,16},{16,20},{28,24},{24,28},{5,1},{1... | collective-permute-start | bytes 1572872 | tf_op jit(solution)/shard_map/ppermute | solution.py:27
  670.2 52.8 %collective-permute-start.107 = (bf16[128,1024]{1,0:T(8,128)(2,1)S(1)}, bf16[128,1024]{1,0:T(8,128)(2,1)S(1)}, u32[]{:S(2)}, u32[]{:S(2)}) collective-permute-start(bf16[128,1024]{1,0:T(8,128)(2,1)S(1)} %slice.1105), channel_id=1, source_target_pairs={{1,0},{0,1},{3,2},{2,3},{5,4},{4,5},{7,6},{6,7},{9,8},{8,9},{11,10... | collective-permute-start | bytes 786440 | tf_op jit(solution)/shard_map/ppermute | solution.py:31
  679.7 46.5 %collective-permute-start.166 = (bf16[1024,128]{1,0:T(8,128)(2,1)S(1)}, bf16[1024,128]{1,0:T(8,128)(2,1)S(1)}, u32[]{:S(2)}, u32[]{:S(2)}) collective-permute-start(bf16[1024,128]{1,0:T(8,128)(2,1)S(1)} %get-tuple-element.93), channel_id=1, source_target_pairs={{4,0},{0,4},{12,8},{8,12},{20,16},{16,20},{28,24},{24,28},{5,1},{1... | collective-permute-start | bytes 786440 | tf_op jit(solution)/shard_map/ppermute | solution.py:27
  706.8 51.3 %collective-permute-start.152 = (bf16[128,1024]{1,0:T(8,128)(2,1)S(1)}, bf16[128,1024]{1,0:T(8,128)(2,1)S(1)}, u32[]{:S(2)}, u32[]{:S(2)}) collective-permute-start(bf16[128,1024]{1,0:T(8,128)(2,1)S(1)} %get-tuple-element.107), channel_id=1, source_target_pairs={{4,0},{0,4},{12,8},{8,12},{20,16},{16,20},{28,24},{24,28},{5,1},{1... | collective-permute-start | bytes 786440 | tf_op jit(solution)/shard_map/ppermute | solution.py:27
  778.3 47.9 %collective-permute-start.115 = (bf16[128,1024]{1,0:T(8,128)(2,1)S(1)}, bf16[128,1024]{1,0:T(8,128)(2,1)S(1)}, u32[]{:S(2)}, u32[]{:S(2)}) collective-permute-start(bf16[128,1024]{1,0:T(8,128)(2,1)S(1)} %slice.1103), channel_id=1, source_target_pairs={{1,0},{0,1},{3,2},{2,3},{5,4},{4,5},{7,6},{6,7},{9,8},{8,9},{11,10... | collective-permute-start | bytes 786440 | tf_op jit(solution)/shard_map/ppermute | solution.py:31
  (289 other events, 3799.5 us)

commit v2 on v1

v2 whole, which is shorter than its diff:
```python
import functools

import jax
import jax.numpy as jnp
from jax import lax
from jax.experimental import pallas as pl
from jax.experimental.pallas import tpu as pltpu
from jax.sharding import PartitionSpec as P

HEAD_DIM = 64
EPSILON = 1e-06
F32 = jnp.float32
BF16 = jnp.bfloat16
LANES = 128
TILE = 256
ROOT_HALF = 0.7071067811865476
BELL = 0.3989422804014327
SCALING = HEAD_DIM**-0.5

RING = (0, 2, 4, 6, 7, 5, 3, 1)


def on_ring():
    return lax.axis_size("frame") == len(RING)


def ring_take(value, step):
    count = len(RING)
    return lax.ppermute(value, "frame", [(RING[(i + step) % count], RING[i]) for i in range(count)])


def row_take(value, bit):
    return lax.ppermute(value, "row", [(i ^ bit, i) for i in range(4)])


def ring_gather(shard, cut):
    ahead, behind = [shard], [shard]
    for _ in range(3):
        ahead.append(ring_take(ahead[-1], 1))
        behind.append(ring_take(behind[-1], -1))
    far_low = ring_take(ahead[3][:cut], 1)
    far_high = ring_take(behind[3][cut:], -1)
    return ahead + [far_low, far_high] + behind[3:0:-1]


def add_pair(a, b):
    return (a.astype(F32) + b.astype(F32)).astype(BF16)


def ring_scatter(pieces):
    ahead = pieces[1:4]
    far_low, far_high = pieces[4:6]
    behind = pieces[8:5:-1]
    cut = far_low.shape[0]
    low = ring_take(far_low, -1)
    high = ring_take(far_high, 1)
    right = jnp.concatenate([add_pair(ahead[2][:cut], low), ahead[2][cut:]])
    left = jnp.concatenate([behind[2][:cut], add_pair(behind[2][cut:], high)])
    for place in (1, 0):
        right = add_pair(ahead[place], ring_take(right, -1))
        left = add_pair(behind[place], ring_take(left, 1))
    return pieces[0], ring_take(right, -1), ring_take(left, 1)


def dot_nt(a, b):
    return lax.dot_general(a, b, (((1,), (1,)), ((), ())), preferred_element_type=F32)


def dot_nn(a, b):
    return lax.dot_general(a, b, (((1,), (0,)), ((), ())), preferred_element_type=F32)


def whole(shape):
    return pl.BlockSpec(shape, lambda *_: (0,) * len(shape))


def column(rows, place):
    return pl.BlockSpec((rows, TILE), lambda j, *_: (0, place(j)))


def cost(us):
    return pl.CostEstimate(flops=int(us * 1.0e9), bytes_accessed=int(us * 2.0e6), transcendentals=0)


def run(kernel, grid, in_specs, out_specs, out_shape, scratch, operands, us, prefetch=0, aliases=None):
    return pl.pallas_call(
        kernel,
        grid_spec=pltpu.PrefetchScalarGridSpec(
            num_scalar_prefetch=prefetch,
            grid=grid,
            in_specs=in_specs,
            out_specs=out_specs,
            scratch_shapes=scratch,
        ),
        out_shape=out_shape,
        input_output_aliases=aliases or {},
        compiler_params=pltpu.CompilerParams(vmem_limit_bytes=56 * 1024 * 1024),
        cost_estimate=cost(us),
    )(*operands)


def shaped(*shape, dtype=F32):
    return jax.ShapeDtypeStruct(shape, dtype)


def norm_parts(values):
    center = values - jnp.mean(values, axis=-1, keepdims=True)
    scale = lax.rsqrt(jnp.mean(center * center, axis=-1, keepdims=True) + EPSILON)
    return center * scale, scale


def norm_back(unit, scale, gain, grad):
    inner = grad * gain
    return scale * (
        inner
        - jnp.mean(inner, axis=-1, keepdims=True)
        - unit * jnp.mean(inner * unit, axis=-1, keepdims=True)
    )


def head_means(values):
    width = values.shape[-1]
    rows = lax.broadcasted_iota(jnp.int32, (width, width), 0) // HEAD_DIM
    cols = lax.broadcasted_iota(jnp.int32, (width, width), 1) // HEAD_DIM
    spread = jnp.where(rows == cols, F32(1.0 / HEAD_DIM), F32(0)).astype(BF16)
    high = values.astype(BF16)
    low = (values - high.astype(F32)).astype(BF16)
    return dot_nn(high, spread) + dot_nn(low, spread)


def head_parts(values):
    center = values - head_means(values)
    scale = lax.rsqrt(head_means(center * center) + EPSILON)
    return center * scale, scale


def head_back(unit, scale, gain, grad):
    inner = grad * gain
    return scale * (inner - head_means(inner) - unit * head_means(inner * unit))


def joined(refs):
    if len(refs) == 1:
        return refs[0][...]
    return jnp.concatenate([ref[...] for ref in refs], axis=0)


def head_mask(shape, head):
    lanes = lax.broadcasted_iota(jnp.int32, shape, 1)
    return (lanes // HEAD_DIM) == head


def live_keys(count, core, length):
    place = lax.broadcasted_iota(jnp.int32, (count, 1), 0)
    quarter = count // 4
    half = place // (2 * quarter)
    chip = (place // quarter) % 2
    slot = (chip * 2 + (half ^ core)) * quarter + place % quarter
    return slot < length


def pack_kernel(with_gains, qkv_ref, out_ref, up_ref, down_ref, gains_ref, at_ref, ff_ref):
    rows = up_ref.shape[1]
    width = qkv_ref.shape[3]
    for i in range(3):
        at_ref[:rows, i * width : (i + 1) * width] = qkv_ref[0, i]
    at_ref[:rows, 3 * width :] = out_ref[0].T
    ff = up_ref.shape[2]
    ff_ref[:, :ff] = up_ref[0]
    ff_ref[:, ff:] = down_ref[0].T
    if with_gains:
        at_ref[rows:, :] = jnp.zeros((16, at_ref.shape[1]), BF16)
        flat = jnp.concatenate([gains_ref[0], gains_ref[1], jnp.zeros((4, rows), BF16)], axis=0)
        at_ref[rows:, :rows] = flat


def gains_kernel(inverse_ref, *refs):
    pieces, (wide_ref, heads_ref) = refs[:-2], refs[-2:]
    for k, piece in enumerate(pieces):
        wide_ref[:, k * LANES : (k + 1) * LANES] = piece[...].astype(F32)
    for k in range(2):
        start = pl.multiple_of(inverse_ref[k] * LANES, LANES)
        heads_ref[:, k * LANES : (k + 1) * LANES] = wide_ref[:, pl.ds(start, LANES)]


def enter_kernel(masked, order_ref, facts_ref, own_ref, far_ref, out_ref):
    rows = own_ref.shape[0]
    chip, core, length = facts_ref[0], facts_ref[1], facts_ref[2]
    for k in range(own_ref.shape[1] // LANES):
        lanes = pl.ds(pl.multiple_of(order_ref[k] * LANES, LANES), LANES)
        for source, place in ((own_ref, chip), (far_ref, 1 - chip)):
            values = source[:, lanes].astype(F32)
            if masked:
                slots = (place * 2 + core) * rows + lax.broadcasted_iota(jnp.int32, (rows, 1), 0)
                values = jnp.where(slots < length, values, 0.0)
            start = pl.multiple_of(place * rows, rows)
            out_ref[pl.ds(start, rows), k * LANES : (k + 1) * LANES] = values


def leave(values_ref, order_ref, facts_ref, out_ref):
    rows = out_ref.shape[0]
    start = pl.multiple_of(facts_ref[0] * rows, rows)
    for k in range(out_ref.shape[1] // LANES):
        lanes = pl.ds(pl.multiple_of(order_ref[k] * LANES, LANES), LANES)
        values = values_ref[pl.ds(start, rows), k * LANES : (k + 1) * LANES]
        out_ref[:, lanes] = values.astype(out_ref.dtype)


def first_norm_kernel(row, h_ref, gains_ref, normed_ref):
    unit, _ = norm_parts(h_ref[...])
    normed_ref[...] = (unit * gains_ref[row : row + 1, :]).astype(BF16)


def total_of(own_ref, far_ref):
    return own_ref[...].astype(F32) + far_ref[...].astype(F32)


def residual_kernel(scale_row, norm_row, h_ref, own_ref, far_ref, gains_ref, next_ref, normed_ref):
    value = h_ref[...] + gains_ref[scale_row : scale_row + 1, :] * total_of(own_ref, far_ref)
    next_ref[...] = value
    unit, _ = norm_parts(value)
    normed_ref[...] = (unit * gains_ref[norm_row : norm_row + 1, :]).astype(BF16)


def output_kernel(scale_row, order_ref, facts_ref, h_ref, own_ref, far_ref, gains_ref, out_ref, held):
    held[...] = h_ref[...] + gains_ref[scale_row : scale_row + 1, :] * total_of(own_ref, far_ref)
    leave(held, order_ref, facts_ref, out_ref)


def seed_kernel(row, grad_ref, own_ref, far_ref, gains_ref, scaled_ref, sums_ref):
    grad = grad_ref[...]
    scaled_ref[...] = (grad * gains_ref[row : row + 1, :]).astype(BF16)
    sums_ref[...] = jnp.sum(grad * total_of(own_ref, far_ref), axis=0, keepdims=True)


def middle_back_kernel(
    base, grad_ref, own_ref, far_ref, middle_ref, b_own_ref, b_far_ref, gains_ref, next_ref, scaled_ref, sums_ref
):
    grad_in = total_of(own_ref, far_ref)
    unit, scale = norm_parts(middle_ref[...])
    sums_ref[0:1, :] = jnp.sum(grad_in * unit, axis=0, keepdims=True)
    grad = grad_ref[...] + norm_back(unit, scale, gains_ref[base + 1 : base + 2, :], grad_in)
    next_ref[...] = grad
    sums_ref[1:2, :] = jnp.sum(grad * total_of(b_own_ref, b_far_ref), axis=0, keepdims=True)
    scaled_ref[...] = (grad * gains_ref[base + 2 : base + 3, :]).astype(BF16)


def first_back_kernel(base, grad_ref, own_ref, far_ref, h_ref, gains_ref, next_ref, sums_ref):
    grad_in = total_of(own_ref, far_ref)
    unit, scale = norm_parts(h_ref[...])
    sums_ref[...] = jnp.sum(grad_in * unit, axis=0, keepdims=True)
    next_ref[...] = grad_ref[...] + norm_back(unit, scale, gains_ref[base : base + 1, :], grad_in)


def last_back_kernel(order_ref, facts_ref, grad_ref, own_ref, far_ref, h_ref, gains_ref, out_ref, sums_ref, held):
    first_back_kernel(0, grad_ref, own_ref, far_ref, h_ref, gains_ref, held, sums_ref)
    leave(held, order_ref, facts_ref, out_ref)


def project_kernel(row_q, count, own_ref, other_ref, *refs):
    pieces = refs[:count]
    heads_ref, q_ref, kv_ref, mixed_ref = refs[count:]
    step = pl.program_id(0)
    weight = joined(pieces)
    half = own_ref.shape[0]
    mixed = jnp.concatenate([dot_nn(own_ref[...], weight), dot_nn(other_ref[...], weight)], axis=0)

    @pl.when(step < 2)
    def _():
        mixed_ref[...] = mixed
        unit, _ = head_parts(mixed)
        gain = jnp.where(step == 0, heads_ref[row_q : row_q + 1, :], heads_ref[row_q + 1 : row_q + 2, :])
        scaled = (unit * gain).astype(BF16)

        @pl.when(step == 0)
        def _():
            q_ref[...] = scaled

        @pl.when(step == 1)
        def _():
            kv_ref[...] = scaled

    @pl.when(step == 2)
    def _():
        kv_ref[...] = mixed.astype(BF16)


def project(normed, pieces, heads, row_q):
    own, other = normed
    half, wide = own.shape
    width = heads.shape[1]
    rows = [min(p.shape[0], limit) for p, limit in pieces]
    return run(
        functools.partial(project_kernel, row_q, len(pieces)),
        (3,),
        [whole(own.shape), whole(other.shape)]
        + [column(r, lambda j: j) for r in rows]
        + [whole(heads.shape)],
        [
            whole((2 * half, width)),
            column(2 * half, lambda j: jnp.maximum(j - 1, 0)),
            column(2 * half, lambda j: jnp.minimum(j, 1)),
        ],
        [
            shaped(2 * half, width, dtype=BF16),
            shaped(2 * half, 2 * width, dtype=BF16),
            shaped(2 * half, 2 * width),
        ],
        [],
        [own, other] + [p for p, _ in pieces] + [heads],
        5,
    )


def project_back_kernel(row_q, count, dq_ref, dkv_ref, mixed_ref, heads_ref, *refs):
    pieces = refs[:count]
    grad_ref, other_ref, own_ref, sums_ref, acc = refs[count:]
    step = pl.program_id(0)

    @pl.when(step == 0)
    def _():
        acc[...] = jnp.zeros_like(acc)

    def normed(incoming, row, place):
        unit, scale = head_parts(mixed_ref[...])
        sums_ref[place : place + 1, :] = jnp.sum(incoming * unit, axis=0, keepdims=True)
        grad_ref[...] = head_back(unit, scale, heads_ref[row : row + 1, :], incoming).astype(BF16)

    @pl.when(step == 0)
    def _():
        normed(dq_ref[...], row_q, 0)

    @pl.when(step == 1)
    def _():
        normed(dkv_ref[...].astype(F32), row_q + 1, 1)

    @pl.when(step == 2)
    def _():
        grad_ref[...] = dkv_ref[...].astype(BF16)

    acc[...] += dot_nt(grad_ref[...], joined(pieces))

    @pl.when(step == 2)
    def _():
        half = own_ref.shape[0]
        own_ref[...] = acc[:half, :]
        other_ref[...] = acc[half:, :].astype(BF16)


def project_back(dq, dkv, mixed, pieces, heads, row_q, wide):
    full, width = dq.shape
    rows = [min(p.shape[0], limit) for p, limit in pieces]
    return run(
        functools.partial(project_back_kernel, row_q, len(pieces)),
        (3,),
        [
            whole(dq.shape),
            column(full, lambda j: jnp.maximum(j - 1, 0)),
            column(full, lambda j: jnp.minimum(j, 1)),
            whole(heads.shape),
        ]
        + [column(r, lambda j: j) for r in rows],
        [column(full, lambda j: j), whole((full // 2, wide)), whole((full // 2, wide)), whole((2, width))],
        [
            shaped(full, 3 * width, dtype=BF16),
            shaped(full // 2, wide, dtype=BF16),
            shaped(full // 2, wide),
            shaped(2, width),
        ],
        [pltpu.VMEM((full, wide), F32)],
        [dq, dkv, mixed, heads] + [p for p, _ in pieces],
        6,
    )


def feed_kernel(count, own_ref, other_ref, *refs):
    ups, downs = refs[:count], refs[count : 2 * count]
    values_ref, active_ref, part_other_ref, part_own_ref, acc = refs[2 * count :]
    step = pl.program_id(0)

    @pl.when(step == 0)
    def _():
        acc[...] = jnp.zeros_like(acc)

    weight = joined(ups)
    half = own_ref.shape[0]
    for source, start in ((own_ref, 0), (other_ref, half)):
        values = dot_nn(source[...], weight)
        values_ref[start : start + half, :] = values
        active_ref[start : start + half, :] = (
            0.5 * values * (1.0 + lax.erf(values * F32(ROOT_HALF)))
        ).astype(BF16)
    acc[...] += dot_nt(active_ref[...], joined(downs))

    @pl.when(step == pl.num_programs(0) - 1)
    def _():
        part_own_ref[...] = acc[:half, :]
        part_other_ref[...] = acc[half:, :].astype(BF16)


def feed(second, pieces, hidden):
    own, other = second
    half, wide = own.shape
    steps = hidden // TILE
    rows = [min(p.shape[0], limit) for p, limit in pieces]
    arrays = [p for p, _ in pieces]
    return run(
        functools.partial(feed_kernel, len(pieces)),
        (steps,),
        [whole(own.shape), whole(other.shape)]
        + [column(r, lambda j: j) for r in rows]
        + [column(r, lambda j: j + steps) for r in rows],
        [
            column(2 * half, lambda j: j),
            column(2 * half, lambda j: j),
            whole((half, wide)),
            whole((half, wide)),
        ],
        [
            shaped(2 * half, hidden),
            shaped(2 * half, hidden, dtype=BF16),
            shaped(half, wide, dtype=BF16),
            shaped(half, wide),
        ],
        [pltpu.VMEM((2 * half, wide), F32)],
        [own, other] + arrays + arrays,
        7,
    )


def feed_back_kernel(count, own_ref, other_ref, values_ref, *refs):
    ups, downs = refs[:count], refs[count : 2 * count]
    grad_ref, part_other_ref, part_own_ref, acc = refs[2 * count :]
    step = pl.program_id(0)

    @pl.when(step == 0)
    def _():
        acc[...] = jnp.zeros_like(acc)

    weight = joined(downs)
    half = own_ref.shape[0]
    for source, start in ((own_ref, 0), (other_ref, half)):
        incoming = dot_nn(source[...], weight)
        values = values_ref[start : start + half, :]
        slope = 0.5 * (1.0 + lax.erf(values * F32(ROOT_HALF))) + values * (
            jnp.exp(-0.5 * values * values) * F32(BELL)
        )
        grad_ref[start : start + half, :] = (incoming * slope).astype(BF16)
    acc[...] += dot_nt(grad_ref[...], joined(ups))

    @pl.when(step == pl.num_programs(0) - 1)
    def _():
        part_own_ref[...] = acc[:half, :]
        part_other_ref[...] = acc[half:, :].astype(BF16)


def feed_back(grads, values, pieces):
    own, other = grads
    half, wide = own.shape
    hidden = values.shape[1]
    steps = hidden // TILE
    rows = [min(p.shape[0], limit) for p, limit in pieces]
    arrays = [p for p, _ in pieces]
    return run(
        functools.partial(feed_back_kernel, len(pieces)),
        (steps,),
        [whole(own.shape), whole(other.shape), column(2 * half, lambda j: j)]
        + [column(r, lambda j: j) for r in rows]
        + [column(r, lambda j: j + steps) for r in rows],
        [column(2 * half, lambda j: j), whole((half, wide)), whole((half, wide))],
        [
            shaped(2 * half, hidden, dtype=BF16),
            shaped(half, wide, dtype=BF16),
            shaped(half, wide),
        ],
        [pltpu.VMEM((2 * half, wide), F32)],
        [own, other, values] + arrays + arrays,
        8,
    )


def weight_kernel(split, rows, a_own, a_other, b_own, b_other, first_ref, second_ref, *refs):
    outs, turned = refs[:-1], refs[-1]
    step = pl.program_id(0)
    half = a_own.shape[0]

    def turn(own, other):
        turned[:, :half] = own[...].T
        turned[:, half:] = other[...].T

    @pl.when(step == 0)
    def _():
        turn(a_own, a_other)

    @pl.when(step == split)
    def _():
        turn(b_own, b_other)

    def store(right):
        start = 0
        for out, count in zip(outs, rows, strict=True):
            out[...] = dot_nn(turned[start : start + count, :], right).astype(BF16)
            start += count

    @pl.when(step < split)
    def _():
        store(first_ref[...])

    @pl.when(step >= split)
    def _():
        store(second_ref[...])


def weight_grads(a, first, b, second, rows, us):
    half, wide = a[0].shape
    split = first.shape[1] // TILE
    steps = split + second.shape[1] // TILE
    return run(
        functools.partial(weight_kernel, split, rows),
        (steps,),
        [whole((half, wide))] * 4
        + [
            column(2 * half, lambda j: jnp.minimum(j, split - 1)),
            column(2 * half, lambda j: jnp.maximum(j - split, 0)),
        ],
        [column(r, lambda j: j) for r in rows],
        [shaped(r, steps * TILE, dtype=BF16) for r in rows],
        [pltpu.VMEM((wide, 2 * half), BF16)],
        [*a, *b, first, second],
        us,
    )


def finish_ff_kernel(own_ref, right_ref, left_ref, *refs):
    up_ref, down_ref = refs[-2:]
    hidden = up_ref.shape[2]
    up_ref[0] = total_of(own_ref.at[:, :hidden], right_ref.at[:, :hidden]) + left_ref[:, :hidden].astype(F32)
    down = total_of(own_ref.at[:, hidden:], right_ref.at[:, hidden:]) + left_ref[:, hidden:].astype(F32)
    down_ref[0] = down.T


def finish_at_kernel(own_ref, right_ref, left_ref, *refs):
    qkv_ref, out_ref = refs[-2:]
    width = qkv_ref.shape[3]
    for i in range(4):
        lanes = slice(i * width, (i + 1) * width)
        part = total_of(own_ref.at[:, lanes], right_ref.at[:, lanes]) + left_ref[:, lanes].astype(F32)
        if i < 3:
            qkv_ref[0, i] = part
        else:
            out_ref[0] = part.T


def finish(kernel, parts, shapes, block, earlier):
    specs = [
        pl.BlockSpec((1,) + s[1:], functools.partial(lambda b, r, *_: (b,) + (0,) * (r - 1), block, len(s)))
        for s in shapes
    ]
    return run(
        kernel,
        (1,),
        [whole(p.shape) for p in parts] + [pl.BlockSpec(memory_space=pl.ANY)] * len(earlier),
        specs,
        [shaped(*s) for s in shapes],
        [],
        [*parts, *earlier],
        2,
        aliases={3 + i: i for i in range(len(earlier))},
    )


def fetch_start(table_ref, sources, ring, buffer, sems, count):
    flen = buffer.shape[1]
    for j in range(count):
        if not ring:
            start = pl.multiple_of(table_ref[j] * flen, flen)
            pltpu.make_async_copy(sources[0].at[pl.ds(start, flen)], buffer.at[j], sems.at[j]).start()
            continue
        for k in range(8):

            @pl.when(table_ref[j] == k)
            def _(j=j, k=k):
                if k == 4:
                    cut = sources[4].shape[0]
                    pltpu.make_async_copy(sources[4], buffer.at[j, pl.ds(0, cut)], sems.at[j]).start()
                    pltpu.make_async_copy(
                        sources[5], buffer.at[j, pl.ds(cut, flen - cut)], sems.at[j]
                    ).start()
                else:
                    source = sources[k if k < 4 else k + 1]
                    pltpu.make_async_copy(source, buffer.at[j], sems.at[j]).start()


def fetch_wait(sources, buffer, sems, j):
    pltpu.make_async_copy(buffer.at[j], buffer.at[j], sems.at[j]).wait()


def attend_kernel(ring, n_kv, count, table_ref, lens_ref, facts_ref, q_ref, *refs):
    sources, pieces = refs[:n_kv], refs[n_kv : n_kv + count]
    out_ref, lse_ref, part_other_ref, part_own_ref = refs[n_kv + count : n_kv + count + 4]
    acc, sums, buffer, sems = refs[n_kv + count + 4 :]
    step = pl.program_id(0)
    steps = buffer.shape[0]
    rows, width = q_ref.shape
    heads = width // HEAD_DIM

    @pl.when(step == 0)
    def _():
        fetch_start(table_ref, sources, ring, buffer, sems, steps)
        acc[...] = jnp.zeros_like(acc)
        sums[...] = jnp.ones_like(sums)
        sums[:heads, :] = jnp.zeros((heads, rows), F32)

    fetch_wait(sources, buffer, sems, step)
    live = live_keys(buffer.shape[1], facts_ref[1], lens_ref[table_ref[step]])
    keys = buffer[step, :, :width]
    values_t = buffer[step, :, width:].T
    queries = q_ref[...]
    for head in range(heads):
        mine = jnp.where(head_mask(queries.shape, head), queries, 0) * BF16(SCALING)
        scores = dot_nt(keys, mine)
        powers = jnp.where(live, jnp.exp(scores), 0.0)
        sums[head : head + 1, :] += jnp.sum(powers, axis=0, keepdims=True)
        lanes = slice(head * HEAD_DIM, (head + 1) * HEAD_DIM)
        acc[lanes, :] += dot_nn(values_t[lanes, :], powers.astype(BF16))

    @pl.when(step == steps - 1)
    def _():
        lse_ref[...] = jnp.log(sums[...])
        for head in range(heads):
            lanes = slice(head * HEAD_DIM, (head + 1) * HEAD_DIM)
            acc[lanes, :] = acc[lanes, :] / sums[head : head + 1, :]
        out_ref[...] = acc[...].T.astype(BF16)
        weight = joined(pieces)
        half = rows // 2
        part_other_ref[...] = dot_nt(out_ref[half:, :], weight).astype(BF16)
        part_own_ref[...] = dot_nt(out_ref[:half, :], weight)


def attend(queries, sources, ring, pieces, table, lens, facts, wide):
    rows, width = queries.shape
    steps = table.shape[0]
    counts = [min(p.shape[0], limit) for p, limit in pieces]
    return run(
        functools.partial(attend_kernel, ring, len(sources), len(pieces)),
        (steps,),
        [whole(queries.shape)]
        + [pl.BlockSpec(memory_space=pl.ANY)] * len(sources)
        + [column(r, lambda j: 3) for r in counts],
        [whole((rows, width)), whole((8, rows)), whole((rows // 2, wide)), whole((rows // 2, wide))],
        [
            shaped(rows, width, dtype=BF16),
            shaped(8, rows),
            shaped(rows // 2, wide, dtype=BF16),
            shaped(rows // 2, wide),
        ],
        [
            pltpu.VMEM((width, rows), F32),
            pltpu.VMEM((8, rows), F32),
            pltpu.VMEM((steps, rows, 2 * width), BF16),
            pltpu.SemaphoreType.DMA((steps,)),
        ],
        [table, lens, facts, queries, *sources] + [p for p, _ in pieces],
        3 + 2 * steps,
        prefetch=3,
    )


def attend_back_kernel(ring, n_kv, count, n_out, table_ref, lens_ref, facts_ref, *refs):
    q_ref, o_ref, lse_ref, g_own_ref, g_other_ref = refs[:5]
    refs = refs[5:]
    sources, pieces = refs[:n_kv], refs[n_kv : n_kv + count]
    dq_ref = refs[n_kv + count]
    outs = refs[n_kv + count + 1 : n_kv + count + 1 + n_out]
    acc, delta, grads, buffer, sems = refs[n_kv + count + 1 + n_out :]
    step = pl.program_id(0)
    steps = buffer.shape[0]
    rows, width = q_ref.shape
    heads = width // HEAD_DIM
    half = rows // 2

    @pl.when(step == 0)
    def _():
        fetch_start(table_ref, sources, ring, buffer, sems, steps)
        acc[...] = jnp.zeros_like(acc)
        if ring:
            for out in outs:
                out[...] = jnp.zeros_like(out)
        weight = joined(pieces)
        grads[:half, :] = dot_nn(g_own_ref[...], weight).astype(BF16)
        grads[half:, :] = dot_nn(g_other_ref[...], weight).astype(BF16)
        turned = (grads[...].astype(F32) * o_ref[...].astype(F32)).T
        for head in range(heads):
            lanes = slice(head * HEAD_DIM, (head + 1) * HEAD_DIM)
            delta[head : head + 1, :] = jnp.sum(turned[lanes, :], axis=0, keepdims=True)

    fetch_wait(sources, buffer, sems, step)
    live = live_keys(buffer.shape[1], facts_ref[1], lens_ref[table_ref[step]])
    keys = buffer[step, :, :width]
    values = buffer[step, :, width:]
    keys_t = keys.T
    queries = q_ref[...]
    incoming = grads[...]
    grad_k = jnp.zeros(keys.shape, F32)
    grad_v = jnp.zeros(keys.shape, F32)
    for head in range(heads):
        inside = head_mask(queries.shape, head)
        mine = jnp.where(inside, queries, 0) * BF16(SCALING)
        mine_g = jnp.where(inside, incoming, 0)
        scores = dot_nt(keys, mine)
        full = jnp.where(live, jnp.exp(scores - lse_ref[head : head + 1, :]), 0.0)
        grad_probs = dot_nt(values, mine_g)
        steep = (full * (grad_probs - delta[head : head + 1, :])).astype(BF16)
        grad_v += dot_nn(full.astype(BF16), mine_g)
        grad_k += dot_nn(steep, mine)
        lanes = slice(head * HEAD_DIM, (head + 1) * HEAD_DIM)
        acc[lanes, :] += dot_nn(keys_t[lanes, :], steep)

    if not ring:
        outs[0][0, :, :width] = grad_k.astype(outs[0].dtype)
        outs[0][0, :, width:] = grad_v.astype(outs[0].dtype)
    else:
        for k in range(8):

            @pl.when(table_ref[step] == k)
            def _(k=k):
                if k == 4:
                    cut = outs[4].shape[0]
                    outs[4][:, :width] = grad_k[:cut].astype(BF16)
                    outs[4][:, width:] = grad_v[:cut].astype(BF16)
                    outs[5][:, :width] = grad_k[cut:].astype(BF16)
                    outs[5][:, width:] = grad_v[cut:].astype(BF16)
                else:
                    out = outs[k if k < 4 else k + 1]
                    out[:, :width] = grad_k.astype(BF16)
                    out[:, width:] = grad_v.astype(BF16)

    @pl.when(step == steps - 1)
    def _():
        dq_ref[...] = acc[...].T * F32(SCALING)


def attend_back(queries, grads, attended, lse, sources, ring, pieces, table, lens, facts, dtype):
    rows, width = queries.shape
    steps = table.shape[0]
    counts = [min(p.shape[0], limit) for p, limit in pieces]
    wide = grads[0].shape[1]
    if ring:
        out_specs = [whole(s.shape) for s in sources]
        out_shape = [shaped(*s.shape, dtype=BF16) for s in sources]
    else:
        out_specs = [pl.BlockSpec((1, rows, 2 * width), lambda j, *_: (j, 0, 0))]
        out_shape = [shaped(steps, rows, 2 * width, dtype=dtype)]
    return run(
        functools.partial(attend_back_kernel, ring, len(sources), len(pieces), len(out_specs)),
        (steps,),
        [
            whole((rows, width)),
            whole((rows, width)),
            whole((8, rows)),
            whole((rows // 2, wide)),
            whole((rows // 2, wide)),
        ]
        + [pl.BlockSpec(memory_space=pl.ANY)] * len(sources)
        + [column(r, lambda j: 3) for r in counts],
        [whole((rows, width))] + out_specs,
        [shaped(rows, width)] + out_shape,
        [
            pltpu.VMEM((width, rows), F32),
            pltpu.VMEM((8, rows), F32),
            pltpu.VMEM((rows, width), BF16),
            pltpu.VMEM((steps, rows, 2 * width), BF16),
            pltpu.SemaphoreType.DMA((steps,)),
        ],
        [table, lens, facts, queries, attended, lse, *grads, *sources] + [p for p, _ in pieces],
        4 + 4 * steps,
        prefetch=3,
    )


def per_device(
    block_input,
    cotangent,
    frame_lengths,
    frame_scenes,
    qkv_weight,
    out_weight,
    up_weight,
    down_weight,
    block_gains,
):
    quarter, wide = block_input.shape
    frames = lax.axis_size("frame")
    ring = on_ring()
    my_frame = lax.axis_index("frame")
    my_row = lax.axis_index("row")
    chip, core = my_row // 2, my_row % 2
    width = qkv_weight.shape[3]
    hidden = up_weight.shape[2]
    shard = wide // frames
    half = 2 * quarter
    facts = jnp.stack([chip, core, frame_lengths[my_frame]]).astype(jnp.int32)

    if ring:
        walk = jnp.array(RING, jnp.int32)
        at = jnp.argmax(walk == my_frame).astype(jnp.int32)
        order = lax.dynamic_slice_in_dim(jnp.concatenate([walk, walk]), at, frames)
        lane_order = order
    else:
        order = jnp.arange(frames, dtype=jnp.int32)
        lane_order = jnp.arange(wide // LANES, dtype=jnp.int32)
    rel_lens = frame_lengths[order]
    other_scene = (frame_scenes[order] != frame_scenes[my_frame]).astype(jnp.int32)
    scene_table = jnp.argsort(other_scene, stable=True)[: frames // 2].astype(jnp.int32)
    frame_table = jnp.zeros((1,), jnp.int32)
    frame_lens = frame_lengths[my_frame].reshape(1)

    qkv_shard = jnp.transpose(qkv_weight, (0, 2, 1, 3))
    if ring:
        packed = []
        for block in range(2):
            lead = shard + (16 if block == 0 else 0)
            pick = lambda s, b=block: pl.BlockSpec((1,) + s[1:], lambda *_: (b,) + (0,) * (len(s) - 1))
            packed.append(
                run(
                    functools.partial(pack_kernel, block == 0),
                    (1,),
                    [
                        pick(qkv_shard.shape),
                        pick(out_weight.shape),
                        pick(up_weight.shape),
                        pick(down_weight.shape),
                        whole(block_gains.shape),
                    ],
                    [whole((lead, 4 * width)), whole((shard, 2 * hidden))],
                    [shaped(lead, 4 * width, dtype=BF16), shaped(shard, 2 * hidden, dtype=BF16)],
                    [],
                    [qkv_shard, out_weight, up_weight, down_weight, block_gains],
                    2,
                )
            )
        limits = [shard] * 4 + [shard // 2] * 2 + [shard] * 3
        weights = []
        for block in range(2):
            at_pieces = ring_gather(packed[block][0], shard // 2)
            ff_pieces = ring_gather(packed[block][1], shard // 2)
            weights.append((list(zip(at_pieces, limits)), list(zip(ff_pieces, limits))))
        raw = [p for p, _ in weights[0][0]]
        gain_sources = raw[:4] + raw[5:]
        gain_specs = [
            pl.BlockSpec((16, LANES), functools.partial(lambda r, *_: (r, 0), (p.shape[0] - 16) // 16))
            for p in gain_sources
        ]
        inverse = jnp.argmax(order[None, :] == (2 * my_row + jnp.arange(2))[:, None], axis=1)
        gains, heads = run(
            gains_kernel,
            (1,),
            gain_specs,
            [whole((16, wide)), whole((16, width))],
            [shaped(16, wide), shaped(16, width)],
            [],
            [inverse.astype(jnp.int32), *gain_sources],
            1,
            prefetch=1,
        )
    else:
        limits = [wide]
        weights = []
        for block in range(2):
            at = jnp.concatenate(
                [qkv_shard[block, 0], qkv_shard[block, 1], qkv_shard[block, 2], out_weight[block].T], axis=1
            )
            ff = jnp.concatenate([up_weight[block], down_weight[block].T], axis=1)
            weights.append(
                tuple([(lax.all_gather(w, "frame", axis=0, tiled=True), wide)] for w in (at, ff))
            )
        gains = lax.all_gather(block_gains, "frame", axis=2, tiled=True).astype(F32).reshape(12, wide)
        gains = jnp.concatenate([gains, jnp.zeros((4, wide), F32)])
        heads = lax.dynamic_slice_in_dim(gains, my_row * width, width, 1)
    piece_rows = limits

    def enter(values, masked):
        return run(
            functools.partial(enter_kernel, masked),
            (1,),
            [whole(values.shape)] * 2,
            whole((half, wide)),
            shaped(half, wide),
            [],
            [lane_order, facts, values, row_take(values, 2)],
            1,
            prefetch=2,
        )

    big = whole((half, wide))
    gspec = whole(gains.shape)

    def reduce_rows(other, own):
        near = (own + row_take(other, 1).astype(F32)).astype(BF16)
        return near, row_take(near, 2)

    h = enter(block_input, False)
    normed = run(
        functools.partial(first_norm_kernel, 0),
        (1,),
        [big, gspec],
        big,
        shaped(half, wide, dtype=BF16),
        [],
        [h, gains],
        1,
    )
    stored = []
    output = None
    for block in range(2):
        base = 6 * block
        at, ff = weights[block]
        normed = (normed, row_take(normed, 1))
        queries, kv, mixed = project(normed, at, heads, base + 4)
        if block == 0:
            sources, walking, table, lens = [kv], False, frame_table, frame_lens
        else:
            table, lens, walking = scene_table, rel_lens, ring
            sources = ring_gather(kv, half) if ring else [lax.all_gather(kv, "frame", axis=0, tiled=True)]
        attended, lse, part_other, part_own = attend(
            queries, sources, walking, at, table, lens, facts, wide
        )
        branch = reduce_rows(part_other, part_own)
        middle, second = run(
            functools.partial(residual_kernel, base + 2, base + 1),
            (1,),
            [big, big, big, gspec],
            [big, big],
            [shaped(half, wide), shaped(half, wide, dtype=BF16)],
            [],
            [h, *branch, gains],
            2,
        )
        second = (second, row_take(second, 1))
        up_values, active, part_other, part_own = feed(second, ff, hidden)
        down = reduce_rows(part_other, part_own)
        stored.append(
            (h, normed, queries, mixed, (sources, walking, table, lens), attended, lse, branch)
            + (middle, second, up_values, active, down)
        )
        if block == 0:
            h, normed = run(
                functools.partial(residual_kernel, base + 3, base + 6),
                (1,),
                [big, big, big, gspec],
                [big, big],
                [shaped(half, wide), shaped(half, wide, dtype=BF16)],
                [],
                [middle, *down, gains],
                2,
            )
        else:
            output = run(
                functools.partial(output_kernel, base + 3),
                (1,),
                [big, big, big, gspec],
                whole((quarter, wide)),
                shaped(quarter, wide, dtype=BF16),
                [pltpu.VMEM((half, wide), F32)],
                [lane_order, facts, middle, *down, gains],
                1,
                prefetch=2,
            )

    grad = enter(cotangent, True)
    at_shapes = [(2, 3, shard, width), (2, width, shard)]
    ff_shapes = [(2, shard, hidden), (2, hidden, shard)]
    at_out, ff_out = [], []
    gain_sums = [None, None]
    input_grad = None
    for block in (1, 0):
        base = 6 * block
        at, ff = weights[block]
        h, normed, queries, mixed, keys, attended, lse, branch, middle, second, up_values, active, down = stored[
            block
        ]
        sources, walking, table, lens = keys
        scaled, sum_three = run(
            functools.partial(seed_kernel, base + 3),
            (1,),
            [big, big, big, gspec],
            [big, whole((1, wide))],
            [shaped(half, wide, dtype=BF16), shaped(1, wide)],
            [],
            [grad, *down, gains],
            1,
        )
        grad_down = (scaled, row_take(scaled, 1))
        grad_up, part_other, part_own = feed_back(grad_down, up_values, ff)
        incoming = reduce_rows(part_other, part_own)
        ff_grads = weight_grads(second, grad_up, grad_down, active, piece_rows, 8)
        grad_middle, scaled, sums_middle = run(
            functools.partial(middle_back_kernel, base),
            (1,),
            [big] * 6 + [gspec],
            [big, big, whole((2, wide))],
            [shaped(half, wide), shaped(half, wide, dtype=BF16), shaped(2, wide)],
            [],
            [grad, *incoming, middle, *branch, gains],
            2,
        )
        grad_branch = (scaled, row_take(scaled, 1))
        dq, *dkv_parts = attend_back(
            queries,
            grad_branch,
            attended,
            lse,
            sources,
            walking,
            at,
            table,
            lens,
            facts,
            F32 if block == 0 else BF16,
        )
        if block == 0:
            dkv = dkv_parts[0][0]
        elif ring:
            own, right, left = ring_scatter(dkv_parts)
            dkv = own.astype(F32) + right.astype(F32) + left.astype(F32)
        else:
            spread = jnp.zeros((frames,) + dkv_parts[0].shape[1:], BF16).at[table].set(dkv_parts[0])
            dkv = lax.psum_scatter(spread, "frame", scatter_dimension=0, tiled=False).astype(F32)
        grad_mixed, part_other, part_own, sums_heads = project_back(
            dq, dkv, mixed, at, heads, base + 4, wide
        )
        incoming = reduce_rows(part_other, part_own)
        at_grads = weight_grads(normed, grad_mixed, grad_branch, attended, piece_rows, 4)
        if block == 1:
            grad, sum_zero = run(
                functools.partial(first_back_kernel, base),
                (1,),
                [big] * 4 + [gspec],
                [big, whole((1, wide))],
                [shaped(half, wide), shaped(1, wide)],
                [],
                [grad_middle, *incoming, h, gains],
                2,
            )
        else:
            input_grad, sum_zero = run(
                last_back_kernel,
                (1,),
                [big] * 4 + [gspec],
                [whole((quarter, wide)), whole((1, wide))],
                [shaped(quarter, wide, dtype=BF16), shaped(1, wide)],
                [pltpu.VMEM((half, wide), F32)],
                [lane_order, facts, grad_middle, *incoming, h, gains],
                2,
                prefetch=2,
            )
        gain_sums[block] = (
            jnp.concatenate([sum_zero, sums_middle, sum_three]) * F32(0.5),
            sums_heads,
        )
        if ring:
            ff_out = finish(finish_ff_kernel, ring_scatter(ff_grads), ff_shapes, block, ff_out)
            at_out = finish(finish_at_kernel, ring_scatter(at_grads), at_shapes, block, at_out)
        else:
            ff_sum = lax.psum_scatter(ff_grads[0], "frame", scatter_dimension=0, tiled=True).astype(F32)
            at_sum = lax.psum_scatter(at_grads[0], "frame", scatter_dimension=0, tiled=True).astype(F32)
            ff_out = [(ff_sum[:, :hidden], ff_sum[:, hidden:].T)] + ff_out
            at_out = [
                (
                    jnp.stack([at_sum[:, i * width : (i + 1) * width] for i in range(3)]),
                    at_sum[:, 3 * width :].T,
                )
            ] + at_out
    if not ring:
        ff_out = [jnp.stack(both) for both in zip(*ff_out, strict=True)]
        at_out = [jnp.stack(both) for both in zip(*at_out, strict=True)]

    rows = jnp.stack([gain_sums[0][0], gain_sums[1][0]])
    blocks = rows.reshape(2, 4, wide // LANES, LANES)
    rows = jnp.zeros_like(blocks).at[:, :, lane_order].set(blocks).reshape(2, 4, wide)
    per_head = lax.dynamic_update_slice_in_dim(
        jnp.zeros((2, 2, wide), F32),
        jnp.stack([gain_sums[0][1], gain_sums[1][1]]),
        my_row * width,
        2,
    )
    total = lax.psum(jnp.concatenate([rows, per_head], axis=1), ("frame", "row"))
    gains_grad = lax.dynamic_slice_in_dim(total, my_frame * shard, shard, 2)
    return (
        output,
        input_grad,
        jnp.transpose(at_out[0], (0, 2, 1, 3)),
        at_out[1],
        ff_out[0],
        ff_out[1],
        gains_grad,
    )


def solution(mesh):
    return jax.shard_map(
        per_device,
        mesh=mesh,
        in_specs=(
            P(("frame", "row"), None),
            P(("frame", "row"), None),
            P(),
            P(),
            P(None, "frame", None, "row"),
            P(None, "row", "frame"),
            P(None, "frame", "row"),
            P(None, "row", "frame"),
            P(None, None, "frame"),
        ),
        out_specs=(
            P(("frame", "row"), None),
            P(("frame", "row"), None),
            P(None, "frame", None, "row"),
            P(None, "row", "frame"),
            P(None, "frame", "row"),
            P(None, "row", "frame"),
            P(None, None, "frame"),
        ),
        check_vma=False,
    )
```

time: 879 us -> 648 us (0.74)
  Pallas kernels: 29 us -> 189 us
  waiting for transfers between devices: 408 us -> 251 us
  starting transfers between devices: 220 us -> 103 us
  matrix products: 60.4 us -> 0 us
  blocking collectives: 63.5 us -> 39.9 us
  other arithmetic: 35.9 us -> 16.6 us
  local copies, waits for them, and re-layouts: 51.7 us -> 33.3 us
    pallas_call x4 -> x36, Pallas kernels: 29 us -> 189 us  [run(): pl.pallas_call(kernel, grid_spec=pltpu.PrefetchScalarGridSpec(num_scalar_...]
    ppermute x174 -> x106, waiting for transfers between devices: 408 us -> 251 us  [the longest x80 203 us: ring_take(): lax.ppermute(value, 'frame', [(RING[(i + step) % count], RING[i]) for i i...]
    ppermute x174 -> x106, starting transfers between devices: 220 us -> 103 us  [the longest x80 83.9 us: ring_take(): lax.ppermute(value, 'frame', [(RING[(i + step) % count], RING[i]) for i i...]
    dot_general x84 -> x0, matrix products: 60.4 us -> none  [the longest x24 17.5 us: dot_t(): lax.dot_general(a, b, (((1,), (1,)), ((), ())), preferred_element_type=F32)]
    all_gather x1 -> x0, blocking collectives: 21.2 us -> none  [per_device(): lax.all_gather(block_gains, 'frame', axis=2, tiled=True).astype(F32)]
    concatenate x17 -> x11, other arithmetic: 9.24 us -> 0.33 us  [the longest x5 0.16 us: ring_scatter(): right = jnp.concatenate([add_pair(ahead[2][:cut], low), ahead[2][cut:]])]
    unnamed x339 -> x254, local copies, waits for them, and re-layouts: 25.4 us -> 22.5 us
  transfers between devices with their start and end apart: 174 -> 106, of which waited for: 80 -> 48; matrix products, arithmetic and copies ran while one was open for 14% -> 3% of each run, Pallas kernels for 1% -> 19%
where the time goes in v2:
time: 648 us; the launch traced here: 637 us
  waiting for transfers between devices  251 us (39%)
  Pallas kernels  189 us (29%)
  starting transfers between devices  103 us (16%)
  blocking collectives  39.9 us (6%)
  local copies, waits for them, and re-layouts  33.3 us (5%)
  other arithmetic  16.6 us (3%)
    ppermute x80, waiting for transfers between devices, ring_take(): lax.ppermute(value, 'frame', [(RING[(i + step) % count], RING[i]) for i i...  203 us
    pallas_call x36, Pallas kernels, run(): pl.pallas_call(kernel, grid_spec=pltpu.PrefetchScalarGridSpec(num_scalar_...  189 us
    ppermute x80, starting transfers between devices, ring_take(): lax.ppermute(value, 'frame', [(RING[(i + step) % count], RING[i]) for i i...  83.9 us
    ppermute x26, waiting for transfers between devices, row_take(): return lax.ppermute(value, 'row', [(i ^ bit, i) for i in range(4)])  48.5 us
    psum x1, blocking collectives, per_device(): lax.psum(jnp.concatenate([rows, per_head], axis=1), ('frame', 'row'))  39.9 us
    unnamed x254, local copies, waits for them, and re-layouts  22.5 us
    ppermute x26, starting transfers between devices, row_take(): return lax.ppermute(value, 'row', [(i ^ bit, i) for i in range(4)])  18.9 us
  transfers between devices with their start and end apart: 106, of which 48 were waited for; matrix products, arithmetic and copies ran while one was open for 3% of the time, Pallas kernels for 19%

profile of v2, /device:TPU:0, one launch (start us, length us, event | category | flops | bytes accessed | tf_op | source)
XLA Modules:
  0.0 637.2 jit_solution(16932502453168450103)
XLA Ops:
  67.4 9.1 %collective-permute-done.14.refs_2_.refs_11_ = bf16[128,2048]{1,0:T(8,128)(2,1)S(1)} collective-permute-done((bf16[128,2048]{1,0:T(8,128)(2,1)S(1)}, bf16[128,2048]{1,0:T(8,128)(2,1)S(1)}, u32[]{:S(2)}, u32[]{:S(2)}) %collective-permute-start.14) | collective-permute-done | bytes 524320 | tf_op jit(solution)/shard_map/ppermute | solution.py:29
  100.0 7.5 %shard_map.160 = (f32[512,1024]{1,0:T(8,128)}, bf16[512,1024]{1,0:T(8,128)(2,1)}, bf16[256,1024]{1,0:T(8,128)(2,1)}, f32[256,1024]{1,0:T(8,128)}) custom-call(bf16[256,1024]{1,0:T(8,128)(2,1)} %get-tuple-element.138.own_ref.a_own, bf16[256,1024]{1,0:T(8,128)(2,1)} %copy-done.71, bf16[128,2048]{1,0:T(8,128)(2,1)} %get-tuple-element.139.refs_0_.refs_9_, ...), custom_call_target="tpu_custom_call" | custom-call | flops 7000000000 | bytes 14000000 | tf_op jit(solution)/shard_map/pallas_call | solution.py:86
  153.5 10.3 %collective-permute-done.32.refs_1_.refs_6_ = bf16[512,512]{1,0:T(8,128)(2,1)S(1)} collective-permute-done((bf16[512,512]{1,0:T(8,128)(2,1)}, bf16[512,512]{1,0:T(8,128)(2,1)S(1)}, u32[]{:S(2)}, u32[]{:S(2)}) %collective-permute-start.32) | collective-permute-done | bytes 524320 | tf_op jit(solution)/shard_map/ppermute | solution.py:29
  165.8 10.1 %collective-permute-done.33.refs_2_.refs_7_ = bf16[512,512]{1,0:T(8,128)(2,1)S(1)} collective-permute-done((bf16[512,512]{1,0:T(8,128)(2,1)S(1)}, bf16[512,512]{1,0:T(8,128)(2,1)S(1)}, u32[]{:S(2)}, u32[]{:S(2)}) %collective-permute-start.33) | collective-permute-done | bytes 524320 | tf_op jit(solution)/shard_map/ppermute | solution.py:29
  179.9 10.8 %collective-permute-done.34.refs_3_.refs_8_ = bf16[512,512]{1,0:T(8,128)(2,1)S(1)} collective-permute-done((bf16[512,512]{1,0:T(8,128)(2,1)S(1)}, bf16[512,512]{1,0:T(8,128)(2,1)S(1)}, u32[]{:S(2)}, u32[]{:S(2)}) %collective-permute-start.34) | collective-permute-done | bytes 524320 | tf_op jit(solution)/shard_map/ppermute | solution.py:29
  203.2 12.0 %shard_map.164 = (bf16[512,256]{1,0:T(8,128)(2,1)}, f32[8,512]{1,0:T(8,128)}, bf16[256,1024]{1,0:T(8,128)(2,1)}, f32[256,1024]{1,0:T(8,128)}) custom-call(s32[4]{0:T(128)} %bitcast.39, s32[8]{0:T(128)} %gather_fusion.1, s32[3]{0:T(128)} %pad_add_fusion.facts_ref, bf16[512,256]{1,0:T(8,128)(2,1)} %get-tuple-element.146.q_ref.refs_0_, ...), custom_call_target="tpu_custom_call" | custom-call | flops 11000000512 | bytes 22000000 | tf_op jit(solution)/shard_map/pallas_call | solution.py:86
  221.6 8.2 %collective-permute-done.44.refs_2_.refs_11_ = bf16[128,2048]{1,0:T(8,128)(2,1)S(1)} collective-permute-done((bf16[128,2048]{1,0:T(8,128)(2,1)}, bf16[128,2048]{1,0:T(8,128)(2,1)S(1)}, u32[]{:S(2)}, u32[]{:S(2)}) %collective-permute-start.44) | collective-permute-done | bytes 524320 | tf_op jit(solution)/shard_map/ppermute | solution.py:29
  253.3 7.6 %shard_map.166 = (f32[512,1024]{1,0:T(8,128)}, bf16[512,1024]{1,0:T(8,128)(2,1)}, bf16[256,1024]{1,0:T(8,128)(2,1)}, f32[256,1024]{1,0:T(8,128)}) custom-call(bf16[256,1024]{1,0:T(8,128)(2,1)} %get-tuple-element.151.own_ref.a_own, bf16[256,1024]{1,0:T(8,128)(2,1)} %copy-done.80, bf16[128,2048]{1,0:T(8,128)(2,1)} %get-tuple-element.152.refs_0_.refs_9_, ...), custom_call_target="tpu_custom_call" | custom-call | flops 7000000000 | bytes 14000000 | tf_op jit(solution)/shard_map/pallas_call | solution.py:86
  267.2 17.8 %collective-permute-done.53.far_ref = bf16[128,1024]{1,0:T(8,128)(2,1)S(1)} collective-permute-done((bf16[128,1024]{1,0:T(8,128)(2,1)S(1)}, bf16[128,1024]{1,0:T(8,128)(2,1)S(1)}, u32[]{:S(2)}, u32[]{:S(2)}) %collective-permute-start.53) | collective-permute-done | bytes 262176 | tf_op jit(solution)/shard_map/ppermute | solution.py:33
  294.8 7.6 %shard_map.170 = (bf16[512,1024]{1,0:T(8,128)(2,1)}, bf16[256,1024]{1,0:T(8,128)(2,1)}, f32[256,1024]{1,0:T(8,128)}) custom-call(bf16[256,1024]{1,0:T(8,128)(2,1)} %get-tuple-element.155.own_ref.b_own, bf16[256,1024]{1,0:T(8,128)(2,1)} %copy-done.84, f32[512,1024]{1,0:T(8,128)} %get-tuple-element.156.values_ref, ...), custom_call_target="tpu_custom_call" | custom-call | flops 8000000000 | bytes 16000000 | tf_op jit(solution)/shard_map/pallas_call | solution.py:86
  307.8 12.2 %collective-permute-done.56.far_ref = bf16[256,1024]{1,0:T(8,128)(2,1)S(1)} collective-permute-done((bf16[256,1024]{1,0:T(8,128)(2,1)S(1)}, bf16[256,1024]{1,0:T(8,128)(2,1)S(1)}, u32[]{:S(2)}, u32[]{:S(2)}) %collective-permute-start.56) | collective-permute-done | bytes 524320 | tf_op jit(solution)/shard_map/ppermute | solution.py:33
  329.2 18.9 %shard_map.172 = (f32[512,256]{1,0:T(8,128)}, bf16[512,512]{1,0:T(8,128)(2,1)}, bf16[512,512]{1,0:T(8,128)(2,1)}, bf16[512,512]{1,0:T(8,128)(2,1)}, bf16[512,512...) custom-call(s32[4]{0:T(128)} %bitcast.40, ...), custom_call_target="tpu_custom_call" | custom-call | flops 20000000000 | bytes 40000000 | tf_op jit(solution)/shard_map/pallas_call | solution.py:86
  349.0 9.1 %shard_map.186 = (bf16[128,2048]{1,0:T(8,128)(2,1)}, bf16[128,2048]{1,0:T(8,128)(2,1)}, bf16[128,2048]{1,0:T(8,128)(2,1)}, bf16[128,2048]{1,0:T(8,128)(2,1)}, bf...) custom-call(bf16[256,1024]{1,0:T(8,128)(2,1)} %get-tuple-element.151, ...), custom_call_target="tpu_custom_call" | custom-call | flops 8000000000 | bytes 16000000 | tf_op jit(solution)/shard_map/pallas_call | solution.py:86
  364.5 8.9 %collective-permute-done.58 = bf16[256,512]{1,0:T(8,128)(2,1)S(1)} collective-permute-done((bf16[256,512]{1,0:T(8,128)(2,1)S(1)}, bf16[256,512]{1,0:T(8,128)(2,1)S(1)}, u32[]{:S(2)}, u32[]{:S(2)}) %collective-permute-start.58) | collective-permute-done | bytes 262176 | tf_op jit(solution)/shard_map/ppermute | solution.py:29
  381.0 7.5 %collective-permute-done.59 = bf16[512,512]{1,0:T(8,128)(2,1)S(1)} collective-permute-done((bf16[512,512]{1,0:T(8,128)(2,1)S(1)}, bf16[512,512]{1,0:T(8,128)(2,1)S(1)}, u32[]{:S(2)}, u32[]{:S(2)}) %collective-permute-start.59) | collective-permute-done | bytes 524320 | tf_op jit(solution)/shard_map/ppermute | solution.py:29
  394.1 15.2 %collective-permute-done.60 = bf16[512,512]{1,0:T(8,128)(2,1)S(1)} collective-permute-done((bf16[512,512]{1,0:T(8,128)(2,1)S(1)}, bf16[512,512]{1,0:T(8,128)(2,1)S(1)}, u32[]{:S(2)}, u32[]{:S(2)}) %collective-permute-start.60) | collective-permute-done | bytes 524320 | tf_op jit(solution)/shard_map/ppermute | solution.py:29
  413.1 11.3 %collective-permute-done.61 = bf16[512,512]{1,0:T(8,128)(2,1)S(1)} collective-permute-done((bf16[512,512]{1,0:T(8,128)(2,1)S(1)}, bf16[512,512]{1,0:T(8,128)(2,1)S(1)}, u32[]{:S(2)}, u32[]{:S(2)}) %collective-permute-start.61) | collective-permute-done | bytes 524320 | tf_op jit(solution)/shard_map/ppermute | solution.py:29
  445.2 8.1 %collective-permute-done.86 = bf16[64,1024]{1,0:T(8,128)(2,1)S(1)} collective-permute-done((bf16[64,1024]{1,0:T(8,128)(2,1)}, bf16[64,1024]{1,0:T(8,128)(2,1)S(1)}, u32[]{:S(2)}, u32[]{:S(2)}) %collective-permute-start.86) | collective-permute-done | bytes 131104 | tf_op jit(solution)/shard_map/ppermute | solution.py:29
  475.0 7.6 %shard_map.176 = (bf16[512,1024]{1,0:T(8,128)(2,1)}, bf16[256,1024]{1,0:T(8,128)(2,1)}, f32[256,1024]{1,0:T(8,128)}) custom-call(bf16[256,1024]{1,0:T(8,128)(2,1)} %get-tuple-element.177.own_ref.b_own, bf16[256,1024]{1,0:T(8,128)(2,1)} %copy-done.95, f32[512,1024]{1,0:T(8,128)} %get-tuple-element.178.values_ref, ...), custom_call_target="tpu_custom_call" | custom-call | flops 8000000000 | bytes 16000000 | tf_op jit(solution)/shard_map/pallas_call | solution.py:86
  482.6 9.1 %shard_map.185 = (bf16[128,2048]{1,0:T(8,128)(2,1)}, bf16[128,2048]{1,0:T(8,128)(2,1)}, bf16[128,2048]{1,0:T(8,128)(2,1)}, bf16[128,2048]{1,0:T(8,128)(2,1)}, bf...) custom-call(bf16[256,1024]{1,0:T(8,128)(2,1)} %get-tuple-element.138, ...), custom_call_target="tpu_custom_call" | custom-call | flops 8000000000 | bytes 16000000 | tf_op jit(solution)/shard_map/pallas_call | solution.py:86
  524.4 8.1 %shard_map.178 = (f32[512,256]{1,0:T(8,128)}, f32[1,512,512]{2,1,0:T(8,128)}) custom-call(s32[1]{0:T(128)} %constant.58.clone.1.table_ref, s32[1]{0:T(128)} %dynamic_slice.14.lens_ref, s32[3]{0:T(128)} %pad_add_fusion.facts_ref, bf16[512,256]{1,0:T(8,128)(2,1)} %get-tuple-element.133.q_ref.refs_0_, bf16[512,256]{1,0:T(8,128)(2,1)} %get-tuple-element.182.refs_1_.second_ref, ...), custom_call_target="tpu_custom_call" | custom-call | flops 8000000000 | bytes 16000000 | tf_op jit(solution)/shard_map/pallas_call | solution.py:86
  532.5 6.9 %shard_map.179 = (bf16[512,768]{1,0:T(8,128)(2,1)}, bf16[256,1024]{1,0:T(8,128)(2,1)}, f32[256,1024]{1,0:T(8,128)}, f32[2,256]{1,0:T(2,128)}) custom-call(f32[512,256]{1,0:T(8,128)} %get-tuple-element.185.dq_ref, f32[512,512]{1,0:T(8,128)} %bitcast.37, f32[512,512]{1,0:T(8,128)} %get-tuple-element.187.mixed_ref, ...), custom_call_target="tpu_custom_call" | custom-call | flops 6000000000 | bytes 12000000 | tf_op jit(solution)/shard_map/pallas_call | solution.py:86
  557.2 10.7 %collective-permute-done.75 = bf16[128,1024]{1,0:T(8,128)(2,1)S(1)} collective-permute-done((bf16[128,1024]{1,0:T(8,128)(2,1)S(1)}, bf16[128,1024]{1,0:T(8,128)(2,1)S(1)}, u32[]{:S(2)}, u32[]{:S(2)}) %collective-permute-start.75) | collective-permute-done | bytes 262176 | tf_op jit(solution)/shard_map/ppermute | solution.py:29
  596.2 39.9 %psum.7 = f32[2,6,1024]{2,1,0:T(8,128)S(1)} all-reduce(f32[2,6,1024]{2,1,0:T(8,128)S(1)} %pad_maximum_fusion.10), channel_id=1, replica_groups=mesh['frame'=8,'row'=4] {'frame','row'}, use_global_device_ids=true, to_apply=%region_4.5 | all-reduce | flops 12288 | bytes 98304 | tf_op jit(solution)/shard_map/psum | solution.py:1087
  (569 shorter events, 358.2 us)
Async XLA Ops:
  7.1 25.6 %collective-permute-start = (bf16[128,1024]{1,0:T(8,128)(2,1)S(1)}, bf16[128,1024]{1,0:T(8,128)(2,1)S(1)}, u32[]{:S(2)}, u32[]{:S(2)}) collective-permute-start(bf16[128,1024]{1,0:T(8,128)(2,1)S(1)} %copy-done.103), channel_id=1, source_target_pairs={{2,0},{3,1},{0,2},{1,3},{6,4},{7,5},{4,6},{5,7},{10,8},{11,9},{8,1... | collective-permute-start | bytes 786440 | tf_op jit(solution)/shard_map/ppermute | solution.py:33
  44.2 18.0 %collective-permute-start.13 = (bf16[128,2048]{1,0:T(8,128)(2,1)S(1)}, bf16[128,2048]{1,0:T(8,128)(2,1)S(1)}, u32[]{:S(2)}, u32[]{:S(2)}) collective-permute-start(bf16[128,2048]{1,0:T(8,128)(2,1)S(1)} %copy-done.65), channel_id=1, source_target_pairs={{8,0},{16,8},{24,16},{28,24},{20,28},{12,20},{4,12},{0,4},{9,1},{1... | collective-permute-start | bytes 1572872 | tf_op jit(solution)/shard_map/ppermute | solution.py:29
  45.7 18.1 %collective-permute-start.17 = (bf16[128,2048]{1,0:T(8,128)(2,1)S(1)}, bf16[128,2048]{1,0:T(8,128)(2,1)S(1)}, u32[]{:S(2)}, u32[]{:S(2)}) collective-permute-start(bf16[128,2048]{1,0:T(8,128)(2,1)S(1)} %copy-done.65), channel_id=1, source_target_pairs={{4,0},{0,8},{8,16},{16,24},{24,28},{28,20},{20,12},{12,4},{5,1},{1... | collective-permute-start | bytes 1572872 | tf_op jit(solution)/shard_map/ppermute | solution.py:29
  177.9 37.3 %collective-permute-start.43 = (bf16[128,2048]{1,0:T(8,128)(2,1)S(1)}, bf16[128,2048]{1,0:T(8,128)(2,1)}, u32[]{:S(2)}, u32[]{:S(2)}) collective-permute-start(bf16[128,2048]{1,0:T(8,128)(2,1)S(1)} %copy-done.74), channel_id=1, source_target_pairs={{8,0},{16,8},{24,16},{28,24},{20,28},{12,20},{4,12},{0,4},{9,1},{1... | collective-permute-start | bytes 1572872 | tf_op jit(solution)/shard_map/ppermute | solution.py:29
  179.5 37.5 %collective-permute-start.47 = (bf16[128,2048]{1,0:T(8,128)(2,1)S(1)}, bf16[128,2048]{1,0:T(8,128)(2,1)}, u32[]{:S(2)}, u32[]{:S(2)}) collective-permute-start(bf16[128,2048]{1,0:T(8,128)(2,1)S(1)} %copy-done.74), channel_id=1, source_target_pairs={{4,0},{0,8},{8,16},{16,24},{24,28},{28,20},{20,12},{12,4},{5,1},{1... | collective-permute-start | bytes 1572872 | tf_op jit(solution)/shard_map/ppermute | solution.py:29
  264.5 24.1 %collective-permute-start.52 = (bf16[256,1024]{1,0:T(8,128)(2,1)S(1)}, bf16[256,1024]{1,0:T(8,128)(2,1)S(1)}, u32[]{:S(2)}, u32[]{:S(2)}) collective-permute-start(bf16[256,1024]{1,0:T(8,128)(2,1)S(1)} %add_convert_fusion.16.own_ref), channel_id=1, source_target_pairs={{2,0},{3,1},{0,2},{1,3},{6,4},{7,5},{4,6},{5,7},{10,8},{11,9},{8,1... | collective-permute-start | bytes 1572872 | tf_op jit(solution)/shard_map/ppermute | solution.py:33
  360.4 29.5 %collective-permute-start.102 = (bf16[64,2048]{1,0:T(8,128)(2,1)}, bf16[64,2048]{1,0:T(8,128)(2,1)S(1)}, u32[]{:S(2)}, u32[]{:S(2)}) collective-permute-start(bf16[64,2048]{1,0:T(8,128)(2,1)} %get-tuple-element.236), channel_id=1, source_target_pairs={{8,0},{16,8},{24,16},{28,24},{20,28},{12,20},{4,12},{0,4},{9,1},{1... | collective-permute-start | bytes 786440 | tf_op jit(solution)/shard_map/ppermute | solution.py:29
  375.0 36.6 %collective-permute-start.99 = (bf16[128,2048]{1,0:T(8,128)(2,1)S(1)}, bf16[128,2048]{1,0:T(8,128)(2,1)S(1)}, u32[]{:S(2)}, u32[]{:S(2)}) collective-permute-start(bf16[128,2048]{1,0:T(8,128)(2,1)S(1)} %pad_maximum_fusion.4), channel_id=1, source_target_pairs={{4,0},{0,8},{8,16},{16,24},{24,28},{28,20},{20,12},{12,4},{5,1},{1... | collective-permute-start | bytes 1572872 | tf_op jit(solution)/shard_map/ppermute | solution.py:29
  388.6 20.7 %collective-permute-start.60 = (bf16[512,512]{1,0:T(8,128)(2,1)S(1)}, bf16[512,512]{1,0:T(8,128)(2,1)S(1)}, u32[]{:S(2)}, u32[]{:S(2)}) collective-permute-start(bf16[512,512]{1,0:T(8,128)(2,1)S(1)} %add_convert_fusion.14), channel_id=1, source_target_pairs={{4,0},{0,8},{8,16},{16,24},{24,28},{28,20},{20,12},{12,4},{5,1},{1... | collective-permute-start | bytes 1572872 | tf_op jit(solution)/shard_map/ppermute | solution.py:29
  393.3 19.8 %collective-permute-start.65 = (bf16[512,512]{1,0:T(8,128)(2,1)S(1)}, bf16[512,512]{1,0:T(8,128)(2,1)S(1)}, u32[]{:S(2)}, u32[]{:S(2)}) collective-permute-start(bf16[512,512]{1,0:T(8,128)(2,1)S(1)} %add_convert_fusion.11), channel_id=1, source_target_pairs={{8,0},{16,8},{24,16},{28,24},{20,28},{12,20},{4,12},{0,4},{9,1},{1... | collective-permute-start | bytes 1572872 | tf_op jit(solution)/shard_map/ppermute | solution.py:29
  410.8 29.1 %collective-permute-start.103 = (bf16[128,2048]{1,0:T(8,128)(2,1)S(1)}, bf16[128,2048]{1,0:T(8,128)(2,1)S(1)}, u32[]{:S(2)}, u32[]{:S(2)}) collective-permute-start(bf16[128,2048]{1,0:T(8,128)(2,1)S(1)} %pad_maximum_fusion.5), channel_id=1, source_target_pairs={{8,0},{16,8},{24,16},{28,24},{20,28},{12,20},{4,12},{0,4},{9,1},{1... | collective-permute-start | bytes 1572872 | tf_op jit(solution)/shard_map/ppermute | solution.py:29
  411.7 44.7 %collective-permute-start.100 = (bf16[128,2048]{1,0:T(8,128)(2,1)S(1)}, bf16[128,2048]{1,0:T(8,128)(2,1)S(1)}, u32[]{:S(2)}, u32[]{:S(2)}) collective-permute-start(bf16[128,2048]{1,0:T(8,128)(2,1)S(1)} %add_convert_fusion.3), channel_id=1, source_target_pairs={{4,0},{0,8},{8,16},{16,24},{24,28},{28,20},{20,12},{12,4},{5,1},{1... | collective-permute-start | bytes 1572872 | tf_op jit(solution)/shard_map/ppermute | solution.py:29
  440.1 30.7 %collective-permute-start.104 = (bf16[128,2048]{1,0:T(8,128)(2,1)S(1)}, bf16[128,2048]{1,0:T(8,128)(2,1)S(1)}, u32[]{:S(2)}, u32[]{:S(2)}) collective-permute-start(bf16[128,2048]{1,0:T(8,128)(2,1)S(1)} %add_convert_fusion.1), channel_id=1, source_target_pairs={{8,0},{16,8},{24,16},{28,24},{20,28},{12,20},{4,12},{0,4},{9,1},{1... | collective-permute-start | bytes 1572872 | tf_op jit(solution)/shard_map/ppermute | solution.py:29
  456.6 36.5 %collective-permute-start.101 = (bf16[128,2048]{1,0:T(8,128)(2,1)S(1)}, bf16[128,2048]{1,0:T(8,128)(2,1)S(1)}, u32[]{:S(2)}, u32[]{:S(2)}) collective-permute-start(bf16[128,2048]{1,0:T(8,128)(2,1)S(1)} %add_convert_fusion.2), channel_id=1, source_target_pairs={{4,0},{0,8},{8,16},{16,24},{24,28},{28,20},{20,12},{12,4},{5,1},{1... | collective-permute-start | bytes 1572872 | tf_op jit(solution)/shard_map/ppermute | solution.py:29
  470.9 22.2 %collective-permute-start.105 = (bf16[128,2048]{1,0:T(8,128)(2,1)S(1)}, bf16[128,2048]{1,0:T(8,128)(2,1)S(1)}, u32[]{:S(2)}, u32[]{:S(2)}) collective-permute-start(bf16[128,2048]{1,0:T(8,128)(2,1)S(1)} %add_convert_fusion), channel_id=1, source_target_pairs={{8,0},{16,8},{24,16},{28,24},{20,28},{12,20},{4,12},{0,4},{9,1},{1... | collective-permute-start | bytes 1572872 | tf_op jit(solution)/shard_map/ppermute | solution.py:29
  472.0 24.6 %collective-permute-start.85 = (bf16[128,1024]{1,0:T(8,128)(2,1)S(1)}, bf16[128,1024]{1,0:T(8,128)(2,1)S(1)}, u32[]{:S(2)}, u32[]{:S(2)}) collective-permute-start(bf16[128,1024]{1,0:T(8,128)(2,1)S(1)} %add_convert_fusion.26), channel_id=1, source_target_pairs={{4,0},{0,8},{8,16},{16,24},{24,28},{28,20},{20,12},{12,4},{5,1},{1... | collective-permute-start | bytes 786440 | tf_op jit(solution)/shard_map/ppermute | solution.py:29
  473.2 23.4 %collective-permute-start.89 = (bf16[128,1024]{1,0:T(8,128)(2,1)S(1)}, bf16[128,1024]{1,0:T(8,128)(2,1)S(1)}, u32[]{:S(2)}, u32[]{:S(2)}) collective-permute-start(bf16[128,1024]{1,0:T(8,128)(2,1)S(1)} %add_convert_fusion.24), channel_id=1, source_target_pairs={{8,0},{16,8},{24,16},{28,24},{20,28},{12,20},{4,12},{0,4},{9,1},{1... | collective-permute-start | bytes 786440 | tf_op jit(solution)/shard_map/ppermute | solution.py:29
  500.8 20.3 %collective-permute-start.91 = (bf16[128,2048]{1,0:T(8,128)(2,1)S(1)}, bf16[128,2048]{1,0:T(8,128)(2,1)S(1)}, u32[]{:S(2)}, u32[]{:S(2)}) collective-permute-start(bf16[128,2048]{1,0:T(8,128)(2,1)S(1)} %pad_maximum_fusion.2), channel_id=1, source_target_pairs={{4,0},{0,8},{8,16},{16,24},{24,28},{28,20},{20,12},{12,4},{5,1},{1... | collective-permute-start | bytes 1572872 | tf_op jit(solution)/shard_map/ppermute | solution.py:29
  521.3 25.2 %collective-permute-start.92 = (bf16[128,2048]{1,0:T(8,128)(2,1)S(1)}, bf16[128,2048]{1,0:T(8,128)(2,1)S(1)}, u32[]{:S(2)}, u32[]{:S(2)}) collective-permute-start(bf16[128,2048]{1,0:T(8,128)(2,1)S(1)} %add_convert_fusion.7), channel_id=1, source_target_pairs={{4,0},{0,8},{8,16},{16,24},{24,28},{28,20},{20,12},{12,4},{5,1},{1... | collective-permute-start | bytes 1572872 | tf_op jit(solution)/shard_map/ppermute | solution.py:29
  522.4 33.6 %collective-permute-start.96 = (bf16[128,2048]{1,0:T(8,128)(2,1)S(1)}, bf16[128,2048]{1,0:T(8,128)(2,1)S(1)}, u32[]{:S(2)}, u32[]{:S(2)}) collective-permute-start(bf16[128,2048]{1,0:T(8,128)(2,1)S(1)} %add_convert_fusion.5), channel_id=1, source_target_pairs={{8,0},{16,8},{24,16},{28,24},{20,28},{12,20},{4,12},{0,4},{9,1},{1... | collective-permute-start | bytes 1572872 | tf_op jit(solution)/shard_map/ppermute | solution.py:29
  546.7 34.3 %collective-permute-start.93 = (bf16[128,2048]{1,0:T(8,128)(2,1)S(1)}, bf16[128,2048]{1,0:T(8,128)(2,1)S(1)}, u32[]{:S(2)}, u32[]{:S(2)}) collective-permute-start(bf16[128,2048]{1,0:T(8,128)(2,1)S(1)} %add_convert_fusion.6), channel_id=1, source_target_pairs={{4,0},{0,8},{8,16},{16,24},{24,28},{28,20},{20,12},{12,4},{5,1},{1... | collective-permute-start | bytes 1572872 | tf_op jit(solution)/shard_map/ppermute | solution.py:29
  547.6 22.9 %collective-permute-start.72 = (bf16[256,1024]{1,0:T(8,128)(2,1)S(1)}, bf16[256,1024]{1,0:T(8,128)(2,1)S(1)}, u32[]{:S(2)}, u32[]{:S(2)}) collective-permute-start(bf16[256,1024]{1,0:T(8,128)(2,1)S(1)} %copy-done.86), channel_id=1, source_target_pairs={{1,0},{0,1},{3,2},{2,3},{5,4},{4,5},{7,6},{6,7},{9,8},{8,9},{11,10... | collective-permute-start | bytes 1572872 | tf_op jit(solution)/shard_map/ppermute | solution.py:33
  556.1 24.8 %collective-permute-start.97 = (bf16[128,2048]{1,0:T(8,128)(2,1)S(1)}, bf16[128,2048]{1,0:T(8,128)(2,1)S(1)}, u32[]{:S(2)}, u32[]{:S(2)}) collective-permute-start(bf16[128,2048]{1,0:T(8,128)(2,1)S(1)} %add_convert_fusion.4), channel_id=1, source_target_pairs={{8,0},{16,8},{24,16},{28,24},{20,28},{12,20},{4,12},{0,4},{9,1},{1... | collective-permute-start | bytes 1572872 | tf_op jit(solution)/shard_map/ppermute | solution.py:29
  570.7 18.9 %collective-permute-start.73 = (bf16[256,1024]{1,0:T(8,128)(2,1)S(1)}, bf16[256,1024]{1,0:T(8,128)(2,1)S(1)}, u32[]{:S(2)}, u32[]{:S(2)}) collective-permute-start(bf16[256,1024]{1,0:T(8,128)(2,1)S(1)} %add_convert_fusion.8.own_ref), channel_id=1, source_target_pairs={{2,0},{3,1},{0,2},{1,3},{6,4},{7,5},{4,6},{5,7},{10,8},{11,9},{8,1... | collective-permute-start | bytes 1572872 | tf_op jit(solution)/shard_map/ppermute | solution.py:33
  (208 other events, 2044.5 us)

commit v3 on v2

--- a/solution.py
+++ b/solution.py
@@ -22,6 +22,14 @@
 
 def on_ring():
     return lax.axis_size("frame") == len(RING)
+
+
+def frame_groups():
+    return [list(RING)] if on_ring() else None
+
+
+def frame_order(frames):
+    return RING if on_ring() else tuple(range(frames))
 
 
 def ring_take(value, step):
@@ -78,13 +86,25 @@
     return pl.BlockSpec((rows, TILE), lambda j, *_: (0, place(j)))
 
 
+WEIGH = 3.0
+
+
 def cost(us):
-    return pl.CostEstimate(flops=int(us * 1.0e9), bytes_accessed=int(us * 2.0e6), transcendentals=0)
-
-
-def run(kernel, grid, in_specs, out_specs, out_shape, scratch, operands, us, prefetch=0, aliases=None):
+    return pl.CostEstimate(
+        flops=int(us * WEIGH * 1.0e9), bytes_accessed=int(us * WEIGH * 2.0e6), transcendentals=0
+    )
+
+
+def run(kernel, grid, in_specs, out_specs, out_shape, scratch, operands, us, prefetch=0, aliases=None, after=()):
+    count = len(operands)
+
+    def body(*refs):
+        kernel(*refs[:count], *refs[count + len(after) :])
+
+    in_specs = list(in_specs) + [pl.BlockSpec(memory_space=pl.ANY)] * len(after)
+    operands = [*operands, *after]
     return pl.pallas_call(
-        kernel,
+        body,
         grid_spec=pltpu.PrefetchScalarGridSpec(
             num_scalar_prefetch=prefetch,
             grid=grid,
@@ -159,35 +179,43 @@
     return slot < length
 
 
-def pack_kernel(with_gains, qkv_ref, out_ref, up_ref, down_ref, gains_ref, at_ref, ff_ref):
-    rows = up_ref.shape[1]
+def pack_at_kernel(qkv_ref, out_ref, at_ref):
+    rows = out_ref.shape[2]
     width = qkv_ref.shape[3]
     for i in range(3):
         at_ref[:rows, i * width : (i + 1) * width] = qkv_ref[0, i]
     at_ref[:rows, 3 * width :] = out_ref[0].T
+
+
+def pack_ff_kernel(up_ref, down_ref, ff_ref):
     ff = up_ref.shape[2]
     ff_ref[:, :ff] = up_ref[0]
     ff_ref[:, ff:] = down_ref[0].T
-    if with_gains:
-        at_ref[rows:, :] = jnp.zeros((16, at_ref.shape[1]), BF16)
-        flat = jnp.concatenate([gains_ref[0], gains_ref[1], jnp.zeros((4, rows), BF16)], axis=0)
-        at_ref[rows:, :rows] = flat
-
-
-def gains_kernel(inverse_ref, *refs):
-    pieces, (wide_ref, heads_ref) = refs[:-2], refs[-2:]
-    for k, piece in enumerate(pieces):
-        wide_ref[:, k * LANES : (k + 1) * LANES] = piece[...].astype(F32)
-    for k in range(2):
-        start = pl.multiple_of(inverse_ref[k] * LANES, LANES)
-        heads_ref[:, k * LANES : (k + 1) * LANES] = wide_ref[:, pl.ds(start, LANES)]
-
-
-def enter_kernel(masked, order_ref, facts_ref, own_ref, far_ref, out_ref):
+
+
+def gain_sums_kernel(order, facts_ref, *refs):
+    out_ref = refs[-1]
+    out_ref[...] = jnp.zeros_like(out_ref)
+    row = facts_ref[0] * 2 + facts_ref[1]
+    for block in range(2):
+        zero, middle, three, heads = refs[4 * block : 4 * block + 4]
+        base = 6 * block
+        for k in range(out_ref.shape[0]):
+            lanes = slice(k * LANES, (k + 1) * LANES)
+            place = order[k]
+            out_ref[place, base : base + 1, :] = zero[:, lanes]
+            out_ref[place, base + 1 : base + 3, :] = middle[:, lanes] * 0.5
+            out_ref[place, base + 3 : base + 4, :] = three[:, lanes] * 0.5
+        for k in range(2):
+            lanes = slice(k * LANES, (k + 1) * LANES)
+            out_ref[row * 2 + k, base + 4 : base + 6, :] = heads[:, lanes]
+
+
+def enter_kernel(masked, order, facts_ref, own_ref, far_ref, out_ref):
     rows = own_ref.shape[0]
     chip, core, length = facts_ref[0], facts_ref[1], facts_ref[2]
-    for k in range(own_ref.shape[1] // LANES):
-        lanes = pl.ds(pl.multiple_of(order_ref[k] * LANES, LANES), LANES)
+    for k in range(len(order)):
+        lanes = slice(order[k] * LANES, (order[k] + 1) * LANES)
         for source, place in ((own_ref, chip), (far_ref, 1 - chip)):
             values = source[:, lanes].astype(F32)
             if masked:
@@ -197,11 +225,11 @@
             out_ref[pl.ds(start, rows), k * LANES : (k + 1) * LANES] = values
 
 
-def leave(values_ref, order_ref, facts_ref, out_ref):
+def leave(values_ref, order, facts_ref, out_ref):
     rows = out_ref.shape[0]
     start = pl.multiple_of(facts_ref[0] * rows, rows)
-    for k in range(out_ref.shape[1] // LANES):
-        lanes = pl.ds(pl.multiple_of(order_ref[k] * LANES, LANES), LANES)
+    for k in range(len(order)):
+        lanes = slice(order[k] * LANES, (order[k] + 1) * LANES)
         values = values_ref[pl.ds(start, rows), k * LANES : (k + 1) * LANES]
         out_ref[:, lanes] = values.astype(out_ref.dtype)
 
@@ -222,9 +250,9 @@
     normed_ref[...] = (unit * gains_ref[norm_row : norm_row + 1, :]).astype(BF16)
 
 
-def output_kernel(scale_row, order_ref, facts_ref, h_ref, own_ref, far_ref, gains_ref, out_ref, held):
+def output_kernel(scale_row, order, facts_ref, h_ref, own_ref, far_ref, gains_ref, out_ref, held):
     held[...] = h_ref[...] + gains_ref[scale_row : scale_row + 1, :] * total_of(own_ref, far_ref)
-    leave(held, order_ref, facts_ref, out_ref)
+    leave(held, order, facts_ref, out_ref)
 
 
 def seed_kernel(row, grad_ref, own_ref, far_ref, gains_ref, scaled_ref, sums_ref):
@@ -245,16 +273,15 @@
     scaled_ref[...] = (grad * gains_ref[base + 2 : base + 3, :]).astype(BF16)
 
 
-def first_back_kernel(base, grad_ref, own_ref, far_ref, h_ref, gains_ref, next_ref, sums_ref):
+def first_back_kernel(base, grad_ref, own_ref, far_ref, h_ref, gains_ref, next_ref):
     grad_in = total_of(own_ref, far_ref)
     unit, scale = norm_parts(h_ref[...])
-    sums_ref[...] = jnp.sum(grad_in * unit, axis=0, keepdims=True)
     next_ref[...] = grad_ref[...] + norm_back(unit, scale, gains_ref[base : base + 1, :], grad_in)
 
 
-def last_back_kernel(order_ref, facts_ref, grad_ref, own_ref, far_ref, h_ref, gains_ref, out_ref, sums_ref, held):
-    first_back_kernel(0, grad_ref, own_ref, far_ref, h_ref, gains_ref, held, sums_ref)
-    leave(held, order_ref, facts_ref, out_ref)
+def last_back_kernel(order, facts_ref, grad_ref, own_ref, far_ref, h_ref, gains_ref, out_ref, held):
+    first_back_kernel(0, grad_ref, own_ref, far_ref, h_ref, gains_ref, held)
+    leave(held, order, facts_ref, out_ref)
 
 
 def project_kernel(row_q, count, own_ref, other_ref, *refs):
@@ -312,9 +339,9 @@
     )
 
 
-def project_back_kernel(row_q, count, dq_ref, dkv_ref, mixed_ref, heads_ref, *refs):
+def project_back_kernel(row_q, count, dq_ref, dkv_ref, mixed_ref, heads_ref, n_own_ref, n_other_ref, gains_ref, *refs):
     pieces = refs[:count]
-    grad_ref, other_ref, own_ref, sums_ref, acc = refs[count:]
+    grad_ref, other_ref, own_ref, sums_ref, zero_ref, acc = refs[count:]
     step = pl.program_id(0)
 
     @pl.when(step == 0)
@@ -345,10 +372,14 @@
         half = own_ref.shape[0]
         own_ref[...] = acc[:half, :]
         other_ref[...] = acc[half:, :].astype(BF16)
-
-
-def project_back(dq, dkv, mixed, pieces, heads, row_q, wide):
+        products = acc[:half, :] * n_own_ref[...].astype(F32) + acc[half:, :] * n_other_ref[...].astype(F32)
+        row_g = row_q - 4
+        zero_ref[...] = jnp.sum(products, axis=0, keepdims=True) / gains_ref[row_g : row_g + 1, :]
+
+
+def project_back(dq, dkv, mixed, pieces, heads, row_q, normed, gains):
     full, width = dq.shape
+    wide = gains.shape[1]
     rows = [min(p.shape[0], limit) for p, limit in pieces]
     return run(
         functools.partial(project_back_kernel, row_q, len(pieces)),
@@ -358,17 +389,27 @@
             column(full, lambda j: jnp.maximum(j - 1, 0)),
             column(full, lambda j: jnp.minimum(j, 1)),
             whole(heads.shape),
+            whole((full // 2, wide)),
+            whole((full // 2, wide)),
+            whole(gains.shape),
         ]
         + [column(r, lambda j: j) for r in rows],
-        [column(full, lambda j: j), whole((full // 2, wide)), whole((full // 2, wide)), whole((2, width))],
+        [
+            column(full, lambda j: j),
+            whole((full // 2, wide)),
+            whole((full // 2, wide)),
+            whole((2, width)),
+            whole((1, wide)),
+        ],
         [
             shaped(full, 3 * width, dtype=BF16),
             shaped(full // 2, wide, dtype=BF16),
             shaped(full // 2, wide),
             shaped(2, width),
+            shaped(1, wide),
         ],
         [pltpu.VMEM((full, wide), F32)],
-        [dq, dkv, mixed, heads] + [p for p, _ in pieces],
+        [dq, dkv, mixed, heads, *normed, gains] + [p for p, _ in pieces],
         6,
     )
 
@@ -479,8 +520,7 @@
     )
 
 
-def weight_kernel(split, rows, a_own, a_other, b_own, b_other, first_ref, second_ref, *refs):
-    outs, turned = refs[:-1], refs[-1]
+def weight_kernel(split, a_own, a_other, b_own, b_other, first_ref, second_ref, out_ref, turned):
     step = pl.program_id(0)
     half = a_own.shape[0]
 
@@ -496,62 +536,52 @@
     def _():
         turn(b_own, b_other)
 
-    def store(right):
-        start = 0
-        for out, count in zip(outs, rows, strict=True):
-            out[...] = dot_nn(turned[start : start + count, :], right).astype(BF16)
-            start += count
-
     @pl.when(step < split)
     def _():
-        store(first_ref[...])
+        out_ref[...] = dot_nn(turned[...], first_ref[...]).astype(BF16)
 
     @pl.when(step >= split)
     def _():
-        store(second_ref[...])
-
-
-def weight_grads(a, first, b, second, rows, us):
+        out_ref[...] = dot_nn(turned[...], second_ref[...]).astype(BF16)
+
+
+def weight_grads(a, first, b, second, us, after):
     half, wide = a[0].shape
     split = first.shape[1] // TILE
     steps = split + second.shape[1] // TILE
     return run(
-        functools.partial(weight_kernel, split, rows),
+        functools.partial(weight_kernel, split),
         (steps,),
         [whole((half, wide))] * 4
         + [
             column(2 * half, lambda j: jnp.minimum(j, split - 1)),
             column(2 * half, lambda j: jnp.maximum(j - split, 0)),
         ],
-        [column(r, lambda j: j) for r in rows],
-        [shaped(r, steps * TILE, dtype=BF16) for r in rows],
+        column(wide, lambda j: j),
+        shaped(wide, steps * TILE, dtype=BF16),
         [pltpu.VMEM((wide, 2 * half), BF16)],
         [*a, *b, first, second],
         us,
-    )
-
-
-def finish_ff_kernel(own_ref, right_ref, left_ref, *refs):
+        after=after,
+    )
+
+
+def finish_ff_kernel(part_ref, *refs):
     up_ref, down_ref = refs[-2:]
     hidden = up_ref.shape[2]
-    up_ref[0] = total_of(own_ref.at[:, :hidden], right_ref.at[:, :hidden]) + left_ref[:, :hidden].astype(F32)
-    down = total_of(own_ref.at[:, hidden:], right_ref.at[:, hidden:]) + left_ref[:, hidden:].astype(F32)
-    down_ref[0] = down.T
-
-
-def finish_at_kernel(own_ref, right_ref, left_ref, *refs):
+    up_ref[0] = part_ref[:, :hidden].astype(F32)
+    down_ref[0] = part_ref[:, hidden:].astype(F32).T
+
+
+def finish_at_kernel(part_ref, *refs):
     qkv_ref, out_ref = refs[-2:]
     width = qkv_ref.shape[3]
-    for i in range(4):
-        lanes = slice(i * width, (i + 1) * width)
-        part = total_of(own_ref.at[:, lanes], right_ref.at[:, lanes]) + left_ref[:, lanes].astype(F32)
-        if i < 3:
-            qkv_ref[0, i] = part
-        else:
-            out_ref[0] = part.T
-
-
-def finish(kernel, parts, shapes, block, earlier):
+    for i in range(3):
+        qkv_ref[0, i] = part_ref[:, i * width : (i + 1) * width].astype(F32)
+    out_ref[0] = part_ref[:, 3 * width :].astype(F32).T
+
+
+def finish(kernel, part, shapes, block, earlier):
     specs = [
         pl.BlockSpec((1,) + s[1:], functools.partial(lambda b, r, *_: (b,) + (0,) * (r - 1), block, len(s)))
         for s in shapes
@@ -559,13 +589,13 @@
     return run(
         kernel,
         (1,),
-        [whole(p.shape) for p in parts] + [pl.BlockSpec(memory_space=pl.ANY)] * len(earlier),
+        [whole(part.shape)] + [pl.BlockSpec(memory_space=pl.ANY)] * len(earlier),
         specs,
         [shaped(*s) for s in shapes],
         [],
-        [*parts, *earlier],
+        [part, *earlier],
         2,
-        aliases={3 + i: i for i in range(len(earlier))},
+        aliases={1 + i: i for i in range(len(earlier))},
     )
 
 
@@ -805,116 +835,110 @@
         walk = jnp.array(RING, jnp.int32)
         at = jnp.argmax(walk == my_frame).astype(jnp.int32)
         order = lax.dynamic_slice_in_dim(jnp.concatenate([walk, walk]), at, frames)
-        lane_order = order
+        lane_order = RING
     else:
         order = jnp.arange(frames, dtype=jnp.int32)
-        lane_order = jnp.arange(wide // LANES, dtype=jnp.int32)
+        lane_order = tuple(range(wide // LANES))
     rel_lens = frame_lengths[order]
     other_scene = (frame_scenes[order] != frame_scenes[my_frame]).astype(jnp.int32)
     scene_table = jnp.argsort(other_scene, stable=True)[: frames // 2].astype(jnp.int32)
     frame_table = jnp.zeros((1,), jnp.int32)
     frame_lens = frame_lengths[my_frame].reshape(1)
 
-    qkv_shard = jnp.transpose(qkv_weight, (0, 2, 1, 3))
-    if ring:
-        packed = []
-        for block in range(2):
-            lead = shard + (16 if block == 0 else 0)
-            pick = lambda s, b=block: pl.BlockSpec((1,) + s[1:], lambda *_: (b,) + (0,) * (len(s) - 1))
-            packed.append(
-                run(
-                    functools.partial(pack_kernel, block == 0),
-                    (1,),
-                    [
-                        pick(qkv_shard.shape),
-                        pick(out_weight.shape),
-                        pick(up_weight.shape),
-                        pick(down_weight.shape),
-                        whole(block_gains.shape),
-                    ],
-                    [whole((lead, 4 * width)), whole((shard, 2 * hidden))],
-                    [shaped(lead, 4 * width, dtype=BF16), shaped(shard, 2 * hidden, dtype=BF16)],
-                    [],
-                    [qkv_shard, out_weight, up_weight, down_weight, block_gains],
-                    2,
-                )
-            )
-        limits = [shard] * 4 + [shard // 2] * 2 + [shard] * 3
-        weights = []
-        for block in range(2):
-            at_pieces = ring_gather(packed[block][0], shard // 2)
-            ff_pieces = ring_gather(packed[block][1], shard // 2)
-            weights.append((list(zip(at_pieces, limits)), list(zip(ff_pieces, limits))))
-        raw = [p for p, _ in weights[0][0]]
-        gain_sources = raw[:4] + raw[5:]
-        gain_specs = [
-            pl.BlockSpec((16, LANES), functools.partial(lambda r, *_: (r, 0), (p.shape[0] - 16) // 16))
-            for p in gain_sources
-        ]
-        inverse = jnp.argmax(order[None, :] == (2 * my_row + jnp.arange(2))[:, None], axis=1)
-        gains, heads = run(
-            gains_kernel,
-            (1,),
-            gain_specs,
-            [whole((16, wide)), whole((16, width))],
-            [shaped(16, wide), shaped(16, width)],
-            [],
-            [inverse.astype(jnp.int32), *gain_sources],
-            1,
-            prefetch=1,
-        )
-    else:
-        limits = [wide]
-        weights = []
-        for block in range(2):
-            at = jnp.concatenate(
-                [qkv_shard[block, 0], qkv_shard[block, 1], qkv_shard[block, 2], out_weight[block].T], axis=1
-            )
-            ff = jnp.concatenate([up_weight[block], down_weight[block].T], axis=1)
-            weights.append(
-                tuple([(lax.all_gather(w, "frame", axis=0, tiled=True), wide)] for w in (at, ff))
-            )
-        gains = lax.all_gather(block_gains, "frame", axis=2, tiled=True).astype(F32).reshape(12, wide)
-        gains = jnp.concatenate([gains, jnp.zeros((4, wide), F32)])
-        heads = lax.dynamic_slice_in_dim(gains, my_row * width, width, 1)
-    piece_rows = limits
-
     def enter(values, masked):
         return run(
-            functools.partial(enter_kernel, masked),
+            functools.partial(enter_kernel, masked, lane_order),
             (1,),
             [whole(values.shape)] * 2,
             whole((half, wide)),
             shaped(half, wide),
             [],
-            [lane_order, facts, values, row_take(values, 2)],
+            [facts, values, row_take(values, 2)],
             1,
-            prefetch=2,
+            prefetch=1,
         )
 
     big = whole((half, wide))
-    gspec = whole(gains.shape)
-
-    def reduce_rows(other, own):
-        near = (own + row_take(other, 1).astype(F32)).astype(BF16)
-        return near, row_take(near, 2)
-
+
+    qkv_shard = jnp.transpose(qkv_weight, (0, 2, 1, 3))
+    if ring:
+        pick = lambda s, b: pl.BlockSpec((1,) + s[1:], lambda *_: (b,) + (0,) * (len(s) - 1))
+
+        def pack_at(block):
+            return run(
+                pack_at_kernel,
+                (1,),
+                [pick(qkv_shard.shape, block), pick(out_weight.shape, block)],
+                whole((shard, 4 * width)),
+                shaped(shard, 4 * width, dtype=BF16),
+                [],
+                [qkv_shard, out_weight],
+                1,
+            )
+
+        def pack_ff(block, after=()):
+            return run(
+                pack_ff_kernel,
+                (1,),
+                [pick(up_weight.shape, block), pick(down_weight.shape, block)],
+                whole((shard, 2 * hidden)),
+                shaped(shard, 2 * hidden, dtype=BF16),
+                [],
+                [up_weight, down_weight],
+                1,
+                after=after,
+            )
+
+    else:
+
+        def pack_at(block):
+            return jnp.concatenate([*qkv_shard[block], out_weight[block].T], axis=1)
+
+        def pack_ff(block, after=()):
+            return jnp.concatenate([up_weight[block], down_weight[block].T], axis=1)
+
+    def gather(packed):
+        return [(lax.all_gather(packed, "frame", axis=0, tiled=True, axis_index_groups=frame_groups()), wide)]
+
+    def scatter(grads):
+        return lax.psum_scatter(
+            grads, "frame", scatter_dimension=0, tiled=True, axis_index_groups=frame_groups()
+        )
+
+    at_zero, ff_zero, at_one = gather(pack_at(0)), gather(pack_ff(0)), gather(pack_at(1))
+    weights = [(at_zero, ff_zero), None]
+    if ring:
+        rows = jnp.concatenate([block_gains[0], block_gains[1], jnp.zeros((4, shard), BF16)]).astype(F32)
+        spread = lax.all_to_all(jnp.broadcast_to(rows[None], (frames, 16, shard)), "frame", 0, 0)
+        gains_abs = jnp.swapaxes(spread, 0, 1).reshape(16, wide)
+    else:
+        gains_abs = lax.all_gather(block_gains, "frame", axis=2, tiled=True).astype(F32).reshape(12, wide)
+        gains_abs = jnp.concatenate([gains_abs, jnp.zeros((4, wide), F32)])
+    heads = lax.dynamic_slice_in_dim(gains_abs, my_row * width, width, 1)
+    gains = jnp.concatenate([gains_abs[:, k * LANES : (k + 1) * LANES] for k in lane_order], axis=1)
     h = enter(block_input, False)
     normed = run(
         functools.partial(first_norm_kernel, 0),
         (1,),
-        [big, gspec],
+        [big, whole(gains.shape)],
         big,
         shaped(half, wide, dtype=BF16),
         [],
         [h, gains],
         1,
     )
+
+    gspec = whole(gains.shape)
+
+    def reduce_rows(other, own):
+        near = (own + row_take(other, 1).astype(F32)).astype(BF16)
+        return near, row_take(near, 2)
+
     stored = []
     output = None
     for block in range(2):
         base = 6 * block
-        at, ff = weights[block]
+        at, ff = weights[block] or (at_one, None)
         normed = (normed, row_take(normed, 1))
         queries, kv, mixed = project(normed, at, heads, base + 4)
         if block == 0:
@@ -922,6 +946,8 @@
         else:
             table, lens, walking = scene_table, rel_lens, ring
             sources = ring_gather(kv, half) if ring else [lax.all_gather(kv, "frame", axis=0, tiled=True)]
+            ff = gather(pack_ff(1, [sources[2], sources[7]] if ring else ()))
+            weights[1] = (at, ff)
         attended, lse, part_other, part_own = attend(
             queries, sources, walking, at, table, lens, facts, wide
         )
@@ -956,15 +982,15 @@
             )
         else:
             output = run(
-                functools.partial(output_kernel, base + 3),
+                functools.partial(output_kernel, base + 3, lane_order),
                 (1,),
                 [big, big, big, gspec],
                 whole((quarter, wide)),
                 shaped(quarter, wide, dtype=BF16),
                 [pltpu.VMEM((half, wide), F32)],
-                [lane_order, facts, middle, *down, gains],
+                [facts, middle, *down, gains],
                 1,
-                prefetch=2,
+                prefetch=1,
             )
 
     grad = enter(cotangent, True)
@@ -973,6 +999,7 @@
     at_out, ff_out = [], []
     gain_sums = [None, None]
     input_grad = None
+    after = []
     for block in (1, 0):
         base = 6 * block
         at, ff = weights[block]
@@ -993,7 +1020,9 @@
         grad_down = (scaled, row_take(scaled, 1))
         grad_up, part_other, part_own = feed_back(grad_down, up_values, ff)
         incoming = reduce_rows(part_other, part_own)
-        ff_grads = weight_grads(second, grad_up, grad_down, active, piece_rows, 8)
+        ff_grads = weight_grads(second, grad_up, grad_down, active, 8, [*after, incoming[0]])
+        ff_sum = scatter(ff_grads)
+        after = [ff_sum]
         grad_middle, scaled, sums_middle = run(
             functools.partial(middle_back_kernel, base),
             (1,),
@@ -1003,6 +1032,7 @@
             [],
             [grad, *incoming, middle, *branch, gains],
             2,
+            after=[ff_grads],
         )
         grad_branch = (scaled, row_take(scaled, 1))
         dq, *dkv_parts = attend_back(
@@ -1026,66 +1056,79 @@
         else:
             spread = jnp.zeros((frames,) + dkv_parts[0].shape[1:], BF16).at[table].set(dkv_parts[0])
             dkv = lax.psum_scatter(spread, "frame", scatter_dimension=0, tiled=False).astype(F32)
-        grad_mixed, part_other, part_own, sums_heads = project_back(
-            dq, dkv, mixed, at, heads, base + 4, wide
+        grad_mixed, part_other, part_own, sums_heads, sum_zero = project_back(
+            dq, dkv, mixed, at, heads, base + 4, normed, gains
         )
+        gain_sums[block] = (sum_zero, sums_middle, sum_three, sums_heads)
         incoming = reduce_rows(part_other, part_own)
-        at_grads = weight_grads(normed, grad_mixed, grad_branch, attended, piece_rows, 4)
+        at_grads = weight_grads(normed, grad_mixed, grad_branch, attended, 4, [*after, incoming[0]])
         if block == 1:
-            grad, sum_zero = run(
+            grad = run(
                 functools.partial(first_back_kernel, base),
                 (1,),
                 [big] * 4 + [gspec],
-                [big, whole((1, wide))],
-                [shaped(half, wide), shaped(1, wide)],
+                big,
+                shaped(half, wide),
                 [],
                 [grad_middle, *incoming, h, gains],
                 2,
+                after=[at_grads],
             )
         else:
-            input_grad, sum_zero = run(
-                last_back_kernel,
+            input_grad = run(
+                functools.partial(last_back_kernel, lane_order),
                 (1,),
                 [big] * 4 + [gspec],
-                [whole((quarter, wide)), whole((1, wide))],
-                [shaped(quarter, wide, dtype=BF16), shaped(1, wide)],
+                whole((quarter, wide)),
+                shaped(quarter, wide, dtype=BF16),
                 [pltpu.VMEM((half, wide), F32)],
-                [lane_order, facts, grad_middle, *incoming, h, gains],
+                [facts, grad_middle, *incoming, h, gains],
                 2,
-                prefetch=2,
+                prefetch=1,
+                after=[at_grads, ff_sum],
             )
-        gain_sums[block] = (
-            jnp.concatenate([sum_zero, sums_middle, sum_three]) * F32(0.5),
-            sums_heads,
-        )
+        at_sum = scatter(at_grads)
+        after = [at_sum]
         if ring:
-            ff_out = finish(finish_ff_kernel, ring_scatter(ff_grads), ff_shapes, block, ff_out)
-            at_out = finish(finish_at_kernel, ring_scatter(at_grads), at_shapes, block, at_out)
+            ff_out = finish(finish_ff_kernel, ff_sum, ff_shapes, block, ff_out)
+            at_out = finish(finish_at_kernel, at_sum, at_shapes, block, at_out)
         else:
-            ff_sum = lax.psum_scatter(ff_grads[0], "frame", scatter_dimension=0, tiled=True).astype(F32)
-            at_sum = lax.psum_scatter(at_grads[0], "frame", scatter_dimension=0, tiled=True).astype(F32)
+            ff_sum, at_sum = ff_sum.astype(F32), at_sum.astype(F32)
             ff_out = [(ff_sum[:, :hidden], ff_sum[:, hidden:].T)] + ff_out
-            at_out = [
-                (
-                    jnp.stack([at_sum[:, i * width : (i + 1) * width] for i in range(3)]),
-                    at_sum[:, 3 * width :].T,
-                )
-            ] + at_out
+            qkv_sum = jnp.stack([at_sum[:, i * width : (i + 1) * width] for i in range(3)])
+            at_out = [(qkv_sum, at_sum[:, 3 * width :].T)] + at_out
     if not ring:
         ff_out = [jnp.stack(both) for both in zip(*ff_out, strict=True)]
         at_out = [jnp.stack(both) for both in zip(*at_out, strict=True)]
 
-    rows = jnp.stack([gain_sums[0][0], gain_sums[1][0]])
-    blocks = rows.reshape(2, 4, wide // LANES, LANES)
-    rows = jnp.zeros_like(blocks).at[:, :, lane_order].set(blocks).reshape(2, 4, wide)
-    per_head = lax.dynamic_update_slice_in_dim(
-        jnp.zeros((2, 2, wide), F32),
-        jnp.stack([gain_sums[0][1], gain_sums[1][1]]),
-        my_row * width,
-        2,
-    )
-    total = lax.psum(jnp.concatenate([rows, per_head], axis=1), ("frame", "row"))
-    gains_grad = lax.dynamic_slice_in_dim(total, my_frame * shard, shard, 2)
+    if ring:
+        operands = [*gain_sums[0], *gain_sums[1]]
+        sent = run(
+            functools.partial(gain_sums_kernel, lane_order),
+            (1,),
+            [whole(v.shape) for v in operands],
+            whole((frames, 16, LANES)),
+            shaped(frames, 16, LANES),
+            [],
+            [facts, *operands],
+            1,
+            prefetch=1,
+        )
+        total = jnp.sum(lax.all_to_all(sent, "frame", 0, 0), axis=0)
+        total = total + row_take(total, 1)
+        total = total + row_take(total, 2)
+        gains_grad = total[:12].reshape(2, 6, LANES)
+    else:
+        rows = [jnp.concatenate([sums[0], sums[1] * F32(0.5), sums[2] * F32(0.5)]) for sums in gain_sums]
+        rows = jnp.stack(rows)
+        per_head = lax.dynamic_update_slice_in_dim(
+            jnp.zeros((2, 2, wide), F32),
+            jnp.stack([gain_sums[0][3], gain_sums[1][3]]),
+            my_row * width,
+            2,
+        )
+        total = lax.psum(jnp.concatenate([rows, per_head], axis=1), ("frame", "row"))
+        gains_grad = lax.dynamic_slice_in_dim(total, my_frame * shard, shard, 2)
     return (
         output,
         input_grad,

time: 648 us -> 556 us (0.86)
  starting transfers between devices: 103 us -> 48.1 us
  blocking collectives: 39.9 us -> 0 us
  between operations: 4.54 us -> 17.2 us
  local copies, waits for them, and re-layouts: 33.3 us -> 22.4 us
    ppermute x80 -> x16, waiting for transfers between devices: 203 us -> 93.1 us  [ring_take(): lax.ppermute(value, 'frame', [(RING[(i + step) % count], RING[i]) for i i...]
    ppermute x80 -> x16, starting transfers between devices: 83.9 us -> 18.8 us  [ring_take(): lax.ppermute(value, 'frame', [(RING[(i + step) % count], RING[i]) for i i...]
    ppermute x26 -> x28, waiting for transfers between devices: 48.5 us -> 109 us  [row_take(): return lax.ppermute(value, 'row', [(i ^ bit, i) for i in range(4)])]
    psum x1 -> x0, blocking collectives: 39.9 us -> none  [per_device(): lax.psum(jnp.concatenate([rows, per_head], axis=1), ('frame', 'row'))]
    all_gather x0 -> x4, waiting for transfers between devices: none -> 33.5 us  [gather(): lax.all_gather(packed, 'frame', axis=0, tiled=True, axis_index_groups=fra...]
    all_to_all x0 -> x2, starting transfers between devices: none -> 11.9 us  [the longest x1 7.25 us: per_device(): lax.all_to_all(jnp.broadcast_to(rows[None], (frames, 16, shard)), 'frame'...]
    reduce_scatter x0 -> x4, waiting for transfers between devices: none -> 8.51 us  [scatter(): lax.psum_scatter(grads, 'frame', scatter_dimension=0, tiled=True, axis_in...]
    all_to_all x0 -> x2, waiting for transfers between devices: none -> 6.62 us  [the longest x1 4.45 us: per_device(): total = jnp.sum(lax.all_to_all(sent, 'frame', 0, 0), axis=0)]
  transfers between devices with their start and end apart: 106 -> 54, of which waited for: 48 -> 44; matrix products, arithmetic and copies ran while one was open for 3% -> 5% of each run, Pallas kernels for 19% -> 26%
where the time goes in v3:
time: 556 us; the launch traced here: 547 us
  waiting for transfers between devices  251 us (45%)
  Pallas kernels  189 us (34%)
  starting transfers between devices  48.1 us (9%)
  local copies, waits for them, and re-layouts  22.4 us (4%)
  other arithmetic  19.3 us (3%)
  between operations  17.2 us (3%)
    pallas_call x38, Pallas kernels, run(): pl.pallas_call(body, grid_spec=pltpu.PrefetchScalarGridSpec(num_scalar_pr...  189 us
    ppermute x28, waiting for transfers between devices, row_take(): return lax.ppermute(value, 'row', [(i ^ bit, i) for i in range(4)])  109 us
    ppermute x16, waiting for transfers between devices, ring_take(): lax.ppermute(value, 'frame', [(RING[(i + step) % count], RING[i]) for i i...  93.1 us
    all_gather x4, waiting for transfers between devices, gather(): lax.all_gather(packed, 'frame', axis=0, tiled=True, axis_index_groups=fra...  33.5 us
    ppermute x16, starting transfers between devices, ring_take(): lax.ppermute(value, 'frame', [(RING[(i + step) % count], RING[i]) for i i...  18.8 us
    ppermute x28, starting transfers between devices, row_take(): return lax.ppermute(value, 'row', [(i ^ bit, i) for i in range(4)])  16.6 us
    unnamed x102, local copies, waits for them, and re-layouts  16 us
    convert_element_type x8, other arithmetic, reduce_rows(): near = (own + row_take(other, 1).astype(F32)).astype(BF16)  12.6 us
  transfers between devices with their start and end apart: 54, of which 44 were waited for; matrix products, arithmetic and copies ran while one was open for 5% of the time, Pallas kernels for 26%

profile of v3, /device:TPU:0, one launch (start us, length us, event | category | flops | bytes accessed | tf_op | source)
XLA Modules:
  0.0 546.5 jit_solution(7485196643699953721)
XLA Ops:
  33.5 13.2 %all-gather.5.cloned.1.call-done.refs_2_.refs_5_.refs_9_.refs_7_ = bf16[1024,1024]{1,0:T(8,128)(2,1)} async-done(((bf16[128,1024]{1,0:T(8,128)(2,1)}), bf16[1024,1024]{1,0:T(8,128)(2,1)}) %all-gather.5.cloned.1.call-update) | async-done | bytes 2097168 | tf_op jit(solution)/shard_map/all_gather | solution.py:901
  64.0 12.4 %collective-permute-done.3.refs_2_.refs_5_ = bf16[256,1024]{1,0:T(8,128)(2,1)S(1)} collective-permute-done((bf16[256,1024]{1,0:T(8,128)(2,1)S(1)}, bf16[256,1024]{1,0:T(8,128)(2,1)S(1)}, u32[]{:S(2)}, u32[]{:S(2)}) %collective-permute-start.3) | collective-permute-done | bytes 524320 | tf_op jit(solution)/shard_map/ppermute | solution.py:41
  82.2 13.1 %all-gather.7.cloned.1.call-done.refs_2_.refs_3_.refs_4_ = bf16[1024,2048]{1,0:T(8,128)(2,1)} async-done(((bf16[128,2048]{1,0:T(8,128)(2,1)}), bf16[1024,2048]{1,0:T(8,128)(2,1)}) %all-gather.7.cloned.1.call-update) | async-done | bytes 4194320 | tf_op jit(solution)/shard_map/all_gather | solution.py:901
  107.8 12.5 %collective-permute-done.6.refs_2_ = bf16[256,1024]{1,0:T(8,128)(2,1)S(1)} collective-permute-done((bf16[256,1024]{1,0:T(8,128)(2,1)S(1)}, bf16[256,1024]{1,0:T(8,128)(2,1)S(1)}, u32[]{:S(2)}, u32[]{:S(2)}) %collective-permute-start.6) | collective-permute-done | bytes 524320 | tf_op jit(solution)/shard_map/ppermute | solution.py:41
  139.4 10.3 %collective-permute-done.12.refs_12_.refs_16_ = bf16[512,512]{1,0:T(8,128)(2,1)S(1)} collective-permute-done((bf16[512,512]{1,0:T(8,128)(2,1)}, bf16[512,512]{1,0:T(8,128)(2,1)S(1)}, u32[]{:S(2)}, u32[]{:S(2)}) %collective-permute-start.12) | collective-permute-done | bytes 524320 | tf_op jit(solution)/shard_map/ppermute | solution.py:37
  151.8 7.5 %collective-permute-done.13.refs_11_.refs_3_.refs_15_ = bf16[512,512]{1,0:T(8,128)(2,1)S(1)} collective-permute-done((bf16[512,512]{1,0:T(8,128)(2,1)S(1)}, bf16[512,512]{1,0:T(8,128)(2,1)S(1)}, u32[]{:S(2)}, u32[]{:S(2)}) %collective-permute-start.13) | collective-permute-done | bytes 524320 | tf_op jit(solution)/shard_map/ppermute | solution.py:37
  167.8 13.2 %collective-permute-done.14.refs_10_.refs_14_ = bf16[512,512]{1,0:T(8,128)(2,1)S(1)} collective-permute-done((bf16[512,512]{1,0:T(8,128)(2,1)}, bf16[512,512]{1,0:T(8,128)(2,1)S(1)}, u32[]{:S(2)}, u32[]{:S(2)}) %collective-permute-start.14) | collective-permute-done | bytes 524320 | tf_op jit(solution)/shard_map/ppermute | solution.py:37
  196.2 11.8 %shard_map.164 = (bf16[512,256]{1,0:T(8,128)(2,1)}, f32[8,512]{1,0:T(8,128)}, bf16[256,1024]{1,0:T(8,128)(2,1)}, f32[256,1024]{1,0:T(8,128)}) custom-call(s32[4]{0:T(128)} %bitcast.21, s32[8]{0:T(128)} %gather_fusion.1, s32[3]{0:T(128)} %pad_add_fusion.refs_0_.refs_2_, bf16[512,256]{1,0:T(8,128)(2,1)} %get-tuple-element.95.refs_3_, ...), custom_call_target="tpu_custom_call" | custom-call | flops 32999999488 | bytes 66000000 | tf_op jit(solution)/shard_map/pallas_call | solution.py:106
  213.2 12.5 %collective-permute-done.17.refs_2_.refs_5_ = bf16[256,1024]{1,0:T(8,128)(2,1)S(1)} collective-permute-done((bf16[256,1024]{1,0:T(8,128)(2,1)S(1)}, bf16[256,1024]{1,0:T(8,128)(2,1)S(1)}, u32[]{:S(2)}, u32[]{:S(2)}) %collective-permute-start.17) | collective-permute-done | bytes 524320 | tf_op jit(solution)/shard_map/ppermute | solution.py:41
  232.2 7.4 %shard_map.167 = (f32[512,1024]{1,0:T(8,128)}, bf16[512,1024]{1,0:T(8,128)(2,1)}, bf16[256,1024]{1,0:T(8,128)(2,1)}, f32[256,1024]{1,0:T(8,128)}) custom-call(bf16[256,1024]{1,0:T(8,128)(2,1)} %get-tuple-element.100.refs_0_, bf16[256,1024]{1,0:T(8,128)(2,1)} %copy-done.33, bf16[1024,2048]{1,0:T(8,128)(2,1)} %all-gather.11.cloned.1.call-done.refs_2_.refs_3_.refs_4_, ...), custom_call_target="tpu_custom_call" | custom-call | flops 20999999488 | bytes 42000000 | tf_op jit(solution)/shard_map/pallas_call | solution.py:106
  266.0 7.6 %shard_map.171 = (bf16[512,1024]{1,0:T(8,128)(2,1)}, bf16[256,1024]{1,0:T(8,128)(2,1)}, f32[256,1024]{1,0:T(8,128)}) custom-call(bf16[256,1024]{1,0:T(8,128)(2,1)} %get-tuple-element.103.refs_0_.refs_2_, bf16[256,1024]{1,0:T(8,128)(2,1)} %copy-done.35, f32[512,1024]{1,0:T(8,128)} %get-tuple-element.104.refs_2_, ...), custom_call_target="tpu_custom_call" | custom-call | flops 24000000000 | bytes 48000000 | tf_op jit(solution)/shard_map/pallas_call | solution.py:106
  278.6 8.7 %shard_map.172.refs_7_ = bf16[1024,2048]{1,0:T(8,128)(2,1)} custom-call(bf16[256,1024]{1,0:T(8,128)(2,1)} %get-tuple-element.100.refs_0_, bf16[256,1024]{1,0:T(8,128)(2,1)} %copy-done.33, bf16[256,1024]{1,0:T(8,128)(2,1)} %get-tuple-element.103.refs_0_.refs_2_, bf16[256,1024]{1,0:T(8,128)(2,1)} %copy-done.35, bf16[512,1024]{1,0:T(8,128)(2,1)} %get-tuple-element.107.refs_4_, ...), custom_call_target="tpu_custom_call" | custom-call | flops 24000000000 | bytes 48000000 | tf_op jit(solution)/shard_map/pallas_call | solution.py:106
  299.1 19.2 %shard_map.174 = (f32[512,256]{1,0:T(8,128)}, bf16[512,512]{1,0:T(8,128)(2,1)}, bf16[512,512]{1,0:T(8,128)(2,1)}, bf16[512,512]{1,0:T(8,128)(2,1)}, bf16[512,512...) custom-call(s32[4]{0:T(128)} %bitcast.22, ...), custom_call_target="tpu_custom_call" | custom-call | flops 60000002048 | bytes 120000000 | tf_op jit(solution)/shard_map/pallas_call | solution.py:106
  322.5 10.7 %collective-permute-done.30 = bf16[256,512]{1,0:T(8,128)(2,1)S(1)} collective-permute-done((bf16[256,512]{1,0:T(8,128)(2,1)}, bf16[256,512]{1,0:T(8,128)(2,1)S(1)}, u32[]{:S(2)}, u32[]{:S(2)}) %collective-permute-start.30) | collective-permute-done | bytes 262176 | tf_op jit(solution)/shard_map/ppermute | solution.py:37
  337.4 21.5 %collective-permute-done.31 = bf16[512,512]{1,0:T(8,128)(2,1)S(1)} collective-permute-done((bf16[512,512]{1,0:T(8,128)(2,1)S(1)}, bf16[512,512]{1,0:T(8,128)(2,1)S(1)}, u32[]{:S(2)}, u32[]{:S(2)}) %collective-permute-start.31) | collective-permute-done | bytes 524320 | tf_op jit(solution)/shard_map/ppermute | solution.py:37
  361.2 11.3 %collective-permute-done.32 = bf16[512,512]{1,0:T(8,128)(2,1)S(1)} collective-permute-done((bf16[512,512]{1,0:T(8,128)(2,1)S(1)}, bf16[512,512]{1,0:T(8,128)(2,1)S(1)}, u32[]{:S(2)}, u32[]{:S(2)}) %collective-permute-start.32) | collective-permute-done | bytes 524320 | tf_op jit(solution)/shard_map/ppermute | solution.py:37
  375.0 10.4 %collective-permute-done.33 = bf16[512,512]{1,0:T(8,128)(2,1)S(1)} collective-permute-done((bf16[512,512]{1,0:T(8,128)(2,1)S(1)}, bf16[512,512]{1,0:T(8,128)(2,1)S(1)}, u32[]{:S(2)}, u32[]{:S(2)}) %collective-permute-start.33) | collective-permute-done | bytes 524320 | tf_op jit(solution)/shard_map/ppermute | solution.py:37
  387.2 7.5 %shard_map.175 = (bf16[512,768]{1,0:T(8,128)(2,1)}, bf16[256,1024]{1,0:T(8,128)(2,1)}, f32[256,1024]{1,0:T(8,128)}, f32[2,256]{1,0:T(2,128)}, f32[1,1024]{1,0:T(1,128)}) custom-call(f32[512,256]{1,0:T(8,128)} %get-tuple-element.113.refs_0_, f32[512,512]{1,0:T(8,128)} %convert_add_fusion.refs_1_, f32[512,512]{1,0:T(8,128)} %get-tuple-element.123.refs_2_, ...), custom_call_target="tpu_custom_call" | custom-call | flops 17999998976 | bytes 36000000 | tf_op jit(solution)/shard_map/pallas_call | solution.py:106
  422.2 7.7 %shard_map.179 = (bf16[512,1024]{1,0:T(8,128)(2,1)}, bf16[256,1024]{1,0:T(8,128)(2,1)}, f32[256,1024]{1,0:T(8,128)}) custom-call(bf16[256,1024]{1,0:T(8,128)(2,1)} %get-tuple-element.127.refs_0_.refs_2_, bf16[256,1024]{1,0:T(8,128)(2,1)} %copy-done.36, f32[512,1024]{1,0:T(8,128)} %get-tuple-element.128.refs_2_, ...), custom_call_target="tpu_custom_call" | custom-call | flops 24000000000 | bytes 48000000 | tf_op jit(solution)/shard_map/pallas_call | solution.py:106
  436.2 8.7 %shard_map.180.refs_7_ = bf16[1024,2048]{1,0:T(8,128)(2,1)} custom-call(bf16[256,1024]{1,0:T(8,128)(2,1)} %get-tuple-element.88.refs_0_, bf16[256,1024]{1,0:T(8,128)(2,1)} %copy-done.23, bf16[256,1024]{1,0:T(8,128)(2,1)} %get-tuple-element.127.refs_0_.refs_2_, bf16[256,1024]{1,0:T(8,128)(2,1)} %copy-done.36, bf16[512,1024]{1,0:T(8,128)(2,1)} %get-tuple-element.131.refs_4_, ...), custom_call_target="tpu_custom_call" | custom-call | flops 24000000000 | bytes 48000000 | tf_op jit(solution)/shard_map/pallas_call | solution.py:106
  447.4 10.6 %collective-permute-done.38.refs_2_ = bf16[256,1024]{1,0:T(8,128)(2,1)S(1)} collective-permute-done((bf16[256,1024]{1,0:T(8,128)(2,1)S(1)}, bf16[256,1024]{1,0:T(8,128)(2,1)S(1)}, u32[]{:S(2)}, u32[]{:S(2)}) %collective-permute-start.38) | collective-permute-done | bytes 524320 | tf_op jit(solution)/shard_map/ppermute | solution.py:41
  466.0 8.2 %shard_map.182 = (f32[512,256]{1,0:T(8,128)}, f32[1,512,512]{2,1,0:T(8,128)}) custom-call(s32[1]{0:T(128)} %constant.50.clone.1.refs_0_, s32[1]{0:T(128)} %dynamic_slice.13.refs_1_, s32[3]{0:T(128)} %pad_add_fusion.refs_0_.refs_2_, bf16[512,256]{1,0:T(8,128)(2,1)} %get-tuple-element.83.refs_3_, bf16[512,256]{1,0:T(8,128)(2,1)} %get-tuple-element.134.refs_4_.refs_5_, ...), custom_call_target="tpu_custom_call" | custom-call | flops 24000000000 | bytes 48000000 | tf_op jit(solution)/shard_map/pallas_call | solution.py:106
  474.2 7.5 %shard_map.183 = (bf16[512,768]{1,0:T(8,128)(2,1)}, bf16[256,1024]{1,0:T(8,128)(2,1)}, f32[256,1024]{1,0:T(8,128)}, f32[2,256]{1,0:T(2,128)}, f32[1,1024]{1,0:T(1,128)}) custom-call(f32[512,256]{1,0:T(8,128)} %get-tuple-element.137.refs_0_, f32[512,512]{1,0:T(8,128)} %bitcast.19, f32[512,512]{1,0:T(8,128)} %get-tuple-element.139.refs_2_, ...), custom_call_target="tpu_custom_call" | custom-call | flops 17999998976 | bytes 36000000 | tf_op jit(solution)/shard_map/pallas_call | solution.py:106
  519.5 11.0 %collective-permute-done.41.refs_3_ = bf16[256,1024]{1,0:T(8,128)(2,1)S(1)} collective-permute-done((bf16[256,1024]{1,0:T(8,128)(2,1)S(1)}, bf16[256,1024]{1,0:T(8,128)(2,1)S(1)}, u32[]{:S(2)}, u32[]{:S(2)}) %collective-permute-start.41) | collective-permute-done | bytes 524320 | tf_op jit(solution)/shard_map/ppermute | solution.py:41
  (277 shorter events, 264.8 us)
Async XLA Ops:
  7.2 39.6 %all-gather.5.cloned.1.call-start = ((), (), s32[]{:S(2)}) async-start(), calls=%async_computation.6 | async-start | bytes 2359296 | tf_op jit(solution)/shard_map/all_gather | solution.py:901
  9.8 15.0 %all-to-all-start = ((f32[8,16,128]{2,1,0:T(8,128)}), f32[8,16,128]{2,1,0:T(8,128)S(1)}, u32[]{:S(2)}, u32[]{:S(2)}) async-start(f32[8,16,128]{2,1,0:T(8,128)} %broadcast_in_dim.14), calls=%async_computation | async-start | bytes 131072 | tf_op jit(solution)/shard_map/all_to_all | solution.py:912
  17.1 78.3 %all-gather.7.cloned.1.call-start = ((), (), s32[]{:S(2)}) async-start(), calls=%async_computation.7 | async-start | bytes 4718592 | tf_op jit(solution)/shard_map/all_gather | solution.py:901
  20.7 110.5 %all-gather.9.cloned.1.call-start = ((), (), s32[]{:S(2)}) async-start(), calls=%async_computation.8 | async-start | bytes 2359296 | tf_op jit(solution)/shard_map/all_gather | solution.py:901
  62.4 14.0 %collective-permute-start.3 = (bf16[256,1024]{1,0:T(8,128)(2,1)S(1)}, bf16[256,1024]{1,0:T(8,128)(2,1)S(1)}, u32[]{:S(2)}, u32[]{:S(2)}) collective-permute-start(bf16[256,1024]{1,0:T(8,128)(2,1)S(1)} %add_convert_fusion.11.refs_1_.refs_4_), channel_id=1, source_target_pairs={{2,0},{3,1},{0,2},{1,3},{6,4},{7,5},{4,6},{5,7},{10,8},{11,9},{8,1... | collective-permute-start | bytes 1572872 | tf_op jit(solution)/shard_map/ppermute | solution.py:41
  81.9 149.6 %all-gather.11.cloned.1.call-start = ((), (), s32[]{:S(2)}) async-start(), calls=%async_computation.9 | async-start | bytes 4718592 | tf_op jit(solution)/shard_map/all_gather | solution.py:901
  106.3 14.0 %collective-permute-start.6 = (bf16[256,1024]{1,0:T(8,128)(2,1)S(1)}, bf16[256,1024]{1,0:T(8,128)(2,1)S(1)}, u32[]{:S(2)}, u32[]{:S(2)}) collective-permute-start(bf16[256,1024]{1,0:T(8,128)(2,1)S(1)} %add_convert_fusion.10.refs_1_), channel_id=1, source_target_pairs={{2,0},{3,1},{0,2},{1,3},{6,4},{7,5},{4,6},{5,7},{10,8},{11,9},{8,1... | collective-permute-start | bytes 1572872 | tf_op jit(solution)/shard_map/ppermute | solution.py:41
  162.8 236.7 %reduce-scatter.5.cloned.1.call-start = ((), (), s32[]{:S(2)}) async-start(), calls=%async_computation.10 | async-start | bytes 4718592 | tf_op jit(solution)/shard_map/reduce_scatter | solution.py:904
  162.9 18.2 %collective-permute-start.14 = (bf16[512,512]{1,0:T(8,128)(2,1)}, bf16[512,512]{1,0:T(8,128)(2,1)S(1)}, u32[]{:S(2)}, u32[]{:S(2)}) collective-permute-start(bf16[512,512]{1,0:T(8,128)(2,1)} %copy-done.29), channel_id=1, source_target_pairs={{4,0},{0,8},{8,16},{16,24},{24,28},{28,20},{20,12},{12,4},{5,1},{1... | collective-permute-start | bytes 1572872 | tf_op jit(solution)/shard_map/ppermute | solution.py:37
  163.9 19.4 %collective-permute-start.10 = (bf16[512,512]{1,0:T(8,128)(2,1)}, bf16[512,512]{1,0:T(8,128)(2,1)S(1)}, u32[]{:S(2)}, u32[]{:S(2)}) collective-permute-start(bf16[512,512]{1,0:T(8,128)(2,1)} %copy-done.30), channel_id=1, source_target_pairs={{8,0},{16,8},{24,16},{28,24},{20,28},{12,20},{4,12},{0,4},{9,1},{1... | collective-permute-start | bytes 1572872 | tf_op jit(solution)/shard_map/ppermute | solution.py:37
  211.6 14.0 %collective-permute-start.17 = (bf16[256,1024]{1,0:T(8,128)(2,1)S(1)}, bf16[256,1024]{1,0:T(8,128)(2,1)S(1)}, u32[]{:S(2)}, u32[]{:S(2)}) collective-permute-start(bf16[256,1024]{1,0:T(8,128)(2,1)S(1)} %add_convert_fusion.9.refs_1_.refs_4_), channel_id=1, source_target_pairs={{2,0},{3,1},{0,2},{1,3},{6,4},{7,5},{4,6},{5,7},{10,8},{11,9},{8,1... | collective-permute-start | bytes 1572872 | tf_op jit(solution)/shard_map/ppermute | solution.py:41
  243.2 16.5 %collective-permute-start.20 = (bf16[256,1024]{1,0:T(8,128)(2,1)S(1)}, bf16[256,1024]{1,0:T(8,128)(2,1)S(1)}, u32[]{:S(2)}, u32[]{:S(2)}) collective-permute-start(bf16[256,1024]{1,0:T(8,128)(2,1)S(1)} %add_convert_fusion.8.refs_2_.refs_1_), channel_id=1, source_target_pairs={{2,0},{3,1},{0,2},{1,3},{6,4},{7,5},{4,6},{5,7},{10,8},{11,9},{8,1... | collective-permute-start | bytes 1572872 | tf_op jit(solution)/shard_map/ppermute | solution.py:41
  277.1 14.0 %collective-permute-start.24 = (bf16[256,1024]{1,0:T(8,128)(2,1)S(1)}, bf16[256,1024]{1,0:T(8,128)(2,1)S(1)}, u32[]{:S(2)}, u32[]{:S(2)}) collective-permute-start(bf16[256,1024]{1,0:T(8,128)(2,1)S(1)} %add_convert_fusion.7.refs_6_.refs_1_), channel_id=1, source_target_pairs={{2,0},{3,1},{0,2},{1,3},{6,4},{7,5},{4,6},{5,7},{10,8},{11,9},{8,1... | collective-permute-start | bytes 1572872 | tf_op jit(solution)/shard_map/ppermute | solution.py:41
  296.2 140.0 %reduce-scatter.7.cloned.1.call-start = ((), (), s32[]{:S(2)}) async-start(), calls=%async_computation.11 | async-start | bytes 2359296 | tf_op jit(solution)/shard_map/reduce_scatter | solution.py:904
  318.3 14.9 %collective-permute-start.30 = (bf16[256,512]{1,0:T(8,128)(2,1)}, bf16[256,512]{1,0:T(8,128)(2,1)S(1)}, u32[]{:S(2)}, u32[]{:S(2)}) collective-permute-start(bf16[256,512]{1,0:T(8,128)(2,1)} %get-tuple-element.122), channel_id=1, source_target_pairs={{8,0},{16,8},{24,16},{28,24},{20,28},{12,20},{4,12},{0,4},{9,1},{1... | collective-permute-start | bytes 786440 | tf_op jit(solution)/shard_map/ppermute | solution.py:37
  322.2 14.8 %collective-permute-start.26 = (bf16[256,512]{1,0:T(8,128)(2,1)}, bf16[256,512]{1,0:T(8,128)(2,1)S(1)}, u32[]{:S(2)}, u32[]{:S(2)}) collective-permute-start(bf16[256,512]{1,0:T(8,128)(2,1)} %get-tuple-element.118), channel_id=1, source_target_pairs={{4,0},{0,8},{8,16},{16,24},{24,28},{28,20},{20,12},{12,4},{5,1},{1... | collective-permute-start | bytes 786440 | tf_op jit(solution)/shard_map/ppermute | solution.py:37
  334.2 24.6 %collective-permute-start.31 = (bf16[512,512]{1,0:T(8,128)(2,1)S(1)}, bf16[512,512]{1,0:T(8,128)(2,1)S(1)}, u32[]{:S(2)}, u32[]{:S(2)}) collective-permute-start(bf16[512,512]{1,0:T(8,128)(2,1)S(1)} %pad_maximum_fusion.1), channel_id=1, source_target_pairs={{8,0},{16,8},{24,16},{28,24},{20,28},{12,20},{4,12},{0,4},{9,1},{1... | collective-permute-start | bytes 1572872 | tf_op jit(solution)/shard_map/ppermute | solution.py:37
  337.1 22.2 %collective-permute-start.27 = (bf16[512,512]{1,0:T(8,128)(2,1)S(1)}, bf16[512,512]{1,0:T(8,128)(2,1)S(1)}, u32[]{:S(2)}, u32[]{:S(2)}) collective-permute-start(bf16[512,512]{1,0:T(8,128)(2,1)S(1)} %pad_maximum_fusion), channel_id=1, source_target_pairs={{4,0},{0,8},{8,16},{16,24},{24,28},{28,20},{20,12},{12,4},{5,1},{1... | collective-permute-start | bytes 1572872 | tf_op jit(solution)/shard_map/ppermute | solution.py:37
  359.0 13.6 %collective-permute-start.32 = (bf16[512,512]{1,0:T(8,128)(2,1)S(1)}, bf16[512,512]{1,0:T(8,128)(2,1)S(1)}, u32[]{:S(2)}, u32[]{:S(2)}) collective-permute-start(bf16[512,512]{1,0:T(8,128)(2,1)S(1)} %add_convert_fusion.4), channel_id=1, source_target_pairs={{8,0},{16,8},{24,16},{28,24},{20,28},{12,20},{4,12},{0,4},{9,1},{1... | collective-permute-start | bytes 1572872 | tf_op jit(solution)/shard_map/ppermute | solution.py:37
  359.5 13.6 %collective-permute-start.28 = (bf16[512,512]{1,0:T(8,128)(2,1)S(1)}, bf16[512,512]{1,0:T(8,128)(2,1)S(1)}, u32[]{:S(2)}, u32[]{:S(2)}) collective-permute-start(bf16[512,512]{1,0:T(8,128)(2,1)S(1)} %add_convert_fusion.6), channel_id=1, source_target_pairs={{4,0},{0,8},{8,16},{16,24},{24,28},{28,20},{20,12},{12,4},{5,1},{1... | collective-permute-start | bytes 1572872 | tf_op jit(solution)/shard_map/ppermute | solution.py:37
  398.3 14.0 %collective-permute-start.35 = (bf16[256,1024]{1,0:T(8,128)(2,1)S(1)}, bf16[256,1024]{1,0:T(8,128)(2,1)S(1)}, u32[]{:S(2)}, u32[]{:S(2)}) collective-permute-start(bf16[256,1024]{1,0:T(8,128)(2,1)S(1)} %add_convert_fusion.2.refs_7_.refs_1_), channel_id=1, source_target_pairs={{2,0},{3,1},{0,2},{1,3},{6,4},{7,5},{4,6},{5,7},{10,8},{11,9},{8,1... | collective-permute-start | bytes 1572872 | tf_op jit(solution)/shard_map/ppermute | solution.py:41
  405.2 87.4 %reduce-scatter.9.cloned.1.call-start = ((), (), s32[]{:S(2)}) async-start(), calls=%async_computation.12 | async-start | bytes 4718592 | tf_op jit(solution)/shard_map/reduce_scatter | solution.py:904
  444.9 92.6 %reduce-scatter.11.cloned.1.call-start = ((), (), s32[]{:S(2)}) async-start(), calls=%async_computation.13 | async-start | bytes 2359296 | tf_op jit(solution)/shard_map/reduce_scatter | solution.py:904
  516.5 14.0 %collective-permute-start.41 = (bf16[256,1024]{1,0:T(8,128)(2,1)S(1)}, bf16[256,1024]{1,0:T(8,128)(2,1)S(1)}, u32[]{:S(2)}, u32[]{:S(2)}) collective-permute-start(bf16[256,1024]{1,0:T(8,128)(2,1)S(1)} %copy-done.12), channel_id=1, source_target_pairs={{2,0},{3,1},{0,2},{1,3},{6,4},{7,5},{4,6},{5,7},{10,8},{11,9},{8,1... | collective-permute-start | bytes 1572872 | tf_op jit(solution)/shard_map/ppermute | solution.py:41
  (78 other events, 628.6 us)
Sparse Core Ops, SparseCore 0:
  10.1 36.6 all-gather.4
  48.3 46.9 all-gather.6
  97.5 33.6 all-gather.8
  162.9 55.8 all-gather.10
  296.3 63.0 reduce-scatter.4
  405.3 30.7 reduce-scatter.6
  445.0 47.5 reduce-scatter.8
  498.5 34.0 reduce-scatter.10

commit v4 on v3

--- a/solution.py
+++ b/solution.py
@@ -67,7 +67,7 @@
     for place in (1, 0):
         right = add_pair(ahead[place], ring_take(right, -1))
         left = add_pair(behind[place], ring_take(left, 1))
-    return pieces[0], ring_take(right, -1), ring_take(left, 1)
+    return (pieces[0], ring_take(right, -1), ring_take(left, 1)), [right, left]
 
 
 def dot_nt(a, b):
@@ -250,15 +250,19 @@
     normed_ref[...] = (unit * gains_ref[norm_row : norm_row + 1, :]).astype(BF16)
 
 
-def output_kernel(scale_row, order, facts_ref, h_ref, own_ref, far_ref, gains_ref, out_ref, held):
-    held[...] = h_ref[...] + gains_ref[scale_row : scale_row + 1, :] * total_of(own_ref, far_ref)
+def add_kernel(own_ref, other_ref, sum_ref):
+    sum_ref[...] = (own_ref[...] + other_ref[...].astype(F32)).astype(BF16)
+
+
+def output_kernel(scale_row, order, facts_ref, h_ref, own_ref, far_ref, gains_ref, grad_ref, out_ref, sums_ref, held):
+    total = total_of(own_ref, far_ref)
+    held[...] = h_ref[...] + gains_ref[scale_row : scale_row + 1, :] * total
+    sums_ref[...] = jnp.sum(grad_ref[...] * total, axis=0, keepdims=True)
     leave(held, order, facts_ref, out_ref)
 
 
-def seed_kernel(row, grad_ref, own_ref, far_ref, gains_ref, scaled_ref, sums_ref):
-    grad = grad_ref[...]
-    scaled_ref[...] = (grad * gains_ref[row : row + 1, :]).astype(BF16)
-    sums_ref[...] = jnp.sum(grad * total_of(own_ref, far_ref), axis=0, keepdims=True)
+def scale_kernel(row, grad_ref, gains_ref, scaled_ref):
+    scaled_ref[...] = (grad_ref[...] * gains_ref[row : row + 1, :]).astype(BF16)
 
 
 def middle_back_kernel(
@@ -273,14 +277,22 @@
     scaled_ref[...] = (grad * gains_ref[base + 2 : base + 3, :]).astype(BF16)
 
 
-def first_back_kernel(base, grad_ref, own_ref, far_ref, h_ref, gains_ref, next_ref):
-    grad_in = total_of(own_ref, far_ref)
+def first_back(base, grad_ref, own_ref, far_ref, h_ref, gains_ref):
     unit, scale = norm_parts(h_ref[...])
-    next_ref[...] = grad_ref[...] + norm_back(unit, scale, gains_ref[base : base + 1, :], grad_in)
+    return grad_ref[...] + norm_back(unit, scale, gains_ref[base : base + 1, :], total_of(own_ref, far_ref))
+
+
+def between_kernel(
+    base, grad_ref, own_ref, far_ref, h_ref, gains_ref, d_own_ref, d_far_ref, next_ref, scaled_ref, sums_ref
+):
+    grad = first_back(base, grad_ref, own_ref, far_ref, h_ref, gains_ref)
+    next_ref[...] = grad
+    scaled_ref[...] = (grad * gains_ref[base - 3 : base - 2, :]).astype(BF16)
+    sums_ref[...] = jnp.sum(grad * total_of(d_own_ref, d_far_ref), axis=0, keepdims=True)
 
 
 def last_back_kernel(order, facts_ref, grad_ref, own_ref, far_ref, h_ref, gains_ref, out_ref, held):
-    first_back_kernel(0, grad_ref, own_ref, far_ref, h_ref, gains_ref, held)
+    held[...] = first_back(0, grad_ref, own_ref, far_ref, h_ref, gains_ref)
     leave(held, order, facts_ref, out_ref)
 
 
@@ -312,7 +324,7 @@
         kv_ref[...] = mixed.astype(BF16)
 
 
-def project(normed, pieces, heads, row_q):
+def project(normed, pieces, heads, row_q, after):
     own, other = normed
     half, wide = own.shape
     width = heads.shape[1]
@@ -336,6 +348,7 @@
         [],
         [own, other] + [p for p, _ in pieces] + [heads],
         5,
+        after=after,
     )
 
 
@@ -377,7 +390,7 @@
         zero_ref[...] = jnp.sum(products, axis=0, keepdims=True) / gains_ref[row_g : row_g + 1, :]
 
 
-def project_back(dq, dkv, mixed, pieces, heads, row_q, normed, gains):
+def project_back(dq, dkv, mixed, pieces, heads, row_q, normed, gains, after):
     full, width = dq.shape
     wide = gains.shape[1]
     rows = [min(p.shape[0], limit) for p, limit in pieces]
@@ -411,6 +424,7 @@
         [pltpu.VMEM((full, wide), F32)],
         [dq, dkv, mixed, heads, *normed, gains] + [p for p, _ in pieces],
         6,
+        after=after,
     )
 
 
@@ -545,6 +559,44 @@
         out_ref[...] = dot_nn(turned[...], second_ref[...]).astype(BF16)
 
 
+def gate_kernel(*refs):
+    pass
+
+
+def gate(value, after):
+    anywhere = pl.BlockSpec(memory_space=pl.ANY)
+    return run(
+        gate_kernel, (1,), [anywhere], anywhere, jax.ShapeDtypeStruct(value.shape, value.dtype), [], [value], 0.1,
+        aliases={0: 0}, after=after,
+    )
+
+
+def one_weight_kernel(own, other, right_ref, out_ref, turned):
+    half = own.shape[0]
+
+    @pl.when(pl.program_id(0) == 0)
+    def _():
+        turned[:, :half] = own[...].T
+        turned[:, half:] = other[...].T
+
+    out_ref[...] = dot_nn(turned[...], right_ref[...]).astype(BF16)
+
+
+def one_weight_grads(a, right, us, after):
+    half, wide = a[0].shape
+    return run(
+        one_weight_kernel,
+        (right.shape[1] // TILE,),
+        [whole((half, wide))] * 2 + [column(2 * half, lambda j: j)],
+        column(wide, lambda j: j),
+        shaped(wide, right.shape[1], dtype=BF16),
+        [pltpu.VMEM((wide, 2 * half), BF16)],
+        [*a, right],
+        us,
+        after=after,
+    )
+
+
 def weight_grads(a, first, b, second, us, after):
     half, wide = a[0].shape
     split = first.shape[1] // TILE
@@ -573,6 +625,11 @@
     down_ref[0] = part_ref[:, hidden:].astype(F32).T
 
 
+def finish_two_kernel(up_part_ref, down_part_ref, up_ref, down_ref):
+    up_ref[0] = up_part_ref[...].astype(F32)
+    down_ref[0] = down_part_ref[...].astype(F32).T
+
+
 def finish_at_kernel(part_ref, *refs):
     qkv_ref, out_ref = refs[-2:]
     width = qkv_ref.shape[3]
@@ -581,7 +638,7 @@
     out_ref[0] = part_ref[:, 3 * width :].astype(F32).T
 
 
-def finish(kernel, part, shapes, block, earlier):
+def finish(kernel, parts, shapes, block, earlier):
     specs = [
         pl.BlockSpec((1,) + s[1:], functools.partial(lambda b, r, *_: (b,) + (0,) * (r - 1), block, len(s)))
         for s in shapes
@@ -589,13 +646,13 @@
     return run(
         kernel,
         (1,),
-        [whole(part.shape)] + [pl.BlockSpec(memory_space=pl.ANY)] * len(earlier),
+        [whole(part.shape) for part in parts] + [pl.BlockSpec(memory_space=pl.ANY)] * len(earlier),
         specs,
         [shaped(*s) for s in shapes],
         [],
-        [part, *earlier],
+        [*parts, *earlier],
         2,
-        aliases={1 + i: i for i in range(len(earlier))},
+        aliases={len(parts) + i: i for i in range(len(earlier))},
     )
 
 
@@ -935,18 +992,30 @@
         return near, row_take(near, 2)
 
     stored = []
-    output = None
+    grad = enter(cotangent, True)
+    scaled = run(
+        functools.partial(scale_kernel, 9),
+        (1,),
+        [big, gspec],
+        big,
+        shaped(half, wide, dtype=BF16),
+        [],
+        [grad, gains],
+        1,
+    )
+    grad_down = (scaled, row_take(scaled, 1))
     for block in range(2):
         base = 6 * block
         at, ff = weights[block] or (at_one, None)
         normed = (normed, row_take(normed, 1))
-        queries, kv, mixed = project(normed, at, heads, base + 4)
+        early = [*grad_down, scene_table, rel_lens] if block == 0 else []
+        queries, kv, mixed = project(normed, at, heads, base + 4, early)
         if block == 0:
             sources, walking, table, lens = [kv], False, frame_table, frame_lens
         else:
             table, lens, walking = scene_table, rel_lens, ring
             sources = ring_gather(kv, half) if ring else [lax.all_gather(kv, "frame", axis=0, tiled=True)]
-            ff = gather(pack_ff(1, [sources[2], sources[7]] if ring else ()))
+            ff = gather(pack_ff(1, sources[4:6] if ring else ()))
             weights[1] = (at, ff)
         attended, lse, part_other, part_own = attend(
             queries, sources, walking, at, table, lens, facts, wide
@@ -964,12 +1033,12 @@
         )
         second = (second, row_take(second, 1))
         up_values, active, part_other, part_own = feed(second, ff, hidden)
-        down = reduce_rows(part_other, part_own)
         stored.append(
             (h, normed, queries, mixed, (sources, walking, table, lens), attended, lse, branch)
-            + (middle, second, up_values, active, down)
+            + (middle, second, up_values, active)
         )
         if block == 0:
+            down_zero = reduce_rows(part_other, part_own)
             h, normed = run(
                 functools.partial(residual_kernel, base + 3, base + 6),
                 (1,),
@@ -977,52 +1046,33 @@
                 [big, big],
                 [shaped(half, wide), shaped(half, wide, dtype=BF16)],
                 [],
-                [middle, *down, gains],
+                [middle, *down_zero, gains],
                 2,
             )
-        else:
-            output = run(
-                functools.partial(output_kernel, base + 3, lane_order),
-                (1,),
-                [big, big, big, gspec],
-                whole((quarter, wide)),
-                shaped(quarter, wide, dtype=BF16),
-                [pltpu.VMEM((half, wide), F32)],
-                [facts, middle, *down, gains],
-                1,
-                prefetch=1,
-            )
-
-    grad = enter(cotangent, True)
+
+    last_other, last_own = row_take(part_other, 1), part_own
     at_shapes = [(2, 3, shard, width), (2, width, shard)]
     ff_shapes = [(2, shard, hidden), (2, hidden, shard)]
     at_out, ff_out = [], []
     gain_sums = [None, None]
     input_grad = None
-    after = []
     for block in (1, 0):
         base = 6 * block
         at, ff = weights[block]
-        h, normed, queries, mixed, keys, attended, lse, branch, middle, second, up_values, active, down = stored[
-            block
-        ]
+        h, normed, queries, mixed, keys, attended, lse, branch, middle, second, up_values, active = stored[block]
         sources, walking, table, lens = keys
-        scaled, sum_three = run(
-            functools.partial(seed_kernel, base + 3),
-            (1,),
-            [big, big, big, gspec],
-            [big, whole((1, wide))],
-            [shaped(half, wide, dtype=BF16), shaped(1, wide)],
-            [],
-            [grad, *down, gains],
-            1,
-        )
-        grad_down = (scaled, row_take(scaled, 1))
         grad_up, part_other, part_own = feed_back(grad_down, up_values, ff)
         incoming = reduce_rows(part_other, part_own)
-        ff_grads = weight_grads(second, grad_up, grad_down, active, 8, [*after, incoming[0]])
-        ff_sum = scatter(ff_grads)
-        after = [ff_sum]
+        if block == 1:
+            up_grads = one_weight_grads(second, grad_up, 5, [incoming[0]])
+            ff_grads = one_weight_grads(grad_down, active, 5, [incoming[0]])
+            up_sum = scatter(up_grads)
+        else:
+            ff_grads = weight_grads(second, grad_up, grad_down, active, 8, [incoming[0]])
+            ff_grads = gate(ff_grads, [at_sum, incoming[1]])
+            ff_sum = scatter(ff_grads)
+            if ring:
+                ff_out = finish(finish_ff_kernel, [ff_sum], ff_shapes, block, ff_out)
         grad_middle, scaled, sums_middle = run(
             functools.partial(middle_back_kernel, base),
             (1,),
@@ -1032,9 +1082,25 @@
             [],
             [grad, *incoming, middle, *branch, gains],
             2,
-            after=[ff_grads],
+            after=[up_grads, ff_grads] if block == 1 else [ff_grads, *(at_out[:1] if ring else [])],
         )
         grad_branch = (scaled, row_take(scaled, 1))
+        if block == 1:
+            near = run(
+                add_kernel, (1,), [big, big], big, shaped(half, wide, dtype=BF16), [], [last_own, last_other], 1,
+                after=[incoming[1]],
+            )
+            output, sum_three = run(
+                functools.partial(output_kernel, base + 3, lane_order),
+                (1,),
+                [big, big, big, gspec, big],
+                [whole((quarter, wide)), whole((1, wide))],
+                [shaped(quarter, wide, dtype=BF16), shaped(1, wide)],
+                [pltpu.VMEM((half, wide), F32)],
+                [facts, middle, near, row_take(near, 2), gains, grad],
+                1,
+                prefetch=1,
+            )
         dq, *dkv_parts = attend_back(
             queries,
             grad_branch,
@@ -1051,29 +1117,36 @@
         if block == 0:
             dkv = dkv_parts[0][0]
         elif ring:
-            own, right, left = ring_scatter(dkv_parts)
+            (own, right, left), sent_last = ring_scatter(dkv_parts)
             dkv = own.astype(F32) + right.astype(F32) + left.astype(F32)
         else:
             spread = jnp.zeros((frames,) + dkv_parts[0].shape[1:], BF16).at[table].set(dkv_parts[0])
             dkv = lax.psum_scatter(spread, "frame", scatter_dimension=0, tiled=False).astype(F32)
+        if block == 1:
+            down_sum = scatter(gate(ff_grads, [*(sent_last if ring else [dkv]), up_sum]))
+            ff_sum = down_sum
+            if ring:
+                ff_out = finish(finish_two_kernel, [up_sum, down_sum], ff_shapes, 1, ff_out)
         grad_mixed, part_other, part_own, sums_heads, sum_zero = project_back(
-            dq, dkv, mixed, at, heads, base + 4, normed, gains
+            dq, dkv, mixed, at, heads, base + 4, normed, gains, [output] if block == 1 else ()
         )
         gain_sums[block] = (sum_zero, sums_middle, sum_three, sums_heads)
         incoming = reduce_rows(part_other, part_own)
-        at_grads = weight_grads(normed, grad_mixed, grad_branch, attended, 4, [*after, incoming[0]])
+        at_grads = weight_grads(normed, grad_mixed, grad_branch, attended, 4, [incoming[0]])
+        at_grads = gate(at_grads, [ff_sum, incoming[1]])
         if block == 1:
-            grad = run(
-                functools.partial(first_back_kernel, base),
+            grad, scaled, sum_three = run(
+                functools.partial(between_kernel, base),
                 (1,),
-                [big] * 4 + [gspec],
-                big,
-                shaped(half, wide),
+                [big] * 4 + [gspec, big, big],
+                [big, big, whole((1, wide))],
+                [shaped(half, wide), shaped(half, wide, dtype=BF16), shaped(1, wide)],
                 [],
-                [grad_middle, *incoming, h, gains],
-                2,
+                [grad_middle, *incoming, h, gains, *down_zero],
+                3,
                 after=[at_grads],
             )
+            grad_down = (scaled, row_take(scaled, 1))
         else:
             input_grad = run(
                 functools.partial(last_back_kernel, lane_order),
@@ -1085,18 +1158,17 @@
                 [facts, grad_middle, *incoming, h, gains],
                 2,
                 prefetch=1,
-                after=[at_grads, ff_sum],
+                after=[],
             )
         at_sum = scatter(at_grads)
-        after = [at_sum]
         if ring:
-            ff_out = finish(finish_ff_kernel, ff_sum, ff_shapes, block, ff_out)
-            at_out = finish(finish_at_kernel, at_sum, at_shapes, block, at_out)
+            at_out = finish(finish_at_kernel, [at_sum], at_shapes, block, at_out)
         else:
-            ff_sum, at_sum = ff_sum.astype(F32), at_sum.astype(F32)
-            ff_out = [(ff_sum[:, :hidden], ff_sum[:, hidden:].T)] + ff_out
-            qkv_sum = jnp.stack([at_sum[:, i * width : (i + 1) * width] for i in range(3)])
-            at_out = [(qkv_sum, at_sum[:, 3 * width :].T)] + at_out
+            ff_parts = [up_sum, down_sum] if block == 1 else [ff_sum[:, :hidden], ff_sum[:, hidden:]]
+            ff_out = [(ff_parts[0].astype(F32), ff_parts[1].astype(F32).T)] + ff_out
+            at_last = at_sum.astype(F32)
+            qkv_sum = jnp.stack([at_last[:, i * width : (i + 1) * width] for i in range(3)])
+            at_out = [(qkv_sum, at_last[:, 3 * width :].T)] + at_out
     if not ring:
         ff_out = [jnp.stack(both) for both in zip(*ff_out, strict=True)]
         at_out = [jnp.stack(both) for both in zip(*at_out, strict=True)]
@@ -1113,6 +1185,7 @@
             [facts, *operands],
             1,
             prefetch=1,
+            after=[input_grad],
         )
         total = jnp.sum(lax.all_to_all(sent, "frame", 0, 0), axis=0)
         total = total + row_take(total, 1)

time: 556 us -> 518 us (0.932)
  waiting for transfers between devices: 251 us -> 211 us
  blocking collectives: 0 us -> 12.3 us
  starting transfers between devices: 48.1 us -> 42.1 us
    ppermute x16, waiting for transfers between devices: 93.1 us -> 70.7 us  [ring_take(): lax.ppermute(value, 'frame', [(RING[(i + step) % count], RING[i]) for i i...]
    ppermute x28, waiting for transfers between devices: 109 us -> 88.6 us  [row_take(): return lax.ppermute(value, 'row', [(i ^ bit, i) for i in range(4)])]
    reduce_scatter x4 -> x5, waiting for transfers between devices: 8.51 us -> 21.6 us  [scatter(): lax.psum_scatter(grads, 'frame', scatter_dimension=0, tiled=True, axis_in...]
    all_to_all x0 -> x1, blocking collectives: none -> 12.3 us  [per_device(): total = jnp.sum(lax.all_to_all(sent, 'frame', 0, 0), axis=0)]
    unnamed x102 -> x108, local copies, waits for them, and re-layouts: 16 us -> 12.7 us
    convert_element_type x8 -> x7, other arithmetic: 12.6 us -> 9.63 us  [reduce_rows(): near = (own + row_take(other, 1).astype(F32)).astype(BF16)]
    pallas_call x38 -> x43, Pallas kernels: 189 us -> 191 us  [run(): pl.pallas_call(body, grid_spec=pltpu.PrefetchScalarGridSpec(num_scalar_pr...]
  transfers between devices with their start and end apart: 54 -> 54, of which waited for: 44 -> 40; matrix products, arithmetic and copies ran while one was open for 5% -> 4% of each run, Pallas kernels for 26% -> 31%
where the time goes in v4:
time: 518 us; the launch traced here: 509 us
  waiting for transfers between devices  211 us (41%)
  Pallas kernels  191 us (37%)
  starting transfers between devices  42.1 us (8%)
  local copies, waits for them, and re-layouts  19.1 us (4%)
  between operations  16.8 us (3%)
  other arithmetic  16.3 us (3%)
  blocking collectives  12.3 us (2%)
    pallas_call x43, Pallas kernels, run(): pl.pallas_call(body, grid_spec=pltpu.PrefetchScalarGridSpec(num_scalar_pr...  191 us
    ppermute x28, waiting for transfers between devices, row_take(): return lax.ppermute(value, 'row', [(i ^ bit, i) for i in range(4)])  88.6 us
    ppermute x16, waiting for transfers between devices, ring_take(): lax.ppermute(value, 'frame', [(RING[(i + step) % count], RING[i]) for i i...  70.7 us
    all_gather x4, waiting for transfers between devices, gather(): lax.all_gather(packed, 'frame', axis=0, tiled=True, axis_index_groups=fra...  28.1 us
    reduce_scatter x5, waiting for transfers between devices, scatter(): lax.psum_scatter(grads, 'frame', scatter_dimension=0, tiled=True, axis_in...  21.6 us
    ppermute x28, starting transfers between devices, row_take(): return lax.ppermute(value, 'row', [(i ^ bit, i) for i in range(4)])  17.1 us
    ppermute x16, starting transfers between devices, ring_take(): lax.ppermute(value, 'frame', [(RING[(i + step) % count], RING[i]) for i i...  16.9 us
    unnamed x108, local copies, waits for them, and re-layouts  12.7 us
  transfers between devices with their start and end apart: 54, of which 40 were waited for; matrix products, arithmetic and copies ran while one was open for 4% of the time, Pallas kernels for 31%

profile of v4, /device:TPU:0, one launch (start us, length us, event | category | flops | bytes accessed | tf_op | source)
XLA Modules:
  0.0 508.6 jit_solution(3621343262752448243)
XLA Ops:
  9.9 7.3 %all-to-all-start = ((f32[8,16,128]{2,1,0:T(8,128)}), f32[8,16,128]{2,1,0:T(8,128)S(1)}, u32[]{:S(2)}, u32[]{:S(2)}) async-start(f32[8,16,128]{2,1,0:T(8,128)} %broadcast_in_dim.14), calls=%async_computation | async-start | bytes 131072 | tf_op jit(solution)/shard_map/all_to_all | solution.py:969
  67.8 12.4 %collective-permute-done.5.refs_2_.refs_5_ = bf16[256,1024]{1,0:T(8,128)(2,1)S(1)} collective-permute-done((bf16[256,1024]{1,0:T(8,128)(2,1)S(1)}, bf16[256,1024]{1,0:T(8,128)(2,1)S(1)}, u32[]{:S(2)}, u32[]{:S(2)}) %collective-permute-start.5) | collective-permute-done | bytes 524320 | tf_op jit(solution)/shard_map/ppermute | solution.py:41
  86.1 9.3 %all-gather.7.cloned.1.call-done.refs_2_.refs_3_.refs_4_ = bf16[1024,2048]{1,0:T(8,128)(2,1)} async-done(((bf16[128,2048]{1,0:T(8,128)(2,1)}), bf16[1024,2048]{1,0:T(8,128)(2,1)}) %all-gather.7.cloned.1.call-update) | async-done | bytes 4194320 | tf_op jit(solution)/shard_map/all_gather | solution.py:958
  95.4 7.4 %shard_map.162 = (f32[512,1024]{1,0:T(8,128)}, bf16[512,1024]{1,0:T(8,128)(2,1)}, bf16[256,1024]{1,0:T(8,128)(2,1)}, f32[256,1024]{1,0:T(8,128)}) custom-call(bf16[256,1024]{1,0:T(8,128)(2,1)} %get-tuple-element.91.refs_0_, bf16[256,1024]{1,0:T(8,128)(2,1)} %copy-done.27, bf16[1024,2048]{1,0:T(8,128)(2,1)} %all-gather.7.cloned.1.call-done.refs_2_.refs_3_.refs_4_, ...), custom_call_target="tpu_custom_call" | custom-call | flops 20999999488 | bytes 42000000 | tf_op jit(solution)/shard_map/pallas_call | solution.py:106
  107.9 12.5 %collective-permute-done.8.refs_2_.refs_6_ = bf16[256,1024]{1,0:T(8,128)(2,1)S(1)} collective-permute-done((bf16[256,1024]{1,0:T(8,128)(2,1)S(1)}, bf16[256,1024]{1,0:T(8,128)(2,1)S(1)}, u32[]{:S(2)}, u32[]{:S(2)}) %collective-permute-start.8) | collective-permute-done | bytes 524320 | tf_op jit(solution)/shard_map/ppermute | solution.py:41
  139.1 10.3 %collective-permute-done.14.refs_12_.refs_16_ = bf16[512,512]{1,0:T(8,128)(2,1)S(1)} collective-permute-done((bf16[512,512]{1,0:T(8,128)(2,1)}, bf16[512,512]{1,0:T(8,128)(2,1)S(1)}, u32[]{:S(2)}, u32[]{:S(2)}) %collective-permute-start.14) | collective-permute-done | bytes 524320 | tf_op jit(solution)/shard_map/ppermute | solution.py:37
  151.4 10.1 %collective-permute-done.15.refs_11_.refs_15_ = bf16[512,512]{1,0:T(8,128)(2,1)S(1)} collective-permute-done((bf16[512,512]{1,0:T(8,128)(2,1)S(1)}, bf16[512,512]{1,0:T(8,128)(2,1)S(1)}, u32[]{:S(2)}, u32[]{:S(2)}) %collective-permute-start.15) | collective-permute-done | bytes 524320 | tf_op jit(solution)/shard_map/ppermute | solution.py:37
  163.5 10.0 %collective-permute-done.16.refs_10_.refs_14_ = bf16[512,512]{1,0:T(8,128)(2,1)S(1)} collective-permute-done((bf16[512,512]{1,0:T(8,128)(2,1)S(1)}, bf16[512,512]{1,0:T(8,128)(2,1)S(1)}, u32[]{:S(2)}, u32[]{:S(2)}) %collective-permute-start.16) | collective-permute-done | bytes 524320 | tf_op jit(solution)/shard_map/ppermute | solution.py:37
  184.0 11.8 %shard_map.166 = (bf16[512,256]{1,0:T(8,128)(2,1)}, f32[8,512]{1,0:T(8,128)}, bf16[256,1024]{1,0:T(8,128)(2,1)}, f32[256,1024]{1,0:T(8,128)}) custom-call(s32[4]{0:T(128)} %bitcast.22, s32[8]{0:T(128)} %gather_fusion.1, s32[3]{0:T(128)} %pad_add_fusion.refs_0_.refs_2_, bf16[512,256]{1,0:T(8,128)(2,1)} %get-tuple-element.96.refs_3_, ...), custom_call_target="tpu_custom_call" | custom-call | flops 32999999488 | bytes 66000000 | tf_op jit(solution)/shard_map/pallas_call | solution.py:106
  200.9 12.5 %collective-permute-done.19.refs_2_.refs_5_ = bf16[256,1024]{1,0:T(8,128)(2,1)S(1)} collective-permute-done((bf16[256,1024]{1,0:T(8,128)(2,1)S(1)}, bf16[256,1024]{1,0:T(8,128)(2,1)S(1)}, u32[]{:S(2)}, u32[]{:S(2)}) %collective-permute-start.19) | collective-permute-done | bytes 524320 | tf_op jit(solution)/shard_map/ppermute | solution.py:41
  219.2 12.0 %all-gather.11.cloned.1.call-done.refs_2_.refs_3_.refs_4_ = bf16[1024,2048]{1,0:T(8,128)(2,1)} async-done(((bf16[128,2048]{1,0:T(8,128)(2,1)}), bf16[1024,2048]{1,0:T(8,128)(2,1)}) %all-gather.11.cloned.1.call-update) | async-done | bytes 4194320 | tf_op jit(solution)/shard_map/all_gather | solution.py:958
  231.3 7.4 %shard_map.169 = (f32[512,1024]{1,0:T(8,128)}, bf16[512,1024]{1,0:T(8,128)(2,1)}, bf16[256,1024]{1,0:T(8,128)(2,1)}, f32[256,1024]{1,0:T(8,128)}) custom-call(bf16[256,1024]{1,0:T(8,128)(2,1)} %get-tuple-element.101.refs_0_, bf16[256,1024]{1,0:T(8,128)(2,1)} %copy-done.41, bf16[1024,2048]{1,0:T(8,128)(2,1)} %all-gather.11.cloned.1.call-done.refs_2_.refs_3_.refs_4_, ...), custom_call_target="tpu_custom_call" | custom-call | flops 20999999488 | bytes 42000000 | tf_op jit(solution)/shard_map/pallas_call | solution.py:106
  238.7 7.6 %shard_map.170 = (bf16[512,1024]{1,0:T(8,128)(2,1)}, bf16[256,1024]{1,0:T(8,128)(2,1)}, f32[256,1024]{1,0:T(8,128)}) custom-call(bf16[256,1024]{1,0:T(8,128)(2,1)} %shard_map.157.refs_4_.refs_0_, bf16[256,1024]{1,0:T(8,128)(2,1)} %copy-done.30, f32[512,1024]{1,0:T(8,128)} %get-tuple-element.104.refs_2_, ...), custom_call_target="tpu_custom_call" | custom-call | flops 24000000000 | bytes 48000000 | tf_op jit(solution)/shard_map/pallas_call | solution.py:106
  271.8 18.9 %shard_map.176 = (f32[512,256]{1,0:T(8,128)}, bf16[512,512]{1,0:T(8,128)(2,1)}, bf16[512,512]{1,0:T(8,128)(2,1)}, bf16[512,512]{1,0:T(8,128)(2,1)}, bf16[512,512...) custom-call(s32[4]{0:T(128)} %bitcast.23, ...), custom_call_target="tpu_custom_call" | custom-call | flops 60000002048 | bytes 120000000 | tf_op jit(solution)/shard_map/pallas_call | solution.py:106
  295.1 9.4 %collective-permute-done.30 = bf16[256,512]{1,0:T(8,128)(2,1)S(1)} collective-permute-done((bf16[256,512]{1,0:T(8,128)(2,1)}, bf16[256,512]{1,0:T(8,128)(2,1)S(1)}, u32[]{:S(2)}, u32[]{:S(2)}) %collective-permute-start.30) | collective-permute-done | bytes 262176 | tf_op jit(solution)/shard_map/ppermute | solution.py:37
  307.8 11.3 %collective-permute-done.31 = bf16[512,512]{1,0:T(8,128)(2,1)S(1)} collective-permute-done((bf16[512,512]{1,0:T(8,128)(2,1)S(1)}, bf16[512,512]{1,0:T(8,128)(2,1)S(1)}, u32[]{:S(2)}, u32[]{:S(2)}) %collective-permute-start.31) | collective-permute-done | bytes 524320 | tf_op jit(solution)/shard_map/ppermute | solution.py:37
  351.3 7.6 %shard_map.177 = (bf16[512,768]{1,0:T(8,128)(2,1)}, bf16[256,1024]{1,0:T(8,128)(2,1)}, f32[256,1024]{1,0:T(8,128)}, f32[2,256]{1,0:T(2,128)}, f32[1,1024]{1,0:T(1,128)}) custom-call(f32[512,256]{1,0:T(8,128)} %get-tuple-element.114.refs_0_, f32[512,512]{1,0:T(8,128)} %convert_add_fusion.refs_1_, f32[512,512]{1,0:T(8,128)} %get-tuple-element.124.refs_2_, ...), custom_call_target="tpu_custom_call" | custom-call | flops 17999998976 | bytes 36000000 | tf_op jit(solution)/shard_map/pallas_call | solution.py:106
  384.4 7.7 %shard_map.182 = (bf16[512,1024]{1,0:T(8,128)(2,1)}, bf16[256,1024]{1,0:T(8,128)(2,1)}, f32[256,1024]{1,0:T(8,128)}) custom-call(bf16[256,1024]{1,0:T(8,128)(2,1)} %get-tuple-element.129.refs_0_.refs_2_, bf16[256,1024]{1,0:T(8,128)(2,1)} %copy-done.42, f32[512,1024]{1,0:T(8,128)} %get-tuple-element.130.refs_2_, ...), custom_call_target="tpu_custom_call" | custom-call | flops 24000000000 | bytes 48000000 | tf_op jit(solution)/shard_map/pallas_call | solution.py:106
  397.2 8.7 %shard_map.183.refs_0_ = bf16[1024,2048]{1,0:T(8,128)(2,1)} custom-call(bf16[256,1024]{1,0:T(8,128)(2,1)} %get-tuple-element.91.refs_0_, bf16[256,1024]{1,0:T(8,128)(2,1)} %copy-done.27, bf16[256,1024]{1,0:T(8,128)(2,1)} %get-tuple-element.129.refs_0_.refs_2_, bf16[256,1024]{1,0:T(8,128)(2,1)} %copy-done.42, bf16[512,1024]{1,0:T(8,128)(2,1)} %get-tuple-element.133.refs_4_, ...), custom_call_target="tpu_custom_call" | custom-call | flops 24000000000 | bytes 48000000 | tf_op jit(solution)/shard_map/pallas_call | solution.py:106
  423.2 8.1 %shard_map.187 = (f32[512,256]{1,0:T(8,128)}, f32[1,512,512]{2,1,0:T(8,128)}) custom-call(s32[1]{0:T(128)} %constant.50.clone.1.refs_0_, s32[1]{0:T(128)} %dynamic_slice.13.refs_1_, s32[3]{0:T(128)} %pad_add_fusion.refs_0_.refs_2_, bf16[512,256]{1,0:T(8,128)(2,1)} %get-tuple-element.86.refs_3_, bf16[512,256]{1,0:T(8,128)(2,1)} %get-tuple-element.137.refs_4_.refs_5_, ...), custom_call_target="tpu_custom_call" | custom-call | flops 24000000000 | bytes 48000000 | tf_op jit(solution)/shard_map/pallas_call | solution.py:106
  431.3 7.6 %shard_map.188 = (bf16[512,768]{1,0:T(8,128)(2,1)}, bf16[256,1024]{1,0:T(8,128)(2,1)}, f32[256,1024]{1,0:T(8,128)}, f32[2,256]{1,0:T(2,128)}, f32[1,1024]{1,0:T(1,128)}) custom-call(f32[512,256]{1,0:T(8,128)} %get-tuple-element.140.refs_0_, f32[512,512]{1,0:T(8,128)} %bitcast.19, f32[512,512]{1,0:T(8,128)} %get-tuple-element.142.refs_2_, ...), custom_call_target="tpu_custom_call" | custom-call | flops 17999998976 | bytes 36000000 | tf_op jit(solution)/shard_map/pallas_call | solution.py:106
  456.5 7.2 %reduce-scatter.12.cloned.1.call-done.refs_1_.refs_0_ = bf16[128,2048]{1,0:T(8,128)(2,1)} async-done(((bf16[1024,2048]{1,0:T(8,128)(2,1)}), bf16[128,2048]{1,0:T(8,128)(2,1)}) %reduce-scatter.12.cloned.1.call-update) | async-done | bytes 524304 | tf_op jit(solution)/shard_map/reduce_scatter | solution.py:961
  469.8 12.3 %all_to_all.10 = f32[8,16,128]{2,1,0:T(8,128)S(1)} all-to-all(f32[8,16,128]{2,1,0:T(8,128)} %shard_map.195), channel_id=1, replica_groups=mesh['frame'=8,'row'=4] {'frame'}, dimensions={0} | all-to-all | bytes 131072 | tf_op jit(solution)/shard_map/all_to_all | solution.py:1190
  489.8 10.1 %reduce-scatter.14.cloned.1.call-done.refs_0_ = bf16[128,1024]{1,0:T(8,128)(2,1)} async-done(((bf16[1024,1024]{1,0:T(8,128)(2,1)}), bf16[128,1024]{1,0:T(8,128)(2,1)}) %reduce-scatter.14.cloned.1.call-update) | async-done | bytes 262160 | tf_op jit(solution)/shard_map/reduce_scatter | solution.py:961
  (289 shorter events, 252.4 us)
Async XLA Ops:
  7.2 42.4 %all-gather.5.cloned.1.call-start = ((), (), s32[]{:S(2)}) async-start(), calls=%async_computation.7 | async-start | bytes 2359296 | tf_op jit(solution)/shard_map/all_gather | solution.py:958
  9.9 15.0 %all-to-all-start = ((f32[8,16,128]{2,1,0:T(8,128)}), f32[8,16,128]{2,1,0:T(8,128)S(1)}, u32[]{:S(2)}, u32[]{:S(2)}) async-start(f32[8,16,128]{2,1,0:T(8,128)} %broadcast_in_dim.14), calls=%async_computation | async-start | bytes 131072 | tf_op jit(solution)/shard_map/all_to_all | solution.py:969
  17.1 78.2 %all-gather.7.cloned.1.call-start = ((), (), s32[]{:S(2)}) async-start(), calls=%async_computation.8 | async-start | bytes 4718592 | tf_op jit(solution)/shard_map/all_gather | solution.py:958
  17.2 19.1 %collective-permute-start = (bf16[128,1024]{1,0:T(8,128)(2,1)S(1)}, bf16[128,1024]{1,0:T(8,128)(2,1)S(1)}, u32[]{:S(2)}, u32[]{:S(2)}) collective-permute-start(bf16[128,1024]{1,0:T(8,128)(2,1)S(1)} %copy-done.45), channel_id=1, source_target_pairs={{2,0},{3,1},{0,2},{1,3},{6,4},{7,5},{4,6},{5,7},{10,8},{11,9},{8,1... | collective-permute-start | bytes 786440 | tf_op jit(solution)/shard_map/ppermute | solution.py:41
  21.3 109.7 %all-gather.9.cloned.1.call-start = ((), (), s32[]{:S(2)}) async-start(), calls=%async_computation.9 | async-start | bytes 2359296 | tf_op jit(solution)/shard_map/all_gather | solution.py:958
  66.3 14.0 %collective-permute-start.5 = (bf16[256,1024]{1,0:T(8,128)(2,1)S(1)}, bf16[256,1024]{1,0:T(8,128)(2,1)S(1)}, u32[]{:S(2)}, u32[]{:S(2)}) collective-permute-start(bf16[256,1024]{1,0:T(8,128)(2,1)S(1)} %add_convert_fusion.10.refs_1_.refs_4_), channel_id=1, source_target_pairs={{2,0},{3,1},{0,2},{1,3},{6,4},{7,5},{4,6},{5,7},{10,8},{11,9},{8,1... | collective-permute-start | bytes 1572872 | tf_op jit(solution)/shard_map/ppermute | solution.py:41
  85.7 145.6 %all-gather.11.cloned.1.call-start = ((), (), s32[]{:S(2)}) async-start(), calls=%async_computation.10 | async-start | bytes 4718592 | tf_op jit(solution)/shard_map/all_gather | solution.py:958
  106.4 14.0 %collective-permute-start.8 = (bf16[256,1024]{1,0:T(8,128)(2,1)S(1)}, bf16[256,1024]{1,0:T(8,128)(2,1)S(1)}, u32[]{:S(2)}, u32[]{:S(2)}) collective-permute-start(bf16[256,1024]{1,0:T(8,128)(2,1)S(1)} %add_convert_fusion.9.refs_1_.refs_5_), channel_id=1, source_target_pairs={{2,0},{3,1},{0,2},{1,3},{6,4},{7,5},{4,6},{5,7},{10,8},{11,9},{8,1... | collective-permute-start | bytes 1572872 | tf_op jit(solution)/shard_map/ppermute | solution.py:41
  183.8 150.6 %reduce-scatter.6.cloned.1.call-start = ((), (), s32[]{:S(2)}) async-start(), calls=%async_computation.11 | async-start | bytes 2359296 | tf_op jit(solution)/shard_map/reduce_scatter | solution.py:961
  199.4 14.0 %collective-permute-start.19 = (bf16[256,1024]{1,0:T(8,128)(2,1)S(1)}, bf16[256,1024]{1,0:T(8,128)(2,1)S(1)}, u32[]{:S(2)}, u32[]{:S(2)}) collective-permute-start(bf16[256,1024]{1,0:T(8,128)(2,1)S(1)} %add_convert_fusion.8.refs_1_.refs_4_), channel_id=1, source_target_pairs={{2,0},{3,1},{0,2},{1,3},{6,4},{7,5},{4,6},{5,7},{10,8},{11,9},{8,1... | collective-permute-start | bytes 1572872 | tf_op jit(solution)/shard_map/ppermute | solution.py:41
  249.8 14.0 %collective-permute-start.23 = (bf16[256,1024]{1,0:T(8,128)(2,1)S(1)}, bf16[256,1024]{1,0:T(8,128)(2,1)S(1)}, u32[]{:S(2)}, u32[]{:S(2)}) collective-permute-start(bf16[256,1024]{1,0:T(8,128)(2,1)S(1)} %add_convert_fusion.7.refs_3_.refs_1_), channel_id=1, source_target_pairs={{2,0},{3,1},{0,2},{1,3},{6,4},{7,5},{4,6},{5,7},{10,8},{11,9},{8,1... | collective-permute-start | bytes 1572872 | tf_op jit(solution)/shard_map/ppermute | solution.py:41
  268.9 107.5 %reduce-scatter.8.cloned.1.call-start = ((), (), s32[]{:S(2)}) async-start(), calls=%async_computation.12 | async-start | bytes 2359296 | tf_op jit(solution)/shard_map/reduce_scatter | solution.py:961
  290.7 13.8 %collective-permute-start.30 = (bf16[256,512]{1,0:T(8,128)(2,1)}, bf16[256,512]{1,0:T(8,128)(2,1)S(1)}, u32[]{:S(2)}, u32[]{:S(2)}) collective-permute-start(bf16[256,512]{1,0:T(8,128)(2,1)} %get-tuple-element.123), channel_id=1, source_target_pairs={{8,0},{16,8},{24,16},{28,24},{20,28},{12,20},{4,12},{0,4},{9,1},{1... | collective-permute-start | bytes 786440 | tf_op jit(solution)/shard_map/ppermute | solution.py:37
  305.6 13.6 %collective-permute-start.31 = (bf16[512,512]{1,0:T(8,128)(2,1)S(1)}, bf16[512,512]{1,0:T(8,128)(2,1)S(1)}, u32[]{:S(2)}, u32[]{:S(2)}) collective-permute-start(bf16[512,512]{1,0:T(8,128)(2,1)S(1)} %pad_maximum_fusion.1), channel_id=1, source_target_pairs={{8,0},{16,8},{24,16},{28,24},{20,28},{12,20},{4,12},{0,4},{9,1},{1... | collective-permute-start | bytes 1572872 | tf_op jit(solution)/shard_map/ppermute | solution.py:37
  306.8 13.5 %collective-permute-start.27 = (bf16[512,512]{1,0:T(8,128)(2,1)S(1)}, bf16[512,512]{1,0:T(8,128)(2,1)S(1)}, u32[]{:S(2)}, u32[]{:S(2)}) collective-permute-start(bf16[512,512]{1,0:T(8,128)(2,1)S(1)} %pad_maximum_fusion), channel_id=1, source_target_pairs={{4,0},{0,8},{8,16},{16,24},{24,28},{28,20},{20,12},{12,4},{5,1},{1... | collective-permute-start | bytes 1572872 | tf_op jit(solution)/shard_map/ppermute | solution.py:37
  307.8 13.7 %collective-permute-start.21 = (bf16[256,1024]{1,0:T(8,128)(2,1)S(1)}, bf16[256,1024]{1,0:T(8,128)(2,1)S(1)}, u32[]{:S(2)}, u32[]{:S(2)}) collective-permute-start(bf16[256,1024]{1,0:T(8,128)(2,1)S(1)} %copy-done.36), channel_id=1, source_target_pairs={{1,0},{0,1},{3,2},{2,3},{5,4},{4,5},{7,6},{6,7},{9,8},{8,9},{11,10... | collective-permute-start | bytes 1572872 | tf_op jit(solution)/shard_map/ppermute | solution.py:41
  332.1 15.7 %collective-permute-start.33 = (bf16[512,512]{1,0:T(8,128)(2,1)S(1)}, bf16[512,512]{1,0:T(8,128)(2,1)S(1)}, u32[]{:S(2)}, u32[]{:S(2)}) collective-permute-start(bf16[512,512]{1,0:T(8,128)(2,1)S(1)} %add_convert_fusion.3.refs_2_), channel_id=1, source_target_pairs={{8,0},{16,8},{24,16},{28,24},{20,28},{12,20},{4,12},{0,4},{9,1},{1... | collective-permute-start | bytes 1572872 | tf_op jit(solution)/shard_map/ppermute | solution.py:37
  333.1 17.0 %collective-permute-start.29 = (bf16[512,512]{1,0:T(8,128)(2,1)S(1)}, bf16[512,512]{1,0:T(8,128)(2,1)S(1)}, u32[]{:S(2)}, u32[]{:S(2)}) collective-permute-start(bf16[512,512]{1,0:T(8,128)(2,1)S(1)} %add_convert_fusion.5.refs_1_), channel_id=1, source_target_pairs={{4,0},{0,8},{8,16},{16,24},{24,28},{28,20},{20,12},{12,4},{5,1},{1... | collective-permute-start | bytes 1572872 | tf_op jit(solution)/shard_map/ppermute | solution.py:37
  334.4 79.4 %reduce-scatter.10.cloned.1.call-start = ((), (), s32[]{:S(2)}) async-start(), calls=%async_computation.13 | async-start | bytes 2359296 | tf_op jit(solution)/shard_map/reduce_scatter | solution.py:961
  362.4 14.0 %collective-permute-start.35 = (bf16[256,1024]{1,0:T(8,128)(2,1)S(1)}, bf16[256,1024]{1,0:T(8,128)(2,1)S(1)}, u32[]{:S(2)}, u32[]{:S(2)}) collective-permute-start(bf16[256,1024]{1,0:T(8,128)(2,1)S(1)} %add_convert_fusion.2.refs_6_.refs_1_), channel_id=1, source_target_pairs={{2,0},{3,1},{0,2},{1,3},{6,4},{7,5},{4,6},{5,7},{10,8},{11,9},{8,1... | collective-permute-start | bytes 1572872 | tf_op jit(solution)/shard_map/ppermute | solution.py:41
  381.5 82.3 %reduce-scatter.12.cloned.1.call-start = ((), (), s32[]{:S(2)}) async-start(), calls=%async_computation.14 | async-start | bytes 4718592 | tf_op jit(solution)/shard_map/reduce_scatter | solution.py:961
  395.5 14.0 %collective-permute-start.38 = (bf16[256,1024]{1,0:T(8,128)(2,1)S(1)}, bf16[256,1024]{1,0:T(8,128)(2,1)S(1)}, u32[]{:S(2)}, u32[]{:S(2)}) collective-permute-start(bf16[256,1024]{1,0:T(8,128)(2,1)S(1)} %add_convert_fusion.1.refs_6_.refs_1_), channel_id=1, source_target_pairs={{2,0},{3,1},{0,2},{1,3},{6,4},{7,5},{4,6},{5,7},{10,8},{11,9},{8,1... | collective-permute-start | bytes 1572872 | tf_op jit(solution)/shard_map/ppermute | solution.py:41
  413.9 86.0 %reduce-scatter.14.cloned.1.call-start = ((), (), s32[]{:S(2)}) async-start(), calls=%async_computation.15 | async-start | bytes 2359296 | tf_op jit(solution)/shard_map/reduce_scatter | solution.py:961
  442.5 14.0 %collective-permute-start.41 = (bf16[256,1024]{1,0:T(8,128)(2,1)S(1)}, bf16[256,1024]{1,0:T(8,128)(2,1)S(1)}, u32[]{:S(2)}, u32[]{:S(2)}) collective-permute-start(bf16[256,1024]{1,0:T(8,128)(2,1)S(1)} %add_convert_fusion.refs_2_.refs_6_), channel_id=1, source_target_pairs={{2,0},{3,1},{0,2},{1,3},{6,4},{7,5},{4,6},{5,7},{10,8},{11,9},{8,1... | collective-permute-start | bytes 1572872 | tf_op jit(solution)/shard_map/ppermute | solution.py:41
  (81 other events, 590.2 us)
Sparse Core Ops, SparseCore 0:
  10.1 36.6 all-gather.4
  48.4 46.9 all-gather.6
  97.5 33.3 all-gather.8
  183.9 47.3 all-gather.10
  269.1 36.9 reduce-scatter.5
  334.5 33.9 reduce-scatter.7
  381.6 32.2 reduce-scatter.9
  416.2 47.5 reduce-scatter.11
  466.0 33.7 reduce-scatter.13

commit v5 on v4

--- a/solution.py
+++ b/solution.py
@@ -530,7 +530,7 @@
         ],
         [pltpu.VMEM((2 * half, wide), F32)],
         [own, other, values] + arrays + arrays,
-        8,
+        3,
     )
 
 
@@ -759,12 +759,11 @@
     sources, pieces = refs[:n_kv], refs[n_kv : n_kv + count]
     dq_ref = refs[n_kv + count]
     outs = refs[n_kv + count + 1 : n_kv + count + 1 + n_out]
-    acc, delta, grads, buffer, sems = refs[n_kv + count + 1 + n_out :]
+    acc, lines, stack_q, stack_g, buffer, sems = refs[n_kv + count + 1 + n_out :]
     step = pl.program_id(0)
     steps = buffer.shape[0]
     rows, width = q_ref.shape
     heads = width // HEAD_DIM
-    half = rows // 2
 
     @pl.when(step == 0)
     def _():
@@ -774,34 +773,30 @@
             for out in outs:
                 out[...] = jnp.zeros_like(out)
         weight = joined(pieces)
-        grads[:half, :] = dot_nn(g_own_ref[...], weight).astype(BF16)
-        grads[half:, :] = dot_nn(g_other_ref[...], weight).astype(BF16)
-        turned = (grads[...].astype(F32) * o_ref[...].astype(F32)).T
+        grads = jnp.concatenate([dot_nn(ref[...], weight).astype(BF16) for ref in (g_own_ref, g_other_ref)], axis=0)
+        turned = (grads.astype(F32) * o_ref[...].astype(F32)).T
         for head in range(heads):
             lanes = slice(head * HEAD_DIM, (head + 1) * HEAD_DIM)
-            delta[head : head + 1, :] = jnp.sum(turned[lanes, :], axis=0, keepdims=True)
+            columns = slice(head * rows, (head + 1) * rows)
+            lines[0:1, columns] = lse_ref[head : head + 1, :]
+            lines[1:2, columns] = jnp.sum(turned[lanes, :], axis=0, keepdims=True)
+            inside = head_mask((rows, width), head)
+            stack_q[columns, :] = jnp.where(inside, q_ref[...], 0) * BF16(SCALING)
+            stack_g[columns, :] = jnp.where(inside, grads, 0)
 
     fetch_wait(sources, buffer, sems, step)
     live = live_keys(buffer.shape[1], facts_ref[1], lens_ref[table_ref[step]])
     keys = buffer[step, :, :width]
-    values = buffer[step, :, width:]
     keys_t = keys.T
-    queries = q_ref[...]
-    incoming = grads[...]
-    grad_k = jnp.zeros(keys.shape, F32)
-    grad_v = jnp.zeros(keys.shape, F32)
+    scores = dot_nt(keys, stack_q[...])
+    full = jnp.where(live, jnp.exp(scores - lines[0:1, :]), 0.0)
+    grad_probs = dot_nt(buffer[step, :, width:], stack_g[...])
+    steep = (full * (grad_probs - lines[1:2, :])).astype(BF16)
+    grad_v = dot_nn(full.astype(BF16), stack_g[...])
+    grad_k = dot_nn(steep, stack_q[...])
     for head in range(heads):
-        inside = head_mask(queries.shape, head)
-        mine = jnp.where(inside, queries, 0) * BF16(SCALING)
-        mine_g = jnp.where(inside, incoming, 0)
-        scores = dot_nt(keys, mine)
-        full = jnp.where(live, jnp.exp(scores - lse_ref[head : head + 1, :]), 0.0)
-        grad_probs = dot_nt(values, mine_g)
-        steep = (full * (grad_probs - delta[head : head + 1, :])).astype(BF16)
-        grad_v += dot_nn(full.astype(BF16), mine_g)
-        grad_k += dot_nn(steep, mine)
         lanes = slice(head * HEAD_DIM, (head + 1) * HEAD_DIM)
-        acc[lanes, :] += dot_nn(keys_t[lanes, :], steep)
+        acc[lanes, :] += dot_nn(keys_t[lanes, :], steep[:, head * rows : (head + 1) * rows])
 
     if not ring:
         outs[0][0, :, :width] = grad_k.astype(outs[0].dtype)
@@ -854,13 +849,14 @@
         [shaped(rows, width)] + out_shape,
         [
             pltpu.VMEM((width, rows), F32),
-            pltpu.VMEM((8, rows), F32),
-            pltpu.VMEM((rows, width), BF16),
+            pltpu.VMEM((8, rows * width // HEAD_DIM), F32),
+            pltpu.VMEM((rows * width // HEAD_DIM, width), BF16),
+            pltpu.VMEM((rows * width // HEAD_DIM, width), BF16),
             pltpu.VMEM((steps, rows, 2 * width), BF16),
             pltpu.SemaphoreType.DMA((steps,)),
         ],
         [table, lens, facts, queries, attended, lse, *grads, *sources] + [p for p, _ in pieces],
-        4 + 4 * steps,
+        1 + 0.5 * steps,
         prefetch=3,
     )
 
@@ -1015,7 +1011,7 @@
         else:
             table, lens, walking = scene_table, rel_lens, ring
             sources = ring_gather(kv, half) if ring else [lax.all_gather(kv, "frame", axis=0, tiled=True)]
-            ff = gather(pack_ff(1, sources[4:6] if ring else ()))
+            ff = gather(pack_ff(1, [sources[3], sources[6]] if ring else ()))
             weights[1] = (at, ff)
         attended, lse, part_other, part_own = attend(
             queries, sources, walking, at, table, lens, facts, wide
@@ -1068,7 +1064,7 @@
             ff_grads = one_weight_grads(grad_down, active, 5, [incoming[0]])
             up_sum = scatter(up_grads)
         else:
-            ff_grads = weight_grads(second, grad_up, grad_down, active, 8, [incoming[0]])
+            ff_grads = weight_grads(second, grad_up, grad_down, active, 3, [incoming[0]])
             ff_grads = gate(ff_grads, [at_sum, incoming[1]])
             ff_sum = scatter(ff_grads)
             if ring:

time: 518 us -> 502 us (0.969)
  waiting for transfers between devices: 211 us -> 192 us
    all_gather x4, waiting for transfers between devices: 28.1 us -> 16.1 us  [gather(): lax.all_gather(packed, 'frame', axis=0, tiled=True, axis_index_groups=fra...]
    reduce_scatter x5, waiting for transfers between devices: 21.6 us -> 15.3 us  [scatter(): lax.psum_scatter(grads, 'frame', scatter_dimension=0, tiled=True, axis_in...]
  transfers between devices with their start and end apart: 54 -> 54, of which waited for: 40 -> 42; matrix products, arithmetic and copies ran while one was open for 4% -> 5% of each run, Pallas kernels for 31% -> 33%
where the time goes in v5:
time: 502 us; the launch traced here: 493 us
  waiting for transfers between devices  192 us (38%)
  Pallas kernels  189 us (38%)
  starting transfers between devices  42.1 us (8%)
  local copies, waits for them, and re-layouts  24.2 us (5%)
  between operations  16.8 us (3%)
  other arithmetic  16.2 us (3%)
  blocking collectives  12.4 us (2%)
    pallas_call x43, Pallas kernels, run(): pl.pallas_call(body, grid_spec=pltpu.PrefetchScalarGridSpec(num_scalar_pr...  189 us
    ppermute x28, waiting for transfers between devices, row_take(): return lax.ppermute(value, 'row', [(i ^ bit, i) for i in range(4)])  91.4 us
    ppermute x16, waiting for transfers between devices, ring_take(): lax.ppermute(value, 'frame', [(RING[(i + step) % count], RING[i]) for i i...  67.6 us
    ppermute x16, starting transfers between devices, ring_take(): lax.ppermute(value, 'frame', [(RING[(i + step) % count], RING[i]) for i i...  20.4 us
    all_gather x4, waiting for transfers between devices, gather(): lax.all_gather(packed, 'frame', axis=0, tiled=True, axis_index_groups=fra...  16.1 us
    unnamed x108, local copies, waits for them, and re-layouts  15.8 us
    reduce_scatter x5, waiting for transfers between devices, scatter(): lax.psum_scatter(grads, 'frame', scatter_dimension=0, tiled=True, axis_in...  15.3 us
    ppermute x28, starting transfers between devices, row_take(): return lax.ppermute(value, 'row', [(i ^ bit, i) for i in range(4)])  13.8 us
  transfers between devices with their start and end apart: 54, of which 42 were waited for; matrix products, arithmetic and copies ran while one was open for 5% of the time, Pallas kernels for 33%

profile of v5, /device:TPU:0, one launch (start us, length us, event | category | flops | bytes accessed | tf_op | source)
XLA Modules:
  0.0 493.0 jit_solution(15925206144606231000)
XLA Ops:
  9.9 7.3 %all-to-all-start = ((f32[8,16,128]{2,1,0:T(8,128)}), f32[8,16,128]{2,1,0:T(8,128)S(1)}, u32[]{:S(2)}, u32[]{:S(2)}) async-start(f32[8,16,128]{2,1,0:T(8,128)} %broadcast_in_dim.14), calls=%async_computation | async-start | bytes 131072 | tf_op jit(solution)/shard_map/all_to_all | solution.py:965
  67.8 12.4 %collective-permute-done.5.refs_2_.refs_5_ = bf16[256,1024]{1,0:T(8,128)(2,1)S(1)} collective-permute-done((bf16[256,1024]{1,0:T(8,128)(2,1)S(1)}, bf16[256,1024]{1,0:T(8,128)(2,1)S(1)}, u32[]{:S(2)}, u32[]{:S(2)}) %collective-permute-start.5) | collective-permute-done | bytes 524320 | tf_op jit(solution)/shard_map/ppermute | solution.py:41
  86.1 9.3 %all-gather.7.cloned.1.call-done.refs_2_.refs_3_.refs_4_ = bf16[1024,2048]{1,0:T(8,128)(2,1)} async-done(((bf16[128,2048]{1,0:T(8,128)(2,1)}), bf16[1024,2048]{1,0:T(8,128)(2,1)}) %all-gather.7.cloned.1.call-update) | async-done | bytes 4194320 | tf_op jit(solution)/shard_map/all_gather | solution.py:954
  95.4 7.4 %shard_map.162 = (f32[512,1024]{1,0:T(8,128)}, bf16[512,1024]{1,0:T(8,128)(2,1)}, bf16[256,1024]{1,0:T(8,128)(2,1)}, f32[256,1024]{1,0:T(8,128)}) custom-call(bf16[256,1024]{1,0:T(8,128)(2,1)} %get-tuple-element.91.refs_0_, bf16[256,1024]{1,0:T(8,128)(2,1)} %copy-done.27, bf16[1024,2048]{1,0:T(8,128)(2,1)} %all-gather.7.cloned.1.call-done.refs_2_.refs_3_.refs_4_, ...), custom_call_target="tpu_custom_call" | custom-call | flops 20999999488 | bytes 42000000 | tf_op jit(solution)/shard_map/pallas_call | solution.py:106
  107.9 12.5 %collective-permute-done.8.refs_2_.refs_6_ = bf16[256,1024]{1,0:T(8,128)(2,1)S(1)} collective-permute-done((bf16[256,1024]{1,0:T(8,128)(2,1)S(1)}, bf16[256,1024]{1,0:T(8,128)(2,1)S(1)}, u32[]{:S(2)}, u32[]{:S(2)}) %collective-permute-start.8) | collective-permute-done | bytes 524320 | tf_op jit(solution)/shard_map/ppermute | solution.py:41
  124.1 6.8 %all-gather.9.cloned.1.call-done.refs_2_.refs_13_.refs_17_.refs_7_ = bf16[1024,1024]{1,0:T(8,128)(2,1)} async-done(((bf16[128,1024]{1,0:T(8,128)(2,1)}), bf16[1024,1024]{1,0:T(8,128)(2,1)}) %all-gather.9.cloned.1.call-update) | async-done | bytes 2097168 | tf_op jit(solution)/shard_map/all_gather | solution.py:954
  139.1 10.3 %collective-permute-done.14.refs_12_.refs_16_ = bf16[512,512]{1,0:T(8,128)(2,1)S(1)} collective-permute-done((bf16[512,512]{1,0:T(8,128)(2,1)}, bf16[512,512]{1,0:T(8,128)(2,1)S(1)}, u32[]{:S(2)}, u32[]{:S(2)}) %collective-permute-start.14) | collective-permute-done | bytes 524320 | tf_op jit(solution)/shard_map/ppermute | solution.py:37
  151.4 10.1 %collective-permute-done.15.refs_11_.refs_15_ = bf16[512,512]{1,0:T(8,128)(2,1)S(1)} collective-permute-done((bf16[512,512]{1,0:T(8,128)(2,1)S(1)}, bf16[512,512]{1,0:T(8,128)(2,1)S(1)}, u32[]{:S(2)}, u32[]{:S(2)}) %collective-permute-start.15) | collective-permute-done | bytes 524320 | tf_op jit(solution)/shard_map/ppermute | solution.py:37
  163.5 7.1 %collective-permute-done.16.refs_10_.refs_3_.refs_14_ = bf16[512,512]{1,0:T(8,128)(2,1)S(1)} collective-permute-done((bf16[512,512]{1,0:T(8,128)(2,1)S(1)}, bf16[512,512]{1,0:T(8,128)(2,1)S(1)}, u32[]{:S(2)}, u32[]{:S(2)}) %collective-permute-start.16) | collective-permute-done | bytes 524320 | tf_op jit(solution)/shard_map/ppermute | solution.py:37
  189.1 11.8 %shard_map.166 = (bf16[512,256]{1,0:T(8,128)(2,1)}, f32[8,512]{1,0:T(8,128)}, bf16[256,1024]{1,0:T(8,128)(2,1)}, f32[256,1024]{1,0:T(8,128)}) custom-call(s32[4]{0:T(128)} %bitcast.22, s32[8]{0:T(128)} %gather_fusion.1, s32[3]{0:T(128)} %pad_add_fusion.refs_0_.refs_2_, bf16[512,256]{1,0:T(8,128)(2,1)} %get-tuple-element.96.refs_3_, ...), custom_call_target="tpu_custom_call" | custom-call | flops 32999999488 | bytes 66000000 | tf_op jit(solution)/shard_map/pallas_call | solution.py:106
  206.0 12.5 %collective-permute-done.19.refs_2_.refs_5_ = bf16[256,1024]{1,0:T(8,128)(2,1)S(1)} collective-permute-done((bf16[256,1024]{1,0:T(8,128)(2,1)S(1)}, bf16[256,1024]{1,0:T(8,128)(2,1)S(1)}, u32[]{:S(2)}, u32[]{:S(2)}) %collective-permute-start.19) | collective-permute-done | bytes 524320 | tf_op jit(solution)/shard_map/ppermute | solution.py:41
  225.1 7.4 %shard_map.169 = (f32[512,1024]{1,0:T(8,128)}, bf16[512,1024]{1,0:T(8,128)(2,1)}, bf16[256,1024]{1,0:T(8,128)(2,1)}, f32[256,1024]{1,0:T(8,128)}) custom-call(bf16[256,1024]{1,0:T(8,128)(2,1)} %get-tuple-element.101.refs_0_, bf16[256,1024]{1,0:T(8,128)(2,1)} %copy-done.41, bf16[1024,2048]{1,0:T(8,128)(2,1)} %all-gather.11.cloned.1.call-done.refs_2_.refs_3_.refs_4_, ...), custom_call_target="tpu_custom_call" | custom-call | flops 20999999488 | bytes 42000000 | tf_op jit(solution)/shard_map/pallas_call | solution.py:106
  232.5 7.6 %shard_map.170 = (bf16[512,1024]{1,0:T(8,128)(2,1)}, bf16[256,1024]{1,0:T(8,128)(2,1)}, f32[256,1024]{1,0:T(8,128)}) custom-call(bf16[256,1024]{1,0:T(8,128)(2,1)} %shard_map.157.refs_4_.refs_0_, bf16[256,1024]{1,0:T(8,128)(2,1)} %copy-done.30, f32[512,1024]{1,0:T(8,128)} %get-tuple-element.104.refs_2_, ...), custom_call_target="tpu_custom_call" | custom-call | flops 8999999488 | bytes 18000000 | tf_op jit(solution)/shard_map/pallas_call | solution.py:106
  265.7 17.6 %shard_map.176 = (f32[512,256]{1,0:T(8,128)}, bf16[512,512]{1,0:T(8,128)(2,1)}, bf16[512,512]{1,0:T(8,128)(2,1)}, bf16[512,512]{1,0:T(8,128)(2,1)}, bf16[512,512...) custom-call(s32[4]{0:T(128)} %bitcast.23, ...), custom_call_target="tpu_custom_call" | custom-call | flops 8999999488 | bytes 18000000 | tf_op jit(solution)/shard_map/pallas_call | solution.py:106
  296.9 9.4 %collective-permute-done.31 = bf16[512,512]{1,0:T(8,128)(2,1)S(1)} collective-permute-done((bf16[512,512]{1,0:T(8,128)(2,1)S(1)}, bf16[512,512]{1,0:T(8,128)(2,1)S(1)}, u32[]{:S(2)}, u32[]{:S(2)}) %collective-permute-start.31) | collective-permute-done | bytes 524320 | tf_op jit(solution)/shard_map/ppermute | solution.py:37
  341.6 7.5 %shard_map.177 = (bf16[512,768]{1,0:T(8,128)(2,1)}, bf16[256,1024]{1,0:T(8,128)(2,1)}, f32[256,1024]{1,0:T(8,128)}, f32[2,256]{1,0:T(2,128)}, f32[1,1024]{1,0:T(1,128)}) custom-call(f32[512,256]{1,0:T(8,128)} %get-tuple-element.114.refs_0_, f32[512,512]{1,0:T(8,128)} %convert_add_fusion.refs_1_, f32[512,512]{1,0:T(8,128)} %get-tuple-element.124.refs_2_, ...), custom_call_target="tpu_custom_call" | custom-call | flops 17999998976 | bytes 36000000 | tf_op jit(solution)/shard_map/pallas_call | solution.py:106
  359.3 7.5 %collective-permute-done.35.refs_2_ = bf16[256,1024]{1,0:T(8,128)(2,1)S(1)} collective-permute-done((bf16[256,1024]{1,0:T(8,128)(2,1)S(1)}, bf16[256,1024]{1,0:T(8,128)(2,1)S(1)}, u32[]{:S(2)}, u32[]{:S(2)}) %collective-permute-start.35) | collective-permute-done | bytes 524320 | tf_op jit(solution)/shard_map/ppermute | solution.py:41
  374.7 7.7 %shard_map.182 = (bf16[512,1024]{1,0:T(8,128)(2,1)}, bf16[256,1024]{1,0:T(8,128)(2,1)}, f32[256,1024]{1,0:T(8,128)}) custom-call(bf16[256,1024]{1,0:T(8,128)(2,1)} %get-tuple-element.129.refs_0_.refs_2_, bf16[256,1024]{1,0:T(8,128)(2,1)} %copy-done.42, f32[512,1024]{1,0:T(8,128)} %get-tuple-element.130.refs_2_, ...), custom_call_target="tpu_custom_call" | custom-call | flops 8999999488 | bytes 18000000 | tf_op jit(solution)/shard_map/pallas_call | solution.py:106
  386.7 8.7 %shard_map.183.refs_0_ = bf16[1024,2048]{1,0:T(8,128)(2,1)} custom-call(bf16[256,1024]{1,0:T(8,128)(2,1)} %get-tuple-element.91.refs_0_, bf16[256,1024]{1,0:T(8,128)(2,1)} %copy-done.27, bf16[256,1024]{1,0:T(8,128)(2,1)} %get-tuple-element.129.refs_0_.refs_2_, bf16[256,1024]{1,0:T(8,128)(2,1)} %copy-done.42, bf16[512,1024]{1,0:T(8,128)(2,1)} %get-tuple-element.133.refs_4_, ...), custom_call_target="tpu_custom_call" | custom-call | flops 8999999488 | bytes 18000000 | tf_op jit(solution)/shard_map/pallas_call | solution.py:106
  410.1 7.7 %shard_map.187 = (f32[512,256]{1,0:T(8,128)}, f32[1,512,512]{2,1,0:T(8,128)}) custom-call(s32[1]{0:T(128)} %constant.50.clone.1.refs_0_, s32[1]{0:T(128)} %dynamic_slice.13.refs_1_, s32[3]{0:T(128)} %pad_add_fusion.refs_0_.refs_2_, bf16[512,256]{1,0:T(8,128)(2,1)} %get-tuple-element.86.refs_3_, bf16[512,256]{1,0:T(8,128)(2,1)} %get-tuple-element.137.refs_4_.refs_5_, ...), custom_call_target="tpu_custom_call" | custom-call | flops 4499999744 | bytes 9000000 | tf_op jit(solution)/shard_map/pallas_call | solution.py:106
  417.7 7.6 %shard_map.188 = (bf16[512,768]{1,0:T(8,128)(2,1)}, bf16[256,1024]{1,0:T(8,128)(2,1)}, f32[256,1024]{1,0:T(8,128)}, f32[2,256]{1,0:T(2,128)}, f32[1,1024]{1,0:T(1,128)}) custom-call(f32[512,256]{1,0:T(8,128)} %get-tuple-element.140.refs_0_, f32[512,512]{1,0:T(8,128)} %bitcast.19, f32[512,512]{1,0:T(8,128)} %get-tuple-element.142.refs_2_, ...), custom_call_target="tpu_custom_call" | custom-call | flops 17999998976 | bytes 36000000 | tf_op jit(solution)/shard_map/pallas_call | solution.py:106
  435.4 7.5 %collective-permute-done.41.refs_3_.refs_2_ = bf16[256,1024]{1,0:T(8,128)(2,1)S(1)} collective-permute-done((bf16[256,1024]{1,0:T(8,128)(2,1)S(1)}, bf16[256,1024]{1,0:T(8,128)(2,1)S(1)}, u32[]{:S(2)}, u32[]{:S(2)}) %collective-permute-start.41) | collective-permute-done | bytes 524320 | tf_op jit(solution)/shard_map/ppermute | solution.py:41
  454.2 12.4 %all_to_all.10 = f32[8,16,128]{2,1,0:T(8,128)S(1)} all-to-all(f32[8,16,128]{2,1,0:T(8,128)} %shard_map.195), channel_id=1, replica_groups=mesh['frame'=8,'row'=4] {'frame'}, dimensions={0} | all-to-all | bytes 131072 | tf_op jit(solution)/shard_map/all_to_all | solution.py:1186
  474.2 10.1 %reduce-scatter.14.cloned.1.call-done.refs_0_ = bf16[128,1024]{1,0:T(8,128)(2,1)} async-done(((bf16[1024,1024]{1,0:T(8,128)(2,1)}), bf16[128,1024]{1,0:T(8,128)(2,1)}) %reduce-scatter.14.cloned.1.call-update) | async-done | bytes 262160 | tf_op jit(solution)/shard_map/reduce_scatter | solution.py:957
  (289 shorter events, 250.1 us)
Async XLA Ops:
  7.2 42.4 %all-gather.5.cloned.1.call-start = ((), (), s32[]{:S(2)}) async-start(), calls=%async_computation.7 | async-start | bytes 2359296 | tf_op jit(solution)/shard_map/all_gather | solution.py:954
  9.9 15.0 %all-to-all-start = ((f32[8,16,128]{2,1,0:T(8,128)}), f32[8,16,128]{2,1,0:T(8,128)S(1)}, u32[]{:S(2)}, u32[]{:S(2)}) async-start(f32[8,16,128]{2,1,0:T(8,128)} %broadcast_in_dim.14), calls=%async_computation | async-start | bytes 131072 | tf_op jit(solution)/shard_map/all_to_all | solution.py:965
  17.1 78.2 %all-gather.7.cloned.1.call-start = ((), (), s32[]{:S(2)}) async-start(), calls=%async_computation.8 | async-start | bytes 4718592 | tf_op jit(solution)/shard_map/all_gather | solution.py:954
  17.2 19.1 %collective-permute-start = (bf16[128,1024]{1,0:T(8,128)(2,1)S(1)}, bf16[128,1024]{1,0:T(8,128)(2,1)S(1)}, u32[]{:S(2)}, u32[]{:S(2)}) collective-permute-start(bf16[128,1024]{1,0:T(8,128)(2,1)S(1)} %copy-done.45), channel_id=1, source_target_pairs={{2,0},{3,1},{0,2},{1,3},{6,4},{7,5},{4,6},{5,7},{10,8},{11,9},{8,1... | collective-permute-start | bytes 786440 | tf_op jit(solution)/shard_map/ppermute | solution.py:41
  21.3 109.7 %all-gather.9.cloned.1.call-start = ((), (), s32[]{:S(2)}) async-start(), calls=%async_computation.9 | async-start | bytes 2359296 | tf_op jit(solution)/shard_map/all_gather | solution.py:954
  36.3 13.3 %collective-permute-start.3 = (bf16[256,1024]{1,0:T(8,128)(2,1)}, bf16[256,1024]{1,0:T(8,128)(2,1)S(1)}, u32[]{:S(2)}, u32[]{:S(2)}) collective-permute-start(bf16[256,1024]{1,0:T(8,128)(2,1)} %shard_map.157.refs_4_.refs_0_), channel_id=1, source_target_pairs={{1,0},{0,1},{3,2},{2,3},{5,4},{4,5},{7,6},{6,7},{9,8},{8,9},{11,10... | collective-permute-start | bytes 1572872 | tf_op jit(solution)/shard_map/ppermute | solution.py:41
  66.3 14.0 %collective-permute-start.5 = (bf16[256,1024]{1,0:T(8,128)(2,1)S(1)}, bf16[256,1024]{1,0:T(8,128)(2,1)S(1)}, u32[]{:S(2)}, u32[]{:S(2)}) collective-permute-start(bf16[256,1024]{1,0:T(8,128)(2,1)S(1)} %add_convert_fusion.10.refs_1_.refs_4_), channel_id=1, source_target_pairs={{2,0},{3,1},{0,2},{1,3},{6,4},{7,5},{4,6},{5,7},{10,8},{11,9},{8,1... | collective-permute-start | bytes 1572872 | tf_op jit(solution)/shard_map/ppermute | solution.py:41
  85.7 138.6 %all-gather.11.cloned.1.call-start = ((), (), s32[]{:S(2)}) async-start(), calls=%async_computation.10 | async-start | bytes 4718592 | tf_op jit(solution)/shard_map/all_gather | solution.py:954
  106.4 14.0 %collective-permute-start.8 = (bf16[256,1024]{1,0:T(8,128)(2,1)S(1)}, bf16[256,1024]{1,0:T(8,128)(2,1)S(1)}, u32[]{:S(2)}, u32[]{:S(2)}) collective-permute-start(bf16[256,1024]{1,0:T(8,128)(2,1)S(1)} %add_convert_fusion.9.refs_1_.refs_5_), channel_id=1, source_target_pairs={{2,0},{3,1},{0,2},{1,3},{6,4},{7,5},{4,6},{5,7},{10,8},{11,9},{8,1... | collective-permute-start | bytes 1572872 | tf_op jit(solution)/shard_map/ppermute | solution.py:41
  174.5 148.0 %reduce-scatter.6.cloned.1.call-start = ((), (), s32[]{:S(2)}) async-start(), calls=%async_computation.11 | async-start | bytes 2359296 | tf_op jit(solution)/shard_map/reduce_scatter | solution.py:957
  204.5 14.0 %collective-permute-start.19 = (bf16[256,1024]{1,0:T(8,128)(2,1)S(1)}, bf16[256,1024]{1,0:T(8,128)(2,1)S(1)}, u32[]{:S(2)}, u32[]{:S(2)}) collective-permute-start(bf16[256,1024]{1,0:T(8,128)(2,1)S(1)} %add_convert_fusion.8.refs_1_.refs_4_), channel_id=1, source_target_pairs={{2,0},{3,1},{0,2},{1,3},{6,4},{7,5},{4,6},{5,7},{10,8},{11,9},{8,1... | collective-permute-start | bytes 1572872 | tf_op jit(solution)/shard_map/ppermute | solution.py:41
  243.7 14.0 %collective-permute-start.23 = (bf16[256,1024]{1,0:T(8,128)(2,1)S(1)}, bf16[256,1024]{1,0:T(8,128)(2,1)S(1)}, u32[]{:S(2)}, u32[]{:S(2)}) collective-permute-start(bf16[256,1024]{1,0:T(8,128)(2,1)S(1)} %add_convert_fusion.7.refs_3_.refs_1_), channel_id=1, source_target_pairs={{2,0},{3,1},{0,2},{1,3},{6,4},{7,5},{4,6},{5,7},{10,8},{11,9},{8,1... | collective-permute-start | bytes 1572872 | tf_op jit(solution)/shard_map/ppermute | solution.py:41
  250.3 116.4 %reduce-scatter.8.cloned.1.call-start = ((), (), s32[]{:S(2)}) async-start(), calls=%async_computation.12 | async-start | bytes 2359296 | tf_op jit(solution)/shard_map/reduce_scatter | solution.py:957
  293.1 13.2 %collective-permute-start.31 = (bf16[512,512]{1,0:T(8,128)(2,1)S(1)}, bf16[512,512]{1,0:T(8,128)(2,1)S(1)}, u32[]{:S(2)}, u32[]{:S(2)}) collective-permute-start(bf16[512,512]{1,0:T(8,128)(2,1)S(1)} %pad_maximum_fusion.1), channel_id=1, source_target_pairs={{8,0},{16,8},{24,16},{28,24},{20,28},{12,20},{4,12},{0,4},{9,1},{1... | collective-permute-start | bytes 1572872 | tf_op jit(solution)/shard_map/ppermute | solution.py:37
  296.5 12.8 %collective-permute-start.27 = (bf16[512,512]{1,0:T(8,128)(2,1)S(1)}, bf16[512,512]{1,0:T(8,128)(2,1)S(1)}, u32[]{:S(2)}, u32[]{:S(2)}) collective-permute-start(bf16[512,512]{1,0:T(8,128)(2,1)S(1)} %pad_maximum_fusion), channel_id=1, source_target_pairs={{4,0},{0,8},{8,16},{16,24},{24,28},{28,20},{20,12},{12,4},{5,1},{1... | collective-permute-start | bytes 1572872 | tf_op jit(solution)/shard_map/ppermute | solution.py:37
  296.9 13.3 %collective-permute-start.21 = (bf16[256,1024]{1,0:T(8,128)(2,1)S(1)}, bf16[256,1024]{1,0:T(8,128)(2,1)S(1)}, u32[]{:S(2)}, u32[]{:S(2)}) collective-permute-start(bf16[256,1024]{1,0:T(8,128)(2,1)S(1)} %copy-done.36), channel_id=1, source_target_pairs={{1,0},{0,1},{3,2},{2,3},{5,4},{4,5},{7,6},{6,7},{9,8},{8,9},{11,10... | collective-permute-start | bytes 1572872 | tf_op jit(solution)/shard_map/ppermute | solution.py:41
  318.8 17.8 %collective-permute-start.33 = (bf16[512,512]{1,0:T(8,128)(2,1)S(1)}, bf16[512,512]{1,0:T(8,128)(2,1)S(1)}, u32[]{:S(2)}, u32[]{:S(2)}) collective-permute-start(bf16[512,512]{1,0:T(8,128)(2,1)S(1)} %add_convert_fusion.3.refs_2_), channel_id=1, source_target_pairs={{8,0},{16,8},{24,16},{28,24},{20,28},{12,20},{4,12},{0,4},{9,1},{1... | collective-permute-start | bytes 1572872 | tf_op jit(solution)/shard_map/ppermute | solution.py:37
  321.6 18.9 %collective-permute-start.29 = (bf16[512,512]{1,0:T(8,128)(2,1)S(1)}, bf16[512,512]{1,0:T(8,128)(2,1)S(1)}, u32[]{:S(2)}, u32[]{:S(2)}) collective-permute-start(bf16[512,512]{1,0:T(8,128)(2,1)S(1)} %add_convert_fusion.5.refs_1_), channel_id=1, source_target_pairs={{4,0},{0,8},{8,16},{16,24},{24,28},{28,20},{20,12},{12,4},{5,1},{1... | collective-permute-start | bytes 1572872 | tf_op jit(solution)/shard_map/ppermute | solution.py:37
  322.6 77.4 %reduce-scatter.10.cloned.1.call-start = ((), (), s32[]{:S(2)}) async-start(), calls=%async_computation.13 | async-start | bytes 2359296 | tf_op jit(solution)/shard_map/reduce_scatter | solution.py:957
  352.7 14.0 %collective-permute-start.35 = (bf16[256,1024]{1,0:T(8,128)(2,1)S(1)}, bf16[256,1024]{1,0:T(8,128)(2,1)S(1)}, u32[]{:S(2)}, u32[]{:S(2)}) collective-permute-start(bf16[256,1024]{1,0:T(8,128)(2,1)S(1)} %add_convert_fusion.2.refs_6_.refs_1_), channel_id=1, source_target_pairs={{2,0},{3,1},{0,2},{1,3},{6,4},{7,5},{4,6},{5,7},{10,8},{11,9},{8,1... | collective-permute-start | bytes 1572872 | tf_op jit(solution)/shard_map/ppermute | solution.py:41
  367.6 80.5 %reduce-scatter.12.cloned.1.call-start = ((), (), s32[]{:S(2)}) async-start(), calls=%async_computation.14 | async-start | bytes 4718592 | tf_op jit(solution)/shard_map/reduce_scatter | solution.py:957
  385.9 14.0 %collective-permute-start.38 = (bf16[256,1024]{1,0:T(8,128)(2,1)S(1)}, bf16[256,1024]{1,0:T(8,128)(2,1)S(1)}, u32[]{:S(2)}, u32[]{:S(2)}) collective-permute-start(bf16[256,1024]{1,0:T(8,128)(2,1)S(1)} %add_convert_fusion.1.refs_6_.refs_1_), channel_id=1, source_target_pairs={{2,0},{3,1},{0,2},{1,3},{6,4},{7,5},{4,6},{5,7},{10,8},{11,9},{8,1... | collective-permute-start | bytes 1572872 | tf_op jit(solution)/shard_map/ppermute | solution.py:41
  400.8 83.5 %reduce-scatter.14.cloned.1.call-start = ((), (), s32[]{:S(2)}) async-start(), calls=%async_computation.15 | async-start | bytes 2359296 | tf_op jit(solution)/shard_map/reduce_scatter | solution.py:957
  428.9 14.1 %collective-permute-start.41 = (bf16[256,1024]{1,0:T(8,128)(2,1)S(1)}, bf16[256,1024]{1,0:T(8,128)(2,1)S(1)}, u32[]{:S(2)}, u32[]{:S(2)}) collective-permute-start(bf16[256,1024]{1,0:T(8,128)(2,1)S(1)} %add_convert_fusion.refs_2_.refs_6_), channel_id=1, source_target_pairs={{2,0},{3,1},{0,2},{1,3},{6,4},{7,5},{4,6},{5,7},{10,8},{11,9},{8,1... | collective-permute-start | bytes 1572872 | tf_op jit(solution)/shard_map/ppermute | solution.py:41
  (81 other events, 512.3 us)
Sparse Core Ops, SparseCore 0:
  10.1 36.6 all-gather.4
  48.4 46.9 all-gather.6
  97.5 33.3 all-gather.8
  174.6 49.4 all-gather.10
  250.5 31.1 reduce-scatter.5
  322.7 32.8 reduce-scatter.7
  367.7 30.5 reduce-scatter.9
  400.9 47.1 reduce-scatter.11
  450.4 33.8 reduce-scatter.13

commit v6 on v5

--- a/solution.py
+++ b/solution.py
@@ -534,6 +534,49 @@
     )
 
 
+def feed_both_kernel(own_ref, other_ref, g_own_ref, g_other_ref, up_ref, down_ref, *refs):
+    active_ref, grad_ref, part_other_ref, part_own_ref, back_other_ref, back_own_ref, acc, back = refs
+    step = pl.program_id(0)
+
+    @pl.when(step == 0)
+    def _():
+        acc[...] = jnp.zeros_like(acc)
+        back[...] = jnp.zeros_like(back)
+
+    up, down = up_ref[...], down_ref[...]
+    half = own_ref.shape[0]
+    for source, g_source, start in ((own_ref, g_own_ref, 0), (other_ref, g_other_ref, half)):
+        values = dot_nn(source[...], up)
+        gate_part = 0.5 * (1.0 + lax.erf(values * F32(ROOT_HALF)))
+        active_ref[start : start + half, :] = (values * gate_part).astype(BF16)
+        slope = gate_part + values * (jnp.exp(-0.5 * values * values) * F32(BELL))
+        grad_ref[start : start + half, :] = (dot_nn(g_source[...], down) * slope).astype(BF16)
+    acc[...] += dot_nt(active_ref[...], down)
+    back[...] += dot_nt(grad_ref[...], up)
+
+    @pl.when(step == pl.num_programs(0) - 1)
+    def _():
+        part_own_ref[...] = acc[:half, :]
+        part_other_ref[...] = acc[half:, :].astype(BF16)
+        back_own_ref[...] = back[:half, :]
+        back_other_ref[...] = back[half:, :].astype(BF16)
+
+
+def feed_both(second, grads, weight, hidden):
+    half, wide = second[0].shape
+    steps = hidden // TILE
+    return run(
+        feed_both_kernel,
+        (steps,),
+        [whole((half, wide))] * 4 + [column(wide, lambda j: j), column(wide, lambda j: j + steps)],
+        [column(2 * half, lambda j: j)] * 2 + [whole((half, wide))] * 4,
+        [shaped(2 * half, hidden, dtype=BF16)] * 2 + [shaped(half, wide, dtype=BF16), shaped(half, wide)] * 2,
+        [pltpu.VMEM((2 * half, wide), F32)] * 2,
+        [*second, *grads, weight, weight],
+        10,
+    )
+
+
 def weight_kernel(split, a_own, a_other, b_own, b_other, first_ref, second_ref, out_ref, turned):
     step = pl.program_id(0)
     half = a_own.shape[0]
@@ -685,7 +728,7 @@
 def attend_kernel(ring, n_kv, count, table_ref, lens_ref, facts_ref, q_ref, *refs):
     sources, pieces = refs[:n_kv], refs[n_kv : n_kv + count]
     out_ref, lse_ref, part_other_ref, part_own_ref = refs[n_kv + count : n_kv + count + 4]
-    acc, sums, buffer, sems = refs[n_kv + count + 4 :]
+    acc, sums, stack, buffer, sems = refs[n_kv + count + 4 :]
     step = pl.program_id(0)
     steps = buffer.shape[0]
     rows, width = q_ref.shape
@@ -695,28 +738,29 @@
     def _():
         fetch_start(table_ref, sources, ring, buffer, sems, steps)
         acc[...] = jnp.zeros_like(acc)
-        sums[...] = jnp.ones_like(sums)
-        sums[:heads, :] = jnp.zeros((heads, rows), F32)
+        sums[...] = jnp.zeros_like(sums)
+        for head in range(heads):
+            mine = jnp.where(head_mask((rows, width), head), q_ref[...], 0) * BF16(SCALING)
+            stack[head * rows : (head + 1) * rows, :] = mine
 
     fetch_wait(sources, buffer, sems, step)
     live = live_keys(buffer.shape[1], facts_ref[1], lens_ref[table_ref[step]])
-    keys = buffer[step, :, :width]
     values_t = buffer[step, :, width:].T
-    queries = q_ref[...]
+    powers = jnp.where(live, jnp.exp(dot_nt(buffer[step, :, :width], stack[...])), 0.0)
+    sums[0:1, :] += jnp.sum(powers, axis=0, keepdims=True)
+    low = powers.astype(BF16)
     for head in range(heads):
-        mine = jnp.where(head_mask(queries.shape, head), queries, 0) * BF16(SCALING)
-        scores = dot_nt(keys, mine)
-        powers = jnp.where(live, jnp.exp(scores), 0.0)
-        sums[head : head + 1, :] += jnp.sum(powers, axis=0, keepdims=True)
         lanes = slice(head * HEAD_DIM, (head + 1) * HEAD_DIM)
-        acc[lanes, :] += dot_nn(values_t[lanes, :], powers.astype(BF16))
+        acc[lanes, :] += dot_nn(values_t[lanes, :], low[:, head * rows : (head + 1) * rows])
 
     @pl.when(step == steps - 1)
     def _():
-        lse_ref[...] = jnp.log(sums[...])
+        lse_ref[...] = jnp.zeros_like(lse_ref)
         for head in range(heads):
             lanes = slice(head * HEAD_DIM, (head + 1) * HEAD_DIM)
-            acc[lanes, :] = acc[lanes, :] / sums[head : head + 1, :]
+            total = sums[0:1, head * rows : (head + 1) * rows]
+            lse_ref[head : head + 1, :] = jnp.log(total)
+            acc[lanes, :] = acc[lanes, :] / total
         out_ref[...] = acc[...].T.astype(BF16)
         weight = joined(pieces)
         half = rows // 2
@@ -743,7 +787,8 @@
         ],
         [
             pltpu.VMEM((width, rows), F32),
-            pltpu.VMEM((8, rows), F32),
+            pltpu.VMEM((8, rows * width // HEAD_DIM), F32),
+            pltpu.VMEM((rows * width // HEAD_DIM, width), BF16),
             pltpu.VMEM((steps, rows, 2 * width), BF16),
             pltpu.SemaphoreType.DMA((steps,)),
         ],
@@ -959,6 +1004,7 @@
         )
 
     at_zero, ff_zero, at_one = gather(pack_at(0)), gather(pack_ff(0)), gather(pack_at(1))
+    ff_one = pack_ff(1)
     weights = [(at_zero, ff_zero), None]
     if ring:
         rows = jnp.concatenate([block_gains[0], block_gains[1], jnp.zeros((4, shard), BF16)]).astype(F32)
@@ -1011,7 +1057,7 @@
         else:
             table, lens, walking = scene_table, rel_lens, ring
             sources = ring_gather(kv, half) if ring else [lax.all_gather(kv, "frame", axis=0, tiled=True)]
-            ff = gather(pack_ff(1, [sources[3], sources[6]] if ring else ()))
+            ff = gather(gate(ff_one, [sources[3], sources[6]]) if ring else ff_one)
             weights[1] = (at, ff)
         attended, lse, part_other, part_own = attend(
             queries, sources, walking, at, table, lens, facts, wide
@@ -1028,7 +1074,12 @@
             2,
         )
         second = (second, row_take(second, 1))
-        up_values, active, part_other, part_own = feed(second, ff, hidden)
+        if block == 0:
+            up_values, active, part_other, part_own = feed(second, ff, hidden)
+        else:
+            both = feed_both(second, grad_down, ff[0][0], hidden)
+            active, grad_up, part_other, part_own, back_other, back_own = both
+            up_values = None
         stored.append(
             (h, normed, queries, mixed, (sources, walking, table, lens), attended, lse, branch)
             + (middle, second, up_values, active)
@@ -1057,7 +1108,10 @@
         at, ff = weights[block]
         h, normed, queries, mixed, keys, attended, lse, branch, middle, second, up_values, active = stored[block]
         sources, walking, table, lens = keys
-        grad_up, part_other, part_own = feed_back(grad_down, up_values, ff)
+        if block == 1:
+            part_other, part_own = back_other, back_own
+        else:
+            grad_up, part_other, part_own = feed_back(grad_down, up_values, ff)
         incoming = reduce_rows(part_other, part_own)
         if block == 1:
             up_grads = one_weight_grads(second, grad_up, 5, [incoming[0]])

time: 502 us -> 492 us (0.980)
  Pallas kernels: 189 us -> 182 us
    pallas_call x43, Pallas kernels: 189 us -> 182 us  [run(): pl.pallas_call(body, grid_spec=pltpu.PrefetchScalarGridSpec(num_scalar_pr...]
    ppermute x16, waiting for transfers between devices: 67.6 us -> 62.6 us  [ring_take(): lax.ppermute(value, 'frame', [(RING[(i + step) % count], RING[i]) for i i...]
  transfers between devices with their start and end apart: 54 -> 54, of which waited for: 42 -> 43; matrix products, arithmetic and copies ran while one was open for 5% -> 5% of each run, Pallas kernels for 33% -> 34%
where the time goes in v6:
time: 492 us; the launch traced here: 483 us
  waiting for transfers between devices  193 us (39%)
  Pallas kernels  182 us (37%)
  starting transfers between devices  40.5 us (8%)
  local copies, waits for them, and re-layouts  22.4 us (5%)
  between operations  16.8 us (3%)
  other arithmetic  16.1 us (3%)
  blocking collectives  12.3 us (2%)
    pallas_call x43, Pallas kernels, run(): pl.pallas_call(body, grid_spec=pltpu.PrefetchScalarGridSpec(num_scalar_pr...  182 us
    ppermute x28, waiting for transfers between devices, row_take(): return lax.ppermute(value, 'row', [(i ^ bit, i) for i in range(4)])  90.9 us
    ppermute x16, waiting for transfers between devices, ring_take(): lax.ppermute(value, 'frame', [(RING[(i + step) % count], RING[i]) for i i...  62.6 us
    all_gather x4, waiting for transfers between devices, gather(): lax.all_gather(packed, 'frame', axis=0, tiled=True, axis_index_groups=fra...  19 us
    reduce_scatter x5, waiting for transfers between devices, scatter(): lax.psum_scatter(grads, 'frame', scatter_dimension=0, tiled=True, axis_in...  18.2 us
    ppermute x16, starting transfers between devices, ring_take(): lax.ppermute(value, 'frame', [(RING[(i + step) % count], RING[i]) for i i...  17.3 us
    ppermute x28, starting transfers between devices, row_take(): return lax.ppermute(value, 'row', [(i ^ bit, i) for i in range(4)])  15.4 us
    unnamed x108, local copies, waits for them, and re-layouts  14.1 us
  transfers between devices with their start and end apart: 54, of which 43 were waited for; matrix products, arithmetic and copies ran while one was open for 5% of the time, Pallas kernels for 34%

profile of v6, /device:TPU:0, one launch (start us, length us, event | category | flops | bytes accessed | tf_op | source)
XLA Modules:
  0.0 482.6 jit_solution(16424672255137959220)
XLA Ops:
  9.9 7.3 %all-to-all-start = ((f32[8,16,128]{2,1,0:T(8,128)}), f32[8,16,128]{2,1,0:T(8,128)S(1)}, u32[]{:S(2)}, u32[]{:S(2)}) async-start(f32[8,16,128]{2,1,0:T(8,128)} %broadcast_in_dim.14), calls=%async_computation | async-start | bytes 131072 | tf_op jit(solution)/shard_map/all_to_all | solution.py:1011
  55.8 6.2 %shard_map.159 = (bf16[512,256]{1,0:T(8,128)(2,1)}, f32[8,512]{1,0:T(8,128)}, bf16[256,1024]{1,0:T(8,128)(2,1)}, f32[256,1024]{1,0:T(8,128)}) custom-call(s32[1]{0:T(128)} %constant.50.clone.1.refs_0_, s32[1]{0:T(128)} %dynamic_slice.13.refs_1_, s32[3]{0:T(128)} %pad_add_fusion.refs_0_.refs_2_, bf16[512,256]{1,0:T(8,128)(2,1)} %get-tuple-element.85.refs_3_, ...), custom_call_target="tpu_custom_call" | custom-call | flops 15000000512 | bytes 30000000 | tf_op jit(solution)/shard_map/pallas_call | solution.py:106
  67.2 12.4 %collective-permute-done.5.refs_2_.refs_5_ = bf16[256,1024]{1,0:T(8,128)(2,1)S(1)} collective-permute-done((bf16[256,1024]{1,0:T(8,128)(2,1)S(1)}, bf16[256,1024]{1,0:T(8,128)(2,1)S(1)}, u32[]{:S(2)}, u32[]{:S(2)}) %collective-permute-start.5) | collective-permute-done | bytes 524320 | tf_op jit(solution)/shard_map/ppermute | solution.py:41
  85.5 9.9 %all-gather.7.cloned.1.call-done.refs_2_.refs_3_.refs_4_ = bf16[1024,2048]{1,0:T(8,128)(2,1)} async-done(((bf16[128,2048]{1,0:T(8,128)(2,1)}), bf16[1024,2048]{1,0:T(8,128)(2,1)}) %all-gather.7.cloned.1.call-update) | async-done | bytes 4194320 | tf_op jit(solution)/shard_map/all_gather | solution.py:999
  95.4 7.3 %shard_map.162 = (f32[512,1024]{1,0:T(8,128)}, bf16[512,1024]{1,0:T(8,128)(2,1)}, bf16[256,1024]{1,0:T(8,128)(2,1)}, f32[256,1024]{1,0:T(8,128)}) custom-call(bf16[256,1024]{1,0:T(8,128)(2,1)} %get-tuple-element.90.refs_0_, bf16[256,1024]{1,0:T(8,128)(2,1)} %copy-done.27, bf16[1024,2048]{1,0:T(8,128)(2,1)} %all-gather.7.cloned.1.call-done.refs_2_.refs_3_.refs_4_, ...), custom_call_target="tpu_custom_call" | custom-call | flops 20999999488 | bytes 42000000 | tf_op jit(solution)/shard_map/pallas_call | solution.py:106
  107.9 12.5 %collective-permute-done.8.refs_2_.refs_6_ = bf16[256,1024]{1,0:T(8,128)(2,1)S(1)} collective-permute-done((bf16[256,1024]{1,0:T(8,128)(2,1)S(1)}, bf16[256,1024]{1,0:T(8,128)(2,1)S(1)}, u32[]{:S(2)}, u32[]{:S(2)}) %collective-permute-start.8) | collective-permute-done | bytes 524320 | tf_op jit(solution)/shard_map/ppermute | solution.py:41
  124.0 6.9 %all-gather.9.cloned.1.call-done.refs_2_.refs_13_.refs_17_.refs_7_ = bf16[1024,1024]{1,0:T(8,128)(2,1)} async-done(((bf16[128,1024]{1,0:T(8,128)(2,1)}), bf16[1024,1024]{1,0:T(8,128)(2,1)}) %all-gather.9.cloned.1.call-update) | async-done | bytes 2097168 | tf_op jit(solution)/shard_map/all_gather | solution.py:999
  139.1 10.3 %collective-permute-done.14.refs_12_.refs_16_ = bf16[512,512]{1,0:T(8,128)(2,1)S(1)} collective-permute-done((bf16[512,512]{1,0:T(8,128)(2,1)}, bf16[512,512]{1,0:T(8,128)(2,1)S(1)}, u32[]{:S(2)}, u32[]{:S(2)}) %collective-permute-start.14) | collective-permute-done | bytes 524320 | tf_op jit(solution)/shard_map/ppermute | solution.py:37
  151.4 10.1 %collective-permute-done.15.refs_11_.refs_15_ = bf16[512,512]{1,0:T(8,128)(2,1)S(1)} collective-permute-done((bf16[512,512]{1,0:T(8,128)(2,1)S(1)}, bf16[512,512]{1,0:T(8,128)(2,1)S(1)}, u32[]{:S(2)}, u32[]{:S(2)}) %collective-permute-start.15) | collective-permute-done | bytes 524320 | tf_op jit(solution)/shard_map/ppermute | solution.py:37
  186.7 10.0 %shard_map.166 = (bf16[512,256]{1,0:T(8,128)(2,1)}, f32[8,512]{1,0:T(8,128)}, bf16[256,1024]{1,0:T(8,128)(2,1)}, f32[256,1024]{1,0:T(8,128)}) custom-call(s32[4]{0:T(128)} %bitcast.22, s32[8]{0:T(128)} %gather_fusion.1, s32[3]{0:T(128)} %pad_add_fusion.refs_0_.refs_2_, bf16[512,256]{1,0:T(8,128)(2,1)} %get-tuple-element.95.refs_3_, ...), custom_call_target="tpu_custom_call" | custom-call | flops 32999999488 | bytes 66000000 | tf_op jit(solution)/shard_map/pallas_call | solution.py:106
  201.3 13.0 %collective-permute-done.19.refs_2_.refs_5_ = bf16[256,1024]{1,0:T(8,128)(2,1)S(1)} collective-permute-done((bf16[256,1024]{1,0:T(8,128)(2,1)S(1)}, bf16[256,1024]{1,0:T(8,128)(2,1)S(1)}, u32[]{:S(2)}, u32[]{:S(2)}) %collective-permute-start.19) | collective-permute-done | bytes 524320 | tf_op jit(solution)/shard_map/ppermute | solution.py:41
  222.3 10.3 %shard_map.170 = (bf16[512,1024]{1,0:T(8,128)(2,1)}, bf16[512,1024]{1,0:T(8,128)(2,1)}, bf16[256,1024]{1,0:T(8,128)(2,1)}, f32[256,1024]{1,0:T(8,128)}, bf16[256,1024]{1,0:T(8,128)(2,1)}, /*index=5*/f32[256,1024]{1,0:T(8,128)}) custom-call(bf16[256,1024]{1,0:T(8,128)(2,1)} %get-tuple-element.100.refs_0_, bf16[256,1024]{1,0:T(8,128)(2,1)} %copy-done.41, ...), custom_call_target="tpu_custom_call" | custom-call | flops 30000001024 | bytes 60000000 | tf_op jit(solution)/shard_map/pallas_call | solution.py:106
  258.3 17.6 %shard_map.176 = (f32[512,256]{1,0:T(8,128)}, bf16[512,512]{1,0:T(8,128)(2,1)}, bf16[512,512]{1,0:T(8,128)(2,1)}, bf16[512,512]{1,0:T(8,128)(2,1)}, bf16[512,512...) custom-call(s32[4]{0:T(128)} %bitcast.23, ...), custom_call_target="tpu_custom_call" | custom-call | flops 8999999488 | bytes 18000000 | tf_op jit(solution)/shard_map/pallas_call | solution.py:106
  288.7 10.6 %collective-permute-done.31 = bf16[512,512]{1,0:T(8,128)(2,1)S(1)} collective-permute-done((bf16[512,512]{1,0:T(8,128)(2,1)S(1)}, bf16[512,512]{1,0:T(8,128)(2,1)S(1)}, u32[]{:S(2)}, u32[]{:S(2)}) %collective-permute-start.31) | collective-permute-done | bytes 524320 | tf_op jit(solution)/shard_map/ppermute | solution.py:37
  329.0 7.5 %shard_map.177 = (bf16[512,768]{1,0:T(8,128)(2,1)}, bf16[256,1024]{1,0:T(8,128)(2,1)}, f32[256,1024]{1,0:T(8,128)}, f32[2,256]{1,0:T(2,128)}, f32[1,1024]{1,0:T(1,128)}) custom-call(f32[512,256]{1,0:T(8,128)} %get-tuple-element.112.refs_0_, f32[512,512]{1,0:T(8,128)} %convert_add_fusion.refs_1_, f32[512,512]{1,0:T(8,128)} %get-tuple-element.122.refs_2_, ...), custom_call_target="tpu_custom_call" | custom-call | flops 17999998976 | bytes 36000000 | tf_op jit(solution)/shard_map/pallas_call | solution.py:106
  346.8 7.3 %collective-permute-done.35.refs_2_ = bf16[256,1024]{1,0:T(8,128)(2,1)S(1)} collective-permute-done((bf16[256,1024]{1,0:T(8,128)(2,1)S(1)}, bf16[256,1024]{1,0:T(8,128)(2,1)S(1)}, u32[]{:S(2)}, u32[]{:S(2)}) %collective-permute-start.35) | collective-permute-done | bytes 524320 | tf_op jit(solution)/shard_map/ppermute | solution.py:41
  362.1 7.7 %shard_map.182 = (bf16[512,1024]{1,0:T(8,128)(2,1)}, bf16[256,1024]{1,0:T(8,128)(2,1)}, f32[256,1024]{1,0:T(8,128)}) custom-call(bf16[256,1024]{1,0:T(8,128)(2,1)} %get-tuple-element.127.refs_0_.refs_2_, bf16[256,1024]{1,0:T(8,128)(2,1)} %copy-done.42, f32[512,1024]{1,0:T(8,128)} %get-tuple-element.128.refs_2_, ...), custom_call_target="tpu_custom_call" | custom-call | flops 8999999488 | bytes 18000000 | tf_op jit(solution)/shard_map/pallas_call | solution.py:106
  374.2 8.7 %shard_map.183.refs_0_ = bf16[1024,2048]{1,0:T(8,128)(2,1)} custom-call(bf16[256,1024]{1,0:T(8,128)(2,1)} %get-tuple-element.90.refs_0_, bf16[256,1024]{1,0:T(8,128)(2,1)} %copy-done.27, bf16[256,1024]{1,0:T(8,128)(2,1)} %get-tuple-element.127.refs_0_.refs_2_, bf16[256,1024]{1,0:T(8,128)(2,1)} %copy-done.42, bf16[512,1024]{1,0:T(8,128)(2,1)} %get-tuple-element.131.refs_4_, ...), custom_call_target="tpu_custom_call" | custom-call | flops 8999999488 | bytes 18000000 | tf_op jit(solution)/shard_map/pallas_call | solution.py:106
  397.4 7.5 %shard_map.187 = (f32[512,256]{1,0:T(8,128)}, f32[1,512,512]{2,1,0:T(8,128)}) custom-call(s32[1]{0:T(128)} %constant.50.clone.1.refs_0_, s32[1]{0:T(128)} %dynamic_slice.13.refs_1_, s32[3]{0:T(128)} %pad_add_fusion.refs_0_.refs_2_, bf16[512,256]{1,0:T(8,128)(2,1)} %get-tuple-element.85.refs_3_, bf16[512,256]{1,0:T(8,128)(2,1)} %get-tuple-element.135.refs_4_.refs_5_, ...), custom_call_target="tpu_custom_call" | custom-call | flops 4499999744 | bytes 9000000 | tf_op jit(solution)/shard_map/pallas_call | solution.py:106
  404.9 7.6 %shard_map.188 = (bf16[512,768]{1,0:T(8,128)(2,1)}, bf16[256,1024]{1,0:T(8,128)(2,1)}, f32[256,1024]{1,0:T(8,128)}, f32[2,256]{1,0:T(2,128)}, f32[1,1024]{1,0:T(1,128)}) custom-call(f32[512,256]{1,0:T(8,128)} %get-tuple-element.138.refs_0_, f32[512,512]{1,0:T(8,128)} %bitcast.19, f32[512,512]{1,0:T(8,128)} %get-tuple-element.140.refs_2_, ...), custom_call_target="tpu_custom_call" | custom-call | flops 17999998976 | bytes 36000000 | tf_op jit(solution)/shard_map/pallas_call | solution.py:106
  423.2 7.0 %collective-permute-done.41.refs_3_.refs_2_ = bf16[256,1024]{1,0:T(8,128)(2,1)S(1)} collective-permute-done((bf16[256,1024]{1,0:T(8,128)(2,1)S(1)}, bf16[256,1024]{1,0:T(8,128)(2,1)S(1)}, u32[]{:S(2)}, u32[]{:S(2)}) %collective-permute-start.41) | collective-permute-done | bytes 524320 | tf_op jit(solution)/shard_map/ppermute | solution.py:41
  430.2 7.5 %reduce-scatter.12.cloned.1.call-done.refs_1_.refs_0_ = bf16[128,2048]{1,0:T(8,128)(2,1)} async-done(((bf16[1024,2048]{1,0:T(8,128)(2,1)}), bf16[128,2048]{1,0:T(8,128)(2,1)}) %reduce-scatter.12.cloned.1.call-update) | async-done | bytes 524304 | tf_op jit(solution)/shard_map/reduce_scatter | solution.py:1002
  443.8 12.3 %all_to_all.10 = f32[8,16,128]{2,1,0:T(8,128)S(1)} all-to-all(f32[8,16,128]{2,1,0:T(8,128)} %shard_map.195), channel_id=1, replica_groups=mesh['frame'=8,'row'=4] {'frame'}, dimensions={0} | all-to-all | bytes 131072 | tf_op jit(solution)/shard_map/all_to_all | solution.py:1240
  463.7 10.1 %reduce-scatter.14.cloned.1.call-done.refs_0_ = bf16[128,1024]{1,0:T(8,128)(2,1)} async-done(((bf16[1024,1024]{1,0:T(8,128)(2,1)}), bf16[128,1024]{1,0:T(8,128)(2,1)}) %reduce-scatter.14.cloned.1.call-update) | async-done | bytes 262160 | tf_op jit(solution)/shard_map/reduce_scatter | solution.py:1002
  (289 shorter events, 238.2 us)
Async XLA Ops:
  7.2 42.4 %all-gather.5.cloned.1.call-start = ((), (), s32[]{:S(2)}) async-start(), calls=%async_computation.7 | async-start | bytes 2359296 | tf_op jit(solution)/shard_map/all_gather | solution.py:999
  9.9 15.0 %all-to-all-start = ((f32[8,16,128]{2,1,0:T(8,128)}), f32[8,16,128]{2,1,0:T(8,128)S(1)}, u32[]{:S(2)}, u32[]{:S(2)}) async-start(f32[8,16,128]{2,1,0:T(8,128)} %broadcast_in_dim.14), calls=%async_computation | async-start | bytes 131072 | tf_op jit(solution)/shard_map/all_to_all | solution.py:1011
  17.1 78.3 %all-gather.7.cloned.1.call-start = ((), (), s32[]{:S(2)}) async-start(), calls=%async_computation.8 | async-start | bytes 4718592 | tf_op jit(solution)/shard_map/all_gather | solution.py:999
  17.2 19.1 %collective-permute-start = (bf16[128,1024]{1,0:T(8,128)(2,1)S(1)}, bf16[128,1024]{1,0:T(8,128)(2,1)S(1)}, u32[]{:S(2)}, u32[]{:S(2)}) collective-permute-start(bf16[128,1024]{1,0:T(8,128)(2,1)S(1)} %copy-done.45), channel_id=1, source_target_pairs={{2,0},{3,1},{0,2},{1,3},{6,4},{7,5},{4,6},{5,7},{10,8},{11,9},{8,1... | collective-permute-start | bytes 786440 | tf_op jit(solution)/shard_map/ppermute | solution.py:41
  21.3 109.7 %all-gather.9.cloned.1.call-start = ((), (), s32[]{:S(2)}) async-start(), calls=%async_computation.9 | async-start | bytes 2359296 | tf_op jit(solution)/shard_map/all_gather | solution.py:999
  36.3 13.2 %collective-permute-start.3 = (bf16[256,1024]{1,0:T(8,128)(2,1)}, bf16[256,1024]{1,0:T(8,128)(2,1)S(1)}, u32[]{:S(2)}, u32[]{:S(2)}) collective-permute-start(bf16[256,1024]{1,0:T(8,128)(2,1)} %shard_map.157.refs_4_.refs_2_.refs_0_), channel_id=1, source_target_pairs={{1,0},{0,1},{3,2},{2,3},{5,4},{4,5},{7,6},{6,7},{9,8},{8,9},{11,10... | collective-permute-start | bytes 1572872 | tf_op jit(solution)/shard_map/ppermute | solution.py:41
  65.6 14.1 %collective-permute-start.5 = (bf16[256,1024]{1,0:T(8,128)(2,1)S(1)}, bf16[256,1024]{1,0:T(8,128)(2,1)S(1)}, u32[]{:S(2)}, u32[]{:S(2)}) collective-permute-start(bf16[256,1024]{1,0:T(8,128)(2,1)S(1)} %add_convert_fusion.10.refs_1_.refs_4_), channel_id=1, source_target_pairs={{2,0},{3,1},{0,2},{1,3},{6,4},{7,5},{4,6},{5,7},{10,8},{11,9},{8,1... | collective-permute-start | bytes 1572872 | tf_op jit(solution)/shard_map/ppermute | solution.py:41
  85.1 137.2 %all-gather.11.cloned.1.call-start = ((), (), s32[]{:S(2)}) async-start(), calls=%async_computation.10 | async-start | bytes 4718592 | tf_op jit(solution)/shard_map/all_gather | solution.py:999
  106.3 14.0 %collective-permute-start.8 = (bf16[256,1024]{1,0:T(8,128)(2,1)S(1)}, bf16[256,1024]{1,0:T(8,128)(2,1)S(1)}, u32[]{:S(2)}, u32[]{:S(2)}) collective-permute-start(bf16[256,1024]{1,0:T(8,128)(2,1)S(1)} %add_convert_fusion.9.refs_1_.refs_5_), channel_id=1, source_target_pairs={{2,0},{3,1},{0,2},{1,3},{6,4},{7,5},{4,6},{5,7},{10,8},{11,9},{8,1... | collective-permute-start | bytes 1572872 | tf_op jit(solution)/shard_map/ppermute | solution.py:41
  172.9 141.3 %reduce-scatter.6.cloned.1.call-start = ((), (), s32[]{:S(2)}) async-start(), calls=%async_computation.11 | async-start | bytes 2359296 | tf_op jit(solution)/shard_map/reduce_scatter | solution.py:1002
  200.3 14.0 %collective-permute-start.19 = (bf16[256,1024]{1,0:T(8,128)(2,1)S(1)}, bf16[256,1024]{1,0:T(8,128)(2,1)S(1)}, u32[]{:S(2)}, u32[]{:S(2)}) collective-permute-start(bf16[256,1024]{1,0:T(8,128)(2,1)S(1)} %add_convert_fusion.8.refs_1_.refs_4_), channel_id=1, source_target_pairs={{2,0},{3,1},{0,2},{1,3},{6,4},{7,5},{4,6},{5,7},{10,8},{11,9},{8,1... | collective-permute-start | bytes 1572872 | tf_op jit(solution)/shard_map/ppermute | solution.py:41
  236.2 14.0 %collective-permute-start.23 = (bf16[256,1024]{1,0:T(8,128)(2,1)S(1)}, bf16[256,1024]{1,0:T(8,128)(2,1)S(1)}, u32[]{:S(2)}, u32[]{:S(2)}) collective-permute-start(bf16[256,1024]{1,0:T(8,128)(2,1)S(1)} %add_convert_fusion.7.refs_3_.refs_1_), channel_id=1, source_target_pairs={{2,0},{3,1},{0,2},{1,3},{6,4},{7,5},{4,6},{5,7},{10,8},{11,9},{8,1... | collective-permute-start | bytes 1572872 | tf_op jit(solution)/shard_map/ppermute | solution.py:41
  242.9 111.2 %reduce-scatter.8.cloned.1.call-start = ((), (), s32[]{:S(2)}) async-start(), calls=%async_computation.12 | async-start | bytes 2359296 | tf_op jit(solution)/shard_map/reduce_scatter | solution.py:1002
  285.7 13.6 %collective-permute-start.31 = (bf16[512,512]{1,0:T(8,128)(2,1)S(1)}, bf16[512,512]{1,0:T(8,128)(2,1)S(1)}, u32[]{:S(2)}, u32[]{:S(2)}) collective-permute-start(bf16[512,512]{1,0:T(8,128)(2,1)S(1)} %pad_maximum_fusion.1), channel_id=1, source_target_pairs={{8,0},{16,8},{24,16},{28,24},{20,28},{12,20},{4,12},{0,4},{9,1},{1... | collective-permute-start | bytes 1572872 | tf_op jit(solution)/shard_map/ppermute | solution.py:37
  287.6 12.9 %collective-permute-start.27 = (bf16[512,512]{1,0:T(8,128)(2,1)S(1)}, bf16[512,512]{1,0:T(8,128)(2,1)S(1)}, u32[]{:S(2)}, u32[]{:S(2)}) collective-permute-start(bf16[512,512]{1,0:T(8,128)(2,1)S(1)} %pad_maximum_fusion), channel_id=1, source_target_pairs={{4,0},{0,8},{8,16},{16,24},{24,28},{28,20},{20,12},{12,4},{5,1},{1... | collective-permute-start | bytes 1572872 | tf_op jit(solution)/shard_map/ppermute | solution.py:37
  288.7 13.2 %collective-permute-start.21 = (bf16[256,1024]{1,0:T(8,128)(2,1)S(1)}, bf16[256,1024]{1,0:T(8,128)(2,1)S(1)}, u32[]{:S(2)}, u32[]{:S(2)}) collective-permute-start(bf16[256,1024]{1,0:T(8,128)(2,1)S(1)} %copy-done.36), channel_id=1, source_target_pairs={{1,0},{0,1},{3,2},{2,3},{5,4},{4,5},{7,6},{6,7},{9,8},{8,9},{11,10... | collective-permute-start | bytes 1572872 | tf_op jit(solution)/shard_map/ppermute | solution.py:41
  312.0 13.3 %collective-permute-start.33 = (bf16[512,512]{1,0:T(8,128)(2,1)S(1)}, bf16[512,512]{1,0:T(8,128)(2,1)S(1)}, u32[]{:S(2)}, u32[]{:S(2)}) collective-permute-start(bf16[512,512]{1,0:T(8,128)(2,1)S(1)} %add_convert_fusion.3.refs_2_), channel_id=1, source_target_pairs={{8,0},{16,8},{24,16},{28,24},{20,28},{12,20},{4,12},{0,4},{9,1},{1... | collective-permute-start | bytes 1572872 | tf_op jit(solution)/shard_map/ppermute | solution.py:37
  313.0 14.8 %collective-permute-start.29 = (bf16[512,512]{1,0:T(8,128)(2,1)S(1)}, bf16[512,512]{1,0:T(8,128)(2,1)S(1)}, u32[]{:S(2)}, u32[]{:S(2)}) collective-permute-start(bf16[512,512]{1,0:T(8,128)(2,1)S(1)} %add_convert_fusion.5.refs_1_), channel_id=1, source_target_pairs={{4,0},{0,8},{8,16},{16,24},{24,28},{28,20},{20,12},{12,4},{5,1},{1... | collective-permute-start | bytes 1572872 | tf_op jit(solution)/shard_map/ppermute | solution.py:37
  314.3 73.6 %reduce-scatter.10.cloned.1.call-start = ((), (), s32[]{:S(2)}) async-start(), calls=%async_computation.13 | async-start | bytes 2359296 | tf_op jit(solution)/shard_map/reduce_scatter | solution.py:1002
  340.1 14.0 %collective-permute-start.35 = (bf16[256,1024]{1,0:T(8,128)(2,1)S(1)}, bf16[256,1024]{1,0:T(8,128)(2,1)S(1)}, u32[]{:S(2)}, u32[]{:S(2)}) collective-permute-start(bf16[256,1024]{1,0:T(8,128)(2,1)S(1)} %add_convert_fusion.2.refs_6_.refs_1_), channel_id=1, source_target_pairs={{2,0},{3,1},{0,2},{1,3},{6,4},{7,5},{4,6},{5,7},{10,8},{11,9},{8,1... | collective-permute-start | bytes 1572872 | tf_op jit(solution)/shard_map/ppermute | solution.py:41
  354.9 82.8 %reduce-scatter.12.cloned.1.call-start = ((), (), s32[]{:S(2)}) async-start(), calls=%async_computation.14 | async-start | bytes 4718592 | tf_op jit(solution)/shard_map/reduce_scatter | solution.py:1002
  373.2 14.0 %collective-permute-start.38 = (bf16[256,1024]{1,0:T(8,128)(2,1)S(1)}, bf16[256,1024]{1,0:T(8,128)(2,1)S(1)}, u32[]{:S(2)}, u32[]{:S(2)}) collective-permute-start(bf16[256,1024]{1,0:T(8,128)(2,1)S(1)} %add_convert_fusion.1.refs_6_.refs_1_), channel_id=1, source_target_pairs={{2,0},{3,1},{0,2},{1,3},{6,4},{7,5},{4,6},{5,7},{10,8},{11,9},{8,1... | collective-permute-start | bytes 1572872 | tf_op jit(solution)/shard_map/ppermute | solution.py:41
  388.1 85.7 %reduce-scatter.14.cloned.1.call-start = ((), (), s32[]{:S(2)}) async-start(), calls=%async_computation.15 | async-start | bytes 2359296 | tf_op jit(solution)/shard_map/reduce_scatter | solution.py:1002
  416.1 14.1 %collective-permute-start.41 = (bf16[256,1024]{1,0:T(8,128)(2,1)S(1)}, bf16[256,1024]{1,0:T(8,128)(2,1)S(1)}, u32[]{:S(2)}, u32[]{:S(2)}) collective-permute-start(bf16[256,1024]{1,0:T(8,128)(2,1)S(1)} %add_convert_fusion.refs_2_.refs_6_), channel_id=1, source_target_pairs={{2,0},{3,1},{0,2},{1,3},{6,4},{7,5},{4,6},{5,7},{10,8},{11,9},{8,1... | collective-permute-start | bytes 1572872 | tf_op jit(solution)/shard_map/ppermute | solution.py:41
  (81 other events, 463.8 us)
Sparse Core Ops, SparseCore 0:
  10.1 36.6 all-gather.4
  48.3 46.9 all-gather.6
  97.5 33.3 all-gather.8
  173.1 49.2 all-gather.10
  243.0 32.6 reduce-scatter.5
  314.4 34.4 reduce-scatter.7
  355.0 32.7 reduce-scatter.9
  390.2 47.5 reduce-scatter.11
  440.0 33.7 reduce-scatter.13

commit v7 on v6

--- a/solution.py
+++ b/solution.py
@@ -239,6 +239,10 @@
     normed_ref[...] = (unit * gains_ref[row : row + 1, :]).astype(BF16)
 
 
+def add_up(ref, value):
+    ref[...] = jnp.where(pl.program_id(0) == 0, value, ref[...] + value)
+
+
 def total_of(own_ref, far_ref):
     return own_ref[...].astype(F32) + far_ref[...].astype(F32)
 
@@ -270,10 +274,11 @@
 ):
     grad_in = total_of(own_ref, far_ref)
     unit, scale = norm_parts(middle_ref[...])
-    sums_ref[0:1, :] = jnp.sum(grad_in * unit, axis=0, keepdims=True)
+    first = jnp.sum(grad_in * unit, axis=0, keepdims=True)
     grad = grad_ref[...] + norm_back(unit, scale, gains_ref[base + 1 : base + 2, :], grad_in)
     next_ref[...] = grad
-    sums_ref[1:2, :] = jnp.sum(grad * total_of(b_own_ref, b_far_ref), axis=0, keepdims=True)
+    second = jnp.sum(grad * total_of(b_own_ref, b_far_ref), axis=0, keepdims=True)
+    add_up(sums_ref, jnp.concatenate([first, second], axis=0))
     scaled_ref[...] = (grad * gains_ref[base + 2 : base + 3, :]).astype(BF16)
 
 
@@ -288,7 +293,7 @@
     grad = first_back(base, grad_ref, own_ref, far_ref, h_ref, gains_ref)
     next_ref[...] = grad
     scaled_ref[...] = (grad * gains_ref[base - 3 : base - 2, :]).astype(BF16)
-    sums_ref[...] = jnp.sum(grad * total_of(d_own_ref, d_far_ref), axis=0, keepdims=True)
+    add_up(sums_ref, jnp.sum(grad * total_of(d_own_ref, d_far_ref), axis=0, keepdims=True))
 
 
 def last_back_kernel(order, facts_ref, grad_ref, own_ref, far_ref, h_ref, gains_ref, out_ref, held):
@@ -957,6 +962,7 @@
         )
 
     big = whole((half, wide))
+    part = pl.BlockSpec((half // 2, wide), lambda j, *_: (j, 0))
 
     qkv_shard = jnp.transpose(qkv_weight, (0, 2, 1, 3))
     if ring:
@@ -1065,9 +1071,9 @@
         branch = reduce_rows(part_other, part_own)
         middle, second = run(
             functools.partial(residual_kernel, base + 2, base + 1),
-            (1,),
-            [big, big, big, gspec],
-            [big, big],
+            (2,),
+            [part, part, part, gspec],
+            [part, part],
             [shaped(half, wide), shaped(half, wide, dtype=BF16)],
             [],
             [h, *branch, gains],
@@ -1088,9 +1094,9 @@
             down_zero = reduce_rows(part_other, part_own)
             h, normed = run(
                 functools.partial(residual_kernel, base + 3, base + 6),
-                (1,),
-                [big, big, big, gspec],
-                [big, big],
+                (2,),
+                [part, part, part, gspec],
+                [part, part],
                 [shaped(half, wide), shaped(half, wide, dtype=BF16)],
                 [],
                 [middle, *down_zero, gains],
@@ -1125,9 +1131,9 @@
                 ff_out = finish(finish_ff_kernel, [ff_sum], ff_shapes, block, ff_out)
         grad_middle, scaled, sums_middle = run(
             functools.partial(middle_back_kernel, base),
-            (1,),
-            [big] * 6 + [gspec],
-            [big, big, whole((2, wide))],
+            (2,),
+            [part] * 6 + [gspec],
+            [part, part, whole((2, wide))],
             [shaped(half, wide), shaped(half, wide, dtype=BF16), shaped(2, wide)],
             [],
             [grad, *incoming, middle, *branch, gains],
@@ -1187,9 +1193,9 @@
         if block == 1:
             grad, scaled, sum_three = run(
                 functools.partial(between_kernel, base),
-                (1,),
-                [big] * 4 + [gspec, big, big],
-                [big, big, whole((1, wide))],
+                (2,),
+                [part] * 4 + [gspec, part, part],
+                [part, part, whole((1, wide))],
                 [shaped(half, wide), shaped(half, wide, dtype=BF16), shaped(1, wide)],
                 [],
                 [grad_middle, *incoming, h, gains, *down_zero],

time: 492 us -> 491 us (level)
  transfers between devices with their start and end apart: 54 -> 54, of which waited for: 43 -> 42; matrix products, arithmetic and copies ran while one was open for 5% -> 5% of each run, Pallas kernels for 34% -> 33%
where the time goes in v7:
time: 491 us; the launch traced here: 482 us
  waiting for transfers between devices  189 us (38%)
  Pallas kernels  180 us (37%)
  starting transfers between devices  43.7 us (9%)
  local copies, waits for them, and re-layouts  23 us (5%)
  between operations  16.8 us (3%)
  other arithmetic  16.1 us (3%)
  blocking collectives  12.4 us (3%)
    pallas_call x43, Pallas kernels, run(): pl.pallas_call(body, grid_spec=pltpu.PrefetchScalarGridSpec(num_scalar_pr...  180 us
    ppermute x28, waiting for transfers between devices, row_take(): return lax.ppermute(value, 'row', [(i ^ bit, i) for i in range(4)])  87.9 us
    ppermute x16, waiting for transfers between devices, ring_take(): lax.ppermute(value, 'frame', [(RING[(i + step) % count], RING[i]) for i i...  64.7 us
    ppermute x28, starting transfers between devices, row_take(): return lax.ppermute(value, 'row', [(i ^ bit, i) for i in range(4)])  18.7 us
    all_gather x4, waiting for transfers between devices, gather(): lax.all_gather(packed, 'frame', axis=0, tiled=True, axis_index_groups=fra...  18.4 us
    ppermute x16, starting transfers between devices, ring_take(): lax.ppermute(value, 'frame', [(RING[(i + step) % count], RING[i]) for i i...  17.1 us
    reduce_scatter x5, waiting for transfers between devices, scatter(): lax.psum_scatter(grads, 'frame', scatter_dimension=0, tiled=True, axis_in...  16.2 us
    unnamed x108, local copies, waits for them, and re-layouts  14.7 us
  transfers between devices with their start and end apart: 54, of which 42 were waited for; matrix products, arithmetic and copies ran while one was open for 5% of the time, Pallas kernels for 33%

profile of v7, /device:TPU:0, one launch (start us, length us, event | category | flops | bytes accessed | tf_op | source)
XLA Modules:
  0.0 481.7 jit_solution(1474997672075199082)
XLA Ops:
  9.9 7.3 %all-to-all-start = ((f32[8,16,128]{2,1,0:T(8,128)}), f32[8,16,128]{2,1,0:T(8,128)S(1)}, u32[]{:S(2)}, u32[]{:S(2)}) async-start(f32[8,16,128]{2,1,0:T(8,128)} %broadcast_in_dim.14), calls=%async_computation | async-start | bytes 131072 | tf_op jit(solution)/shard_map/all_to_all | solution.py:1017
  55.8 6.2 %shard_map.159 = (bf16[512,256]{1,0:T(8,128)(2,1)}, f32[8,512]{1,0:T(8,128)}, bf16[256,1024]{1,0:T(8,128)(2,1)}, f32[256,1024]{1,0:T(8,128)}) custom-call(s32[1]{0:T(128)} %constant.50.clone.1.refs_0_, s32[1]{0:T(128)} %dynamic_slice.13.refs_1_, s32[3]{0:T(128)} %pad_add_fusion.refs_0_.refs_2_, bf16[512,256]{1,0:T(8,128)(2,1)} %get-tuple-element.85.refs_3_, ...), custom_call_target="tpu_custom_call" | custom-call | flops 15000000512 | bytes 30000000 | tf_op jit(solution)/shard_map/pallas_call | solution.py:106
  67.2 12.4 %collective-permute-done.5.refs_2_.refs_5_ = bf16[256,1024]{1,0:T(8,128)(2,1)S(1)} collective-permute-done((bf16[256,1024]{1,0:T(8,128)(2,1)S(1)}, bf16[256,1024]{1,0:T(8,128)(2,1)S(1)}, u32[]{:S(2)}, u32[]{:S(2)}) %collective-permute-start.5) | collective-permute-done | bytes 524320 | tf_op jit(solution)/shard_map/ppermute | solution.py:41
  85.3 10.1 %all-gather.7.cloned.1.call-done.refs_2_.refs_3_.refs_4_ = bf16[1024,2048]{1,0:T(8,128)(2,1)} async-done(((bf16[128,2048]{1,0:T(8,128)(2,1)}), bf16[1024,2048]{1,0:T(8,128)(2,1)}) %all-gather.7.cloned.1.call-update) | async-done | bytes 4194320 | tf_op jit(solution)/shard_map/all_gather | solution.py:1005
  95.4 7.3 %shard_map.162 = (f32[512,1024]{1,0:T(8,128)}, bf16[512,1024]{1,0:T(8,128)(2,1)}, bf16[256,1024]{1,0:T(8,128)(2,1)}, f32[256,1024]{1,0:T(8,128)}) custom-call(bf16[256,1024]{1,0:T(8,128)(2,1)} %get-tuple-element.90.refs_0_, bf16[256,1024]{1,0:T(8,128)(2,1)} %copy-done.27, bf16[1024,2048]{1,0:T(8,128)(2,1)} %all-gather.7.cloned.1.call-done.refs_2_.refs_3_.refs_4_, ...), custom_call_target="tpu_custom_call" | custom-call | flops 20999999488 | bytes 42000000 | tf_op jit(solution)/shard_map/pallas_call | solution.py:106
  107.9 12.5 %collective-permute-done.8.refs_2_.refs_6_ = bf16[256,1024]{1,0:T(8,128)(2,1)S(1)} collective-permute-done((bf16[256,1024]{1,0:T(8,128)(2,1)S(1)}, bf16[256,1024]{1,0:T(8,128)(2,1)S(1)}, u32[]{:S(2)}, u32[]{:S(2)}) %collective-permute-start.8) | collective-permute-done | bytes 524320 | tf_op jit(solution)/shard_map/ppermute | solution.py:41
  123.9 7.1 %all-gather.9.cloned.1.call-done.refs_2_.refs_13_.refs_17_.refs_7_ = bf16[1024,1024]{1,0:T(8,128)(2,1)} async-done(((bf16[128,1024]{1,0:T(8,128)(2,1)}), bf16[1024,1024]{1,0:T(8,128)(2,1)}) %all-gather.9.cloned.1.call-update) | async-done | bytes 2097168 | tf_op jit(solution)/shard_map/all_gather | solution.py:1005
  139.1 10.3 %collective-permute-done.14.refs_12_.refs_16_ = bf16[512,512]{1,0:T(8,128)(2,1)S(1)} collective-permute-done((bf16[512,512]{1,0:T(8,128)(2,1)}, bf16[512,512]{1,0:T(8,128)(2,1)S(1)}, u32[]{:S(2)}, u32[]{:S(2)}) %collective-permute-start.14) | collective-permute-done | bytes 524320 | tf_op jit(solution)/shard_map/ppermute | solution.py:37
  151.4 10.1 %collective-permute-done.15.refs_11_.refs_15_ = bf16[512,512]{1,0:T(8,128)(2,1)S(1)} collective-permute-done((bf16[512,512]{1,0:T(8,128)(2,1)S(1)}, bf16[512,512]{1,0:T(8,128)(2,1)S(1)}, u32[]{:S(2)}, u32[]{:S(2)}) %collective-permute-start.15) | collective-permute-done | bytes 524320 | tf_op jit(solution)/shard_map/ppermute | solution.py:37
  180.9 6.2 %collective-permute-done.13.refs_8_.refs_12_ = bf16[256,512]{1,0:T(8,128)(2,1)S(1)} collective-permute-done((bf16[256,512]{1,0:T(8,128)(2,1)S(1)}, bf16[256,512]{1,0:T(8,128)(2,1)S(1)}, u32[]{:S(2)}, u32[]{:S(2)}) %collective-permute-start.13) | collective-permute-done | bytes 262176 | tf_op jit(solution)/shard_map/ppermute | solution.py:37
  187.8 10.0 %shard_map.166 = (bf16[512,256]{1,0:T(8,128)(2,1)}, f32[8,512]{1,0:T(8,128)}, bf16[256,1024]{1,0:T(8,128)(2,1)}, f32[256,1024]{1,0:T(8,128)}) custom-call(s32[4]{0:T(128)} %bitcast.22, s32[8]{0:T(128)} %gather_fusion.1, s32[3]{0:T(128)} %pad_add_fusion.refs_0_.refs_2_, bf16[512,256]{1,0:T(8,128)(2,1)} %get-tuple-element.95.refs_3_, ...), custom_call_target="tpu_custom_call" | custom-call | flops 32999999488 | bytes 66000000 | tf_op jit(solution)/shard_map/pallas_call | solution.py:106
  203.2 12.2 %collective-permute-done.19.refs_2_.refs_5_ = bf16[256,1024]{1,0:T(8,128)(2,1)S(1)} collective-permute-done((bf16[256,1024]{1,0:T(8,128)(2,1)S(1)}, bf16[256,1024]{1,0:T(8,128)(2,1)S(1)}, u32[]{:S(2)}, u32[]{:S(2)}) %collective-permute-start.19) | collective-permute-done | bytes 524320 | tf_op jit(solution)/shard_map/ppermute | solution.py:41
  222.3 10.3 %shard_map.170 = (bf16[512,1024]{1,0:T(8,128)(2,1)}, bf16[512,1024]{1,0:T(8,128)(2,1)}, bf16[256,1024]{1,0:T(8,128)(2,1)}, f32[256,1024]{1,0:T(8,128)}, bf16[256,1024]{1,0:T(8,128)(2,1)}, /*index=5*/f32[256,1024]{1,0:T(8,128)}) custom-call(bf16[256,1024]{1,0:T(8,128)(2,1)} %get-tuple-element.100.refs_0_, bf16[256,1024]{1,0:T(8,128)(2,1)} %copy-done.41, ...), custom_call_target="tpu_custom_call" | custom-call | flops 30000001024 | bytes 60000000 | tf_op jit(solution)/shard_map/pallas_call | solution.py:106
  258.0 17.6 %shard_map.176 = (f32[512,256]{1,0:T(8,128)}, bf16[512,512]{1,0:T(8,128)(2,1)}, bf16[512,512]{1,0:T(8,128)(2,1)}, bf16[512,512]{1,0:T(8,128)(2,1)}, bf16[512,512...) custom-call(s32[4]{0:T(128)} %bitcast.23, ...), custom_call_target="tpu_custom_call" | custom-call | flops 8999999488 | bytes 18000000 | tf_op jit(solution)/shard_map/pallas_call | solution.py:106
  288.2 10.3 %collective-permute-done.31 = bf16[512,512]{1,0:T(8,128)(2,1)S(1)} collective-permute-done((bf16[512,512]{1,0:T(8,128)(2,1)S(1)}, bf16[512,512]{1,0:T(8,128)(2,1)S(1)}, u32[]{:S(2)}, u32[]{:S(2)}) %collective-permute-start.31) | collective-permute-done | bytes 524320 | tf_op jit(solution)/shard_map/ppermute | solution.py:37
  329.8 7.5 %shard_map.177 = (bf16[512,768]{1,0:T(8,128)(2,1)}, bf16[256,1024]{1,0:T(8,128)(2,1)}, f32[256,1024]{1,0:T(8,128)}, f32[2,256]{1,0:T(2,128)}, f32[1,1024]{1,0:T(1,128)}) custom-call(f32[512,256]{1,0:T(8,128)} %get-tuple-element.112.refs_0_, f32[512,512]{1,0:T(8,128)} %convert_add_fusion.refs_1_, f32[512,512]{1,0:T(8,128)} %get-tuple-element.122.refs_2_, ...), custom_call_target="tpu_custom_call" | custom-call | flops 17999998976 | bytes 36000000 | tf_op jit(solution)/shard_map/pallas_call | solution.py:106
  348.5 6.5 %collective-permute-done.35.refs_2_ = bf16[256,1024]{1,0:T(8,128)(2,1)S(1)} collective-permute-done((bf16[256,1024]{1,0:T(8,128)(2,1)S(1)}, bf16[256,1024]{1,0:T(8,128)(2,1)S(1)}, u32[]{:S(2)}, u32[]{:S(2)}) %collective-permute-start.35) | collective-permute-done | bytes 524320 | tf_op jit(solution)/shard_map/ppermute | solution.py:41
  362.7 7.7 %shard_map.182 = (bf16[512,1024]{1,0:T(8,128)(2,1)}, bf16[256,1024]{1,0:T(8,128)(2,1)}, f32[256,1024]{1,0:T(8,128)}) custom-call(bf16[256,1024]{1,0:T(8,128)(2,1)} %get-tuple-element.127.refs_0_.refs_2_, bf16[256,1024]{1,0:T(8,128)(2,1)} %copy-done.42, f32[512,1024]{1,0:T(8,128)} %get-tuple-element.128.refs_2_, ...), custom_call_target="tpu_custom_call" | custom-call | flops 8999999488 | bytes 18000000 | tf_op jit(solution)/shard_map/pallas_call | solution.py:106
  375.8 8.7 %shard_map.183.refs_0_ = bf16[1024,2048]{1,0:T(8,128)(2,1)} custom-call(bf16[256,1024]{1,0:T(8,128)(2,1)} %get-tuple-element.90.refs_0_, bf16[256,1024]{1,0:T(8,128)(2,1)} %copy-done.27, bf16[256,1024]{1,0:T(8,128)(2,1)} %get-tuple-element.127.refs_0_.refs_2_, bf16[256,1024]{1,0:T(8,128)(2,1)} %copy-done.42, bf16[512,1024]{1,0:T(8,128)(2,1)} %get-tuple-element.131.refs_4_, ...), custom_call_target="tpu_custom_call" | custom-call | flops 8999999488 | bytes 18000000 | tf_op jit(solution)/shard_map/pallas_call | solution.py:106
  397.8 7.6 %shard_map.187 = (f32[512,256]{1,0:T(8,128)}, f32[1,512,512]{2,1,0:T(8,128)}) custom-call(s32[1]{0:T(128)} %constant.50.clone.1.refs_0_, s32[1]{0:T(128)} %dynamic_slice.13.refs_1_, s32[3]{0:T(128)} %pad_add_fusion.refs_0_.refs_2_, bf16[512,256]{1,0:T(8,128)(2,1)} %get-tuple-element.85.refs_3_, bf16[512,256]{1,0:T(8,128)(2,1)} %get-tuple-element.135.refs_4_.refs_5_, ...), custom_call_target="tpu_custom_call" | custom-call | flops 4499999744 | bytes 9000000 | tf_op jit(solution)/shard_map/pallas_call | solution.py:106
  405.4 7.6 %shard_map.188 = (bf16[512,768]{1,0:T(8,128)(2,1)}, bf16[256,1024]{1,0:T(8,128)(2,1)}, f32[256,1024]{1,0:T(8,128)}, f32[2,256]{1,0:T(2,128)}, f32[1,1024]{1,0:T(1,128)}) custom-call(f32[512,256]{1,0:T(8,128)} %get-tuple-element.138.refs_0_, f32[512,512]{1,0:T(8,128)} %bitcast.19, f32[512,512]{1,0:T(8,128)} %get-tuple-element.140.refs_2_, ...), custom_call_target="tpu_custom_call" | custom-call | flops 17999998976 | bytes 36000000 | tf_op jit(solution)/shard_map/pallas_call | solution.py:106
  424.1 6.5 %collective-permute-done.41.refs_3_.refs_2_ = bf16[256,1024]{1,0:T(8,128)(2,1)S(1)} collective-permute-done((bf16[256,1024]{1,0:T(8,128)(2,1)S(1)}, bf16[256,1024]{1,0:T(8,128)(2,1)S(1)}, u32[]{:S(2)}, u32[]{:S(2)}) %collective-permute-start.41) | collective-permute-done | bytes 524320 | tf_op jit(solution)/shard_map/ppermute | solution.py:41
  442.8 12.4 %all_to_all.10 = f32[8,16,128]{2,1,0:T(8,128)S(1)} all-to-all(f32[8,16,128]{2,1,0:T(8,128)} %shard_map.195), channel_id=1, replica_groups=mesh['frame'=8,'row'=4] {'frame'}, dimensions={0} | all-to-all | bytes 131072 | tf_op jit(solution)/shard_map/all_to_all | solution.py:1246
  462.8 10.1 %reduce-scatter.14.cloned.1.call-done.refs_0_ = bf16[128,1024]{1,0:T(8,128)(2,1)} async-done(((bf16[1024,1024]{1,0:T(8,128)(2,1)}), bf16[128,1024]{1,0:T(8,128)(2,1)}) %reduce-scatter.14.cloned.1.call-update) | async-done | bytes 262160 | tf_op jit(solution)/shard_map/reduce_scatter | solution.py:1008
  (289 shorter events, 240.5 us)
Async XLA Ops:
  7.2 42.4 %all-gather.5.cloned.1.call-start = ((), (), s32[]{:S(2)}) async-start(), calls=%async_computation.7 | async-start | bytes 2359296 | tf_op jit(solution)/shard_map/all_gather | solution.py:1005
  9.9 15.0 %all-to-all-start = ((f32[8,16,128]{2,1,0:T(8,128)}), f32[8,16,128]{2,1,0:T(8,128)S(1)}, u32[]{:S(2)}, u32[]{:S(2)}) async-start(f32[8,16,128]{2,1,0:T(8,128)} %broadcast_in_dim.14), calls=%async_computation | async-start | bytes 131072 | tf_op jit(solution)/shard_map/all_to_all | solution.py:1017
  17.1 78.3 %all-gather.7.cloned.1.call-start = ((), (), s32[]{:S(2)}) async-start(), calls=%async_computation.8 | async-start | bytes 4718592 | tf_op jit(solution)/shard_map/all_gather | solution.py:1005
  17.2 19.1 %collective-permute-start = (bf16[128,1024]{1,0:T(8,128)(2,1)S(1)}, bf16[128,1024]{1,0:T(8,128)(2,1)S(1)}, u32[]{:S(2)}, u32[]{:S(2)}) collective-permute-start(bf16[128,1024]{1,0:T(8,128)(2,1)S(1)} %copy-done.45), channel_id=1, source_target_pairs={{2,0},{3,1},{0,2},{1,3},{6,4},{7,5},{4,6},{5,7},{10,8},{11,9},{8,1... | collective-permute-start | bytes 786440 | tf_op jit(solution)/shard_map/ppermute | solution.py:41
  21.3 109.7 %all-gather.9.cloned.1.call-start = ((), (), s32[]{:S(2)}) async-start(), calls=%async_computation.9 | async-start | bytes 2359296 | tf_op jit(solution)/shard_map/all_gather | solution.py:1005
  36.3 13.2 %collective-permute-start.3 = (bf16[256,1024]{1,0:T(8,128)(2,1)}, bf16[256,1024]{1,0:T(8,128)(2,1)S(1)}, u32[]{:S(2)}, u32[]{:S(2)}) collective-permute-start(bf16[256,1024]{1,0:T(8,128)(2,1)} %shard_map.157.refs_4_.refs_2_.refs_0_), channel_id=1, source_target_pairs={{1,0},{0,1},{3,2},{2,3},{5,4},{4,5},{7,6},{6,7},{9,8},{8,9},{11,10... | collective-permute-start | bytes 1572872 | tf_op jit(solution)/shard_map/ppermute | solution.py:41
  65.6 14.1 %collective-permute-start.5 = (bf16[256,1024]{1,0:T(8,128)(2,1)S(1)}, bf16[256,1024]{1,0:T(8,128)(2,1)S(1)}, u32[]{:S(2)}, u32[]{:S(2)}) collective-permute-start(bf16[256,1024]{1,0:T(8,128)(2,1)S(1)} %add_convert_fusion.10.refs_1_.refs_4_), channel_id=1, source_target_pairs={{2,0},{3,1},{0,2},{1,3},{6,4},{7,5},{4,6},{5,7},{10,8},{11,9},{8,1... | collective-permute-start | bytes 1572872 | tf_op jit(solution)/shard_map/ppermute | solution.py:41
  84.9 137.4 %all-gather.11.cloned.1.call-start = ((), (), s32[]{:S(2)}) async-start(), calls=%async_computation.10 | async-start | bytes 4718592 | tf_op jit(solution)/shard_map/all_gather | solution.py:1005
  106.3 14.0 %collective-permute-start.8 = (bf16[256,1024]{1,0:T(8,128)(2,1)S(1)}, bf16[256,1024]{1,0:T(8,128)(2,1)S(1)}, u32[]{:S(2)}, u32[]{:S(2)}) collective-permute-start(bf16[256,1024]{1,0:T(8,128)(2,1)S(1)} %add_convert_fusion.9.refs_1_.refs_5_), channel_id=1, source_target_pairs={{2,0},{3,1},{0,2},{1,3},{6,4},{7,5},{4,6},{5,7},{10,8},{11,9},{8,1... | collective-permute-start | bytes 1572872 | tf_op jit(solution)/shard_map/ppermute | solution.py:41
  172.9 140.6 %reduce-scatter.6.cloned.1.call-start = ((), (), s32[]{:S(2)}) async-start(), calls=%async_computation.11 | async-start | bytes 2359296 | tf_op jit(solution)/shard_map/reduce_scatter | solution.py:1008
  201.4 14.0 %collective-permute-start.19 = (bf16[256,1024]{1,0:T(8,128)(2,1)S(1)}, bf16[256,1024]{1,0:T(8,128)(2,1)S(1)}, u32[]{:S(2)}, u32[]{:S(2)}) collective-permute-start(bf16[256,1024]{1,0:T(8,128)(2,1)S(1)} %add_convert_fusion.8.refs_1_.refs_4_), channel_id=1, source_target_pairs={{2,0},{3,1},{0,2},{1,3},{6,4},{7,5},{4,6},{5,7},{10,8},{11,9},{8,1... | collective-permute-start | bytes 1572872 | tf_op jit(solution)/shard_map/ppermute | solution.py:41
  236.2 14.0 %collective-permute-start.23 = (bf16[256,1024]{1,0:T(8,128)(2,1)S(1)}, bf16[256,1024]{1,0:T(8,128)(2,1)S(1)}, u32[]{:S(2)}, u32[]{:S(2)}) collective-permute-start(bf16[256,1024]{1,0:T(8,128)(2,1)S(1)} %add_convert_fusion.7.refs_3_.refs_1_), channel_id=1, source_target_pairs={{2,0},{3,1},{0,2},{1,3},{6,4},{7,5},{4,6},{5,7},{10,8},{11,9},{8,1... | collective-permute-start | bytes 1572872 | tf_op jit(solution)/shard_map/ppermute | solution.py:41
  242.9 112.1 %reduce-scatter.8.cloned.1.call-start = ((), (), s32[]{:S(2)}) async-start(), calls=%async_computation.12 | async-start | bytes 2359296 | tf_op jit(solution)/shard_map/reduce_scatter | solution.py:1008
  285.3 13.2 %collective-permute-start.31 = (bf16[512,512]{1,0:T(8,128)(2,1)S(1)}, bf16[512,512]{1,0:T(8,128)(2,1)S(1)}, u32[]{:S(2)}, u32[]{:S(2)}) collective-permute-start(bf16[512,512]{1,0:T(8,128)(2,1)S(1)} %pad_maximum_fusion.1), channel_id=1, source_target_pairs={{8,0},{16,8},{24,16},{28,24},{20,28},{12,20},{4,12},{0,4},{9,1},{1... | collective-permute-start | bytes 1572872 | tf_op jit(solution)/shard_map/ppermute | solution.py:37
  287.4 12.9 %collective-permute-start.27 = (bf16[512,512]{1,0:T(8,128)(2,1)S(1)}, bf16[512,512]{1,0:T(8,128)(2,1)S(1)}, u32[]{:S(2)}, u32[]{:S(2)}) collective-permute-start(bf16[512,512]{1,0:T(8,128)(2,1)S(1)} %pad_maximum_fusion), channel_id=1, source_target_pairs={{4,0},{0,8},{8,16},{16,24},{24,28},{28,20},{20,12},{12,4},{5,1},{1... | collective-permute-start | bytes 1572872 | tf_op jit(solution)/shard_map/ppermute | solution.py:37
  288.2 13.0 %collective-permute-start.21 = (bf16[256,1024]{1,0:T(8,128)(2,1)S(1)}, bf16[256,1024]{1,0:T(8,128)(2,1)S(1)}, u32[]{:S(2)}, u32[]{:S(2)}) collective-permute-start(bf16[256,1024]{1,0:T(8,128)(2,1)S(1)} %copy-done.36), channel_id=1, source_target_pairs={{1,0},{0,1},{3,2},{2,3},{5,4},{4,5},{7,6},{6,7},{9,8},{8,9},{11,10... | collective-permute-start | bytes 1572872 | tf_op jit(solution)/shard_map/ppermute | solution.py:41
  311.3 14.1 %collective-permute-start.33 = (bf16[512,512]{1,0:T(8,128)(2,1)S(1)}, bf16[512,512]{1,0:T(8,128)(2,1)S(1)}, u32[]{:S(2)}, u32[]{:S(2)}) collective-permute-start(bf16[512,512]{1,0:T(8,128)(2,1)S(1)} %add_convert_fusion.3.refs_2_), channel_id=1, source_target_pairs={{8,0},{16,8},{24,16},{28,24},{20,28},{12,20},{4,12},{0,4},{9,1},{1... | collective-permute-start | bytes 1572872 | tf_op jit(solution)/shard_map/ppermute | solution.py:37
  312.7 15.9 %collective-permute-start.29 = (bf16[512,512]{1,0:T(8,128)(2,1)S(1)}, bf16[512,512]{1,0:T(8,128)(2,1)S(1)}, u32[]{:S(2)}, u32[]{:S(2)}) collective-permute-start(bf16[512,512]{1,0:T(8,128)(2,1)S(1)} %add_convert_fusion.5.refs_1_), channel_id=1, source_target_pairs={{4,0},{0,8},{8,16},{16,24},{24,28},{28,20},{20,12},{12,4},{5,1},{1... | collective-permute-start | bytes 1572872 | tf_op jit(solution)/shard_map/ppermute | solution.py:37
  313.6 74.4 %reduce-scatter.10.cloned.1.call-start = ((), (), s32[]{:S(2)}) async-start(), calls=%async_computation.13 | async-start | bytes 2359296 | tf_op jit(solution)/shard_map/reduce_scatter | solution.py:1008
  340.8 14.2 %collective-permute-start.35 = (bf16[256,1024]{1,0:T(8,128)(2,1)S(1)}, bf16[256,1024]{1,0:T(8,128)(2,1)S(1)}, u32[]{:S(2)}, u32[]{:S(2)}) collective-permute-start(bf16[256,1024]{1,0:T(8,128)(2,1)S(1)} %add_convert_fusion.2.refs_6_.refs_1_), channel_id=1, source_target_pairs={{2,0},{3,1},{0,2},{1,3},{6,4},{7,5},{4,6},{5,7},{10,8},{11,9},{8,1... | collective-permute-start | bytes 1572872 | tf_op jit(solution)/shard_map/ppermute | solution.py:41
  355.9 80.9 %reduce-scatter.12.cloned.1.call-start = ((), (), s32[]{:S(2)}) async-start(), calls=%async_computation.14 | async-start | bytes 4718592 | tf_op jit(solution)/shard_map/reduce_scatter | solution.py:1008
  373.9 14.1 %collective-permute-start.38 = (bf16[256,1024]{1,0:T(8,128)(2,1)S(1)}, bf16[256,1024]{1,0:T(8,128)(2,1)S(1)}, u32[]{:S(2)}, u32[]{:S(2)}) collective-permute-start(bf16[256,1024]{1,0:T(8,128)(2,1)S(1)} %add_convert_fusion.1.refs_6_.refs_1_), channel_id=1, source_target_pairs={{2,0},{3,1},{0,2},{1,3},{6,4},{7,5},{4,6},{5,7},{10,8},{11,9},{8,1... | collective-permute-start | bytes 1572872 | tf_op jit(solution)/shard_map/ppermute | solution.py:41
  388.8 84.1 %reduce-scatter.14.cloned.1.call-start = ((), (), s32[]{:S(2)}) async-start(), calls=%async_computation.15 | async-start | bytes 2359296 | tf_op jit(solution)/shard_map/reduce_scatter | solution.py:1008
  416.6 14.0 %collective-permute-start.41 = (bf16[256,1024]{1,0:T(8,128)(2,1)S(1)}, bf16[256,1024]{1,0:T(8,128)(2,1)S(1)}, u32[]{:S(2)}, u32[]{:S(2)}) collective-permute-start(bf16[256,1024]{1,0:T(8,128)(2,1)S(1)} %add_convert_fusion.refs_2_.refs_6_), channel_id=1, source_target_pairs={{2,0},{3,1},{0,2},{1,3},{6,4},{7,5},{4,6},{5,7},{10,8},{11,9},{8,1... | collective-permute-start | bytes 1572872 | tf_op jit(solution)/shard_map/ppermute | solution.py:41
  (81 other events, 467.0 us)
Sparse Core Ops, SparseCore 0:
  10.1 36.6 all-gather.4
  48.3 46.9 all-gather.6
  97.5 33.3 all-gather.8
  173.1 49.2 all-gather.10
  243.0 31.7 reduce-scatter.5
  313.7 33.8 reduce-scatter.7
  356.0 30.8 reduce-scatter.9
  389.2 47.5 reduce-scatter.11
  439.1 33.8 reduce-scatter.13

commit v8 on v7

--- a/solution.py
+++ b/solution.py
@@ -237,6 +237,16 @@
 def first_norm_kernel(row, h_ref, gains_ref, normed_ref):
     unit, _ = norm_parts(h_ref[...])
     normed_ref[...] = (unit * gains_ref[row : row + 1, :]).astype(BF16)
+
+
+def accumulate(ref, make):
+    @pl.when(pl.program_id(0) == 0)
+    def _():
+        ref[...] = make()
+
+    @pl.when(pl.program_id(0) > 0)
+    def _():
+        ref[...] += make()
 
 
 def add_up(ref, value):
@@ -362,10 +372,6 @@
     grad_ref, other_ref, own_ref, sums_ref, zero_ref, acc = refs[count:]
     step = pl.program_id(0)
 
-    @pl.when(step == 0)
-    def _():
-        acc[...] = jnp.zeros_like(acc)
-
     def normed(incoming, row, place):
         unit, scale = head_parts(mixed_ref[...])
         sums_ref[place : place + 1, :] = jnp.sum(incoming * unit, axis=0, keepdims=True)
@@ -383,7 +389,7 @@
     def _():
         grad_ref[...] = dkv_ref[...].astype(BF16)
 
-    acc[...] += dot_nt(grad_ref[...], joined(pieces))
+    accumulate(acc, lambda: dot_nt(grad_ref[...], joined(pieces)))
 
     @pl.when(step == 2)
     def _():
@@ -438,10 +444,6 @@
     values_ref, active_ref, part_other_ref, part_own_ref, acc = refs[2 * count :]
     step = pl.program_id(0)
 
-    @pl.when(step == 0)
-    def _():
-        acc[...] = jnp.zeros_like(acc)
-
     weight = joined(ups)
     half = own_ref.shape[0]
     for source, start in ((own_ref, 0), (other_ref, half)):
@@ -450,7 +452,7 @@
         active_ref[start : start + half, :] = (
             0.5 * values * (1.0 + lax.erf(values * F32(ROOT_HALF)))
         ).astype(BF16)
-    acc[...] += dot_nt(active_ref[...], joined(downs))
+    accumulate(acc, lambda: dot_nt(active_ref[...], joined(downs)))
 
     @pl.when(step == pl.num_programs(0) - 1)
     def _():
@@ -493,10 +495,6 @@
     grad_ref, part_other_ref, part_own_ref, acc = refs[2 * count :]
     step = pl.program_id(0)
 
-    @pl.when(step == 0)
-    def _():
-        acc[...] = jnp.zeros_like(acc)
-
     weight = joined(downs)
     half = own_ref.shape[0]
     for source, start in ((own_ref, 0), (other_ref, half)):
@@ -506,7 +504,7 @@
             jnp.exp(-0.5 * values * values) * F32(BELL)
         )
         grad_ref[start : start + half, :] = (incoming * slope).astype(BF16)
-    acc[...] += dot_nt(grad_ref[...], joined(ups))
+    accumulate(acc, lambda: dot_nt(grad_ref[...], joined(ups)))
 
     @pl.when(step == pl.num_programs(0) - 1)
     def _():
@@ -543,11 +541,6 @@
     active_ref, grad_ref, part_other_ref, part_own_ref, back_other_ref, back_own_ref, acc, back = refs
     step = pl.program_id(0)
 
-    @pl.when(step == 0)
-    def _():
-        acc[...] = jnp.zeros_like(acc)
-        back[...] = jnp.zeros_like(back)
-
     up, down = up_ref[...], down_ref[...]
     half = own_ref.shape[0]
     for source, g_source, start in ((own_ref, g_own_ref, 0), (other_ref, g_other_ref, half)):
@@ -556,8 +549,8 @@
         active_ref[start : start + half, :] = (values * gate_part).astype(BF16)
         slope = gate_part + values * (jnp.exp(-0.5 * values * values) * F32(BELL))
         grad_ref[start : start + half, :] = (dot_nn(g_source[...], down) * slope).astype(BF16)
-    acc[...] += dot_nt(active_ref[...], down)
-    back[...] += dot_nt(grad_ref[...], up)
+    accumulate(acc, lambda: dot_nt(active_ref[...], down))
+    accumulate(back, lambda: dot_nt(grad_ref[...], up))
 
     @pl.when(step == pl.num_programs(0) - 1)
     def _():

time: 491 us -> 493 us (level)
  transfers between devices with their start and end apart: 54 -> 54, of which waited for: 42 -> 41; matrix products, arithmetic and copies ran while one was open for 5% -> 5% of each run, Pallas kernels for 33% -> 33%
where the time goes in v8:
time: 493 us; the launch traced here: 483 us
  waiting for transfers between devices  193 us (39%)
  Pallas kernels  182 us (37%)
  starting transfers between devices  40.6 us (8%)
  local copies, waits for them, and re-layouts  23.1 us (5%)
  between operations  16.8 us (3%)
  other arithmetic  16 us (3%)
  blocking collectives  12.3 us (2%)
    pallas_call x43, Pallas kernels, run(): pl.pallas_call(body, grid_spec=pltpu.PrefetchScalarGridSpec(num_scalar_pr...  182 us
    ppermute x28, waiting for transfers between devices, row_take(): return lax.ppermute(value, 'row', [(i ^ bit, i) for i in range(4)])  90.7 us
    ppermute x16, waiting for transfers between devices, ring_take(): lax.ppermute(value, 'frame', [(RING[(i + step) % count], RING[i]) for i i...  64.3 us
    all_gather x4, waiting for transfers between devices, gather(): lax.all_gather(packed, 'frame', axis=0, tiled=True, axis_index_groups=fra...  18.8 us
    ppermute x16, starting transfers between devices, ring_take(): lax.ppermute(value, 'frame', [(RING[(i + step) % count], RING[i]) for i i...  17.1 us
    reduce_scatter x5, waiting for transfers between devices, scatter(): lax.psum_scatter(grads, 'frame', scatter_dimension=0, tiled=True, axis_in...  16.8 us
    ppermute x28, starting transfers between devices, row_take(): return lax.ppermute(value, 'row', [(i ^ bit, i) for i in range(4)])  15.6 us
    unnamed x108, local copies, waits for them, and re-layouts  14.8 us
  transfers between devices with their start and end apart: 54, of which 41 were waited for; matrix products, arithmetic and copies ran while one was open for 5% of the time, Pallas kernels for 33%

profile of v8, /device:TPU:0, one launch (start us, length us, event | category | flops | bytes accessed | tf_op | source)
XLA Modules:
  0.0 482.9 jit_solution(10866161825283276801)
XLA Ops:
  9.9 7.3 %all-to-all-start = ((f32[8,16,128]{2,1,0:T(8,128)}), f32[8,16,128]{2,1,0:T(8,128)S(1)}, u32[]{:S(2)}, u32[]{:S(2)}) async-start(f32[8,16,128]{2,1,0:T(8,128)} %broadcast_in_dim.14), calls=%async_computation | async-start | bytes 131072 | tf_op jit(solution)/shard_map/all_to_all | solution.py:1010
  67.2 12.4 %collective-permute-done.5.refs_2_.refs_5_ = bf16[256,1024]{1,0:T(8,128)(2,1)S(1)} collective-permute-done((bf16[256,1024]{1,0:T(8,128)(2,1)S(1)}, bf16[256,1024]{1,0:T(8,128)(2,1)S(1)}, u32[]{:S(2)}, u32[]{:S(2)}) %collective-permute-start.5) | collective-permute-done | bytes 524320 | tf_op jit(solution)/shard_map/ppermute | solution.py:41
  85.3 10.1 %all-gather.7.cloned.1.call-done.refs_2_.refs_3_.refs_4_ = bf16[1024,2048]{1,0:T(8,128)(2,1)} async-done(((bf16[128,2048]{1,0:T(8,128)(2,1)}), bf16[1024,2048]{1,0:T(8,128)(2,1)}) %all-gather.7.cloned.1.call-update) | async-done | bytes 4194320 | tf_op jit(solution)/shard_map/all_gather | solution.py:998
  95.4 7.6 %shard_map.162 = (f32[512,1024]{1,0:T(8,128)}, bf16[512,1024]{1,0:T(8,128)(2,1)}, bf16[256,1024]{1,0:T(8,128)(2,1)}, f32[256,1024]{1,0:T(8,128)}) custom-call(bf16[256,1024]{1,0:T(8,128)(2,1)} %get-tuple-element.90.refs_0_, bf16[256,1024]{1,0:T(8,128)(2,1)} %copy-done.27, bf16[1024,2048]{1,0:T(8,128)(2,1)} %all-gather.7.cloned.1.call-done.refs_2_.refs_3_.refs_4_, ...), custom_call_target="tpu_custom_call" | custom-call | flops 20999999488 | bytes 42000000 | tf_op jit(solution)/shard_map/pallas_call | solution.py:106
  108.1 12.5 %collective-permute-done.8.refs_2_.refs_6_ = bf16[256,1024]{1,0:T(8,128)(2,1)S(1)} collective-permute-done((bf16[256,1024]{1,0:T(8,128)(2,1)S(1)}, bf16[256,1024]{1,0:T(8,128)(2,1)S(1)}, u32[]{:S(2)}, u32[]{:S(2)}) %collective-permute-start.8) | collective-permute-done | bytes 524320 | tf_op jit(solution)/shard_map/ppermute | solution.py:41
  124.1 6.8 %all-gather.9.cloned.1.call-done.refs_2_.refs_13_.refs_17_.refs_7_ = bf16[1024,1024]{1,0:T(8,128)(2,1)} async-done(((bf16[128,1024]{1,0:T(8,128)(2,1)}), bf16[1024,1024]{1,0:T(8,128)(2,1)}) %all-gather.9.cloned.1.call-update) | async-done | bytes 2097168 | tf_op jit(solution)/shard_map/all_gather | solution.py:998
  139.1 10.3 %collective-permute-done.14.refs_12_.refs_16_ = bf16[512,512]{1,0:T(8,128)(2,1)S(1)} collective-permute-done((bf16[512,512]{1,0:T(8,128)(2,1)}, bf16[512,512]{1,0:T(8,128)(2,1)S(1)}, u32[]{:S(2)}, u32[]{:S(2)}) %collective-permute-start.14) | collective-permute-done | bytes 524320 | tf_op jit(solution)/shard_map/ppermute | solution.py:37
  151.4 10.1 %collective-permute-done.15.refs_11_.refs_15_ = bf16[512,512]{1,0:T(8,128)(2,1)S(1)} collective-permute-done((bf16[512,512]{1,0:T(8,128)(2,1)S(1)}, bf16[512,512]{1,0:T(8,128)(2,1)S(1)}, u32[]{:S(2)}, u32[]{:S(2)}) %collective-permute-start.15) | collective-permute-done | bytes 524320 | tf_op jit(solution)/shard_map/ppermute | solution.py:37
  180.4 6.3 %collective-permute-done.13.refs_8_.refs_12_ = bf16[256,512]{1,0:T(8,128)(2,1)S(1)} collective-permute-done((bf16[256,512]{1,0:T(8,128)(2,1)S(1)}, bf16[256,512]{1,0:T(8,128)(2,1)S(1)}, u32[]{:S(2)}, u32[]{:S(2)}) %collective-permute-start.13) | collective-permute-done | bytes 262176 | tf_op jit(solution)/shard_map/ppermute | solution.py:37
  187.4 10.0 %shard_map.166 = (bf16[512,256]{1,0:T(8,128)(2,1)}, f32[8,512]{1,0:T(8,128)}, bf16[256,1024]{1,0:T(8,128)(2,1)}, f32[256,1024]{1,0:T(8,128)}) custom-call(s32[4]{0:T(128)} %bitcast.22, s32[8]{0:T(128)} %gather_fusion.1, s32[3]{0:T(128)} %pad_add_fusion.refs_0_.refs_2_, bf16[512,256]{1,0:T(8,128)(2,1)} %get-tuple-element.95.refs_3_, ...), custom_call_target="tpu_custom_call" | custom-call | flops 32999999488 | bytes 66000000 | tf_op jit(solution)/shard_map/pallas_call | solution.py:106
  202.3 12.7 %collective-permute-done.19.refs_2_.refs_5_ = bf16[256,1024]{1,0:T(8,128)(2,1)S(1)} collective-permute-done((bf16[256,1024]{1,0:T(8,128)(2,1)S(1)}, bf16[256,1024]{1,0:T(8,128)(2,1)S(1)}, u32[]{:S(2)}, u32[]{:S(2)}) %collective-permute-start.19) | collective-permute-done | bytes 524320 | tf_op jit(solution)/shard_map/ppermute | solution.py:41
  222.4 11.3 %shard_map.170 = (bf16[512,1024]{1,0:T(8,128)(2,1)}, bf16[512,1024]{1,0:T(8,128)(2,1)}, bf16[256,1024]{1,0:T(8,128)(2,1)}, f32[256,1024]{1,0:T(8,128)}, bf16[256,1024]{1,0:T(8,128)(2,1)}, /*index=5*/f32[256,1024]{1,0:T(8,128)}) custom-call(bf16[256,1024]{1,0:T(8,128)(2,1)} %get-tuple-element.100.refs_0_, bf16[256,1024]{1,0:T(8,128)(2,1)} %copy-done.41, ...), custom_call_target="tpu_custom_call" | custom-call | flops 30000001024 | bytes 60000000 | tf_op jit(solution)/shard_map/pallas_call | solution.py:106
  259.1 17.6 %shard_map.176 = (f32[512,256]{1,0:T(8,128)}, bf16[512,512]{1,0:T(8,128)(2,1)}, bf16[512,512]{1,0:T(8,128)(2,1)}, bf16[512,512]{1,0:T(8,128)(2,1)}, bf16[512,512...) custom-call(s32[4]{0:T(128)} %bitcast.23, ...), custom_call_target="tpu_custom_call" | custom-call | flops 8999999488 | bytes 18000000 | tf_op jit(solution)/shard_map/pallas_call | solution.py:106
  289.4 10.5 %collective-permute-done.31 = bf16[512,512]{1,0:T(8,128)(2,1)S(1)} collective-permute-done((bf16[512,512]{1,0:T(8,128)(2,1)S(1)}, bf16[512,512]{1,0:T(8,128)(2,1)S(1)}, u32[]{:S(2)}, u32[]{:S(2)}) %collective-permute-start.31) | collective-permute-done | bytes 524320 | tf_op jit(solution)/shard_map/ppermute | solution.py:37
  330.7 7.4 %shard_map.177 = (bf16[512,768]{1,0:T(8,128)(2,1)}, bf16[256,1024]{1,0:T(8,128)(2,1)}, f32[256,1024]{1,0:T(8,128)}, f32[2,256]{1,0:T(2,128)}, f32[1,1024]{1,0:T(1,128)}) custom-call(f32[512,256]{1,0:T(8,128)} %get-tuple-element.112.refs_0_, f32[512,512]{1,0:T(8,128)} %convert_add_fusion.refs_1_, f32[512,512]{1,0:T(8,128)} %get-tuple-element.122.refs_2_, ...), custom_call_target="tpu_custom_call" | custom-call | flops 17999998976 | bytes 36000000 | tf_op jit(solution)/shard_map/pallas_call | solution.py:106
  348.4 7.3 %collective-permute-done.35.refs_2_ = bf16[256,1024]{1,0:T(8,128)(2,1)S(1)} collective-permute-done((bf16[256,1024]{1,0:T(8,128)(2,1)S(1)}, bf16[256,1024]{1,0:T(8,128)(2,1)S(1)}, u32[]{:S(2)}, u32[]{:S(2)}) %collective-permute-start.35) | collective-permute-done | bytes 524320 | tf_op jit(solution)/shard_map/ppermute | solution.py:41
  363.4 7.9 %shard_map.182 = (bf16[512,1024]{1,0:T(8,128)(2,1)}, bf16[256,1024]{1,0:T(8,128)(2,1)}, f32[256,1024]{1,0:T(8,128)}) custom-call(bf16[256,1024]{1,0:T(8,128)(2,1)} %get-tuple-element.127.refs_0_.refs_2_, bf16[256,1024]{1,0:T(8,128)(2,1)} %copy-done.42, f32[512,1024]{1,0:T(8,128)} %get-tuple-element.128.refs_2_, ...), custom_call_target="tpu_custom_call" | custom-call | flops 8999999488 | bytes 18000000 | tf_op jit(solution)/shard_map/pallas_call | solution.py:106
  375.8 8.7 %shard_map.183.refs_0_ = bf16[1024,2048]{1,0:T(8,128)(2,1)} custom-call(bf16[256,1024]{1,0:T(8,128)(2,1)} %get-tuple-element.90.refs_0_, bf16[256,1024]{1,0:T(8,128)(2,1)} %copy-done.27, bf16[256,1024]{1,0:T(8,128)(2,1)} %get-tuple-element.127.refs_0_.refs_2_, bf16[256,1024]{1,0:T(8,128)(2,1)} %copy-done.42, bf16[512,1024]{1,0:T(8,128)(2,1)} %get-tuple-element.131.refs_4_, ...), custom_call_target="tpu_custom_call" | custom-call | flops 8999999488 | bytes 18000000 | tf_op jit(solution)/shard_map/pallas_call | solution.py:106
  398.7 7.6 %shard_map.187 = (f32[512,256]{1,0:T(8,128)}, f32[1,512,512]{2,1,0:T(8,128)}) custom-call(s32[1]{0:T(128)} %constant.50.clone.1.refs_0_, s32[1]{0:T(128)} %dynamic_slice.13.refs_1_, s32[3]{0:T(128)} %pad_add_fusion.refs_0_.refs_2_, bf16[512,256]{1,0:T(8,128)(2,1)} %get-tuple-element.85.refs_3_, bf16[512,256]{1,0:T(8,128)(2,1)} %get-tuple-element.135.refs_4_.refs_5_, ...), custom_call_target="tpu_custom_call" | custom-call | flops 4499999744 | bytes 9000000 | tf_op jit(solution)/shard_map/pallas_call | solution.py:106
  406.3 7.5 %shard_map.188 = (bf16[512,768]{1,0:T(8,128)(2,1)}, bf16[256,1024]{1,0:T(8,128)(2,1)}, f32[256,1024]{1,0:T(8,128)}, f32[2,256]{1,0:T(2,128)}, f32[1,1024]{1,0:T(1,128)}) custom-call(f32[512,256]{1,0:T(8,128)} %get-tuple-element.138.refs_0_, f32[512,512]{1,0:T(8,128)} %bitcast.19, f32[512,512]{1,0:T(8,128)} %get-tuple-element.140.refs_2_, ...), custom_call_target="tpu_custom_call" | custom-call | flops 17999998976 | bytes 36000000 | tf_op jit(solution)/shard_map/pallas_call | solution.py:106
  424.1 7.3 %collective-permute-done.41.refs_3_.refs_2_ = bf16[256,1024]{1,0:T(8,128)(2,1)S(1)} collective-permute-done((bf16[256,1024]{1,0:T(8,128)(2,1)S(1)}, bf16[256,1024]{1,0:T(8,128)(2,1)S(1)}, u32[]{:S(2)}, u32[]{:S(2)}) %collective-permute-start.41) | collective-permute-done | bytes 524320 | tf_op jit(solution)/shard_map/ppermute | solution.py:41
  431.4 6.7 %reduce-scatter.12.cloned.1.call-done.refs_1_.refs_0_ = bf16[128,2048]{1,0:T(8,128)(2,1)} async-done(((bf16[1024,2048]{1,0:T(8,128)(2,1)}), bf16[128,2048]{1,0:T(8,128)(2,1)}) %reduce-scatter.12.cloned.1.call-update) | async-done | bytes 524304 | tf_op jit(solution)/shard_map/reduce_scatter | solution.py:1001
  444.1 12.3 %all_to_all.10 = f32[8,16,128]{2,1,0:T(8,128)S(1)} all-to-all(f32[8,16,128]{2,1,0:T(8,128)} %shard_map.195), channel_id=1, replica_groups=mesh['frame'=8,'row'=4] {'frame'}, dimensions={0} | all-to-all | bytes 131072 | tf_op jit(solution)/shard_map/all_to_all | solution.py:1239
  464.1 10.1 %reduce-scatter.14.cloned.1.call-done.refs_0_ = bf16[128,1024]{1,0:T(8,128)(2,1)} async-done(((bf16[1024,1024]{1,0:T(8,128)(2,1)}), bf16[128,1024]{1,0:T(8,128)(2,1)}) %reduce-scatter.14.cloned.1.call-update) | async-done | bytes 262160 | tf_op jit(solution)/shard_map/reduce_scatter | solution.py:1001
  (289 shorter events, 238.0 us)
Async XLA Ops:
  7.2 42.4 %all-gather.5.cloned.1.call-start = ((), (), s32[]{:S(2)}) async-start(), calls=%async_computation.7 | async-start | bytes 2359296 | tf_op jit(solution)/shard_map/all_gather | solution.py:998
  9.9 15.0 %all-to-all-start = ((f32[8,16,128]{2,1,0:T(8,128)}), f32[8,16,128]{2,1,0:T(8,128)S(1)}, u32[]{:S(2)}, u32[]{:S(2)}) async-start(f32[8,16,128]{2,1,0:T(8,128)} %broadcast_in_dim.14), calls=%async_computation | async-start | bytes 131072 | tf_op jit(solution)/shard_map/all_to_all | solution.py:1010
  17.1 78.3 %all-gather.7.cloned.1.call-start = ((), (), s32[]{:S(2)}) async-start(), calls=%async_computation.8 | async-start | bytes 4718592 | tf_op jit(solution)/shard_map/all_gather | solution.py:998
  17.2 19.1 %collective-permute-start = (bf16[128,1024]{1,0:T(8,128)(2,1)S(1)}, bf16[128,1024]{1,0:T(8,128)(2,1)S(1)}, u32[]{:S(2)}, u32[]{:S(2)}) collective-permute-start(bf16[128,1024]{1,0:T(8,128)(2,1)S(1)} %copy-done.45), channel_id=1, source_target_pairs={{2,0},{3,1},{0,2},{1,3},{6,4},{7,5},{4,6},{5,7},{10,8},{11,9},{8,1... | collective-permute-start | bytes 786440 | tf_op jit(solution)/shard_map/ppermute | solution.py:41
  21.3 109.7 %all-gather.9.cloned.1.call-start = ((), (), s32[]{:S(2)}) async-start(), calls=%async_computation.9 | async-start | bytes 2359296 | tf_op jit(solution)/shard_map/all_gather | solution.py:998
  36.3 13.2 %collective-permute-start.3 = (bf16[256,1024]{1,0:T(8,128)(2,1)}, bf16[256,1024]{1,0:T(8,128)(2,1)S(1)}, u32[]{:S(2)}, u32[]{:S(2)}) collective-permute-start(bf16[256,1024]{1,0:T(8,128)(2,1)} %shard_map.157.refs_4_.refs_2_.refs_0_), channel_id=1, source_target_pairs={{1,0},{0,1},{3,2},{2,3},{5,4},{4,5},{7,6},{6,7},{9,8},{8,9},{11,10... | collective-permute-start | bytes 1572872 | tf_op jit(solution)/shard_map/ppermute | solution.py:41
  65.6 14.1 %collective-permute-start.5 = (bf16[256,1024]{1,0:T(8,128)(2,1)S(1)}, bf16[256,1024]{1,0:T(8,128)(2,1)S(1)}, u32[]{:S(2)}, u32[]{:S(2)}) collective-permute-start(bf16[256,1024]{1,0:T(8,128)(2,1)S(1)} %add_convert_fusion.10.refs_1_.refs_4_), channel_id=1, source_target_pairs={{2,0},{3,1},{0,2},{1,3},{6,4},{7,5},{4,6},{5,7},{10,8},{11,9},{8,1... | collective-permute-start | bytes 1572872 | tf_op jit(solution)/shard_map/ppermute | solution.py:41
  84.9 137.5 %all-gather.11.cloned.1.call-start = ((), (), s32[]{:S(2)}) async-start(), calls=%async_computation.10 | async-start | bytes 4718592 | tf_op jit(solution)/shard_map/all_gather | solution.py:998
  106.5 14.0 %collective-permute-start.8 = (bf16[256,1024]{1,0:T(8,128)(2,1)S(1)}, bf16[256,1024]{1,0:T(8,128)(2,1)S(1)}, u32[]{:S(2)}, u32[]{:S(2)}) collective-permute-start(bf16[256,1024]{1,0:T(8,128)(2,1)S(1)} %add_convert_fusion.9.refs_1_.refs_5_), channel_id=1, source_target_pairs={{2,0},{3,1},{0,2},{1,3},{6,4},{7,5},{4,6},{5,7},{10,8},{11,9},{8,1... | collective-permute-start | bytes 1572872 | tf_op jit(solution)/shard_map/ppermute | solution.py:41
  173.0 141.7 %reduce-scatter.6.cloned.1.call-start = ((), (), s32[]{:S(2)}) async-start(), calls=%async_computation.11 | async-start | bytes 2359296 | tf_op jit(solution)/shard_map/reduce_scatter | solution.py:1001
  200.9 14.0 %collective-permute-start.19 = (bf16[256,1024]{1,0:T(8,128)(2,1)S(1)}, bf16[256,1024]{1,0:T(8,128)(2,1)S(1)}, u32[]{:S(2)}, u32[]{:S(2)}) collective-permute-start(bf16[256,1024]{1,0:T(8,128)(2,1)S(1)} %add_convert_fusion.8.refs_1_.refs_4_), channel_id=1, source_target_pairs={{2,0},{3,1},{0,2},{1,3},{6,4},{7,5},{4,6},{5,7},{10,8},{11,9},{8,1... | collective-permute-start | bytes 1572872 | tf_op jit(solution)/shard_map/ppermute | solution.py:41
  237.3 14.0 %collective-permute-start.23 = (bf16[256,1024]{1,0:T(8,128)(2,1)S(1)}, bf16[256,1024]{1,0:T(8,128)(2,1)S(1)}, u32[]{:S(2)}, u32[]{:S(2)}) collective-permute-start(bf16[256,1024]{1,0:T(8,128)(2,1)S(1)} %add_convert_fusion.7.refs_3_.refs_1_), channel_id=1, source_target_pairs={{2,0},{3,1},{0,2},{1,3},{6,4},{7,5},{4,6},{5,7},{10,8},{11,9},{8,1... | collective-permute-start | bytes 1572872 | tf_op jit(solution)/shard_map/ppermute | solution.py:41
  244.0 111.7 %reduce-scatter.8.cloned.1.call-start = ((), (), s32[]{:S(2)}) async-start(), calls=%async_computation.12 | async-start | bytes 2359296 | tf_op jit(solution)/shard_map/reduce_scatter | solution.py:1001
  286.4 13.4 %collective-permute-start.31 = (bf16[512,512]{1,0:T(8,128)(2,1)S(1)}, bf16[512,512]{1,0:T(8,128)(2,1)S(1)}, u32[]{:S(2)}, u32[]{:S(2)}) collective-permute-start(bf16[512,512]{1,0:T(8,128)(2,1)S(1)} %pad_maximum_fusion.1), channel_id=1, source_target_pairs={{8,0},{16,8},{24,16},{28,24},{20,28},{12,20},{4,12},{0,4},{9,1},{1... | collective-permute-start | bytes 1572872 | tf_op jit(solution)/shard_map/ppermute | solution.py:37
  288.7 12.9 %collective-permute-start.27 = (bf16[512,512]{1,0:T(8,128)(2,1)S(1)}, bf16[512,512]{1,0:T(8,128)(2,1)S(1)}, u32[]{:S(2)}, u32[]{:S(2)}) collective-permute-start(bf16[512,512]{1,0:T(8,128)(2,1)S(1)} %pad_maximum_fusion), channel_id=1, source_target_pairs={{4,0},{0,8},{8,16},{16,24},{24,28},{28,20},{20,12},{12,4},{5,1},{1... | collective-permute-start | bytes 1572872 | tf_op jit(solution)/shard_map/ppermute | solution.py:37
  289.4 13.0 %collective-permute-start.21 = (bf16[256,1024]{1,0:T(8,128)(2,1)S(1)}, bf16[256,1024]{1,0:T(8,128)(2,1)S(1)}, u32[]{:S(2)}, u32[]{:S(2)}) collective-permute-start(bf16[256,1024]{1,0:T(8,128)(2,1)S(1)} %copy-done.36), channel_id=1, source_target_pairs={{1,0},{0,1},{3,2},{2,3},{5,4},{4,5},{7,6},{6,7},{9,8},{8,9},{11,10... | collective-permute-start | bytes 1572872 | tf_op jit(solution)/shard_map/ppermute | solution.py:41
  312.4 14.1 %collective-permute-start.33 = (bf16[512,512]{1,0:T(8,128)(2,1)S(1)}, bf16[512,512]{1,0:T(8,128)(2,1)S(1)}, u32[]{:S(2)}, u32[]{:S(2)}) collective-permute-start(bf16[512,512]{1,0:T(8,128)(2,1)S(1)} %add_convert_fusion.3.refs_2_), channel_id=1, source_target_pairs={{8,0},{16,8},{24,16},{28,24},{20,28},{12,20},{4,12},{0,4},{9,1},{1... | collective-permute-start | bytes 1572872 | tf_op jit(solution)/shard_map/ppermute | solution.py:37
  314.0 15.5 %collective-permute-start.29 = (bf16[512,512]{1,0:T(8,128)(2,1)S(1)}, bf16[512,512]{1,0:T(8,128)(2,1)S(1)}, u32[]{:S(2)}, u32[]{:S(2)}) collective-permute-start(bf16[512,512]{1,0:T(8,128)(2,1)S(1)} %add_convert_fusion.5.refs_1_), channel_id=1, source_target_pairs={{4,0},{0,8},{8,16},{16,24},{24,28},{28,20},{20,12},{12,4},{5,1},{1... | collective-permute-start | bytes 1572872 | tf_op jit(solution)/shard_map/ppermute | solution.py:37
  314.8 74.0 %reduce-scatter.10.cloned.1.call-start = ((), (), s32[]{:S(2)}) async-start(), calls=%async_computation.13 | async-start | bytes 2359296 | tf_op jit(solution)/shard_map/reduce_scatter | solution.py:1001
  341.7 14.0 %collective-permute-start.35 = (bf16[256,1024]{1,0:T(8,128)(2,1)S(1)}, bf16[256,1024]{1,0:T(8,128)(2,1)S(1)}, u32[]{:S(2)}, u32[]{:S(2)}) collective-permute-start(bf16[256,1024]{1,0:T(8,128)(2,1)S(1)} %add_convert_fusion.2.refs_6_.refs_1_), channel_id=1, source_target_pairs={{2,0},{3,1},{0,2},{1,3},{6,4},{7,5},{4,6},{5,7},{10,8},{11,9},{8,1... | collective-permute-start | bytes 1572872 | tf_op jit(solution)/shard_map/ppermute | solution.py:41
  356.5 81.5 %reduce-scatter.12.cloned.1.call-start = ((), (), s32[]{:S(2)}) async-start(), calls=%async_computation.14 | async-start | bytes 4718592 | tf_op jit(solution)/shard_map/reduce_scatter | solution.py:1001
  374.8 14.1 %collective-permute-start.38 = (bf16[256,1024]{1,0:T(8,128)(2,1)S(1)}, bf16[256,1024]{1,0:T(8,128)(2,1)S(1)}, u32[]{:S(2)}, u32[]{:S(2)}) collective-permute-start(bf16[256,1024]{1,0:T(8,128)(2,1)S(1)} %add_convert_fusion.1.refs_6_.refs_1_), channel_id=1, source_target_pairs={{2,0},{3,1},{0,2},{1,3},{6,4},{7,5},{4,6},{5,7},{10,8},{11,9},{8,1... | collective-permute-start | bytes 1572872 | tf_op jit(solution)/shard_map/ppermute | solution.py:41
  389.7 84.5 %reduce-scatter.14.cloned.1.call-start = ((), (), s32[]{:S(2)}) async-start(), calls=%async_computation.15 | async-start | bytes 2359296 | tf_op jit(solution)/shard_map/reduce_scatter | solution.py:1001
  417.4 14.0 %collective-permute-start.41 = (bf16[256,1024]{1,0:T(8,128)(2,1)S(1)}, bf16[256,1024]{1,0:T(8,128)(2,1)S(1)}, u32[]{:S(2)}, u32[]{:S(2)}) collective-permute-start(bf16[256,1024]{1,0:T(8,128)(2,1)S(1)} %add_convert_fusion.refs_2_.refs_6_), channel_id=1, source_target_pairs={{2,0},{3,1},{0,2},{1,3},{6,4},{7,5},{4,6},{5,7},{10,8},{11,9},{8,1... | collective-permute-start | bytes 1572872 | tf_op jit(solution)/shard_map/ppermute | solution.py:41
  (81 other events, 464.0 us)
Sparse Core Ops, SparseCore 0:
  10.1 36.6 all-gather.4
  48.3 46.9 all-gather.6
  97.5 33.3 all-gather.8
  173.1 49.3 all-gather.10
  244.1 32.2 reduce-scatter.5
  315.0 34.0 reduce-scatter.7
  356.7 31.4 reduce-scatter.9
  390.4 47.6 reduce-scatter.11
  440.4 33.7 reduce-scatter.13
